TPU v7x, 32 devices: a whole 2x2x4 slice. The times are simulated.
32 devices in a mesh: blk: 8 (over y, x, core), grp: 4 (over z).
Axes of the slice: x: 2, y: 2, z: 4, core: 2. Of those that a mesh axis runs over, the one named last changes fastest.
Arguments:
- source_embed: bfloat16 [16384, 768], P(('blk', 'grp')), may hold values from -60 to 60
- target_embed: bfloat16 [1024, 768], P('blk'), may hold values from -18 to 18
- target_init: float32 [1024], P('blk'), may hold values from -6 to 6
- source_logw: float32 [16384], P(('blk', 'grp')), may hold values from -2 to 2
- target_logw: float32 [1024], P('blk'), may hold values from -2 to 2
Outputs:
- row_pot: float32 [16384], P(('blk', 'grp'))
- column_pot: float32 [1024], P('blk')
All inputs are finite; a program needn't handle non-finite values.
Results may differ from a plain program's by a relative error of at most 0.0003.
Values may be sent and summed in bfloat16 or wider, within the bound.
No kernel may reach another device: no remote copies, remote signals or barrier semaphores. Data moves between devices by JAX's collectives and lax.ppermute only.
A program may use at most 128 MiB of HBM per device.

v0:
```python
import functools
import math

import jax
import jax.numpy as jnp
from jax import lax
from jax.experimental import pallas as pl
from jax.experimental.pallas import tpu as pltpu
from jax.sharding import Mesh, PartitionSpec as P

ITERS = 2
epsilon = 0.1
inverse_eps = 10.0
LOG2E = math.log2(math.e)
LN2 = math.log(2.0)
LANES = 128
SUBLANES = 8
SPARE = 16


def fetch(array, axis, step, size):
    return lax.ppermute(array, axis, [(i ^ step, i) for i in range(size)])


def after(value, other):
    return lax.optimization_barrier((value, other))[0]


def encode(smalls, depth):
    high = lax.reduce_precision(smalls, 8, 7)
    rest = smalls - high
    middle = lax.reduce_precision(rest, 8, 7)
    parts = jnp.stack([high, middle, rest - middle]).astype(jnp.bfloat16).reshape(-1)
    return jnp.pad(parts, (0, SPARE * depth - parts.shape[0])).reshape(SPARE, depth)


def decode(rows, shape):
    count = 3 * math.prod(shape)
    parts = rows.reshape(-1)[:count].reshape(3, *shape).astype(jnp.float32)
    return (parts[0] + parts[1]) + parts[2]


def doubled(held, step, chips):
    return jnp.concatenate([held, fetch(held, "chip", step, chips)])


def gather_any(array, small, chips):
    pair = jnp.stack([array, fetch(array, "core", 1, 2)])[None]
    smalls = jnp.stack([small, fetch(small, "core", 1, 2)])[None]
    step = 1
    while step < chips:
        pair = doubled(pair, step, chips)
        smalls = doubled(smalls, step, chips)
        step *= 2
    return pair.reshape(-1, array.shape[1]), smalls.reshape(-1, *small.shape)


def gather_square(array, small):
    width, depth = array.shape
    half = width // 2
    sibling = fetch(array, "core", 1, 2)
    over_x = fetch(array, "chip", 1, 4)
    over_y = fetch(array, "chip", 2, 4)
    small_x = fetch(after(small, sibling), "chip", 1, 4)
    rows = encode(jnp.stack([small, small_x]), depth)
    tie = (small_x[0, 0] * 0.0).astype(array.dtype)
    far_a = fetch(jnp.concatenate([over_x[:half], rows]), "chip", 2, 4)
    far_b = fetch(over_y[half:] + tie, "chip", 1, 4)
    sibling_x = fetch(jnp.concatenate([over_x, rows]), "core", 1, 2)
    sibling_y = fetch(over_y, "core", 1, 2)
    sibling_far_a = fetch(far_a, "core", 1, 2)
    sibling_far_b = fetch(far_b, "core", 1, 2)
    pair = (2, 2, width)
    smalls = jnp.stack(
        [
            jnp.concatenate([jnp.stack([small, small_x]), decode(far_a[half:], (2, *small.shape))]),
            jnp.concatenate(
                [
                    decode(sibling_x[width:], (2, *small.shape)),
                    decode(sibling_far_a[half:], (2, *small.shape)),
                ]
            ),
        ],
        axis=1,
    )
    pieces = [
        array,
        sibling,
        over_x,
        sibling_x,
        over_y,
        sibling_y,
        far_a,
        far_b,
        sibling_far_a,
        sibling_far_b,
    ]
    places = [(k * width, width) for k in range(6)]
    places += [(6 * width + k * half, half) for k in range(4)]
    return pieces, places, smalls.reshape(-1, *small.shape)


def as_column(row):
    size = row.shape[1]
    here = lax.broadcasted_iota(jnp.int32, (LANES, LANES), 0)
    there = lax.broadcasted_iota(jnp.int32, (LANES, LANES), 1)
    parts = []
    for start in range(0, size, LANES):
        wide = jnp.broadcast_to(row[:, start : start + LANES], (LANES, LANES))
        parts.append(jnp.sum(jnp.where(here == there, wide, 0.0), axis=1, keepdims=True))
    return jnp.concatenate(parts, axis=0)


def as_row(column):
    size = column.shape[0]
    here = lax.broadcasted_iota(jnp.int32, (LANES, LANES), 0)
    there = lax.broadcasted_iota(jnp.int32, (LANES, LANES), 1)
    parts = []
    for start in range(0, size, LANES):
        wide = jnp.broadcast_to(column[start : start + LANES], (LANES, LANES))
        parts.append(jnp.sum(jnp.where(here == there, wide, 0.0), axis=0, keepdims=True))
    return jnp.concatenate(parts, axis=1)


def half_sweep(scaled, columns, logw, row_pot_of, partial_of):
    rows, width = scaled.shape
    blocks = width // LANES
    chunk = 64
    for start in range(0, rows, chunk):
        at = pl.ds(start, chunk)
        top = None
        for p in range(blocks):
            score = scaled[at, p * LANES : (p + 1) * LANES] + columns[p]
            top = score if top is None else jnp.maximum(top, score)
        top = jnp.max(top, axis=1, keepdims=True)
        total = None
        for p in range(blocks):
            score = scaled[at, p * LANES : (p + 1) * LANES] + columns[p]
            term = jnp.exp2(score - top)
            total = term if total is None else total + term
        total = jnp.sum(total, axis=1, keepdims=True)
        row_pot_of[at, :] = jnp.broadcast_to(
            logw[start : start + chunk] - (top + jnp.log2(total)), (chunk, LANES)
        )
    for p in range(blocks):
        lanes = slice(p * LANES, (p + 1) * LANES)
        top = None
        for start in range(0, rows, chunk):
            at = pl.ds(start, chunk)
            score = scaled[at, lanes] + row_pot_of[at, :]
            score = jnp.max(score.reshape(chunk // SUBLANES, SUBLANES, LANES), axis=0)
            top = score if top is None else jnp.maximum(top, score)
        top = jnp.max(top, axis=0, keepdims=True)
        total = None
        for start in range(0, rows, chunk):
            at = pl.ds(start, chunk)
            term = jnp.exp2(scaled[at, lanes] + row_pot_of[at, :] - top)
            term = jnp.sum(term.reshape(chunk // SUBLANES, SUBLANES, LANES), axis=0)
            total = term if total is None else total + term
        total = jnp.sum(total, axis=0, keepdims=True)
        partial_of(p, top + jnp.log2(total))


def first_kernel(places, factor, *refs):
    count = len(places)
    source, pieces = refs[0], refs[1 : count + 1]
    init, logw, scaled, message, targets, row_pot, ordered = refs[count + 1 :]
    me = lax.axis_index("chip") * 2 + lax.axis_index("core")
    width = targets.shape[0]
    group = 2 * LANES
    for piece, (start, size) in zip(pieces, places):
        targets[start : start + size, :] = piece[0:size, :]
    for start in range(0, width, group):
        product = lax.dot_general(
            source[...],
            targets[start : start + group, :],
            (((1,), (1,)), ((), ())),
            preferred_element_type=jnp.float32,
        )
        scaled[:, start : start + group] = product * factor
    columns = [init[p : p + 1, :] * (inverse_eps * LOG2E) for p in range(width // LANES)]
    logw = as_column(logw[...] * LOG2E)

    def partial_of(p, value):
        ordered[pl.ds(jnp.bitwise_xor(me, p), 1), :] = value

    half_sweep(scaled, columns, logw, row_pot, partial_of)
    message[...] = jnp.broadcast_to(ordered[...][None], message.shape)


def second_kernel(scaled, got, target_logw, logw, row_out, message, row_pot, ordered):
    me = lax.axis_index("chip") * 2 + lax.axis_index("core")
    blocks = scaled.shape[1] // LANES
    copies = message.shape[0] // blocks
    values = got[...]
    top = jnp.max(values, axis=0)
    ordered[...] = top + jnp.log2(jnp.sum(jnp.exp2(values - top[None]), axis=0))
    columns = []
    for p in range(blocks):
        total = ordered[pl.ds(jnp.bitwise_xor(me, p), 1), :]
        columns.append(target_logw[p : p + 1, :] * LOG2E - total)

    def partial_of(p, value):
        at = pl.ds(jnp.bitwise_xor(me, p) * copies, copies)
        message[at, :] = jnp.broadcast_to(value, (copies, LANES))

    half_sweep(scaled, columns, as_column(logw[...] * LOG2E), row_pot, partial_of)
    row_out[...] = as_row(row_pot[:, 0:1]) * (epsilon * LN2)


def lse(values):
    top = jnp.max(values, axis=0)
    return top + jnp.log(jnp.sum(jnp.exp(values - top[None]), axis=0))


def solution(mesh):
    blk, grp = mesh.shape["blk"], mesh.shape["grp"]
    chips = blk // 2
    mesh = Mesh(mesh.devices.reshape(chips, 2, grp), ("chip", "core", "grp"))
    everyone = ("chip", "core", "grp")

    def shards_square(source_embed, target_embed, target_init, source_logw, target_logw):
        rows, depth = source_embed.shape
        width = target_embed.shape[0]
        small = jnp.stack([target_init, target_logw])
        pieces, places, smalls = gather_square(target_embed, small)
        vmem = pl.BlockSpec(memory_space=pltpu.VMEM)
        params = pltpu.CompilerParams(vmem_limit_bytes=24 * 1024 * 1024)
        logw = source_logw.reshape(1, rows)
        scaled, message = pl.pallas_call(
            functools.partial(first_kernel, places, inverse_eps * LOG2E / math.sqrt(depth)),
            out_shape=(
                jax.ShapeDtypeStruct((rows, blk * width), jnp.float32),
                jax.ShapeDtypeStruct((blk * grp, blk, width), jnp.float32),
            ),
            in_specs=[vmem] * (len(pieces) + 3),
            out_specs=(vmem, vmem),
            scratch_shapes=[
                pltpu.VMEM((blk * width, depth), target_embed.dtype),
                pltpu.VMEM((rows, LANES), jnp.float32),
                pltpu.VMEM((blk, width), jnp.float32),
            ],
            compiler_params=params,
        )(source_embed, *pieces, smalls[:, 0], logw)
        got = lax.all_to_all(message, everyone, 0, 0)
        row_pot, message = pl.pallas_call(
            second_kernel,
            out_shape=(
                jax.ShapeDtypeStruct((1, rows), jnp.float32),
                jax.ShapeDtypeStruct((blk * grp, width), jnp.float32),
            ),
            in_specs=[vmem] * 4,
            out_specs=(vmem, vmem),
            scratch_shapes=[
                pltpu.VMEM((rows, LANES), jnp.float32),
                pltpu.VMEM((blk, width), jnp.float32),
            ],
            compiler_params=params,
        )(scaled, got, smalls[:, 1], logw)
        got = lax.all_to_all(message, everyone, 0, 0)
        top = jnp.max(got, axis=0)
        total = top + jnp.log2(jnp.sum(jnp.exp2(got - top[None]), axis=0))
        return row_pot.reshape(rows), epsilon * target_logw - (epsilon * LN2) * total

    def shards_any(source_embed, target_embed, target_init, source_logw, target_logw):
        width, depth = target_embed.shape
        factor = -1.0 / math.sqrt(depth)
        me = lax.axis_index("chip") * 2 + lax.axis_index("core")

        def swap_order(values):
            parts = values.reshape(blk, width)
            step = 1
            while step < blk:
                pairs = parts.reshape(blk // (2 * step), 2, step, width)
                pairs = jnp.where(me & step, pairs[:, ::-1], pairs)
                parts = pairs.reshape(blk, width)
                step *= 2
            return parts

        small = jnp.stack([target_init, target_logw])
        targets, smalls = gather_any(target_embed, small, chips)
        cost = (
            lax.dot_general(
                source_embed, targets, (((1,), (1,)), ((), ())), preferred_element_type=jnp.float32
            )
            * factor
        )
        column_pot, logw_all = smalls[:, 0].reshape(-1), smalls[:, 1].reshape(-1)
        for iteration in range(ITERS):
            scores = (column_pot[None, :] - cost) * inverse_eps
            row_top = jnp.max(scores, axis=1)
            row_sum = jnp.sum(jnp.exp(scores - row_top[:, None]), axis=1)
            row_pot = epsilon * source_logw - epsilon * (row_top + jnp.log(row_sum))
            part = swap_order(lse((row_pot[:, None] - cost) * inverse_eps))
            if iteration < ITERS - 1:
                copies = jnp.broadcast_to(part[None], (blk * grp, blk, width))
                got = lax.all_to_all(copies, everyone, 0, 0)
                total = swap_order(lse(got)).reshape(-1)
                column_pot = epsilon * logw_all - epsilon * total
            else:
                copies = jnp.broadcast_to(part[:, None], (blk, grp, width)).reshape(blk * grp, width)
                got = lax.all_to_all(copies, everyone, 0, 0)
                own_column = epsilon * target_logw - epsilon * lse(got)
        return row_pot, own_column

    rows_spec, blk_spec = P(("chip", "core", "grp")), P(("chip", "core"))
    in_specs = (rows_spec, blk_spec, blk_spec, rows_spec, blk_spec)
    out_specs = (rows_spec, blk_spec)
    shards = shards_square if chips == 4 else shards_any
    return jax.shard_map(shards, mesh=mesh, in_specs=in_specs, out_specs=out_specs, check_vma=False)
```

profile of v0, /device:TPU:0, one launch (start us, length us, event | category | flops | bytes accessed | tf_op | source)
XLA Modules:
  0.0 48.9 jit_solution(11350535529306517686)
XLA Ops:
  0.6 0.0 copy-start.3
  0.6 0.5 %collective-permute-start = (bf16[128,768]{1,0:T(8,128)(2,1)}, bf16[128,768]{1,0:T(8,128)(2,1)S(1)}, u32[]{:S(2)}, u32[]{:S(2)}) collective-permute-start(bf16[128,768]{1,0:T(8,128)(2,1)} %refs_1_.1), channel_id=1, source_target_pairs={{4,0},{0,4},{5,1},{1,5},{6,2},{2,6},{7,3},{3,7},{12,8},{8,12},{13,... | collective-permute-start | bytes 589832 | tf_op jit(solution)/shard_map/ppermute | solution.py:22
  1.2 2.6 %collective-permute-start.1 = (bf16[128,768]{1,0:T(8,128)(2,1)}, bf16[128,768]{1,0:T(8,128)(2,1)S(1)}, u32[]{:S(2)}, u32[]{:S(2)}) collective-permute-start(bf16[128,768]{1,0:T(8,128)(2,1)} %refs_1_.1), channel_id=1, source_target_pairs={{8,0},{0,8},{24,16},{16,24},{9,1},{1,9},{25,17},{17,25},{10,2},{2,... | collective-permute-start | bytes 589832 | tf_op jit(solution)/shard_map/ppermute | solution.py:22
  3.7 1.5 %collective-permute-start.4 = (bf16[128,768]{1,0:T(8,128)(2,1)}, bf16[128,768]{1,0:T(8,128)(2,1)S(1)}, u32[]{:S(2)}, u32[]{:S(2)}) collective-permute-start(bf16[128,768]{1,0:T(8,128)(2,1)} %refs_1_.1), channel_id=1, source_target_pairs={{16,0},{24,8},{0,16},{8,24},{17,1},{25,9},{1,17},{9,25},{18,2},{26... | collective-permute-start | bytes 589832 | tf_op jit(solution)/shard_map/ppermute | solution.py:22
  5.2 0.7 %fusion.4 = (f32[1,1,2,128]{3,2,1,0:T(2,128)S(1)}, f32[2,128]{1,0:T(2,128)S(1)}) fusion(f32[1,128]{1,0:T(1,128)} %bitcast.41, f32[1,128]{1,0:T(1,128)} %bitcast.42), kind=kLoop, calls=%fused_computation.30 | loop fusion | flops 256 | bytes 3072 | tf_op jit(solution)/shard_map/stack | solution.py:65
  5.9 0.0 collective-permute-done.refs_2_
  5.9 0.6 %collective-permute-start.2 = (f32[2,128]{1,0:T(2,128)S(1)}, f32[2,128]{1,0:T(2,128)S(1)}, u32[]{:S(2)}, u32[]{:S(2)}) collective-permute-start(f32[2,128]{1,0:T(2,128)S(1)} %get-tuple-element.7), channel_id=1, source_target_pairs={{8,0},{0,8},{24,16},{16,24},{9,1},{1,9},{25,17},{17,25},{10,2},{2,... | collective-permute-start | bytes 3080 | tf_op jit(solution)/shard_map/ppermute | solution.py:22
  6.5 2.9 %collective-permute-done.1.refs_3_ = bf16[128,768]{1,0:T(8,128)(2,1)S(1)} collective-permute-done((bf16[128,768]{1,0:T(8,128)(2,1)}, bf16[128,768]{1,0:T(8,128)(2,1)S(1)}, u32[]{:S(2)}, u32[]{:S(2)}) %collective-permute-start.1) | collective-permute-done | bytes 196640 | tf_op jit(solution)/shard_map/ppermute | solution.py:22
  9.5 1.5 %collective-permute-done.4.refs_5_ = bf16[128,768]{1,0:T(8,128)(2,1)S(1)} collective-permute-done((bf16[128,768]{1,0:T(8,128)(2,1)}, bf16[128,768]{1,0:T(8,128)(2,1)S(1)}, u32[]{:S(2)}, u32[]{:S(2)}) %collective-permute-start.4) | collective-permute-done | bytes 196640 | tf_op jit(solution)/shard_map/ppermute | solution.py:22
  10.9 0.0 collective-permute-start.5
  10.9 0.0 collective-permute-done.2
  11.0 1.6 %collective-permute-start.6 = (bf16[80,768]{1,0:T(8,128)(2,1)S(1)}, bf16[80,768]{1,0:T(8,128)(2,1)S(1)}, u32[]{:S(2)}, u32[]{:S(2)}) collective-permute-start(bf16[80,768]{1,0:T(8,128)(2,1)S(1)} %pad_maximum_fusion.1), channel_id=1, source_target_pairs={{16,0},{24,8},{0,16},{8,24},{17,1},{25,9},{1,17},{9,25},{18,2},{26... | collective-permute-start | bytes 368648 | tf_op jit(solution)/shard_map/ppermute | solution.py:22
  12.6 0.5 %slice.62 = f32[1,1]{1,0:T(1,128)} slice(f32[2,128]{1,0:T(2,128)S(1)} %collective-permute-done.2), slice={[0:1], [0:1]} | slice | bytes 8 | tf_op jit(solution)/shard_map/slice | solution.py:66
  13.8 0.6 %collective-permute-start.7 = (bf16[64,768]{1,0:T(8,128)(2,1)S(1)}, bf16[64,768]{1,0:T(8,128)(2,1)S(1)}, u32[]{:S(2)}, u32[]{:S(2)}) collective-permute-start(bf16[64,768]{1,0:T(8,128)(2,1)S(1)} %slice_add_fusion), channel_id=1, source_target_pairs={{8,0},{0,8},{24,16},{16,24},{9,1},{1,9},{25,17},{17,25},{10,2},{2,... | collective-permute-start | bytes 294920 | tf_op jit(solution)/shard_map/ppermute | solution.py:22
  14.4 0.1 collective-permute-start.3
  14.5 4.3 %collective-permute-done.7.refs_8_ = bf16[64,768]{1,0:T(8,128)(2,1)S(1)} collective-permute-done((bf16[64,768]{1,0:T(8,128)(2,1)S(1)}, bf16[64,768]{1,0:T(8,128)(2,1)S(1)}, u32[]{:S(2)}, u32[]{:S(2)}) %collective-permute-start.7) | collective-permute-done | bytes 98336 | tf_op jit(solution)/shard_map/ppermute | solution.py:22
  18.8 0.0 collective-permute-start.9
  18.8 0.0 collective-permute-done.6.refs_7_
  18.9 0.6 %collective-permute-start.8 = (bf16[80,768]{1,0:T(8,128)(2,1)S(1)}, bf16[80,768]{1,0:T(8,128)(2,1)S(1)}, u32[]{:S(2)}, u32[]{:S(2)}) collective-permute-start(bf16[80,768]{1,0:T(8,128)(2,1)S(1)} %collective-permute-done.6.refs_7_), channel_id=1, source_target_pairs={{4,0},{0,4},{5,1},{1,5},{6,2},{2,6},{7,3},{3,7},{12,8},{8,12},{13,... | collective-permute-start | bytes 368648 | tf_op jit(solution)/shard_map/ppermute | solution.py:22
  19.4 0.0 collective-permute-done.3.refs_4_
  19.5 0.9 %collective-permute-done.8.refs_9_ = bf16[80,768]{1,0:T(8,128)(2,1)S(1)} collective-permute-done((bf16[80,768]{1,0:T(8,128)(2,1)S(1)}, bf16[80,768]{1,0:T(8,128)(2,1)S(1)}, u32[]{:S(2)}, u32[]{:S(2)}) %collective-permute-start.8) | collective-permute-done | bytes 122912 | tf_op jit(solution)/shard_map/ppermute | solution.py:22
  20.5 0.0 collective-permute-done.5.refs_6_
  20.5 0.0 collective-permute-done.9.refs_10_
  20.5 0.0 copy-start
  20.5 1.1 %copy-done = bf16[512,768]{1,0:T(8,128)(2,1)S(1)} copy-done((bf16[512,768]{1,0:T(8,128)(2,1)S(1)}, bf16[512,768]{1,0:T(8,128)(2,1)}, u32[]{:S(2)}) %copy-start) | copy-done | bytes 786456
  21.7 0.0 copy-start.1
  21.7 0.9 %copy-done.1 = bf16[128,768]{1,0:T(8,128)(2,1)S(1)} copy-done((bf16[128,768]{1,0:T(8,128)(2,1)S(1)}, bf16[128,768]{1,0:T(8,128)(2,1)}, u32[]{:S(2)}) %copy-start.1) | copy-done | bytes 196632
  22.6 0.0 copy-start.2
  22.6 0.7 %copy-done.2 = f32[512]{0:T(512)S(1)} copy-done((f32[512]{0:T(512)S(1)}, f32[512]{0:T(512)}, u32[]{:S(2)}) %copy-start.2) | copy-done | bytes 2072
  23.3 0.0 copy-start.4
  23.3 2.1 %shard_map.68 = (f32[512,1024]{1,0:T(8,128)S(1)}, f32[32,8,128]{2,1,0:T(8,128)S(1)}) custom-call(bf16[512,768]{1,0:T(8,128)(2,1)S(1)} %copy-done, bf16[128,768]{1,0:T(8,128)(2,1)S(1)} %copy-done.1, bf16[128,768]{1,0:T(8,128)(2,1)S(1)} %collective-permute-done.refs_2_, bf16[128,768]{1,0:T(8,128)(2,1)S(1)} %collective-permute-done.1.refs_3_, ...), custom_call_target="tpu_custom_call" | custom-call | tf_op jit(solution)/shard_map/pallas_call | solution.py:230
  25.3 12.2 %all_to_all.17.got = f32[32,8,128]{2,1,0:T(8,128)S(1)} all-to-all(f32[32,8,128]{2,1,0:T(8,128)S(1)} %get-tuple-element.9), channel_id=1, replica_groups=mesh['chip'=4,'core'=2,'grp'=4] {'chip','core','grp'}, dimensions={0} | all-to-all | bytes 262144 | tf_op jit(solution)/shard_map/all_to_all | solution.py:245
  37.5 0.0 copy-done.3
  37.5 2.0 %shard_map.69 = (f32[1,512]{1,0:T(1,128)}, f32[32,128]{1,0:T(8,128)S(1)}) custom-call(f32[512,1024]{1,0:T(8,128)S(1)} %get-tuple-element.8.scaled, f32[32,8,128]{2,1,0:T(8,128)S(1)} %all_to_all.17.got, f32[8,128]{1,0:T(8,128)S(1)} %get-tuple-element.12.target_logw, f32[1,512]{1,0:T(1,128)S(1)} %bitcast.33), custom_call_target="tpu_custom_call" | custom-call | tf_op jit(solution)/shard_map/pallas_call | solution.py:246
  39.5 8.8 %all_to_all.18 = f32[32,1,128]{2,1,0:T(1,128)S(1)} all-to-all(f32[32,1,128]{2,1,0:T(1,128)S(1)} %bitcast.31), channel_id=1, replica_groups=mesh['chip'=4,'core'=2,'grp'=4] {'chip','core','grp'}, dimensions={0} | all-to-all | bytes 32768 | tf_op jit(solution)/shard_map/all_to_all | solution.py:260
  48.3 0.1 reduce_max.9
  48.4 0.0 copy-done.4
  48.4 0.5 %multiply_subtract_fusion = f32[128]{0:T(128)} fusion(f32[128]{0:T(128)S(1)} %reduce_max.9, f32[128]{0:T(128)S(1)} %exponential_reduce_fusion, f32[128]{0:T(128)S(1)} %copy-done.4), kind=kLoop, calls=%fused_computation.29 | loop fusion | flops 640 | bytes 2048 | tf_op jit(solution)/shard_map/sub | solution.py:263
  (25 shorter events, 0.3 us)
Async XLA Ops:
  0.6 36.9 %copy-start.3 = (f32[512]{0:T(512)S(1)}, f32[512]{0:T(512)}, u32[]{:S(2)}) copy-start(f32[512]{0:T(512)} %param.8) | copy-start | bytes 6148
  0.6 5.3 %collective-permute-start = (bf16[128,768]{1,0:T(8,128)(2,1)}, bf16[128,768]{1,0:T(8,128)(2,1)S(1)}, u32[]{:S(2)}, u32[]{:S(2)}) collective-permute-start(bf16[128,768]{1,0:T(8,128)(2,1)} %refs_1_.1), channel_id=1, source_target_pairs={{4,0},{0,4},{5,1},{1,5},{6,2},{2,6},{7,3},{3,7},{12,8},{8,12},{13,... | collective-permute-start | bytes 589832 | tf_op jit(solution)/shard_map/ppermute | solution.py:22
  1.2 8.3 %collective-permute-start.1 = (bf16[128,768]{1,0:T(8,128)(2,1)}, bf16[128,768]{1,0:T(8,128)(2,1)S(1)}, u32[]{:S(2)}, u32[]{:S(2)}) collective-permute-start(bf16[128,768]{1,0:T(8,128)(2,1)} %refs_1_.1), channel_id=1, source_target_pairs={{8,0},{0,8},{24,16},{16,24},{9,1},{1,9},{25,17},{17,25},{10,2},{2,... | collective-permute-start | bytes 589832 | tf_op jit(solution)/shard_map/ppermute | solution.py:22
  3.7 7.2 %collective-permute-start.4 = (bf16[128,768]{1,0:T(8,128)(2,1)}, bf16[128,768]{1,0:T(8,128)(2,1)S(1)}, u32[]{:S(2)}, u32[]{:S(2)}) collective-permute-start(bf16[128,768]{1,0:T(8,128)(2,1)} %refs_1_.1), channel_id=1, source_target_pairs={{16,0},{24,8},{0,16},{8,24},{17,1},{25,9},{1,17},{9,25},{18,2},{26... | collective-permute-start | bytes 589832 | tf_op jit(solution)/shard_map/ppermute | solution.py:22
  5.9 5.0 %collective-permute-start.2 = (f32[2,128]{1,0:T(2,128)S(1)}, f32[2,128]{1,0:T(2,128)S(1)}, u32[]{:S(2)}, u32[]{:S(2)}) collective-permute-start(f32[2,128]{1,0:T(2,128)S(1)} %get-tuple-element.7), channel_id=1, source_target_pairs={{8,0},{0,8},{24,16},{16,24},{9,1},{1,9},{25,17},{17,25},{10,2},{2,... | collective-permute-start | bytes 3080 | tf_op jit(solution)/shard_map/ppermute | solution.py:22
  10.9 9.6 %collective-permute-start.5 = (bf16[128,768]{1,0:T(8,128)(2,1)S(1)}, bf16[128,768]{1,0:T(8,128)(2,1)S(1)}, u32[]{:S(2)}, u32[]{:S(2)}) collective-permute-start(bf16[128,768]{1,0:T(8,128)(2,1)S(1)} %collective-permute-done.4.refs_5_), channel_id=1, source_target_pairs={{4,0},{0,4},{5,1},{1,5},{6,2},{2,6},{7,3},{3,7},{12,8},{8,12},{13,... | collective-permute-start | bytes 589832 | tf_op jit(solution)/shard_map/ppermute | solution.py:22
  11.0 7.8 %collective-permute-start.6 = (bf16[80,768]{1,0:T(8,128)(2,1)S(1)}, bf16[80,768]{1,0:T(8,128)(2,1)S(1)}, u32[]{:S(2)}, u32[]{:S(2)}) collective-permute-start(bf16[80,768]{1,0:T(8,128)(2,1)S(1)} %pad_maximum_fusion.1), channel_id=1, source_target_pairs={{16,0},{24,8},{0,16},{8,24},{17,1},{25,9},{1,17},{9,25},{18,2},{26... | collective-permute-start | bytes 368648 | tf_op jit(solution)/shard_map/ppermute | solution.py:22
  13.8 5.0 %collective-permute-start.7 = (bf16[64,768]{1,0:T(8,128)(2,1)S(1)}, bf16[64,768]{1,0:T(8,128)(2,1)S(1)}, u32[]{:S(2)}, u32[]{:S(2)}) collective-permute-start(bf16[64,768]{1,0:T(8,128)(2,1)S(1)} %slice_add_fusion), channel_id=1, source_target_pairs={{8,0},{0,8},{24,16},{16,24},{9,1},{1,9},{25,17},{17,25},{10,2},{2,... | collective-permute-start | bytes 294920 | tf_op jit(solution)/shard_map/ppermute | solution.py:22
  14.4 5.0 %collective-permute-start.3 = (bf16[144,768]{1,0:T(8,128)(2,1)S(1)}, bf16[144,768]{1,0:T(8,128)(2,1)S(1)}, u32[]{:S(2)}, u32[]{:S(2)}) collective-permute-start(bf16[144,768]{1,0:T(8,128)(2,1)S(1)} %pad_maximum_fusion), channel_id=1, source_target_pairs={{4,0},{0,4},{5,1},{1,5},{6,2},{2,6},{7,3},{3,7},{12,8},{8,12},{13,... | collective-permute-start | bytes 663560 | tf_op jit(solution)/shard_map/ppermute | solution.py:22
  18.8 1.7 %collective-permute-start.9 = (bf16[64,768]{1,0:T(8,128)(2,1)S(1)}, bf16[64,768]{1,0:T(8,128)(2,1)S(1)}, u32[]{:S(2)}, u32[]{:S(2)}) collective-permute-start(bf16[64,768]{1,0:T(8,128)(2,1)S(1)} %collective-permute-done.7.refs_8_), channel_id=1, source_target_pairs={{4,0},{0,4},{5,1},{1,5},{6,2},{2,6},{7,3},{3,7},{12,8},{8,12},{13,... | collective-permute-start | bytes 294920 | tf_op jit(solution)/shard_map/ppermute | solution.py:22
  18.9 1.5 %collective-permute-start.8 = (bf16[80,768]{1,0:T(8,128)(2,1)S(1)}, bf16[80,768]{1,0:T(8,128)(2,1)S(1)}, u32[]{:S(2)}, u32[]{:S(2)}) collective-permute-start(bf16[80,768]{1,0:T(8,128)(2,1)S(1)} %collective-permute-done.6.refs_7_), channel_id=1, source_target_pairs={{4,0},{0,4},{5,1},{1,5},{6,2},{2,6},{7,3},{3,7},{12,8},{8,12},{13,... | collective-permute-start | bytes 368648 | tf_op jit(solution)/shard_map/ppermute | solution.py:22
  20.5 1.1 %copy-start = (bf16[512,768]{1,0:T(8,128)(2,1)S(1)}, bf16[512,768]{1,0:T(8,128)(2,1)}, u32[]{:S(2)}) copy-start(bf16[512,768]{1,0:T(8,128)(2,1)} %refs_0_.1) | copy-start | bytes 2359300
  21.7 0.9 %copy-start.1 = (bf16[128,768]{1,0:T(8,128)(2,1)S(1)}, bf16[128,768]{1,0:T(8,128)(2,1)}, u32[]{:S(2)}) copy-start(bf16[128,768]{1,0:T(8,128)(2,1)} %refs_1_.1) | copy-start | bytes 589828
  22.6 0.7 %copy-start.2 = (f32[512]{0:T(512)S(1)}, f32[512]{0:T(512)}, u32[]{:S(2)}) copy-start(f32[512]{0:T(512)} %param.8) | copy-start | bytes 6148
  23.3 25.2 %copy-start.4 = (f32[128]{0:T(128)S(1)}, f32[128]{0:T(128)}, u32[]{:S(2)}) copy-start(f32[128]{0:T(128)} %param.9) | copy-start | bytes 1540
where the time goes:
time: 49.2 us; the launch traced here: 48.9 us
  blocking collectives  21 us (43%)
  waiting for transfers between devices  9.59 us (19%)
  starting transfers between devices  8.03 us (16%)
  Pallas kernels  4.02 us (8%)
  local copies, waits for them, and re-layouts  3.41 us (7%)
  between operations  1.45 us (3%)
  other arithmetic  1.4 us (3%)
    all_to_all x2, blocking collectives, shards_square(): got = lax.all_to_all(message, everyone, 0, 0)  21 us
    ppermute x10, waiting for transfers between devices, fetch(): return lax.ppermute(array, axis, [(i ^ step, i) for i in range(size)])  9.59 us
    ppermute x10, starting transfers between devices, fetch(): return lax.ppermute(array, axis, [(i ^ step, i) for i in range(size)])  8.03 us
    unnamed x10, local copies, waits for them, and re-layouts  2.75 us
    pallas_call x1, Pallas kernels, shards_square(): pl.pallas_call(functools.partial(first_kernel, places, inverse_eps * LOG2...  2.06 us
    pallas_call x1, Pallas kernels, shards_square(): pl.pallas_call(second_kernel, out_shape=(jax.ShapeDtypeStruct((1, rows),...  1.96 us
  transfers between devices with their start and end apart: 10, of which 4 were waited for; matrix products, arithmetic and copies ran while one was open for 3% of the time, Pallas kernels for 0%

commit v1 on v0

v1 whole, which is shorter than its diff:
```python
import functools
import math

import jax
import jax.numpy as jnp
from jax import lax
from jax.experimental import pallas as pl
from jax.experimental.pallas import tpu as pltpu
from jax.sharding import Mesh, PartitionSpec as P

ITERS = 2
epsilon = 0.1
inverse_eps = 10.0
LOG2E = math.log2(math.e)
LN2 = math.log(2.0)
LANES = 128
SUBLANES = 8


def fetch(array, axis, step, size):
    return lax.ppermute(array, axis, [(i ^ step, i) for i in range(size)])


def doubled(held, step, chips):
    return jnp.concatenate([held, fetch(held, "chip", step, chips)])


def gather_any(array, small, chips):
    pair = jnp.stack([array, fetch(array, "core", 1, 2)])[None]
    smalls = jnp.stack([small, fetch(small, "core", 1, 2)])[None]
    step = 1
    while step < chips:
        pair = doubled(pair, step, chips)
        smalls = doubled(smalls, step, chips)
        step *= 2
    return pair.reshape(-1, array.shape[1]), smalls.reshape(-1, *small.shape)


def as_column(row):
    size = row.shape[1]
    here = lax.broadcasted_iota(jnp.int32, (LANES, LANES), 0)
    there = lax.broadcasted_iota(jnp.int32, (LANES, LANES), 1)
    parts = []
    for start in range(0, size, LANES):
        wide = jnp.broadcast_to(row[:, start : start + LANES], (LANES, LANES))
        parts.append(jnp.sum(jnp.where(here == there, wide, 0.0), axis=1, keepdims=True))
    return jnp.concatenate(parts, axis=0)


def as_row(column):
    size = column.shape[0]
    here = lax.broadcasted_iota(jnp.int32, (LANES, LANES), 0)
    there = lax.broadcasted_iota(jnp.int32, (LANES, LANES), 1)
    parts = []
    for start in range(0, size, LANES):
        wide = jnp.broadcast_to(column[start : start + LANES], (LANES, LANES))
        parts.append(jnp.sum(jnp.where(here == there, wide, 0.0), axis=0, keepdims=True))
    return jnp.concatenate(parts, axis=1)


def half_sweep(score_of, columns, rows, logw, row_pot_of, partial_of, rows_done=lambda: None):
    blocks = len(columns)
    chunk = 64
    chunks = [pl.ds(start, chunk) for start in range(0, rows, chunk)]
    tops = []
    for at in chunks:
        top = None
        for p in range(blocks):
            score = score_of(at, p) + columns[p]
            top = score if top is None else jnp.maximum(top, score)
        tops.append(jnp.max(top, axis=1, keepdims=True))
    for at, top in zip(chunks, tops):
        total = None
        for p in range(blocks):
            term = jnp.exp2(score_of(at, p) + (columns[p] - top))
            total = term if total is None else total + term
        total = jnp.sum(total, axis=1, keepdims=True)
        row_pot_of[at, :] = logw[at, :] - (top + jnp.log2(total))
    rows_done()
    folds = (chunk // SUBLANES, SUBLANES, LANES)
    found = [[] for _ in range(blocks)]
    for at in chunks:
        row_pot = row_pot_of[at, :]
        for p in range(blocks):
            score = score_of(at, p) + row_pot
            top = jnp.max(score.reshape(folds), axis=0)
            term = jnp.exp2(score.reshape(folds) - top[None])
            found[p].append((top, jnp.sum(term, axis=0)))
    for p in range(blocks):
        top = functools.reduce(jnp.maximum, [each for each, _ in found[p]])
        top = jnp.max(top, axis=0, keepdims=True)
        total = sum(each * jnp.exp2(at_top - top) for at_top, each in found[p])
        partial_of(p, top + jnp.log2(jnp.sum(total, axis=0, keepdims=True)))


def products(source, targets, factor, out):
    group = 2 * LANES
    for start in range(0, targets.shape[0], group):
        product = lax.dot_general(
            source[...],
            targets[start : start + group, :],
            (((1,), (1,)), ((), ())),
            preferred_element_type=jnp.float32,
        )
        out[:, start : start + group] = product * factor


def early_kernel(
    factor, source, own, init, target_logw, logw, sibling, held, scaled, small, row_logw,
    targets, init_row, logw_row, rows_row, sems,
):
    width = own.shape[0]
    copies = [
        pltpu.make_async_copy(source, held, sems.at[0]),
        pltpu.make_async_copy(own, targets.at[0:width], sems.at[1]),
        pltpu.make_async_copy(init, init_row, sems.at[2]),
        pltpu.make_async_copy(target_logw, logw_row, sems.at[3]),
        pltpu.make_async_copy(logw, rows_row, sems.at[4]),
    ]
    for copy in copies:
        copy.start()
    targets[width : 2 * width, :] = sibling[...]
    for copy in copies:
        copy.wait()
    small[0:1, :] = init_row[...]
    small[1:2, :] = logw_row[...]
    row_logw[...] = jnp.broadcast_to(as_column(rows_row[...] * LOG2E), row_logw.shape)
    products(held, targets, factor, scaled)


def half_kernel(start, block, small_x, small_y, half):
    half[...] = block[start : start + half.shape[0], :]


def middle_kernel(factor, source, over_x, sibling_x, over_y, sibling_y, scaled, targets):
    width = over_x.shape[0]
    for k, piece in enumerate((over_x, sibling_x, over_y, sibling_y)):
        targets[k * width : (k + 1) * width, :] = piece[...]
    products(source, targets, factor, scaled)


def blocks_of(parts):
    return [(part, k * LANES) for part in parts for k in range(part.shape[1] // LANES)]


def first_kernel(
    factor, source, far_a, far_b, sibling_a, sibling_b, early, middle, smalls, sibling_smalls, logw,
    late, message, targets, row_pot, ordered,
):
    me = lax.axis_index("chip") * 2 + lax.axis_index("core")
    half = far_a.shape[0]
    for k, piece in enumerate((far_a, far_b, sibling_a, sibling_b)):
        targets[k * half : (k + 1) * half, :] = piece[...]
    products(source, targets, factor, late)
    places = blocks_of((early, middle, late))
    columns = [
        (smalls, sibling_smalls)[p % 2][p // 2, 0:1, :] * (inverse_eps * LOG2E)
        for p in range(len(places))
    ]

    def score_of(at, p):
        part, lane = places[p]
        return part[at, lane : lane + LANES]

    def partial_of(p, value):
        ordered[pl.ds(jnp.bitwise_xor(me, p), 1), :] = value

    half_sweep(score_of, columns, early.shape[0], logw, row_pot, partial_of)
    message[...] = jnp.broadcast_to(ordered[...][None], message.shape)


def second_kernel(
    early, middle, late, got, smalls, sibling_smalls, logw, row_out, message, row_pot, ordered,
    row, sem,
):
    me = lax.axis_index("chip") * 2 + lax.axis_index("core")
    places = blocks_of((early, middle, late))
    copies = message.shape[0] // len(places)
    values = got[...]
    top = jnp.max(values, axis=0)
    ordered[...] = top + jnp.log2(jnp.sum(jnp.exp2(values - top[None]), axis=0))
    columns = []
    for p in range(len(places)):
        total = ordered[pl.ds(jnp.bitwise_xor(me, p), 1), :]
        columns.append((smalls, sibling_smalls)[p % 2][p // 2, 1:2, :] * LOG2E - total)

    def score_of(at, p):
        part, lane = places[p]
        return part[at, lane : lane + LANES]

    def partial_of(p, value):
        at = pl.ds(jnp.bitwise_xor(me, p) * copies, copies)
        message[at, :] = jnp.broadcast_to(value, (copies, LANES))

    copy = pltpu.make_async_copy(row, row_out, sem)

    def rows_done():
        row[...] = as_row(row_pot[:, 0:1]) * (epsilon * LN2)
        copy.start()

    half_sweep(score_of, columns, early.shape[0], logw, row_pot, partial_of, rows_done)
    copy.wait()


def lse(values):
    top = jnp.max(values, axis=0)
    return top + jnp.log(jnp.sum(jnp.exp(values - top[None]), axis=0))


def solution(mesh):
    blk, grp = mesh.shape["blk"], mesh.shape["grp"]
    chips = blk // 2
    mesh = Mesh(mesh.devices.reshape(chips, 2, grp), ("chip", "core", "grp"))
    everyone = ("chip", "core", "grp")

    def shards_square(source_embed, target_embed, target_init, source_logw, target_logw):
        rows, depth = source_embed.shape
        width = target_embed.shape[0]
        half = width // 2
        factor = inverse_eps * LOG2E / math.sqrt(depth)
        vmem, hbm = pl.BlockSpec(memory_space=pltpu.VMEM), pl.BlockSpec(memory_space=pltpu.HBM)
        params = pltpu.CompilerParams(vmem_limit_bytes=16 * 1024 * 1024)

        def values(*shape):
            return jax.ShapeDtypeStruct(shape, jnp.float32)

        def cost(targets, sweeps):
            return pl.CostEstimate(
                flops=2 * rows * targets * depth + 16 * sweeps * rows * blk * width,
                transcendentals=2 * sweeps * rows * blk * width,
                bytes_accessed=2 * (rows + targets) * depth,
            )

        def targets_of(count):
            return pltpu.VMEM((count * width, depth), target_embed.dtype)

        sibling = fetch(target_embed, "core", 1, 2)
        over_x = fetch(target_embed, "chip", 1, 4)
        over_y = fetch(target_embed, "chip", 2, 4)
        source, early, small, logw = pl.pallas_call(
            functools.partial(early_kernel, factor),
            out_shape=(
                jax.ShapeDtypeStruct((rows, depth), source_embed.dtype),
                values(rows, 2 * width),
                values(2, width),
                values(rows, LANES),
            ),
            in_specs=[hbm] * 5 + [vmem],
            out_specs=(vmem,) * 4,
            scratch_shapes=[
                targets_of(2),
                pltpu.VMEM((1, width), jnp.float32),
                pltpu.VMEM((1, width), jnp.float32),
                pltpu.VMEM((1, rows), jnp.float32),
                pltpu.SemaphoreType.DMA((5,)),
            ],
            compiler_params=params,
            cost_estimate=cost(2 * width, 0),
        )(
            *(
                pltpu.with_memory_space_constraint(argument, pltpu.HBM)
                for argument in (
                    source_embed,
                    target_embed,
                    target_init.reshape(1, width),
                    target_logw.reshape(1, width),
                    source_logw.reshape(1, rows),
                )
            ),
            sibling,
        )
        smalls = [small] + [fetch(small, "chip", step, 4) for step in range(1, 4)]

        def half_of(block, start):
            return pl.pallas_call(
                functools.partial(half_kernel, start),
                out_shape=jax.ShapeDtypeStruct((half, depth), block.dtype),
                in_specs=[vmem] * 3,
                out_specs=vmem,
                compiler_params=params,
            )(block, smalls[1], smalls[2])

        far_a = fetch(half_of(over_x, 0), "chip", 2, 4)
        far_b = fetch(half_of(over_y, half), "chip", 1, 4)
        smalls = jnp.stack(smalls)
        sibling_x = fetch(over_x, "core", 1, 2)
        sibling_y = fetch(over_y, "core", 1, 2)
        sibling_smalls = fetch(smalls, "core", 1, 2)
        middle = pl.pallas_call(
            functools.partial(middle_kernel, factor),
            out_shape=values(rows, 4 * width),
            in_specs=[vmem] * 5,
            out_specs=vmem,
            scratch_shapes=[targets_of(4)],
            compiler_params=params,
            cost_estimate=cost(4 * width, 0),
        )(source, over_x, sibling_x, over_y, sibling_y)
        sibling_a = fetch(far_a, "core", 1, 2)
        sibling_b = fetch(far_b, "core", 1, 2)
        row_scratch = pltpu.VMEM((rows, LANES), jnp.float32)
        block_scratch = pltpu.VMEM((blk, width), jnp.float32)
        late, message = pl.pallas_call(
            functools.partial(first_kernel, factor),
            out_shape=(values(rows, 2 * width), values(blk * grp, blk, width)),
            in_specs=[vmem] * 10,
            out_specs=(vmem, vmem),
            scratch_shapes=[targets_of(2), row_scratch, block_scratch],
            compiler_params=params,
            cost_estimate=cost(2 * width, 1),
        )(source, far_a, far_b, sibling_a, sibling_b, early, middle, smalls, sibling_smalls, logw)
        got = lax.all_to_all(message, everyone, 0, 0)
        row_pot, message = pl.pallas_call(
            second_kernel,
            out_shape=(values(1, rows), values(blk * grp, width)),
            in_specs=[vmem] * 7,
            out_specs=(hbm, vmem),
            scratch_shapes=[
                row_scratch,
                block_scratch,
                pltpu.VMEM((1, rows), jnp.float32),
                pltpu.SemaphoreType.DMA,
            ],
            compiler_params=params,
            cost_estimate=cost(0, 1),
        )(early, middle, late, got, smalls, sibling_smalls, logw)
        got = lax.all_to_all(message, everyone, 0, 0)
        top = jnp.max(got, axis=0)
        total = top + jnp.log2(jnp.sum(jnp.exp2(got - top[None]), axis=0))
        return row_pot.reshape(rows), epsilon * target_logw - (epsilon * LN2) * total

    def shards_any(source_embed, target_embed, target_init, source_logw, target_logw):
        width, depth = target_embed.shape
        factor = -1.0 / math.sqrt(depth)
        me = lax.axis_index("chip") * 2 + lax.axis_index("core")

        def swap_order(values):
            parts = values.reshape(blk, width)
            step = 1
            while step < blk:
                pairs = parts.reshape(blk // (2 * step), 2, step, width)
                pairs = jnp.where(me & step, pairs[:, ::-1], pairs)
                parts = pairs.reshape(blk, width)
                step *= 2
            return parts

        small = jnp.stack([target_init, target_logw])
        targets, smalls = gather_any(target_embed, small, chips)
        cost = (
            lax.dot_general(
                source_embed, targets, (((1,), (1,)), ((), ())), preferred_element_type=jnp.float32
            )
            * factor
        )
        column_pot, logw_all = smalls[:, 0].reshape(-1), smalls[:, 1].reshape(-1)
        for iteration in range(ITERS):
            scores = (column_pot[None, :] - cost) * inverse_eps
            row_top = jnp.max(scores, axis=1)
            row_sum = jnp.sum(jnp.exp(scores - row_top[:, None]), axis=1)
            row_pot = epsilon * source_logw - epsilon * (row_top + jnp.log(row_sum))
            part = swap_order(lse((row_pot[:, None] - cost) * inverse_eps))
            if iteration < ITERS - 1:
                copies = jnp.broadcast_to(part[None], (blk * grp, blk, width))
                got = lax.all_to_all(copies, everyone, 0, 0)
                total = swap_order(lse(got)).reshape(-1)
                column_pot = epsilon * logw_all - epsilon * total
            else:
                copies = jnp.broadcast_to(part[:, None], (blk, grp, width)).reshape(blk * grp, width)
                got = lax.all_to_all(copies, everyone, 0, 0)
                own_column = epsilon * target_logw - epsilon * lse(got)
        return row_pot, own_column

    rows_spec, blk_spec = P(("chip", "core", "grp")), P(("chip", "core"))
    in_specs = (rows_spec, blk_spec, blk_spec, rows_spec, blk_spec)
    out_specs = (rows_spec, blk_spec)
    shards = shards_square if chips == 4 else shards_any
    return jax.shard_map(shards, mesh=mesh, in_specs=in_specs, out_specs=out_specs, check_vma=False)
```

time: 49.2 us -> 45.7 us (0.929)
  waiting for transfers between devices: 9.59 us -> 6.05 us
  local copies, waits for them, and re-layouts: 3.41 us -> 0.63 us
  starting transfers between devices: 8.03 us -> 10.4 us
  Pallas kernels: 4.02 us -> 5.13 us
  blocking collectives: 21 us -> 22 us
  other arithmetic: 1.4 us -> 0.6 us
  between operations: 1.45 us -> 0.7 us
    ppermute x10 -> x13, waiting for transfers between devices: 9.59 us -> 6.05 us  [fetch(): return lax.ppermute(array, axis, [(i ^ step, i) for i in range(size)])]
    ppermute x10 -> x13, starting transfers between devices: 8.03 us -> 10.4 us  [fetch(): return lax.ppermute(array, axis, [(i ^ step, i) for i in range(size)])]
    unnamed x10 -> x2, local copies, waits for them, and re-layouts: 2.75 us -> 0.63 us
    pallas_call x2 -> x6, Pallas kernels: 4.02 us -> 5.13 us  [the longest x1 1.65 us: shards_square(): pl.pallas_call(second_kernel, out_shape=(values(1, rows), values(blk * gr...]
    all_to_all x2, blocking collectives: 21 us -> 22 us  [shards_square(): got = lax.all_to_all(message, everyone, 0, 0)]
    another operation x4 -> x1, other arithmetic: 0.71 us -> 0.01 us  [shards_square(): smalls = jnp.stack(smalls)]
    slice x5 -> x0, local copies, waits for them, and re-layouts: 0.54 us -> none  [the longest x1 0.51 us: gather_square(): tie = (small_x[0, 0] * 0.0).astype(array.dtype)]
  transfers between devices with their start and end apart: 10 -> 13, of which waited for: 4 -> 7; matrix products, arithmetic and copies ran while one was open for 3% -> 0% of each run, Pallas kernels for 0% -> 5%
where the time goes in v1:
time: 45.7 us; the launch traced here: 45.5 us
  blocking collectives  22 us (48%)
  starting transfers between devices  10.4 us (23%)
  waiting for transfers between devices  6.05 us (13%)
  Pallas kernels  5.13 us (11%)
  between operations  0.7 us (2%)
  local copies, waits for them, and re-layouts  0.63 us (1%)
  other arithmetic  0.6 us (1%)
    all_to_all x2, blocking collectives, shards_square(): got = lax.all_to_all(message, everyone, 0, 0)  22 us
    ppermute x13, starting transfers between devices, fetch(): return lax.ppermute(array, axis, [(i ^ step, i) for i in range(size)])  10.4 us
    ppermute x13, waiting for transfers between devices, fetch(): return lax.ppermute(array, axis, [(i ^ step, i) for i in range(size)])  6.05 us
    pallas_call x1, Pallas kernels, shards_square(): pl.pallas_call(second_kernel, out_shape=(values(1, rows), values(blk * gr...  1.65 us
    pallas_call x1, Pallas kernels, shards_square(): pl.pallas_call(functools.partial(early_kernel, factor), out_shape=(jax.Sh...  1.65 us
    pallas_call x1, Pallas kernels, shards_square(): pl.pallas_call(functools.partial(first_kernel, factor), out_shape=(values...  1.22 us
  transfers between devices with their start and end apart: 13, of which 7 were waited for; matrix products, arithmetic and copies ran while one was open for 0% of the time, Pallas kernels for 5%

profile of v1, /device:TPU:0, one launch (start us, length us, event | category | flops | bytes accessed | tf_op | source)
XLA Modules:
  0.0 45.5 jit_solution(14505706171593576184)
XLA Ops:
  0.6 0.5 %collective-permute-start = (bf16[128,768]{1,0:T(8,128)(2,1)}, bf16[128,768]{1,0:T(8,128)(2,1)S(1)}, u32[]{:S(2)}, u32[]{:S(2)}) collective-permute-start(bf16[128,768]{1,0:T(8,128)(2,1)} %own.1), channel_id=1, source_target_pairs={{4,0},{0,4},{5,1},{1,5},{6,2},{2,6},{7,3},{3,7},{12,8},{8,12},{13,... | collective-permute-start | bytes 589832 | tf_op jit(solution)/shard_map/ppermute | solution.py:21
  1.1 2.6 %collective-permute-start.1 = (bf16[128,768]{1,0:T(8,128)(2,1)}, bf16[128,768]{1,0:T(8,128)(2,1)S(1)}, u32[]{:S(2)}, u32[]{:S(2)}) collective-permute-start(bf16[128,768]{1,0:T(8,128)(2,1)} %own.1), channel_id=1, source_target_pairs={{8,0},{0,8},{24,16},{16,24},{9,1},{1,9},{25,17},{17,25},{10,2},{2,... | collective-permute-start | bytes 589832 | tf_op jit(solution)/shard_map/ppermute | solution.py:21
  3.7 1.5 %collective-permute-start.3 = (bf16[128,768]{1,0:T(8,128)(2,1)}, bf16[128,768]{1,0:T(8,128)(2,1)S(1)}, u32[]{:S(2)}, u32[]{:S(2)}) collective-permute-start(bf16[128,768]{1,0:T(8,128)(2,1)} %own.1), channel_id=1, source_target_pairs={{16,0},{24,8},{0,16},{8,24},{17,1},{25,9},{1,17},{9,25},{18,2},{26... | collective-permute-start | bytes 589832 | tf_op jit(solution)/shard_map/ppermute | solution.py:21
  5.2 0.0 collective-permute-done.sibling
  5.2 1.6 %shard_map.68 = (bf16[512,768]{1,0:T(8,128)(2,1)S(1)}, f32[512,256]{1,0:T(8,128)S(1)}, f32[2,128]{1,0:T(2,128)S(1)}, f32[512,128]{1,0:T(8,128)S(1)}) custom-call(bf16[512,768]{1,0:T(8,128)(2,1)} %source.1, bf16[128,768]{1,0:T(8,128)(2,1)} %own.1, f32[1,128]{1,0:T(1,128)} %bitcast.20, f32[1,128]{1,0:T(1,128)} %bitcast.18, f32[1,512]{1,0:T(1,128)} %bitcast.17, ...), custom_call_target="tpu_custom_call" | custom-call | flops 201326592 | bytes 1179648 | tf_op jit(solution)/shard_map/pallas_call | solution.py:240
  6.9 0.6 %collective-permute-start.5 = (f32[2,128]{1,0:T(2,128)S(1)}, f32[2,128]{1,0:T(2,128)S(1)}, u32[]{:S(2)}, u32[]{:S(2)}) collective-permute-start(f32[2,128]{1,0:T(2,128)S(1)} %get-tuple-element.12), channel_id=1, source_target_pairs={{8,0},{0,8},{24,16},{16,24},{9,1},{1,9},{25,17},{17,25},{10,2},{2,... | collective-permute-start | bytes 3080 | tf_op jit(solution)/shard_map/ppermute | solution.py:21
  7.5 1.0 %collective-permute-start.6 = (f32[2,128]{1,0:T(2,128)S(1)}, f32[2,128]{1,0:T(2,128)S(1)}, u32[]{:S(2)}, u32[]{:S(2)}) collective-permute-start(f32[2,128]{1,0:T(2,128)S(1)} %get-tuple-element.12), channel_id=1, source_target_pairs={{16,0},{24,8},{0,16},{8,24},{17,1},{25,9},{1,17},{9,25},{18,2},{26... | collective-permute-start | bytes 3080 | tf_op jit(solution)/shard_map/ppermute | solution.py:21
  8.5 0.9 %collective-permute-done.1.over_x.block = bf16[128,768]{1,0:T(8,128)(2,1)S(1)} collective-permute-done((bf16[128,768]{1,0:T(8,128)(2,1)}, bf16[128,768]{1,0:T(8,128)(2,1)S(1)}, u32[]{:S(2)}, u32[]{:S(2)}) %collective-permute-start.1) | collective-permute-done | bytes 196640 | tf_op jit(solution)/shard_map/ppermute | solution.py:21
  9.4 1.1 %collective-permute-done.5.small_x = f32[2,128]{1,0:T(2,128)S(1)} collective-permute-done((f32[2,128]{1,0:T(2,128)S(1)}, f32[2,128]{1,0:T(2,128)S(1)}, u32[]{:S(2)}, u32[]{:S(2)}) %collective-permute-start.5) | collective-permute-done | bytes 1056 | tf_op jit(solution)/shard_map/ppermute | solution.py:21
  10.5 0.5 %collective-permute-done.6.small_y = f32[2,128]{1,0:T(2,128)S(1)} collective-permute-done((f32[2,128]{1,0:T(2,128)S(1)}, f32[2,128]{1,0:T(2,128)S(1)}, u32[]{:S(2)}, u32[]{:S(2)}) %collective-permute-start.6) | collective-permute-done | bytes 1056 | tf_op jit(solution)/shard_map/ppermute | solution.py:21
  11.1 1.5 %collective-permute-start.7 = (bf16[64,768]{1,0:T(8,128)(2,1)S(1)}, bf16[64,768]{1,0:T(8,128)(2,1)S(1)}, u32[]{:S(2)}, u32[]{:S(2)}) collective-permute-start(bf16[64,768]{1,0:T(8,128)(2,1)S(1)} %shard_map.70), channel_id=1, source_target_pairs={{16,0},{24,8},{0,16},{8,24},{17,1},{25,9},{1,17},{9,25},{18,2},{26... | collective-permute-start | bytes 294920 | tf_op jit(solution)/shard_map/ppermute | solution.py:21
  12.6 0.0 collective-permute-done.3.over_y.block
  12.6 0.6 %collective-permute-start.8 = (bf16[64,768]{1,0:T(8,128)(2,1)S(1)}, bf16[64,768]{1,0:T(8,128)(2,1)S(1)}, u32[]{:S(2)}, u32[]{:S(2)}) collective-permute-start(bf16[64,768]{1,0:T(8,128)(2,1)S(1)} %shard_map.71), channel_id=1, source_target_pairs={{8,0},{0,8},{24,16},{16,24},{9,1},{1,9},{25,17},{17,25},{10,2},{2,... | collective-permute-start | bytes 294920 | tf_op jit(solution)/shard_map/ppermute | solution.py:21
  13.2 0.0 collective-permute-start.2
  13.2 0.5 %collective-permute-start.4 = (bf16[128,768]{1,0:T(8,128)(2,1)S(1)}, bf16[128,768]{1,0:T(8,128)(2,1)S(1)}, u32[]{:S(2)}, u32[]{:S(2)}) collective-permute-start(bf16[128,768]{1,0:T(8,128)(2,1)S(1)} %collective-permute-done.3.over_y.block), channel_id=1, source_target_pairs={{4,0},{0,4},{5,1},{1,5},{6,2},{2,6},{7,3},{3,7},{12,8},{8,12},{13,... | collective-permute-start | bytes 589832 | tf_op jit(solution)/shard_map/ppermute | solution.py:21
  13.7 1.5 %collective-permute-start.11 = (f32[2,128]{1,0:T(2,128)S(1)}, f32[2,128]{1,0:T(2,128)S(1)}, u32[]{:S(2)}, u32[]{:S(2)}) collective-permute-start(f32[2,128]{1,0:T(2,128)S(1)} %get-tuple-element.12), channel_id=1, source_target_pairs={{24,0},{16,8},{8,16},{0,24},{25,1},{17,9},{9,17},{1,25},{26,2},{18... | collective-permute-start | bytes 3080 | tf_op jit(solution)/shard_map/ppermute | solution.py:21
  15.2 0.5 %collective-permute-done.7.far_a = bf16[64,768]{1,0:T(8,128)(2,1)S(1)} collective-permute-done((bf16[64,768]{1,0:T(8,128)(2,1)S(1)}, bf16[64,768]{1,0:T(8,128)(2,1)S(1)}, u32[]{:S(2)}, u32[]{:S(2)}) %collective-permute-start.7) | collective-permute-done | bytes 98336 | tf_op jit(solution)/shard_map/ppermute | solution.py:21
  15.8 0.0 collective-permute-start.9
  15.8 1.5 %collective-permute-done.8.far_b = bf16[64,768]{1,0:T(8,128)(2,1)S(1)} collective-permute-done((bf16[64,768]{1,0:T(8,128)(2,1)S(1)}, bf16[64,768]{1,0:T(8,128)(2,1)S(1)}, u32[]{:S(2)}, u32[]{:S(2)}) %collective-permute-start.8) | collective-permute-done | bytes 98336 | tf_op jit(solution)/shard_map/ppermute | solution.py:21
  17.2 0.0 collective-permute-start.10
  17.3 0.9 %collective-permute-done.11 = f32[2,128]{1,0:T(2,128)S(1)} collective-permute-done((f32[2,128]{1,0:T(2,128)S(1)}, f32[2,128]{1,0:T(2,128)S(1)}, u32[]{:S(2)}, u32[]{:S(2)}) %collective-permute-start.11) | collective-permute-done | bytes 1056 | tf_op jit(solution)/shard_map/ppermute | solution.py:21
  18.2 0.0 collective-permute-start.12
  18.2 0.0 collective-permute-done.2.sibling_x
  18.2 0.0 collective-permute-done.4.sibling_y
  18.2 0.6 %shard_map.69.middle = f32[512,512]{1,0:T(8,128)S(1)} custom-call(bf16[512,768]{1,0:T(8,128)(2,1)S(1)} %get-tuple-element.11.source, bf16[128,768]{1,0:T(8,128)(2,1)S(1)} %collective-permute-done.1.over_x.block, bf16[128,768]{1,0:T(8,128)(2,1)S(1)} %collective-permute-done.2.sibling_x, bf16[128,768]{1,0:T(8,128)(2,1)S(1)} %collective-permute-done.3.over_y.block, ...), custom_call_target="tpu_custom_call" | custom-call | flops 402653184 | bytes 1572864 | tf_op jit(solution)/shard_map/pallas_call | solution.py:289
  18.8 0.5 %collective-permute-done.12.sibling_smalls = f32[4,2,128]{2,1,0:T(2,128)S(1)} collective-permute-done((f32[4,2,128]{2,1,0:T(2,128)S(1)}, f32[4,2,128]{2,1,0:T(2,128)S(1)}, u32[]{:S(2)}, u32[]{:S(2)}) %collective-permute-start.12) | collective-permute-done | bytes 4128 | tf_op jit(solution)/shard_map/ppermute | solution.py:21
  19.4 0.0 collective-permute-done.9.sibling_a
  19.4 0.0 collective-permute-done.10.sibling_b
  19.4 1.2 %shard_map.72 = (f32[512,256]{1,0:T(8,128)S(1)}, f32[32,8,128]{2,1,0:T(8,128)S(1)}) custom-call(bf16[512,768]{1,0:T(8,128)(2,1)S(1)} %get-tuple-element.11.source, bf16[64,768]{1,0:T(8,128)(2,1)S(1)} %collective-permute-done.7.far_a, bf16[64,768]{1,0:T(8,128)(2,1)S(1)} %collective-permute-done.8.far_b, bf16[64,768]{1,0:T(8,128)(2,1)S(1)} %collective-permute-done.9.sibling_a, ...), custom_call_target="tpu_custom_call" | custom-call | flops 209715200 | bytes 1179648 | tf_op jit(solution)/shard_map/pallas_call | solution.py:302
  20.6 13.1 %all_to_all.17.got = f32[32,8,128]{2,1,0:T(8,128)S(1)} all-to-all(f32[32,8,128]{2,1,0:T(8,128)S(1)} %get-tuple-element.15), channel_id=1, replica_groups=mesh['chip'=4,'core'=2,'grp'=4] {'chip','core','grp'}, dimensions={0} | all-to-all | bytes 262144 | tf_op jit(solution)/shard_map/all_to_all | solution.py:311
  33.7 1.6 %shard_map.73 = (f32[1,512]{1,0:T(1,128)}, f32[32,128]{1,0:T(8,128)S(1)}) custom-call(f32[512,256]{1,0:T(8,128)S(1)} %get-tuple-element.10.early, f32[512,512]{1,0:T(8,128)S(1)} %shard_map.69.middle, f32[512,256]{1,0:T(8,128)S(1)} %get-tuple-element.14.late, f32[32,8,128]{2,1,0:T(8,128)S(1)} %all_to_all.17.got, f32[4,2,128]{2,1,0:T(2,128)S(1)} %pad_maximum_fusion.smalls, ...), custom_call_target="tpu_custom_call" | custom-call | flops 8388608 | bytes 786432 | tf_op jit(solution)/shard_map/pallas_call | solution.py:312
  35.4 8.9 %all_to_all.18 = f32[32,1,128]{2,1,0:T(1,128)S(1)} all-to-all(f32[32,1,128]{2,1,0:T(1,128)S(1)} %bitcast.12), channel_id=1, replica_groups=mesh['chip'=4,'core'=2,'grp'=4] {'chip','core','grp'}, dimensions={0} | all-to-all | bytes 32768 | tf_op jit(solution)/shard_map/all_to_all | solution.py:326
  44.3 0.1 reduce_max.9
  44.3 0.0 copy-start
  44.3 0.6 %copy-done = f32[128]{0:T(128)S(1)} copy-done((f32[128]{0:T(128)S(1)}, f32[128]{0:T(128)}, u32[]{:S(2)}) %copy-start) | copy-done | bytes 536
  45.0 0.5 %multiply_subtract_fusion = f32[128]{0:T(128)} fusion(f32[128]{0:T(128)S(1)} %reduce_max.9, f32[128]{0:T(128)S(1)} %exponential_reduce_fusion, f32[128]{0:T(128)S(1)} %copy-done), kind=kLoop, calls=%fused_computation.2 | loop fusion | flops 640 | bytes 2048 | tf_op jit(solution)/shard_map/sub | solution.py:329
  (4 shorter events, 0.0 us)
Async XLA Ops:
  0.6 4.6 %collective-permute-start = (bf16[128,768]{1,0:T(8,128)(2,1)}, bf16[128,768]{1,0:T(8,128)(2,1)S(1)}, u32[]{:S(2)}, u32[]{:S(2)}) collective-permute-start(bf16[128,768]{1,0:T(8,128)(2,1)} %own.1), channel_id=1, source_target_pairs={{4,0},{0,4},{5,1},{1,5},{6,2},{2,6},{7,3},{3,7},{12,8},{8,12},{13,... | collective-permute-start | bytes 589832 | tf_op jit(solution)/shard_map/ppermute | solution.py:21
  1.1 8.3 %collective-permute-start.1 = (bf16[128,768]{1,0:T(8,128)(2,1)}, bf16[128,768]{1,0:T(8,128)(2,1)S(1)}, u32[]{:S(2)}, u32[]{:S(2)}) collective-permute-start(bf16[128,768]{1,0:T(8,128)(2,1)} %own.1), channel_id=1, source_target_pairs={{8,0},{0,8},{24,16},{16,24},{9,1},{1,9},{25,17},{17,25},{10,2},{2,... | collective-permute-start | bytes 589832 | tf_op jit(solution)/shard_map/ppermute | solution.py:21
  3.7 8.8 %collective-permute-start.3 = (bf16[128,768]{1,0:T(8,128)(2,1)}, bf16[128,768]{1,0:T(8,128)(2,1)S(1)}, u32[]{:S(2)}, u32[]{:S(2)}) collective-permute-start(bf16[128,768]{1,0:T(8,128)(2,1)} %own.1), channel_id=1, source_target_pairs={{16,0},{24,8},{0,16},{8,24},{17,1},{25,9},{1,17},{9,25},{18,2},{26... | collective-permute-start | bytes 589832 | tf_op jit(solution)/shard_map/ppermute | solution.py:21
  6.9 3.6 %collective-permute-start.5 = (f32[2,128]{1,0:T(2,128)S(1)}, f32[2,128]{1,0:T(2,128)S(1)}, u32[]{:S(2)}, u32[]{:S(2)}) collective-permute-start(f32[2,128]{1,0:T(2,128)S(1)} %get-tuple-element.12), channel_id=1, source_target_pairs={{8,0},{0,8},{24,16},{16,24},{9,1},{1,9},{25,17},{17,25},{10,2},{2,... | collective-permute-start | bytes 3080 | tf_op jit(solution)/shard_map/ppermute | solution.py:21
  7.5 3.6 %collective-permute-start.6 = (f32[2,128]{1,0:T(2,128)S(1)}, f32[2,128]{1,0:T(2,128)S(1)}, u32[]{:S(2)}, u32[]{:S(2)}) collective-permute-start(f32[2,128]{1,0:T(2,128)S(1)} %get-tuple-element.12), channel_id=1, source_target_pairs={{16,0},{24,8},{0,16},{8,24},{17,1},{25,9},{1,17},{9,25},{18,2},{26... | collective-permute-start | bytes 3080 | tf_op jit(solution)/shard_map/ppermute | solution.py:21
  11.1 4.7 %collective-permute-start.7 = (bf16[64,768]{1,0:T(8,128)(2,1)S(1)}, bf16[64,768]{1,0:T(8,128)(2,1)S(1)}, u32[]{:S(2)}, u32[]{:S(2)}) collective-permute-start(bf16[64,768]{1,0:T(8,128)(2,1)S(1)} %shard_map.70), channel_id=1, source_target_pairs={{16,0},{24,8},{0,16},{8,24},{17,1},{25,9},{1,17},{9,25},{18,2},{26... | collective-permute-start | bytes 294920 | tf_op jit(solution)/shard_map/ppermute | solution.py:21
  12.6 4.7 %collective-permute-start.8 = (bf16[64,768]{1,0:T(8,128)(2,1)S(1)}, bf16[64,768]{1,0:T(8,128)(2,1)S(1)}, u32[]{:S(2)}, u32[]{:S(2)}) collective-permute-start(bf16[64,768]{1,0:T(8,128)(2,1)S(1)} %shard_map.71), channel_id=1, source_target_pairs={{8,0},{0,8},{24,16},{16,24},{9,1},{1,9},{25,17},{17,25},{10,2},{2,... | collective-permute-start | bytes 294920 | tf_op jit(solution)/shard_map/ppermute | solution.py:21
  13.2 5.0 %collective-permute-start.2 = (bf16[128,768]{1,0:T(8,128)(2,1)S(1)}, bf16[128,768]{1,0:T(8,128)(2,1)S(1)}, u32[]{:S(2)}, u32[]{:S(2)}) collective-permute-start(bf16[128,768]{1,0:T(8,128)(2,1)S(1)} %collective-permute-done.1.over_x.block), channel_id=1, source_target_pairs={{4,0},{0,4},{5,1},{1,5},{6,2},{2,6},{7,3},{3,7},{12,8},{8,12},{13,... | collective-permute-start | bytes 589832 | tf_op jit(solution)/shard_map/ppermute | solution.py:21
  13.2 5.0 %collective-permute-start.4 = (bf16[128,768]{1,0:T(8,128)(2,1)S(1)}, bf16[128,768]{1,0:T(8,128)(2,1)S(1)}, u32[]{:S(2)}, u32[]{:S(2)}) collective-permute-start(bf16[128,768]{1,0:T(8,128)(2,1)S(1)} %collective-permute-done.3.over_y.block), channel_id=1, source_target_pairs={{4,0},{0,4},{5,1},{1,5},{6,2},{2,6},{7,3},{3,7},{12,8},{8,12},{13,... | collective-permute-start | bytes 589832 | tf_op jit(solution)/shard_map/ppermute | solution.py:21
  13.7 4.5 %collective-permute-start.11 = (f32[2,128]{1,0:T(2,128)S(1)}, f32[2,128]{1,0:T(2,128)S(1)}, u32[]{:S(2)}, u32[]{:S(2)}) collective-permute-start(f32[2,128]{1,0:T(2,128)S(1)} %get-tuple-element.12), channel_id=1, source_target_pairs={{24,0},{16,8},{8,16},{0,24},{25,1},{17,9},{9,17},{1,25},{26,2},{18... | collective-permute-start | bytes 3080 | tf_op jit(solution)/shard_map/ppermute | solution.py:21
  15.8 3.6 %collective-permute-start.9 = (bf16[64,768]{1,0:T(8,128)(2,1)S(1)}, bf16[64,768]{1,0:T(8,128)(2,1)S(1)}, u32[]{:S(2)}, u32[]{:S(2)}) collective-permute-start(bf16[64,768]{1,0:T(8,128)(2,1)S(1)} %collective-permute-done.7.far_a), channel_id=1, source_target_pairs={{4,0},{0,4},{5,1},{1,5},{6,2},{2,6},{7,3},{3,7},{12,8},{8,12},{13,... | collective-permute-start | bytes 294920 | tf_op jit(solution)/shard_map/ppermute | solution.py:21
  17.2 2.1 %collective-permute-start.10 = (bf16[64,768]{1,0:T(8,128)(2,1)S(1)}, bf16[64,768]{1,0:T(8,128)(2,1)S(1)}, u32[]{:S(2)}, u32[]{:S(2)}) collective-permute-start(bf16[64,768]{1,0:T(8,128)(2,1)S(1)} %collective-permute-done.8.far_b), channel_id=1, source_target_pairs={{4,0},{0,4},{5,1},{1,5},{6,2},{2,6},{7,3},{3,7},{12,8},{8,12},{13,... | collective-permute-start | bytes 294920 | tf_op jit(solution)/shard_map/ppermute | solution.py:21
  18.2 1.2 %collective-permute-start.12 = (f32[4,2,128]{2,1,0:T(2,128)S(1)}, f32[4,2,128]{2,1,0:T(2,128)S(1)}, u32[]{:S(2)}, u32[]{:S(2)}) collective-permute-start(f32[4,2,128]{2,1,0:T(2,128)S(1)} %pad_maximum_fusion.smalls), channel_id=1, source_target_pairs={{4,0},{0,4},{5,1},{1,5},{6,2},{2,6},{7,3},{3,7},{12,8},{8,12},{13,... | collective-permute-start | bytes 12296 | tf_op jit(solution)/shard_map/ppermute | solution.py:21
  44.3 0.7 %copy-start = (f32[128]{0:T(128)S(1)}, f32[128]{0:T(128)}, u32[]{:S(2)}) copy-start(f32[128]{0:T(128)} %param.9) | copy-start | bytes 1540

commit v2 on v1

--- a/solution.py
+++ b/solution.py
@@ -14,6 +14,7 @@
 LOG2E = math.log2(math.e)
 LN2 = math.log(2.0)
 LANES = 128
+SPARE = 16
 SUBLANES = 8
 
 
@@ -58,7 +59,7 @@
     return jnp.concatenate(parts, axis=1)
 
 
-def half_sweep(score_of, columns, rows, logw, row_pot_of, partial_of, rows_done=lambda: None):
+def half_sweep(score_of, columns, rows, logw, row_pot_of, partial_of):
     blocks = len(columns)
     chunk = 64
     chunks = [pl.ds(start, chunk) for start in range(0, rows, chunk)]
@@ -76,7 +77,6 @@
             total = term if total is None else total + term
         total = jnp.sum(total, axis=1, keepdims=True)
         row_pot_of[at, :] = logw[at, :] - (top + jnp.log2(total))
-    rows_done()
     folds = (chunk // SUBLANES, SUBLANES, LANES)
     found = [[] for _ in range(blocks)]
     for at in chunks:
@@ -128,35 +128,55 @@
     products(held, targets, factor, scaled)
 
 
-def half_kernel(start, block, small_x, small_y, half):
-    half[...] = block[start : start + half.shape[0], :]
-
-
-def middle_kernel(factor, source, over_x, sibling_x, over_y, sibling_y, scaled, targets):
-    width = over_x.shape[0]
-    for k, piece in enumerate((over_x, sibling_x, over_y, sibling_y)):
-        targets[k * width : (k + 1) * width, :] = piece[...]
+def pack_kernel(block, small, small_x, half, whole):
+    rows, kept = block.shape[0], half.shape[0] - SPARE
+    whole[0:rows, :] = block[...]
+    half[0:kept, :] = block[0:kept, :]
+    filler = jnp.zeros((SPARE - 4, LANES), jnp.float32)
+    rest = jnp.concatenate([small[...], small_x[...], filler], axis=0)
+    for k in range(block.shape[1] // LANES):
+        lanes = slice(k * LANES, (k + 1) * LANES)
+        part = (rest if k < 3 else jnp.zeros_like(rest)).astype(block.dtype)
+        half[kept:, lanes] = part
+        whole[rows:, lanes] = part
+        rest = rest - part.astype(jnp.float32)
+
+
+def unpack(message):
+    rows = message.shape[0] - SPARE
+    parts = [
+        message[rows:, k * LANES : (k + 1) * LANES].astype(jnp.float32)[0:4] for k in range(3)
+    ]
+    return (parts[0] + parts[1]) + parts[2]
+
+
+def pieces_kernel(factor, *refs):
+    source, pieces, (scaled, targets) = refs[0], refs[1:-2], refs[-2:]
+    rows = targets.shape[0] // len(pieces)
+    for k, piece in enumerate(pieces):
+        targets[k * rows : (k + 1) * rows, :] = piece[0:rows, :]
     products(source, targets, factor, scaled)
 
 
-def blocks_of(parts):
+def block_places(parts):
     return [(part, k * LANES) for part in parts for k in range(part.shape[1] // LANES)]
 
 
 def first_kernel(
-    factor, source, far_a, far_b, sibling_a, sibling_b, early, middle, smalls, sibling_smalls, logw,
-    late, message, targets, row_pot, ordered,
+    early, middle, late, small, small_x, far_a, sibling_x, sibling_a, logw,
+    message, target_logw, row_pot, ordered,
 ):
     me = lax.axis_index("chip") * 2 + lax.axis_index("core")
-    half = far_a.shape[0]
-    for k, piece in enumerate((far_a, far_b, sibling_a, sibling_b)):
-        targets[k * half : (k + 1) * half, :] = piece[...]
-    products(source, targets, factor, late)
-    places = blocks_of((early, middle, late))
-    columns = [
-        (smalls, sibling_smalls)[p % 2][p // 2, 0:1, :] * (inverse_eps * LOG2E)
-        for p in range(len(places))
-    ]
+    places = block_places((early, middle, late))
+    smalls = (
+        jnp.concatenate([small[...], small_x[...], unpack(far_a)], axis=0),
+        jnp.concatenate([unpack(sibling_x), unpack(sibling_a)], axis=0),
+    )
+    columns = []
+    for p in range(len(places)):
+        pair = smalls[p % 2][p // 2 * 2 : p // 2 * 2 + 2]
+        columns.append(pair[0:1] * (inverse_eps * LOG2E))
+        target_logw[p : p + 1, :] = pair[1:2]
 
     def score_of(at, p):
         part, lane = places[p]
@@ -170,11 +190,10 @@
 
 
 def second_kernel(
-    early, middle, late, got, smalls, sibling_smalls, logw, row_out, message, row_pot, ordered,
-    row, sem,
+    early, middle, late, got, target_logw, logw, row, message, row_pot, ordered
 ):
     me = lax.axis_index("chip") * 2 + lax.axis_index("core")
-    places = blocks_of((early, middle, late))
+    places = block_places((early, middle, late))
     copies = message.shape[0] // len(places)
     values = got[...]
     top = jnp.max(values, axis=0)
@@ -182,7 +201,7 @@
     columns = []
     for p in range(len(places)):
         total = ordered[pl.ds(jnp.bitwise_xor(me, p), 1), :]
-        columns.append((smalls, sibling_smalls)[p % 2][p // 2, 1:2, :] * LOG2E - total)
+        columns.append(target_logw[p : p + 1, :] * LOG2E - total)
 
     def score_of(at, p):
         part, lane = places[p]
@@ -192,14 +211,16 @@
         at = pl.ds(jnp.bitwise_xor(me, p) * copies, copies)
         message[at, :] = jnp.broadcast_to(value, (copies, LANES))
 
-    copy = pltpu.make_async_copy(row, row_out, sem)
-
-    def rows_done():
-        row[...] = as_row(row_pot[:, 0:1]) * (epsilon * LN2)
-        copy.start()
-
-    half_sweep(score_of, columns, early.shape[0], logw, row_pot, partial_of, rows_done)
-    copy.wait()
+    half_sweep(score_of, columns, early.shape[0], logw, row_pot, partial_of)
+    row[...] = as_row(row_pot[:, 0:1]) * (epsilon * LN2)
+
+
+def last_kernel(got, small, row, row_out, column_out):
+    values = got[...]
+    top = jnp.max(values, axis=0, keepdims=True)
+    total = top + jnp.log2(jnp.sum(jnp.exp2(values - top), axis=0, keepdims=True))
+    column_out[...] = epsilon * small[1:2, :] - (epsilon * LN2) * total
+    row_out[...] = row[...]
 
 
 def lse(values):
@@ -269,64 +290,67 @@
             ),
             sibling,
         )
-        smalls = [small] + [fetch(small, "chip", step, 4) for step in range(1, 4)]
-
-        def half_of(block, start):
-            return pl.pallas_call(
-                functools.partial(half_kernel, start),
-                out_shape=jax.ShapeDtypeStruct((half, depth), block.dtype),
-                in_specs=[vmem] * 3,
-                out_specs=vmem,
-                compiler_params=params,
-            )(block, smalls[1], smalls[2])
-
-        far_a = fetch(half_of(over_x, 0), "chip", 2, 4)
-        far_b = fetch(half_of(over_y, half), "chip", 1, 4)
-        smalls = jnp.stack(smalls)
-        sibling_x = fetch(over_x, "core", 1, 2)
+        small_x = fetch(small, "chip", 1, 4)
+        def block_of(size):
+            return jax.ShapeDtypeStruct((size, depth), target_embed.dtype)
+
+        packed_half, packed_x = pl.pallas_call(
+            pack_kernel,
+            out_shape=(block_of(half + SPARE), block_of(width + SPARE)),
+            in_specs=[vmem] * 3,
+            out_specs=(vmem, vmem),
+            compiler_params=params,
+        )(over_x, small, small_x)
+        far_a = fetch(packed_half, "chip", 2, 4)
+        far_b = fetch(over_y[half:], "chip", 1, 4)
+        sibling_x = fetch(packed_x, "core", 1, 2)
         sibling_y = fetch(over_y, "core", 1, 2)
-        sibling_smalls = fetch(smalls, "core", 1, 2)
-        middle = pl.pallas_call(
-            functools.partial(middle_kernel, factor),
-            out_shape=values(rows, 4 * width),
-            in_specs=[vmem] * 5,
-            out_specs=vmem,
-            scratch_shapes=[targets_of(4)],
-            compiler_params=params,
-            cost_estimate=cost(4 * width, 0),
-        )(source, over_x, sibling_x, over_y, sibling_y)
         sibling_a = fetch(far_a, "core", 1, 2)
         sibling_b = fetch(far_b, "core", 1, 2)
+
+        def products_of(count, weight, *pieces):
+            return pl.pallas_call(
+                functools.partial(pieces_kernel, factor),
+                out_shape=values(rows, count * width),
+                in_specs=[vmem] * (1 + len(pieces)),
+                out_specs=vmem,
+                scratch_shapes=[targets_of(count)],
+                compiler_params=params,
+                cost_estimate=cost(weight * width, 0),
+            )(source, *pieces)
+
+        middle = products_of(4, 0, over_x, sibling_x, over_y, sibling_y)
+        late = products_of(2, 40, far_a, far_b, sibling_a, sibling_b)
         row_scratch = pltpu.VMEM((rows, LANES), jnp.float32)
         block_scratch = pltpu.VMEM((blk, width), jnp.float32)
-        late, message = pl.pallas_call(
-            functools.partial(first_kernel, factor),
-            out_shape=(values(rows, 2 * width), values(blk * grp, blk, width)),
-            in_specs=[vmem] * 10,
+        message, logw_all = pl.pallas_call(
+            first_kernel,
+            out_shape=(values(blk * grp, blk, width), values(blk, width)),
+            in_specs=[vmem] * 9,
             out_specs=(vmem, vmem),
-            scratch_shapes=[targets_of(2), row_scratch, block_scratch],
+            scratch_shapes=[row_scratch, block_scratch],
             compiler_params=params,
-            cost_estimate=cost(2 * width, 1),
-        )(source, far_a, far_b, sibling_a, sibling_b, early, middle, smalls, sibling_smalls, logw)
+            cost_estimate=cost(0, 1),
+        )(early, middle, late, small, small_x, far_a, sibling_x, sibling_a, logw)
         got = lax.all_to_all(message, everyone, 0, 0)
-        row_pot, message = pl.pallas_call(
+        row, message = pl.pallas_call(
             second_kernel,
             out_shape=(values(1, rows), values(blk * grp, width)),
-            in_specs=[vmem] * 7,
-            out_specs=(hbm, vmem),
-            scratch_shapes=[
-                row_scratch,
-                block_scratch,
-                pltpu.VMEM((1, rows), jnp.float32),
-                pltpu.SemaphoreType.DMA,
-            ],
+            in_specs=[vmem] * 6,
+            out_specs=(vmem, vmem),
+            scratch_shapes=[row_scratch, block_scratch],
             compiler_params=params,
             cost_estimate=cost(0, 1),
-        )(early, middle, late, got, smalls, sibling_smalls, logw)
+        )(early, middle, late, got, logw_all, logw)
         got = lax.all_to_all(message, everyone, 0, 0)
-        top = jnp.max(got, axis=0)
-        total = top + jnp.log2(jnp.sum(jnp.exp2(got - top[None]), axis=0))
-        return row_pot.reshape(rows), epsilon * target_logw - (epsilon * LN2) * total
+        row_pot, column_pot = pl.pallas_call(
+            last_kernel,
+            out_shape=(values(1, rows), values(1, width)),
+            in_specs=[vmem] * 3,
+            out_specs=(vmem, vmem),
+            compiler_params=params,
+        )(got, small, row)
+        return row_pot.reshape(rows), column_pot.reshape(width)
 
     def shards_any(source_embed, target_embed, target_init, source_logw, target_logw):
         width, depth = target_embed.shape

time: 45.7 us -> 43.1 us (0.943)
  starting transfers between devices: 10.4 us -> 8.07 us
  waiting for transfers between devices: 6.05 us -> 6.94 us
  local copies, waits for them, and re-layouts: 0.63 us -> 0.01 us
  other arithmetic: 0.6 us -> 0 us
    ppermute x13 -> x10, starting transfers between devices: 10.4 us -> 8.07 us  [fetch(): return lax.ppermute(array, axis, [(i ^ step, i) for i in range(size)])]
    ppermute x13 -> x10, waiting for transfers between devices: 6.05 us -> 6.94 us  [fetch(): return lax.ppermute(array, axis, [(i ^ step, i) for i in range(size)])]
    pallas_call x4 -> x5, Pallas kernels: 1.83 us -> 2.57 us  [the longest x2 1 us: products_of(): pl.pallas_call(functools.partial(pieces_kernel, factor), out_shape=values...]
    unnamed x2 -> x0, local copies, waits for them, and re-layouts: 0.63 us -> none
    pallas_call x1, Pallas kernels: 1.65 us -> 1.07 us  [shards_square(): pl.pallas_call(second_kernel, out_shape=(values(1, rows), values(blk * gr...]
    sub x1 -> x0, other arithmetic: 0.52 us -> none  [shards_square(): epsilon * target_logw - epsilon * LN2 * total]
  transfers between devices with their start and end apart: 13 -> 10, of which waited for: 7 -> 5; matrix products, arithmetic and copies ran while one was open for 0% -> 0% of each run, Pallas kernels for 5% -> 5%
where the time goes in v2:
time: 43.1 us; the launch traced here: 43 us
  blocking collectives  22 us (51%)
  starting transfers between devices  8.07 us (19%)
  waiting for transfers between devices  6.94 us (16%)
  Pallas kernels  5.29 us (12%)
  between operations  0.68 us (2%)
    all_to_all x2, blocking collectives, shards_square(): got = lax.all_to_all(message, everyone, 0, 0)  22 us
    ppermute x10, starting transfers between devices, fetch(): return lax.ppermute(array, axis, [(i ^ step, i) for i in range(size)])  8.07 us
    ppermute x10, waiting for transfers between devices, fetch(): return lax.ppermute(array, axis, [(i ^ step, i) for i in range(size)])  6.94 us
    pallas_call x1, Pallas kernels, shards_square(): pl.pallas_call(functools.partial(early_kernel, factor), out_shape=(jax.Sh...  1.65 us
    pallas_call x1, Pallas kernels, shards_square(): pl.pallas_call(second_kernel, out_shape=(values(1, rows), values(blk * gr...  1.07 us
    pallas_call x2, Pallas kernels, products_of(): pl.pallas_call(functools.partial(pieces_kernel, factor), out_shape=values...  1 us
    pallas_call x1, Pallas kernels, shards_square(): pl.pallas_call(first_kernel, out_shape=(values(blk * grp, blk, width), va...  0.96 us
  transfers between devices with their start and end apart: 10, of which 5 were waited for; matrix products, arithmetic and copies ran while one was open for 0% of the time, Pallas kernels for 5%

profile of v2, /device:TPU:0, one launch (start us, length us, event | category | flops | bytes accessed | tf_op | source)
XLA Modules:
  0.0 43.0 jit_solution(3426186438092382231)
XLA Ops:
  0.6 0.5 %collective-permute-start = (bf16[128,768]{1,0:T(8,128)(2,1)}, bf16[128,768]{1,0:T(8,128)(2,1)S(1)}, u32[]{:S(2)}, u32[]{:S(2)}) collective-permute-start(bf16[128,768]{1,0:T(8,128)(2,1)} %own.1), channel_id=1, source_target_pairs={{4,0},{0,4},{5,1},{1,5},{6,2},{2,6},{7,3},{3,7},{12,8},{8,12},{13,... | collective-permute-start | bytes 589832 | tf_op jit(solution)/shard_map/ppermute | solution.py:22
  1.1 2.6 %collective-permute-start.1 = (bf16[128,768]{1,0:T(8,128)(2,1)}, bf16[128,768]{1,0:T(8,128)(2,1)S(1)}, u32[]{:S(2)}, u32[]{:S(2)}) collective-permute-start(bf16[128,768]{1,0:T(8,128)(2,1)} %own.1), channel_id=1, source_target_pairs={{8,0},{0,8},{24,16},{16,24},{9,1},{1,9},{25,17},{17,25},{10,2},{2,... | collective-permute-start | bytes 589832 | tf_op jit(solution)/shard_map/ppermute | solution.py:22
  3.7 1.5 %collective-permute-start.4 = (bf16[128,768]{1,0:T(8,128)(2,1)}, bf16[128,768]{1,0:T(8,128)(2,1)S(1)}, u32[]{:S(2)}, u32[]{:S(2)}) collective-permute-start(bf16[128,768]{1,0:T(8,128)(2,1)} %own.1), channel_id=1, source_target_pairs={{16,0},{24,8},{0,16},{8,24},{17,1},{25,9},{1,17},{9,25},{18,2},{26... | collective-permute-start | bytes 589832 | tf_op jit(solution)/shard_map/ppermute | solution.py:22
  5.2 0.0 collective-permute-done.sibling
  5.2 1.6 %shard_map.68 = (bf16[512,768]{1,0:T(8,128)(2,1)S(1)}, f32[512,256]{1,0:T(8,128)S(1)}, f32[2,128]{1,0:T(2,128)S(1)}, f32[512,128]{1,0:T(8,128)S(1)}) custom-call(bf16[512,768]{1,0:T(8,128)(2,1)} %source.1, bf16[128,768]{1,0:T(8,128)(2,1)} %own.1, f32[1,128]{1,0:T(1,128)} %bitcast.12, f32[1,128]{1,0:T(1,128)} %bitcast.13, f32[1,512]{1,0:T(1,128)} %bitcast.11, ...), custom_call_target="tpu_custom_call" | custom-call | flops 201326592 | bytes 1179648 | tf_op jit(solution)/shard_map/pallas_call | solution.py:261
  6.9 0.6 %collective-permute-start.2 = (f32[2,128]{1,0:T(2,128)S(1)}, f32[2,128]{1,0:T(2,128)S(1)}, u32[]{:S(2)}, u32[]{:S(2)}) collective-permute-start(f32[2,128]{1,0:T(2,128)S(1)} %get-tuple-element.16.small), channel_id=1, source_target_pairs={{8,0},{0,8},{24,16},{16,24},{9,1},{1,9},{25,17},{17,25},{10,2},{2,... | collective-permute-start | bytes 3080 | tf_op jit(solution)/shard_map/ppermute | solution.py:22
  7.5 1.9 %collective-permute-done.1.block.refs_1_ = bf16[128,768]{1,0:T(8,128)(2,1)S(1)} collective-permute-done((bf16[128,768]{1,0:T(8,128)(2,1)}, bf16[128,768]{1,0:T(8,128)(2,1)S(1)}, u32[]{:S(2)}, u32[]{:S(2)}) %collective-permute-start.1) | collective-permute-done | bytes 196640 | tf_op jit(solution)/shard_map/ppermute | solution.py:22
  9.4 1.1 %collective-permute-done.2.small_x = f32[2,128]{1,0:T(2,128)S(1)} collective-permute-done((f32[2,128]{1,0:T(2,128)S(1)}, f32[2,128]{1,0:T(2,128)S(1)}, u32[]{:S(2)}, u32[]{:S(2)}) %collective-permute-start.2) | collective-permute-done | bytes 1056 | tf_op jit(solution)/shard_map/ppermute | solution.py:22
  10.6 0.8 %collective-permute-start.6 = (bf16[80,768]{1,0:T(8,128)(2,1)S(1)}, bf16[80,768]{1,0:T(8,128)(2,1)S(1)}, u32[]{:S(2)}, u32[]{:S(2)}) collective-permute-start(bf16[80,768]{1,0:T(8,128)(2,1)S(1)} %get-tuple-element.18), channel_id=1, source_target_pairs={{16,0},{24,8},{0,16},{8,24},{17,1},{25,9},{1,17},{9,25},{18,2},{26... | collective-permute-start | bytes 368648 | tf_op jit(solution)/shard_map/ppermute | solution.py:22
  11.4 0.0 collective-permute-start.3
  11.4 0.0 collective-permute-done.4.refs_3_
  11.4 0.5 %collective-permute-start.5 = (bf16[128,768]{1,0:T(8,128)(2,1)S(1)}, bf16[128,768]{1,0:T(8,128)(2,1)S(1)}, u32[]{:S(2)}, u32[]{:S(2)}) collective-permute-start(bf16[128,768]{1,0:T(8,128)(2,1)S(1)} %collective-permute-done.4.refs_3_), channel_id=1, source_target_pairs={{4,0},{0,4},{5,1},{1,5},{6,2},{2,6},{7,3},{3,7},{12,8},{8,12},{13,... | collective-permute-start | bytes 589832 | tf_op jit(solution)/shard_map/ppermute | solution.py:22
  11.9 1.6 %collective-permute-start.7 = (bf16[64,768]{1,0:T(8,128)(2,1)S(1)}, bf16[64,768]{1,0:T(8,128)(2,1)S(1)}, u32[]{:S(2)}, u32[]{:S(2)}) collective-permute-start(bf16[64,768]{1,0:T(8,128)(2,1)S(1)} %slice.4), channel_id=1, source_target_pairs={{8,0},{0,8},{24,16},{16,24},{9,1},{1,9},{25,17},{17,25},{10,2},{2,... | collective-permute-start | bytes 294920 | tf_op jit(solution)/shard_map/ppermute | solution.py:22
  13.4 2.1 %collective-permute-done.6.refs_1_.far_a = bf16[80,768]{1,0:T(8,128)(2,1)S(1)} collective-permute-done((bf16[80,768]{1,0:T(8,128)(2,1)S(1)}, bf16[80,768]{1,0:T(8,128)(2,1)S(1)}, u32[]{:S(2)}, u32[]{:S(2)}) %collective-permute-start.6) | collective-permute-done | bytes 122912 | tf_op jit(solution)/shard_map/ppermute | solution.py:22
  15.5 0.0 collective-permute-start.8
  15.5 1.1 %collective-permute-done.7.refs_2_ = bf16[64,768]{1,0:T(8,128)(2,1)S(1)} collective-permute-done((bf16[64,768]{1,0:T(8,128)(2,1)S(1)}, bf16[64,768]{1,0:T(8,128)(2,1)S(1)}, u32[]{:S(2)}, u32[]{:S(2)}) %collective-permute-start.7) | collective-permute-done | bytes 98336 | tf_op jit(solution)/shard_map/ppermute | solution.py:22
  16.7 0.0 collective-permute-start.9
  16.7 0.0 collective-permute-done.5.refs_4_
  16.7 0.0 collective-permute-done.3.refs_2_.sibling_x
  16.7 0.6 %shard_map.70.middle = f32[512,512]{1,0:T(8,128)S(1)} custom-call(bf16[512,768]{1,0:T(8,128)(2,1)S(1)} %get-tuple-element.15.refs_0_, bf16[128,768]{1,0:T(8,128)(2,1)S(1)} %collective-permute-done.1.block.refs_1_, bf16[144,768]{1,0:T(8,128)(2,1)S(1)} %collective-permute-done.3.refs_2_.sibling_x, bf16[128,768]{1,0:T(8,128)(2,1)S(1)} %collective-permute-done.4.refs_3_, ...), custom_call_target="tpu_custom_call" | custom-call | bytes 786432 | tf_op jit(solution)/shard_map/pallas_call | solution.py:312
  17.3 0.7 %collective-permute-done.9.refs_4_ = bf16[64,768]{1,0:T(8,128)(2,1)S(1)} collective-permute-done((bf16[64,768]{1,0:T(8,128)(2,1)S(1)}, bf16[64,768]{1,0:T(8,128)(2,1)S(1)}, u32[]{:S(2)}, u32[]{:S(2)}) %collective-permute-start.9) | collective-permute-done | bytes 98336 | tf_op jit(solution)/shard_map/ppermute | solution.py:22
  18.0 0.0 collective-permute-done.8.refs_3_.sibling_a
  18.0 0.4 shard_map.71.late
  18.4 1.0 %shard_map.72 = (f32[32,8,128]{2,1,0:T(8,128)S(1)}, f32[8,128]{1,0:T(8,128)S(1)}) custom-call(f32[512,256]{1,0:T(8,128)S(1)} %get-tuple-element.14.early, f32[512,512]{1,0:T(8,128)S(1)} %shard_map.70.middle, f32[512,256]{1,0:T(8,128)S(1)} %shard_map.71.late, f32[2,128]{1,0:T(2,128)S(1)} %get-tuple-element.16.small, ...), custom_call_target="tpu_custom_call" | custom-call | flops 8388608 | bytes 786432 | tf_op jit(solution)/shard_map/pallas_call | solution.py:326
  19.3 13.1 %all_to_all.16.got = f32[32,8,128]{2,1,0:T(8,128)S(1)} all-to-all(f32[32,8,128]{2,1,0:T(8,128)S(1)} %get-tuple-element.20), channel_id=1, replica_groups=mesh['chip'=4,'core'=2,'grp'=4] {'chip','core','grp'}, dimensions={0} | all-to-all | bytes 262144 | tf_op jit(solution)/shard_map/all_to_all | solution.py:335
  32.4 1.1 %shard_map.73 = (f32[1,512]{1,0:T(1,128)S(1)}, f32[32,128]{1,0:T(8,128)S(1)}) custom-call(f32[512,256]{1,0:T(8,128)S(1)} %get-tuple-element.14.early, f32[512,512]{1,0:T(8,128)S(1)} %shard_map.70.middle, f32[512,256]{1,0:T(8,128)S(1)} %shard_map.71.late, f32[32,8,128]{2,1,0:T(8,128)S(1)} %all_to_all.16.got, f32[8,128]{1,0:T(8,128)S(1)} %get-tuple-element.21.target_logw, ...), custom_call_target="tpu_custom_call" | custom-call | flops 8388608 | bytes 786432 | tf_op jit(solution)/shard_map/pallas_call | solution.py:336
  33.5 8.9 %all_to_all.17 = f32[32,1,128]{2,1,0:T(1,128)S(1)} all-to-all(f32[32,1,128]{2,1,0:T(1,128)S(1)} %bitcast.10), channel_id=1, replica_groups=mesh['chip'=4,'core'=2,'grp'=4] {'chip','core','grp'}, dimensions={0} | all-to-all | bytes 32768 | tf_op jit(solution)/shard_map/all_to_all | solution.py:345
  42.4 0.6 %shard_map.74 = (f32[1,512]{1,0:T(1,128)}, f32[1,128]{1,0:T(1,128)}) custom-call(f32[32,128]{1,0:T(8,128)S(1)} %bitcast.9, f32[2,128]{1,0:T(2,128)S(1)} %get-tuple-element.16.small, f32[1,512]{1,0:T(1,128)S(1)} %get-tuple-element.23.row), custom_call_target="tpu_custom_call" | custom-call | tf_op jit(solution)/shard_map/pallas_call | solution.py:346
  (2 shorter events, 0.0 us)
Async XLA Ops:
  0.6 4.6 %collective-permute-start = (bf16[128,768]{1,0:T(8,128)(2,1)}, bf16[128,768]{1,0:T(8,128)(2,1)S(1)}, u32[]{:S(2)}, u32[]{:S(2)}) collective-permute-start(bf16[128,768]{1,0:T(8,128)(2,1)} %own.1), channel_id=1, source_target_pairs={{4,0},{0,4},{5,1},{1,5},{6,2},{2,6},{7,3},{3,7},{12,8},{8,12},{13,... | collective-permute-start | bytes 589832 | tf_op jit(solution)/shard_map/ppermute | solution.py:22
  1.1 8.3 %collective-permute-start.1 = (bf16[128,768]{1,0:T(8,128)(2,1)}, bf16[128,768]{1,0:T(8,128)(2,1)S(1)}, u32[]{:S(2)}, u32[]{:S(2)}) collective-permute-start(bf16[128,768]{1,0:T(8,128)(2,1)} %own.1), channel_id=1, source_target_pairs={{8,0},{0,8},{24,16},{16,24},{9,1},{1,9},{25,17},{17,25},{10,2},{2,... | collective-permute-start | bytes 589832 | tf_op jit(solution)/shard_map/ppermute | solution.py:22
  3.7 7.7 %collective-permute-start.4 = (bf16[128,768]{1,0:T(8,128)(2,1)}, bf16[128,768]{1,0:T(8,128)(2,1)S(1)}, u32[]{:S(2)}, u32[]{:S(2)}) collective-permute-start(bf16[128,768]{1,0:T(8,128)(2,1)} %own.1), channel_id=1, source_target_pairs={{16,0},{24,8},{0,16},{8,24},{17,1},{25,9},{1,17},{9,25},{18,2},{26... | collective-permute-start | bytes 589832 | tf_op jit(solution)/shard_map/ppermute | solution.py:22
  6.9 3.6 %collective-permute-start.2 = (f32[2,128]{1,0:T(2,128)S(1)}, f32[2,128]{1,0:T(2,128)S(1)}, u32[]{:S(2)}, u32[]{:S(2)}) collective-permute-start(f32[2,128]{1,0:T(2,128)S(1)} %get-tuple-element.16.small), channel_id=1, source_target_pairs={{8,0},{0,8},{24,16},{16,24},{9,1},{1,9},{25,17},{17,25},{10,2},{2,... | collective-permute-start | bytes 3080 | tf_op jit(solution)/shard_map/ppermute | solution.py:22
  10.6 4.9 %collective-permute-start.6 = (bf16[80,768]{1,0:T(8,128)(2,1)S(1)}, bf16[80,768]{1,0:T(8,128)(2,1)S(1)}, u32[]{:S(2)}, u32[]{:S(2)}) collective-permute-start(bf16[80,768]{1,0:T(8,128)(2,1)S(1)} %get-tuple-element.18), channel_id=1, source_target_pairs={{16,0},{24,8},{0,16},{8,24},{17,1},{25,9},{1,17},{9,25},{18,2},{26... | collective-permute-start | bytes 368648 | tf_op jit(solution)/shard_map/ppermute | solution.py:22
  11.4 5.3 %collective-permute-start.3 = (bf16[144,768]{1,0:T(8,128)(2,1)S(1)}, bf16[144,768]{1,0:T(8,128)(2,1)S(1)}, u32[]{:S(2)}, u32[]{:S(2)}) collective-permute-start(bf16[144,768]{1,0:T(8,128)(2,1)S(1)} %get-tuple-element.17), channel_id=1, source_target_pairs={{4,0},{0,4},{5,1},{1,5},{6,2},{2,6},{7,3},{3,7},{12,8},{8,12},{13,... | collective-permute-start | bytes 663560 | tf_op jit(solution)/shard_map/ppermute | solution.py:22
  11.4 5.3 %collective-permute-start.5 = (bf16[128,768]{1,0:T(8,128)(2,1)S(1)}, bf16[128,768]{1,0:T(8,128)(2,1)S(1)}, u32[]{:S(2)}, u32[]{:S(2)}) collective-permute-start(bf16[128,768]{1,0:T(8,128)(2,1)S(1)} %collective-permute-done.4.refs_3_), channel_id=1, source_target_pairs={{4,0},{0,4},{5,1},{1,5},{6,2},{2,6},{7,3},{3,7},{12,8},{8,12},{13,... | collective-permute-start | bytes 589832 | tf_op jit(solution)/shard_map/ppermute | solution.py:22
  11.9 4.8 %collective-permute-start.7 = (bf16[64,768]{1,0:T(8,128)(2,1)S(1)}, bf16[64,768]{1,0:T(8,128)(2,1)S(1)}, u32[]{:S(2)}, u32[]{:S(2)}) collective-permute-start(bf16[64,768]{1,0:T(8,128)(2,1)S(1)} %slice.4), channel_id=1, source_target_pairs={{8,0},{0,8},{24,16},{16,24},{9,1},{1,9},{25,17},{17,25},{10,2},{2,... | collective-permute-start | bytes 294920 | tf_op jit(solution)/shard_map/ppermute | solution.py:22
  15.5 2.5 %collective-permute-start.8 = (bf16[80,768]{1,0:T(8,128)(2,1)S(1)}, bf16[80,768]{1,0:T(8,128)(2,1)S(1)}, u32[]{:S(2)}, u32[]{:S(2)}) collective-permute-start(bf16[80,768]{1,0:T(8,128)(2,1)S(1)} %collective-permute-done.6.refs_1_.far_a), channel_id=1, source_target_pairs={{4,0},{0,4},{5,1},{1,5},{6,2},{2,6},{7,3},{3,7},{12,8},{8,12},{13,... | collective-permute-start | bytes 368648 | tf_op jit(solution)/shard_map/ppermute | solution.py:22
  16.7 1.3 %collective-permute-start.9 = (bf16[64,768]{1,0:T(8,128)(2,1)S(1)}, bf16[64,768]{1,0:T(8,128)(2,1)S(1)}, u32[]{:S(2)}, u32[]{:S(2)}) collective-permute-start(bf16[64,768]{1,0:T(8,128)(2,1)S(1)} %collective-permute-done.7.refs_2_), channel_id=1, source_target_pairs={{4,0},{0,4},{5,1},{1,5},{6,2},{2,6},{7,3},{3,7},{12,8},{8,12},{13,... | collective-permute-start | bytes 294920 | tf_op jit(solution)/shard_map/ppermute | solution.py:22

commit v3 on v2

--- a/solution.py
+++ b/solution.py
@@ -105,56 +105,93 @@
         out[:, start : start + group] = product * factor
 
 
-def early_kernel(
-    factor, source, own, init, target_logw, logw, sibling, held, scaled, small, row_logw,
-    targets, init_row, logw_row, rows_row, sems,
+def head_kernel(
+    own, init, target_logw, first, second, whole, small, first_plain, second_plain, init_row,
+    logw_row, sems,
 ):
-    width = own.shape[0]
+    rows, half = own.shape[0], first_plain.shape[0]
     copies = [
-        pltpu.make_async_copy(source, held, sems.at[0]),
-        pltpu.make_async_copy(own, targets.at[0:width], sems.at[1]),
-        pltpu.make_async_copy(init, init_row, sems.at[2]),
-        pltpu.make_async_copy(target_logw, logw_row, sems.at[3]),
-        pltpu.make_async_copy(logw, rows_row, sems.at[4]),
+        pltpu.make_async_copy(own, whole.at[0:rows], sems.at[0]),
+        pltpu.make_async_copy(init, init_row, sems.at[1]),
+        pltpu.make_async_copy(target_logw, logw_row, sems.at[2]),
     ]
     for copy in copies:
         copy.start()
-    targets[width : 2 * width, :] = sibling[...]
     for copy in copies:
         copy.wait()
+    for out in (first, first_plain):
+        out[0:half, :] = whole[0:half, :]
+    for out in (second, second_plain):
+        out[0:half, :] = whole[half:rows, :]
     small[0:1, :] = init_row[...]
     small[1:2, :] = logw_row[...]
-    row_logw[...] = jnp.broadcast_to(as_column(rows_row[...] * LOG2E), row_logw.shape)
-    products(held, targets, factor, scaled)
-
-
-def pack_kernel(block, small, small_x, half, whole):
-    rows, kept = block.shape[0], half.shape[0] - SPARE
-    whole[0:rows, :] = block[...]
-    half[0:kept, :] = block[0:kept, :]
-    filler = jnp.zeros((SPARE - 4, LANES), jnp.float32)
-    rest = jnp.concatenate([small[...], small_x[...], filler], axis=0)
-    for k in range(block.shape[1] // LANES):
+    filler = jnp.zeros((SPARE - 2, LANES), jnp.float32)
+    rest = jnp.concatenate([init_row[...], logw_row[...], filler], axis=0)
+    for k in range(whole.shape[1] // LANES):
         lanes = slice(k * LANES, (k + 1) * LANES)
-        part = (rest if k < 3 else jnp.zeros_like(rest)).astype(block.dtype)
-        half[kept:, lanes] = part
+        part = (rest if k < 3 else jnp.zeros_like(rest)).astype(whole.dtype)
+        first[half:, lanes] = part
+        second[half:, lanes] = part
         whole[rows:, lanes] = part
         rest = rest - part.astype(jnp.float32)
 
 
-def unpack(message):
-    rows = message.shape[0] - SPARE
+def source_kernel(source, logw, whole, held, row_logw, passed, rows_row, sems):
+    copies = [
+        pltpu.make_async_copy(source, held, sems.at[0]),
+        pltpu.make_async_copy(logw, rows_row, sems.at[1]),
+    ]
+    for copy in copies:
+        copy.start()
+    passed[...] = whole[...]
+    for copy in copies:
+        copy.wait()
+    row_logw[...] = jnp.broadcast_to(as_column(rows_row[...] * LOG2E), row_logw.shape)
+
+
+def sibling_kernel(whole, x_first, x_second, y_first, y_second, out):
+    half = x_second.shape[0]
+    block = 2 * half + SPARE
+    out[0:block, :] = whole[...]
+    out[block : block + half, :] = x_first[0:half, :]
+    out[block + half : block + 2 * half, :] = x_second[...]
+    out[block + 2 * half : 2 * block, :] = x_first[half:, :]
+    out[2 * block : 2 * block + half, :] = y_first[...]
+    out[2 * block + half : 3 * block, :] = y_second[...]
+
+
+def unpack(message, end=None):
+    end = message.shape[0] if end is None else end
     parts = [
-        message[rows:, k * LANES : (k + 1) * LANES].astype(jnp.float32)[0:4] for k in range(3)
+        message[end - SPARE : end, k * LANES : (k + 1) * LANES].astype(jnp.float32)[0:2]
+        for k in range(3)
     ]
     return (parts[0] + parts[1]) + parts[2]
 
 
-def pieces_kernel(factor, *refs):
-    source, pieces, (scaled, targets) = refs[0], refs[1:-2], refs[-2:]
-    rows = targets.shape[0] // len(pieces)
-    for k, piece in enumerate(pieces):
-        targets[k * rows : (k + 1) * rows, :] = piece[0:rows, :]
+def near_kernel(factor, source, whole, x_first, x_second, y_first, y_second, sibling, scaled, targets):
+    half = x_second.shape[0]
+    width = 2 * half
+    block = width + SPARE
+    targets[0:width, :] = whole[0:width, :]
+    for k, piece in enumerate((x_first, x_second)):
+        targets[2 * width + k * half : 2 * width + (k + 1) * half, :] = piece[0:half, :]
+    for k, piece in enumerate((y_first, y_second)):
+        targets[4 * width + k * half : 4 * width + (k + 1) * half, :] = piece[0:half, :]
+    for k in range(3):
+        start = (2 * k + 1) * width
+        targets[start : start + width, :] = sibling[k * block : k * block + width, :]
+    products(source, targets, factor, scaled)
+
+
+def pass_kernel(message, out):
+    out[...] = message[...]
+
+
+def far_kernel(factor, source, far_a, far_b, sibling_a, sibling_b, near, scaled, targets):
+    half = targets.shape[0] // 4
+    for k, piece in enumerate((far_a, far_b, sibling_a, sibling_b)):
+        targets[k * half : (k + 1) * half, :] = piece[0:half, :]
     products(source, targets, factor, scaled)
 
 
@@ -163,20 +200,20 @@
 
 
 def first_kernel(
-    early, middle, late, small, small_x, far_a, sibling_x, sibling_a, logw,
-    message, target_logw, row_pot, ordered,
+    near, far, small, x_first, y_second, far_a, sibling, sibling_a,
+    logw, message, target_logw, row_pot, ordered,
 ):
     me = lax.axis_index("chip") * 2 + lax.axis_index("core")
-    places = block_places((early, middle, late))
-    smalls = (
-        jnp.concatenate([small[...], small_x[...], unpack(far_a)], axis=0),
-        jnp.concatenate([unpack(sibling_x), unpack(sibling_a)], axis=0),
-    )
+    places = block_places((near, far))
+    block = sibling.shape[0] // 3
+    smalls = [small[...], unpack(sibling, block)]
+    smalls += [unpack(x_first), unpack(sibling, 2 * block)]
+    smalls += [unpack(y_second), unpack(sibling, 3 * block)]
+    smalls += [unpack(far_a), unpack(sibling_a)]
     columns = []
     for p in range(len(places)):
-        pair = smalls[p % 2][p // 2 * 2 : p // 2 * 2 + 2]
-        columns.append(pair[0:1] * (inverse_eps * LOG2E))
-        target_logw[p : p + 1, :] = pair[1:2]
+        columns.append(smalls[p][0:1] * (inverse_eps * LOG2E))
+        target_logw[p : p + 1, :] = smalls[p][1:2]
 
     def score_of(at, p):
         part, lane = places[p]
@@ -185,15 +222,15 @@
     def partial_of(p, value):
         ordered[pl.ds(jnp.bitwise_xor(me, p), 1), :] = value
 
-    half_sweep(score_of, columns, early.shape[0], logw, row_pot, partial_of)
+    half_sweep(score_of, columns, near.shape[0], logw, row_pot, partial_of)
     message[...] = jnp.broadcast_to(ordered[...][None], message.shape)
 
 
 def second_kernel(
-    early, middle, late, got, target_logw, logw, row, message, row_pot, ordered
+    near, far, got, target_logw, logw, row, message, row_pot, ordered
 ):
     me = lax.axis_index("chip") * 2 + lax.axis_index("core")
-    places = block_places((early, middle, late))
+    places = block_places((near, far))
     copies = message.shape[0] // len(places)
     values = got[...]
     top = jnp.max(values, axis=0)
@@ -211,7 +248,7 @@
         at = pl.ds(jnp.bitwise_xor(me, p) * copies, copies)
         message[at, :] = jnp.broadcast_to(value, (copies, LANES))
 
-    half_sweep(score_of, columns, early.shape[0], logw, row_pot, partial_of)
+    half_sweep(score_of, columns, near.shape[0], logw, row_pot, partial_of)
     row[...] = as_row(row_pot[:, 0:1]) * (epsilon * LN2)
 
 
@@ -252,75 +289,86 @@
                 bytes_accessed=2 * (rows + targets) * depth,
             )
 
-        def targets_of(count):
-            return pltpu.VMEM((count * width, depth), target_embed.dtype)
-
-        sibling = fetch(target_embed, "core", 1, 2)
-        over_x = fetch(target_embed, "chip", 1, 4)
-        over_y = fetch(target_embed, "chip", 2, 4)
-        source, early, small, logw = pl.pallas_call(
-            functools.partial(early_kernel, factor),
+        def block_of(size):
+            return jax.ShapeDtypeStruct((size, depth), target_embed.dtype)
+
+        def in_hbm(*arrays):
+            return [pltpu.with_memory_space_constraint(each, pltpu.HBM) for each in arrays]
+
+        first, second, whole, small, first_plain, second_plain = pl.pallas_call(
+            head_kernel,
+            out_shape=(
+                block_of(half + SPARE),
+                block_of(half + SPARE),
+                block_of(width + SPARE),
+                values(2, width),
+                block_of(half),
+                block_of(half),
+            ),
+            in_specs=[hbm] * 3,
+            out_specs=(vmem,) * 6,
+            scratch_shapes=[
+                pltpu.VMEM((1, width), jnp.float32),
+                pltpu.VMEM((1, width), jnp.float32),
+                pltpu.SemaphoreType.DMA((3,)),
+            ],
+            compiler_params=params,
+        )(*in_hbm(target_embed, target_init.reshape(1, width), target_logw.reshape(1, width)))
+        x_first = fetch(first, "chip", 1, 4)
+        y_second = fetch(second, "chip", 2, 4)
+        x_second = fetch(second_plain, "chip", 1, 4)
+        y_first = fetch(first_plain, "chip", 2, 4)
+        far_a = fetch(x_first, "chip", 2, 4)
+        far_b = fetch(y_second, "chip", 1, 4)
+        source, logw, passed = pl.pallas_call(
+            source_kernel,
             out_shape=(
                 jax.ShapeDtypeStruct((rows, depth), source_embed.dtype),
-                values(rows, 2 * width),
-                values(2, width),
                 values(rows, LANES),
+                block_of(width + SPARE),
             ),
-            in_specs=[hbm] * 5 + [vmem],
-            out_specs=(vmem,) * 4,
-            scratch_shapes=[
-                targets_of(2),
-                pltpu.VMEM((1, width), jnp.float32),
-                pltpu.VMEM((1, width), jnp.float32),
-                pltpu.VMEM((1, rows), jnp.float32),
-                pltpu.SemaphoreType.DMA((5,)),
-            ],
-            compiler_params=params,
-            cost_estimate=cost(2 * width, 0),
-        )(
-            *(
-                pltpu.with_memory_space_constraint(argument, pltpu.HBM)
-                for argument in (
-                    source_embed,
-                    target_embed,
-                    target_init.reshape(1, width),
-                    target_logw.reshape(1, width),
-                    source_logw.reshape(1, rows),
-                )
-            ),
-            sibling,
-        )
-        small_x = fetch(small, "chip", 1, 4)
-        def block_of(size):
-            return jax.ShapeDtypeStruct((size, depth), target_embed.dtype)
-
-        packed_half, packed_x = pl.pallas_call(
-            pack_kernel,
-            out_shape=(block_of(half + SPARE), block_of(width + SPARE)),
-            in_specs=[vmem] * 3,
-            out_specs=(vmem, vmem),
-            compiler_params=params,
-        )(over_x, small, small_x)
-        far_a = fetch(packed_half, "chip", 2, 4)
-        far_b = fetch(over_y[half:], "chip", 1, 4)
-        sibling_x = fetch(packed_x, "core", 1, 2)
-        sibling_y = fetch(over_y, "core", 1, 2)
-        sibling_a = fetch(far_a, "core", 1, 2)
-        sibling_b = fetch(far_b, "core", 1, 2)
-
-        def products_of(count, weight, *pieces):
+            in_specs=[hbm] * 2 + [vmem],
+            out_specs=(vmem,) * 3,
+            scratch_shapes=[pltpu.VMEM((1, rows), jnp.float32), pltpu.SemaphoreType.DMA((2,))],
+            compiler_params=params,
+        )(*in_hbm(source_embed, source_logw.reshape(1, rows)), whole)
+        near = (x_first, x_second, y_first, y_second)
+        sibling = pl.pallas_call(
+            sibling_kernel,
+            out_shape=block_of(3 * (width + SPARE)),
+            in_specs=[vmem] * 5,
+            out_specs=vmem,
+            compiler_params=params,
+            cost_estimate=cost(0, 0),
+        )(passed, *near)
+        sibling = fetch(sibling, "core", 1, 2)
+
+        def passed_on(message, weight):
             return pl.pallas_call(
-                functools.partial(pieces_kernel, factor),
-                out_shape=values(rows, count * width),
+                pass_kernel,
+                out_shape=jax.ShapeDtypeStruct(message.shape, message.dtype),
+                in_specs=[vmem],
+                out_specs=vmem,
+                compiler_params=params,
+                cost_estimate=cost(weight * width, 0),
+            )(message)
+
+        sibling_a = fetch(passed_on(far_a, 0), "core", 1, 2)
+        sibling_b = fetch(passed_on(far_b, 50), "core", 1, 2)
+
+        def products_of(kernel, blocks, weight, *pieces):
+            return pl.pallas_call(
+                functools.partial(kernel, factor),
+                out_shape=values(rows, blocks * width),
                 in_specs=[vmem] * (1 + len(pieces)),
                 out_specs=vmem,
-                scratch_shapes=[targets_of(count)],
+                scratch_shapes=[pltpu.VMEM((blocks * width, depth), target_embed.dtype)],
                 compiler_params=params,
                 cost_estimate=cost(weight * width, 0),
             )(source, *pieces)
 
-        middle = products_of(4, 0, over_x, sibling_x, over_y, sibling_y)
-        late = products_of(2, 40, far_a, far_b, sibling_a, sibling_b)
+        scores_near = products_of(near_kernel, 6, 0, whole, *near, sibling)
+        scores_far = products_of(far_kernel, 2, 0, far_a, far_b, sibling_a, sibling_b, scores_near)
         row_scratch = pltpu.VMEM((rows, LANES), jnp.float32)
         block_scratch = pltpu.VMEM((blk, width), jnp.float32)
         message, logw_all = pl.pallas_call(
@@ -331,17 +379,27 @@
             scratch_shapes=[row_scratch, block_scratch],
             compiler_params=params,
             cost_estimate=cost(0, 1),
-        )(early, middle, late, small, small_x, far_a, sibling_x, sibling_a, logw)
+        )(
+            scores_near,
+            scores_far,
+            small,
+            x_first,
+            y_second,
+            far_a,
+            sibling,
+            sibling_a,
+            logw,
+        )
         got = lax.all_to_all(message, everyone, 0, 0)
         row, message = pl.pallas_call(
             second_kernel,
             out_shape=(values(1, rows), values(blk * grp, width)),
-            in_specs=[vmem] * 6,
+            in_specs=[vmem] * 5,
             out_specs=(vmem, vmem),
             scratch_shapes=[row_scratch, block_scratch],
             compiler_params=params,
             cost_estimate=cost(0, 1),
-        )(early, middle, late, got, logw_all, logw)
+        )(scores_near, scores_far, got, logw_all, logw)
         got = lax.all_to_all(message, everyone, 0, 0)
         row_pot, column_pot = pl.pallas_call(
             last_kernel,

time: 43.1 us -> 42.4 us (0.984)
  waiting for transfers between devices: 6.94 us -> 3.7 us
  starting transfers between devices: 8.07 us -> 9.4 us
  Pallas kernels: 5.29 us -> 6.26 us
    ppermute x10 -> x9, waiting for transfers between devices: 6.94 us -> 3.7 us  [fetch(): return lax.ppermute(array, axis, [(i ^ step, i) for i in range(size)])]
    ppermute x10 -> x9, starting transfers between devices: 8.07 us -> 9.4 us  [fetch(): return lax.ppermute(array, axis, [(i ^ step, i) for i in range(size)])]
    pallas_call x4 -> x7, Pallas kernels: 2.68 us -> 3.66 us  [the longest x1 1.4 us: shards_square(): pl.pallas_call(source_kernel, out_shape=(jax.ShapeDtypeStruct((rows, dept...]
  transfers between devices with their start and end apart: 10 -> 9, of which waited for: 5 -> 5; matrix products, arithmetic and copies ran while one was open for 0% -> 0% of each run, Pallas kernels for 5% -> 5%
where the time goes in v3:
time: 42.4 us; the launch traced here: 42.2 us
  blocking collectives  22.1 us (52%)
  starting transfers between devices  9.4 us (22%)
  Pallas kernels  6.26 us (15%)
  waiting for transfers between devices  3.7 us (9%)
  between operations  0.73 us (2%)
    all_to_all x2, blocking collectives, shards_square(): got = lax.all_to_all(message, everyone, 0, 0)  22.1 us
    ppermute x9, starting transfers between devices, fetch(): return lax.ppermute(array, axis, [(i ^ step, i) for i in range(size)])  9.4 us
    ppermute x9, waiting for transfers between devices, fetch(): return lax.ppermute(array, axis, [(i ^ step, i) for i in range(size)])  3.7 us
    pallas_call x1, Pallas kernels, shards_square(): pl.pallas_call(source_kernel, out_shape=(jax.ShapeDtypeStruct((rows, dept...  1.4 us
    pallas_call x2, Pallas kernels, products_of(): pl.pallas_call(functools.partial(kernel, factor), out_shape=values(rows,...  1.21 us
    pallas_call x1, Pallas kernels, shards_square(): pl.pallas_call(second_kernel, out_shape=(values(1, rows), values(blk * gr...  1.06 us
    pallas_call x1, Pallas kernels, shards_square(): pl.pallas_call(head_kernel, out_shape=(block_of(half + SPARE), block_of(h...  0.99 us
    pallas_call x1, Pallas kernels, shards_square(): pl.pallas_call(first_kernel, out_shape=(values(blk * grp, blk, width), va...  0.96 us
  transfers between devices with their start and end apart: 9, of which 5 were waited for; matrix products, arithmetic and copies ran while one was open for 0% of the time, Pallas kernels for 5%

profile of v3, /device:TPU:0, one launch (start us, length us, event | category | flops | bytes accessed | tf_op | source)
XLA Modules:
  0.0 42.2 jit_solution(11786519235240161919)
XLA Ops:
  0.6 1.0 %shard_map.68 = (bf16[80,768]{1,0:T(8,128)(2,1)S(1)}, bf16[80,768]{1,0:T(8,128)(2,1)S(1)}, bf16[144,768]{1,0:T(8,128)(2,1)S(1)}, f32[2,128]{1,0:T(2,128)S(1)}, b...) custom-call(bf16[128,768]{1,0:T(8,128)(2,1)} %own.1, f32[1,128]{1,0:T(1,128)} %bitcast.12, f32[1,128]{1,0:T(1,128)} %bitcast.13), custom_call_target="tpu_custom_call" | custom-call | tf_op jit(solution)/shard_map/pallas_call | solution.py:298
  1.6 3.0 %collective-permute-start = (bf16[80,768]{1,0:T(8,128)(2,1)S(1)}, bf16[80,768]{1,0:T(8,128)(2,1)S(1)}, u32[]{:S(2)}, u32[]{:S(2)}) collective-permute-start(bf16[80,768]{1,0:T(8,128)(2,1)S(1)} %get-tuple-element.19), channel_id=1, source_target_pairs={{8,0},{0,8},{24,16},{16,24},{9,1},{1,9},{25,17},{17,25},{10,2},{2,... | collective-permute-start | bytes 368648 | tf_op jit(solution)/shard_map/ppermute | solution.py:22
  4.6 1.5 %collective-permute-start.3 = (bf16[80,768]{1,0:T(8,128)(2,1)S(1)}, bf16[80,768]{1,0:T(8,128)(2,1)S(1)}, u32[]{:S(2)}, u32[]{:S(2)}) collective-permute-start(bf16[80,768]{1,0:T(8,128)(2,1)S(1)} %get-tuple-element.22), channel_id=1, source_target_pairs={{16,0},{24,8},{0,16},{8,24},{17,1},{25,9},{1,17},{9,25},{18,2},{26... | collective-permute-start | bytes 368648 | tf_op jit(solution)/shard_map/ppermute | solution.py:22
  6.2 0.5 %collective-permute-start.1 = (bf16[64,768]{1,0:T(8,128)(2,1)S(1)}, bf16[64,768]{1,0:T(8,128)(2,1)S(1)}, u32[]{:S(2)}, u32[]{:S(2)}) collective-permute-start(bf16[64,768]{1,0:T(8,128)(2,1)S(1)} %get-tuple-element.20), channel_id=1, source_target_pairs={{8,0},{0,8},{24,16},{16,24},{9,1},{1,9},{25,17},{17,25},{10,2},{2,... | collective-permute-start | bytes 294920 | tf_op jit(solution)/shard_map/ppermute | solution.py:22
  6.7 0.1 collective-permute-start.2
  6.7 1.5 %collective-permute-done.x_first = bf16[80,768]{1,0:T(8,128)(2,1)S(1)} collective-permute-done((bf16[80,768]{1,0:T(8,128)(2,1)S(1)}, bf16[80,768]{1,0:T(8,128)(2,1)S(1)}, u32[]{:S(2)}, u32[]{:S(2)}) %collective-permute-start) | collective-permute-done | bytes 122912 | tf_op jit(solution)/shard_map/ppermute | solution.py:22
  8.3 2.5 %collective-permute-start.5 = (bf16[80,768]{1,0:T(8,128)(2,1)S(1)}, bf16[80,768]{1,0:T(8,128)(2,1)S(1)}, u32[]{:S(2)}, u32[]{:S(2)}) collective-permute-start(bf16[80,768]{1,0:T(8,128)(2,1)S(1)} %collective-permute-done.x_first), channel_id=1, source_target_pairs={{16,0},{24,8},{0,16},{8,24},{17,1},{25,9},{1,17},{9,25},{18,2},{26... | collective-permute-start | bytes 368648 | tf_op jit(solution)/shard_map/ppermute | solution.py:22
  10.8 0.0 collective-permute-done.3.y_second
  10.8 1.5 %collective-permute-start.6 = (bf16[80,768]{1,0:T(8,128)(2,1)S(1)}, bf16[80,768]{1,0:T(8,128)(2,1)S(1)}, u32[]{:S(2)}, u32[]{:S(2)}) collective-permute-start(bf16[80,768]{1,0:T(8,128)(2,1)S(1)} %collective-permute-done.3.y_second), channel_id=1, source_target_pairs={{8,0},{0,8},{24,16},{16,24},{9,1},{1,9},{25,17},{17,25},{10,2},{2,... | collective-permute-start | bytes 368648 | tf_op jit(solution)/shard_map/ppermute | solution.py:22
  12.3 1.4 %shard_map.69 = (bf16[512,768]{1,0:T(8,128)(2,1)S(1)}, f32[512,128]{1,0:T(8,128)S(1)}, bf16[144,768]{1,0:T(8,128)(2,1)S(1)}) custom-call(bf16[512,768]{1,0:T(8,128)(2,1)} %source.1, f32[1,512]{1,0:T(1,128)} %bitcast.11, bf16[144,768]{1,0:T(8,128)(2,1)S(1)} %get-tuple-element.17.whole), custom_call_target="tpu_custom_call" | custom-call | tf_op jit(solution)/shard_map/pallas_call | solution.py:323
  13.7 0.0 collective-permute-done.1.x_second
  13.7 0.0 collective-permute-done.2.y_first
  13.8 0.1 collective-permute-start.4
  13.8 0.4 collective-permute-done.5.message.far_a
  14.3 0.1 collective-permute-start.7
  14.4 1.2 %collective-permute-done.6.message.far_b = bf16[80,768]{1,0:T(8,128)(2,1)S(1)} collective-permute-done((bf16[80,768]{1,0:T(8,128)(2,1)S(1)}, bf16[80,768]{1,0:T(8,128)(2,1)S(1)}, u32[]{:S(2)}, u32[]{:S(2)}) %collective-permute-start.6) | collective-permute-done | bytes 122912 | tf_op jit(solution)/shard_map/ppermute | solution.py:22
  15.7 0.1 collective-permute-start.8
  15.8 0.2 collective-permute-done.4.sibling
  15.9 0.8 %shard_map.71.near = f32[512,768]{1,0:T(8,128)S(1)} custom-call(bf16[512,768]{1,0:T(8,128)(2,1)S(1)} %get-tuple-element.18.source, bf16[144,768]{1,0:T(8,128)(2,1)S(1)} %get-tuple-element.17.whole, bf16[80,768]{1,0:T(8,128)(2,1)S(1)} %collective-permute-done.x_first, bf16[64,768]{1,0:T(8,128)(2,1)S(1)} %collective-permute-done.1.x_second, ...), custom_call_target="tpu_custom_call" | custom-call | bytes 786432 | tf_op jit(solution)/shard_map/pallas_call | solution.py:360
  16.7 0.0 collective-permute-done.7.sibling_a
  16.8 0.3 collective-permute-done.8.sibling_b
  17.1 0.4 shard_map.74.far
  17.5 1.0 %shard_map.75 = (f32[32,8,128]{2,1,0:T(8,128)S(1)}, f32[8,128]{1,0:T(8,128)S(1)}) custom-call(f32[512,768]{1,0:T(8,128)S(1)} %shard_map.71.near, f32[512,256]{1,0:T(8,128)S(1)} %shard_map.74.far, f32[2,128]{1,0:T(2,128)S(1)} %get-tuple-element.24.small, bf16[80,768]{1,0:T(8,128)(2,1)S(1)} %collective-permute-done.x_first, ...), custom_call_target="tpu_custom_call" | custom-call | flops 8388608 | bytes 786432 | tf_op jit(solution)/shard_map/pallas_call | solution.py:374
  18.4 13.2 %all_to_all.16.got = f32[32,8,128]{2,1,0:T(8,128)S(1)} all-to-all(f32[32,8,128]{2,1,0:T(8,128)S(1)} %get-tuple-element.26), channel_id=1, replica_groups=mesh['chip'=4,'core'=2,'grp'=4] {'chip','core','grp'}, dimensions={0} | all-to-all | bytes 262144 | tf_op jit(solution)/shard_map/all_to_all | solution.py:393
  31.7 1.1 %shard_map.76 = (f32[1,512]{1,0:T(1,128)S(1)}, f32[32,128]{1,0:T(8,128)S(1)}) custom-call(f32[512,768]{1,0:T(8,128)S(1)} %shard_map.71.near, f32[512,256]{1,0:T(8,128)S(1)} %shard_map.74.far, f32[32,8,128]{2,1,0:T(8,128)S(1)} %all_to_all.16.got, f32[8,128]{1,0:T(8,128)S(1)} %get-tuple-element.27.target_logw, f32[512,128]{1,0:T(8,128)S(1)} %get-tuple-element.25.logw), custom_call_target="tpu_custom_call" | custom-call | flops 8388608 | bytes 786432 | tf_op jit(solution)/shard_map/pallas_call | solution.py:394
  32.7 8.9 %all_to_all.17 = f32[32,1,128]{2,1,0:T(1,128)S(1)} all-to-all(f32[32,1,128]{2,1,0:T(1,128)S(1)} %bitcast.10), channel_id=1, replica_groups=mesh['chip'=4,'core'=2,'grp'=4] {'chip','core','grp'}, dimensions={0} | all-to-all | bytes 32768 | tf_op jit(solution)/shard_map/all_to_all | solution.py:403
  41.6 0.6 %shard_map.77 = (f32[1,512]{1,0:T(1,128)}, f32[1,128]{1,0:T(1,128)}) custom-call(f32[32,128]{1,0:T(8,128)S(1)} %bitcast.9, f32[2,128]{1,0:T(2,128)S(1)} %get-tuple-element.24.small, f32[1,512]{1,0:T(1,128)S(1)} %get-tuple-element.29.row), custom_call_target="tpu_custom_call" | custom-call | tf_op jit(solution)/shard_map/pallas_call | solution.py:404
  (3 shorter events, 0.1 us)
Async XLA Ops:
  1.6 6.6 %collective-permute-start = (bf16[80,768]{1,0:T(8,128)(2,1)S(1)}, bf16[80,768]{1,0:T(8,128)(2,1)S(1)}, u32[]{:S(2)}, u32[]{:S(2)}) collective-permute-start(bf16[80,768]{1,0:T(8,128)(2,1)S(1)} %get-tuple-element.19), channel_id=1, source_target_pairs={{8,0},{0,8},{24,16},{16,24},{9,1},{1,9},{25,17},{17,25},{10,2},{2,... | collective-permute-start | bytes 368648 | tf_op jit(solution)/shard_map/ppermute | solution.py:22
  4.6 6.1 %collective-permute-start.3 = (bf16[80,768]{1,0:T(8,128)(2,1)S(1)}, bf16[80,768]{1,0:T(8,128)(2,1)S(1)}, u32[]{:S(2)}, u32[]{:S(2)}) collective-permute-start(bf16[80,768]{1,0:T(8,128)(2,1)S(1)} %get-tuple-element.22), channel_id=1, source_target_pairs={{16,0},{24,8},{0,16},{8,24},{17,1},{25,9},{1,17},{9,25},{18,2},{26... | collective-permute-start | bytes 368648 | tf_op jit(solution)/shard_map/ppermute | solution.py:22
  6.2 7.5 %collective-permute-start.1 = (bf16[64,768]{1,0:T(8,128)(2,1)S(1)}, bf16[64,768]{1,0:T(8,128)(2,1)S(1)}, u32[]{:S(2)}, u32[]{:S(2)}) collective-permute-start(bf16[64,768]{1,0:T(8,128)(2,1)S(1)} %get-tuple-element.20), channel_id=1, source_target_pairs={{8,0},{0,8},{24,16},{16,24},{9,1},{1,9},{25,17},{17,25},{10,2},{2,... | collective-permute-start | bytes 294920 | tf_op jit(solution)/shard_map/ppermute | solution.py:22
  6.7 7.0 %collective-permute-start.2 = (bf16[64,768]{1,0:T(8,128)(2,1)S(1)}, bf16[64,768]{1,0:T(8,128)(2,1)S(1)}, u32[]{:S(2)}, u32[]{:S(2)}) collective-permute-start(bf16[64,768]{1,0:T(8,128)(2,1)S(1)} %get-tuple-element.21), channel_id=1, source_target_pairs={{16,0},{24,8},{0,16},{8,24},{17,1},{25,9},{1,17},{9,25},{18,2},{26... | collective-permute-start | bytes 294920 | tf_op jit(solution)/shard_map/ppermute | solution.py:22
  8.3 6.0 %collective-permute-start.5 = (bf16[80,768]{1,0:T(8,128)(2,1)S(1)}, bf16[80,768]{1,0:T(8,128)(2,1)S(1)}, u32[]{:S(2)}, u32[]{:S(2)}) collective-permute-start(bf16[80,768]{1,0:T(8,128)(2,1)S(1)} %collective-permute-done.x_first), channel_id=1, source_target_pairs={{16,0},{24,8},{0,16},{8,24},{17,1},{25,9},{1,17},{9,25},{18,2},{26... | collective-permute-start | bytes 368648 | tf_op jit(solution)/shard_map/ppermute | solution.py:22
  10.8 4.9 %collective-permute-start.6 = (bf16[80,768]{1,0:T(8,128)(2,1)S(1)}, bf16[80,768]{1,0:T(8,128)(2,1)S(1)}, u32[]{:S(2)}, u32[]{:S(2)}) collective-permute-start(bf16[80,768]{1,0:T(8,128)(2,1)S(1)} %collective-permute-done.3.y_second), channel_id=1, source_target_pairs={{8,0},{0,8},{24,16},{16,24},{9,1},{1,9},{25,17},{17,25},{10,2},{2,... | collective-permute-start | bytes 368648 | tf_op jit(solution)/shard_map/ppermute | solution.py:22
  13.8 2.2 %collective-permute-start.4 = (bf16[432,768]{1,0:T(8,128)(2,1)S(1)}, bf16[432,768]{1,0:T(8,128)(2,1)S(1)}, u32[]{:S(2)}, u32[]{:S(2)}) collective-permute-start(bf16[432,768]{1,0:T(8,128)(2,1)S(1)} %shard_map.70), channel_id=1, source_target_pairs={{4,0},{0,4},{5,1},{1,5},{6,2},{2,6},{7,3},{3,7},{12,8},{8,12},{13,... | collective-permute-start | bytes 1990664 | tf_op jit(solution)/shard_map/ppermute | solution.py:22
  14.3 2.5 %collective-permute-start.7 = (bf16[80,768]{1,0:T(8,128)(2,1)S(1)}, bf16[80,768]{1,0:T(8,128)(2,1)S(1)}, u32[]{:S(2)}, u32[]{:S(2)}) collective-permute-start(bf16[80,768]{1,0:T(8,128)(2,1)S(1)} %shard_map.72), channel_id=1, source_target_pairs={{4,0},{0,4},{5,1},{1,5},{6,2},{2,6},{7,3},{3,7},{12,8},{8,12},{13,... | collective-permute-start | bytes 368648 | tf_op jit(solution)/shard_map/ppermute | solution.py:22
  15.7 1.4 %collective-permute-start.8 = (bf16[80,768]{1,0:T(8,128)(2,1)S(1)}, bf16[80,768]{1,0:T(8,128)(2,1)S(1)}, u32[]{:S(2)}, u32[]{:S(2)}) collective-permute-start(bf16[80,768]{1,0:T(8,128)(2,1)S(1)} %shard_map.73), channel_id=1, source_target_pairs={{4,0},{0,4},{5,1},{1,5},{6,2},{2,6},{7,3},{3,7},{12,8},{8,12},{13,... | collective-permute-start | bytes 368648 | tf_op jit(solution)/shard_map/ppermute | solution.py:22

commit v4 on v3

--- a/solution.py
+++ b/solution.py
@@ -14,7 +14,7 @@
 LOG2E = math.log2(math.e)
 LN2 = math.log(2.0)
 LANES = 128
-SPARE = 16
+SPARE = 8
 SUBLANES = 8
 
 
@@ -203,7 +203,7 @@
     near, far, small, x_first, y_second, far_a, sibling, sibling_a,
     logw, message, target_logw, row_pot, ordered,
 ):
-    me = lax.axis_index("chip") * 2 + lax.axis_index("core")
+    me = lax.axis_index("blk")
     places = block_places((near, far))
     block = sibling.shape[0] // 3
     smalls = [small[...], unpack(sibling, block)]
@@ -227,11 +227,10 @@
 
 
 def second_kernel(
-    near, far, got, target_logw, logw, row, message, row_pot, ordered
+    copies, near, far, got, target_logw, logw, row, message, row_pot, ordered
 ):
-    me = lax.axis_index("chip") * 2 + lax.axis_index("core")
+    me = lax.axis_index("blk")
     places = block_places((near, far))
-    copies = message.shape[0] // len(places)
     values = got[...]
     top = jnp.max(values, axis=0)
     ordered[...] = top + jnp.log2(jnp.sum(jnp.exp2(values - top[None]), axis=0))
@@ -245,7 +244,7 @@
         return part[at, lane : lane + LANES]
 
     def partial_of(p, value):
-        at = pl.ds(jnp.bitwise_xor(me, p) * copies, copies)
+        at = pl.ds((len(places) - 1 - jnp.bitwise_xor(me, p)) * copies, copies)
         message[at, :] = jnp.broadcast_to(value, (copies, LANES))
 
     half_sweep(score_of, columns, near.shape[0], logw, row_pot, partial_of)
@@ -268,7 +267,6 @@
 def solution(mesh):
     blk, grp = mesh.shape["blk"], mesh.shape["grp"]
     chips = blk // 2
-    mesh = Mesh(mesh.devices.reshape(chips, 2, grp), ("chip", "core", "grp"))
     everyone = ("chip", "core", "grp")
 
     def shards_square(source_embed, target_embed, target_init, source_logw, target_logw):
@@ -288,6 +286,13 @@
                 transcendentals=2 * sweeps * rows * blk * width,
                 bytes_accessed=2 * (rows + targets) * depth,
             )
+
+        def over(array, step):
+            return lax.ppermute(array, "blk", [(i ^ step, i) for i in range(blk)])
+
+        def exchange(message):
+            order = list(range(blk * grp))[::-1]
+            return lax.all_to_all(message, ("blk", "grp"), 0, 0, axis_index_groups=[order])
 
         def block_of(size):
             return jax.ShapeDtypeStruct((size, depth), target_embed.dtype)
@@ -314,12 +319,12 @@
             ],
             compiler_params=params,
         )(*in_hbm(target_embed, target_init.reshape(1, width), target_logw.reshape(1, width)))
-        x_first = fetch(first, "chip", 1, 4)
-        y_second = fetch(second, "chip", 2, 4)
-        x_second = fetch(second_plain, "chip", 1, 4)
-        y_first = fetch(first_plain, "chip", 2, 4)
-        far_a = fetch(x_first, "chip", 2, 4)
-        far_b = fetch(y_second, "chip", 1, 4)
+        x_first = over(first, 1 * 2)
+        y_second = over(second, 2 * 2)
+        x_second = over(second_plain, 1 * 2)
+        y_first = over(first_plain, 2 * 2)
+        far_a = over(x_first, 2 * 2)
+        far_b = over(y_second, 1 * 2)
         source, logw, passed = pl.pallas_call(
             source_kernel,
             out_shape=(
@@ -341,7 +346,7 @@
             compiler_params=params,
             cost_estimate=cost(0, 0),
         )(passed, *near)
-        sibling = fetch(sibling, "core", 1, 2)
+        sibling = over(sibling, 1)
 
         def passed_on(message, weight):
             return pl.pallas_call(
@@ -353,8 +358,8 @@
                 cost_estimate=cost(weight * width, 0),
             )(message)
 
-        sibling_a = fetch(passed_on(far_a, 0), "core", 1, 2)
-        sibling_b = fetch(passed_on(far_b, 50), "core", 1, 2)
+        sibling_a = over(passed_on(far_a, 0), 1)
+        sibling_b = over(passed_on(far_b, 50), 1)
 
         def products_of(kernel, blocks, weight, *pieces):
             return pl.pallas_call(
@@ -390,9 +395,9 @@
             sibling_a,
             logw,
         )
-        got = lax.all_to_all(message, everyone, 0, 0)
+        got = exchange(message)
         row, message = pl.pallas_call(
-            second_kernel,
+            functools.partial(second_kernel, grp),
             out_shape=(values(1, rows), values(blk * grp, width)),
             in_specs=[vmem] * 5,
             out_specs=(vmem, vmem),
@@ -400,7 +405,7 @@
             compiler_params=params,
             cost_estimate=cost(0, 1),
         )(scores_near, scores_far, got, logw_all, logw)
-        got = lax.all_to_all(message, everyone, 0, 0)
+        got = exchange(message)
         row_pot, column_pot = pl.pallas_call(
             last_kernel,
             out_shape=(values(1, rows), values(1, width)),
@@ -451,8 +456,13 @@
                 own_column = epsilon * target_logw - epsilon * lse(got)
         return row_pot, own_column
 
-    rows_spec, blk_spec = P(("chip", "core", "grp")), P(("chip", "core"))
+    if chips == 4:
+        shards = shards_square
+        rows_spec, blk_spec = P(("blk", "grp")), P("blk")
+    else:
+        shards = shards_any
+        rows_spec, blk_spec = P(everyone), P(("chip", "core"))
+        mesh = Mesh(mesh.devices.reshape(chips, 2, grp), everyone)
     in_specs = (rows_spec, blk_spec, blk_spec, rows_spec, blk_spec)
     out_specs = (rows_spec, blk_spec)
-    shards = shards_square if chips == 4 else shards_any
     return jax.shard_map(shards, mesh=mesh, in_specs=in_specs, out_specs=out_specs, check_vma=False)

time: 42.4 us -> 41.6 us (0.981)
  waiting for transfers between devices: 3.7 us -> 3.04 us
    ppermute x9, waiting for transfers between devices: 3.7 us -> 3.04 us  [over(): return lax.ppermute(array, 'blk', [(i ^ step, i) for i in range(blk)])]
  transfers between devices with their start and end apart: 9 -> 9, of which waited for: 5 -> 6; matrix products, arithmetic and copies ran while one was open for 0% -> 0% of each run, Pallas kernels for 5% -> 5%
where the time goes in v4:
time: 41.6 us; the launch traced here: 41.4 us
  blocking collectives  21.7 us (52%)
  starting transfers between devices  9.61 us (23%)
  Pallas kernels  6.27 us (15%)
  waiting for transfers between devices  3.04 us (7%)
  between operations  0.73 us (2%)
    all_to_all x2, blocking collectives, exchange(): lax.all_to_all(message, ('blk', 'grp'), 0, 0, axis_index_groups=[order])  21.7 us
    ppermute x9, starting transfers between devices, over(): return lax.ppermute(array, 'blk', [(i ^ step, i) for i in range(blk)])  9.61 us
    ppermute x9, waiting for transfers between devices, over(): return lax.ppermute(array, 'blk', [(i ^ step, i) for i in range(blk)])  3.04 us
    pallas_call x1, Pallas kernels, shards_square(): pl.pallas_call(source_kernel, out_shape=(jax.ShapeDtypeStruct((rows, dept...  1.4 us
    pallas_call x2, Pallas kernels, products_of(): pl.pallas_call(functools.partial(kernel, factor), out_shape=values(rows,...  1.21 us
    pallas_call x1, Pallas kernels, shards_square(): pl.pallas_call(functools.partial(second_kernel, grp), out_shape=(values(1...  1.06 us
    pallas_call x1, Pallas kernels, shards_square(): pl.pallas_call(head_kernel, out_shape=(block_of(half + SPARE), block_of(h...  0.99 us
    pallas_call x1, Pallas kernels, shards_square(): pl.pallas_call(first_kernel, out_shape=(values(blk * grp, blk, width), va...  0.97 us
  transfers between devices with their start and end apart: 9, of which 6 were waited for; matrix products, arithmetic and copies ran while one was open for 0% of the time, Pallas kernels for 5%

profile of v4, /device:TPU:0, one launch (start us, length us, event | category | flops | bytes accessed | tf_op | source)
XLA Modules:
  0.0 41.4 jit_solution(8522640256823658308)
XLA Ops:
  0.6 1.0 %shard_map.68 = (bf16[72,768]{1,0:T(8,128)(2,1)S(1)}, bf16[72,768]{1,0:T(8,128)(2,1)S(1)}, bf16[136,768]{1,0:T(8,128)(2,1)S(1)}, f32[2,128]{1,0:T(2,128)S(1)}, b...) custom-call(bf16[128,768]{1,0:T(8,128)(2,1)} %own.1, f32[1,128]{1,0:T(1,128)} %bitcast.12, f32[1,128]{1,0:T(1,128)} %bitcast.13), custom_call_target="tpu_custom_call" | custom-call | tf_op jit(solution)/shard_map/pallas_call | solution.py:303
  1.6 3.0 %collective-permute-start = (bf16[72,768]{1,0:T(8,128)(2,1)S(1)}, bf16[72,768]{1,0:T(8,128)(2,1)S(1)}, u32[]{:S(2)}, u32[]{:S(2)}) collective-permute-start(bf16[72,768]{1,0:T(8,128)(2,1)S(1)} %get-tuple-element.19), channel_id=1, source_target_pairs={{8,0},{12,4},{0,8},{4,12},{24,16},{28,20},{16,24},{20,28},{9,1},{1... | collective-permute-start | bytes 331784 | tf_op jit(solution)/shard_map/ppermute | solution.py:291
  4.6 1.5 %collective-permute-start.3 = (bf16[72,768]{1,0:T(8,128)(2,1)S(1)}, bf16[72,768]{1,0:T(8,128)(2,1)S(1)}, u32[]{:S(2)}, u32[]{:S(2)}) collective-permute-start(bf16[72,768]{1,0:T(8,128)(2,1)S(1)} %get-tuple-element.22), channel_id=1, source_target_pairs={{16,0},{20,4},{24,8},{28,12},{0,16},{4,20},{8,24},{12,28},{17,1},{... | collective-permute-start | bytes 331784 | tf_op jit(solution)/shard_map/ppermute | solution.py:291
  6.2 0.5 %collective-permute-start.1 = (bf16[64,768]{1,0:T(8,128)(2,1)S(1)}, bf16[64,768]{1,0:T(8,128)(2,1)S(1)}, u32[]{:S(2)}, u32[]{:S(2)}) collective-permute-start(bf16[64,768]{1,0:T(8,128)(2,1)S(1)} %get-tuple-element.20), channel_id=1, source_target_pairs={{8,0},{12,4},{0,8},{4,12},{24,16},{28,20},{16,24},{20,28},{9,1},{1... | collective-permute-start | bytes 294920 | tf_op jit(solution)/shard_map/ppermute | solution.py:291
  6.7 0.1 collective-permute-start.2
  6.7 1.1 %collective-permute-done.x_first = bf16[72,768]{1,0:T(8,128)(2,1)S(1)} collective-permute-done((bf16[72,768]{1,0:T(8,128)(2,1)S(1)}, bf16[72,768]{1,0:T(8,128)(2,1)S(1)}, u32[]{:S(2)}, u32[]{:S(2)}) %collective-permute-start) | collective-permute-done | bytes 110624 | tf_op jit(solution)/shard_map/ppermute | solution.py:291
  7.8 2.6 %collective-permute-start.5 = (bf16[72,768]{1,0:T(8,128)(2,1)S(1)}, bf16[72,768]{1,0:T(8,128)(2,1)S(1)}, u32[]{:S(2)}, u32[]{:S(2)}) collective-permute-start(bf16[72,768]{1,0:T(8,128)(2,1)S(1)} %collective-permute-done.x_first), channel_id=1, source_target_pairs={{16,0},{20,4},{24,8},{28,12},{0,16},{4,20},{8,24},{12,28},{17,1},{... | collective-permute-start | bytes 331784 | tf_op jit(solution)/shard_map/ppermute | solution.py:291
  10.4 0.1 collective-permute-done.3.y_second
  10.5 1.5 %collective-permute-start.6 = (bf16[72,768]{1,0:T(8,128)(2,1)S(1)}, bf16[72,768]{1,0:T(8,128)(2,1)S(1)}, u32[]{:S(2)}, u32[]{:S(2)}) collective-permute-start(bf16[72,768]{1,0:T(8,128)(2,1)S(1)} %collective-permute-done.3.y_second), channel_id=1, source_target_pairs={{8,0},{12,4},{0,8},{4,12},{24,16},{28,20},{16,24},{20,28},{9,1},{1... | collective-permute-start | bytes 331784 | tf_op jit(solution)/shard_map/ppermute | solution.py:291
  12.0 1.4 %shard_map.69 = (bf16[512,768]{1,0:T(8,128)(2,1)S(1)}, f32[512,128]{1,0:T(8,128)S(1)}, bf16[136,768]{1,0:T(8,128)(2,1)S(1)}) custom-call(bf16[512,768]{1,0:T(8,128)(2,1)} %source.1, f32[1,512]{1,0:T(1,128)} %bitcast.11, bf16[136,768]{1,0:T(8,128)(2,1)S(1)} %get-tuple-element.17.whole), custom_call_target="tpu_custom_call" | custom-call | tf_op jit(solution)/shard_map/pallas_call | solution.py:328
  13.4 0.0 collective-permute-done.1.x_second
  13.4 0.0 collective-permute-done.2.y_first
  13.5 0.1 collective-permute-start.4
  13.6 0.3 collective-permute-done.5.message.far_a
  13.9 0.3 collective-permute-start.7
  14.1 1.1 %collective-permute-done.6.message.far_b = bf16[72,768]{1,0:T(8,128)(2,1)S(1)} collective-permute-done((bf16[72,768]{1,0:T(8,128)(2,1)S(1)}, bf16[72,768]{1,0:T(8,128)(2,1)S(1)}, u32[]{:S(2)}, u32[]{:S(2)}) %collective-permute-start.6) | collective-permute-done | bytes 110624 | tf_op jit(solution)/shard_map/ppermute | solution.py:291
  15.2 0.1 collective-permute-start.8
  15.3 0.3 collective-permute-done.4.sibling
  15.6 0.8 %shard_map.71.near = f32[512,768]{1,0:T(8,128)S(1)} custom-call(bf16[512,768]{1,0:T(8,128)(2,1)S(1)} %get-tuple-element.18.source, bf16[136,768]{1,0:T(8,128)(2,1)S(1)} %get-tuple-element.17.whole, bf16[72,768]{1,0:T(8,128)(2,1)S(1)} %collective-permute-done.x_first, bf16[64,768]{1,0:T(8,128)(2,1)S(1)} %collective-permute-done.1.x_second, ...), custom_call_target="tpu_custom_call" | custom-call | bytes 786432 | tf_op jit(solution)/shard_map/pallas_call | solution.py:365
  16.4 0.0 collective-permute-done.7.sibling_a
  16.4 0.2 collective-permute-done.8.sibling_b
  16.6 0.4 shard_map.74.far
  17.0 1.0 %shard_map.75 = (f32[32,8,128]{2,1,0:T(8,128)S(1)}, f32[8,128]{1,0:T(8,128)S(1)}) custom-call(f32[512,768]{1,0:T(8,128)S(1)} %shard_map.71.near, f32[512,256]{1,0:T(8,128)S(1)} %shard_map.74.far, f32[2,128]{1,0:T(2,128)S(1)} %get-tuple-element.24.small, bf16[72,768]{1,0:T(8,128)(2,1)S(1)} %collective-permute-done.x_first, ...), custom_call_target="tpu_custom_call" | custom-call | flops 8388608 | bytes 786432 | tf_op jit(solution)/shard_map/pallas_call | solution.py:379
  18.0 12.7 %all_to_all.16.got = f32[32,8,128]{2,1,0:T(8,128)S(1)} all-to-all(f32[32,8,128]{2,1,0:T(8,128)S(1)} %get-tuple-element.26), channel_id=1, replica_groups={{31,30,29,28,27,26,25,24,23,22,21,20,19,18,17,16,15,14,13,12,11,10,9,8,..., dimensions={0} | all-to-all | bytes 262144 | tf_op jit(solution)/shard_map/all_to_all | solution.py:295
  30.7 1.1 %shard_map.76 = (f32[1,512]{1,0:T(1,128)S(1)}, f32[32,128]{1,0:T(8,128)S(1)}) custom-call(f32[512,768]{1,0:T(8,128)S(1)} %shard_map.71.near, f32[512,256]{1,0:T(8,128)S(1)} %shard_map.74.far, f32[32,8,128]{2,1,0:T(8,128)S(1)} %all_to_all.16.got, f32[8,128]{1,0:T(8,128)S(1)} %get-tuple-element.27.target_logw, f32[512,128]{1,0:T(8,128)S(1)} %get-tuple-element.25.logw), custom_call_target="tpu_custom_call" | custom-call | flops 8388608 | bytes 786432 | tf_op jit(solution)/shard_map/pallas_call | solution.py:399
  31.8 9.0 %all_to_all.17 = f32[32,1,128]{2,1,0:T(1,128)S(1)} all-to-all(f32[32,1,128]{2,1,0:T(1,128)S(1)} %bitcast.10), channel_id=1, replica_groups={{31,30,29,28,27,26,25,24,23,22,21,20,19,18,17,16,15,14,13,12,11,10,9,8,..., dimensions={0} | all-to-all | bytes 32768 | tf_op jit(solution)/shard_map/all_to_all | solution.py:295
  40.8 0.6 %shard_map.77 = (f32[1,512]{1,0:T(1,128)}, f32[1,128]{1,0:T(1,128)}) custom-call(f32[32,128]{1,0:T(8,128)S(1)} %bitcast.9, f32[2,128]{1,0:T(2,128)S(1)} %get-tuple-element.24.small, f32[1,512]{1,0:T(1,128)S(1)} %get-tuple-element.29.row), custom_call_target="tpu_custom_call" | custom-call | tf_op jit(solution)/shard_map/pallas_call | solution.py:409
  (3 shorter events, 0.1 us)
Async XLA Ops:
  1.6 6.2 %collective-permute-start = (bf16[72,768]{1,0:T(8,128)(2,1)S(1)}, bf16[72,768]{1,0:T(8,128)(2,1)S(1)}, u32[]{:S(2)}, u32[]{:S(2)}) collective-permute-start(bf16[72,768]{1,0:T(8,128)(2,1)S(1)} %get-tuple-element.19), channel_id=1, source_target_pairs={{8,0},{12,4},{0,8},{4,12},{24,16},{28,20},{16,24},{20,28},{9,1},{1... | collective-permute-start | bytes 331784 | tf_op jit(solution)/shard_map/ppermute | solution.py:291
  4.6 5.9 %collective-permute-start.3 = (bf16[72,768]{1,0:T(8,128)(2,1)S(1)}, bf16[72,768]{1,0:T(8,128)(2,1)S(1)}, u32[]{:S(2)}, u32[]{:S(2)}) collective-permute-start(bf16[72,768]{1,0:T(8,128)(2,1)S(1)} %get-tuple-element.22), channel_id=1, source_target_pairs={{16,0},{20,4},{24,8},{28,12},{0,16},{4,20},{8,24},{12,28},{17,1},{... | collective-permute-start | bytes 331784 | tf_op jit(solution)/shard_map/ppermute | solution.py:291
  6.2 7.3 %collective-permute-start.1 = (bf16[64,768]{1,0:T(8,128)(2,1)S(1)}, bf16[64,768]{1,0:T(8,128)(2,1)S(1)}, u32[]{:S(2)}, u32[]{:S(2)}) collective-permute-start(bf16[64,768]{1,0:T(8,128)(2,1)S(1)} %get-tuple-element.20), channel_id=1, source_target_pairs={{8,0},{12,4},{0,8},{4,12},{24,16},{28,20},{16,24},{20,28},{9,1},{1... | collective-permute-start | bytes 294920 | tf_op jit(solution)/shard_map/ppermute | solution.py:291
  6.7 6.7 %collective-permute-start.2 = (bf16[64,768]{1,0:T(8,128)(2,1)S(1)}, bf16[64,768]{1,0:T(8,128)(2,1)S(1)}, u32[]{:S(2)}, u32[]{:S(2)}) collective-permute-start(bf16[64,768]{1,0:T(8,128)(2,1)S(1)} %get-tuple-element.21), channel_id=1, source_target_pairs={{16,0},{20,4},{24,8},{28,12},{0,16},{4,20},{8,24},{12,28},{17,1},{... | collective-permute-start | bytes 294920 | tf_op jit(solution)/shard_map/ppermute | solution.py:291
  7.8 6.0 %collective-permute-start.5 = (bf16[72,768]{1,0:T(8,128)(2,1)S(1)}, bf16[72,768]{1,0:T(8,128)(2,1)S(1)}, u32[]{:S(2)}, u32[]{:S(2)}) collective-permute-start(bf16[72,768]{1,0:T(8,128)(2,1)S(1)} %collective-permute-done.x_first), channel_id=1, source_target_pairs={{16,0},{20,4},{24,8},{28,12},{0,16},{4,20},{8,24},{12,28},{17,1},{... | collective-permute-start | bytes 331784 | tf_op jit(solution)/shard_map/ppermute | solution.py:291
  10.5 4.7 %collective-permute-start.6 = (bf16[72,768]{1,0:T(8,128)(2,1)S(1)}, bf16[72,768]{1,0:T(8,128)(2,1)S(1)}, u32[]{:S(2)}, u32[]{:S(2)}) collective-permute-start(bf16[72,768]{1,0:T(8,128)(2,1)S(1)} %collective-permute-done.3.y_second), channel_id=1, source_target_pairs={{8,0},{12,4},{0,8},{4,12},{24,16},{28,20},{16,24},{20,28},{9,1},{1... | collective-permute-start | bytes 331784 | tf_op jit(solution)/shard_map/ppermute | solution.py:291
  13.5 2.1 %collective-permute-start.4 = (bf16[408,768]{1,0:T(8,128)(2,1)S(1)}, bf16[408,768]{1,0:T(8,128)(2,1)S(1)}, u32[]{:S(2)}, u32[]{:S(2)}) collective-permute-start(bf16[408,768]{1,0:T(8,128)(2,1)S(1)} %shard_map.70), channel_id=1, source_target_pairs={{4,0},{0,4},{12,8},{8,12},{20,16},{16,20},{28,24},{24,28},{5,1},{1... | collective-permute-start | bytes 1880072 | tf_op jit(solution)/shard_map/ppermute | solution.py:291
  13.9 2.6 %collective-permute-start.7 = (bf16[72,768]{1,0:T(8,128)(2,1)S(1)}, bf16[72,768]{1,0:T(8,128)(2,1)S(1)}, u32[]{:S(2)}, u32[]{:S(2)}) collective-permute-start(bf16[72,768]{1,0:T(8,128)(2,1)S(1)} %shard_map.72), channel_id=1, source_target_pairs={{4,0},{0,4},{12,8},{8,12},{20,16},{16,20},{28,24},{24,28},{5,1},{1... | collective-permute-start | bytes 331784 | tf_op jit(solution)/shard_map/ppermute | solution.py:291
  15.2 1.4 %collective-permute-start.8 = (bf16[72,768]{1,0:T(8,128)(2,1)S(1)}, bf16[72,768]{1,0:T(8,128)(2,1)S(1)}, u32[]{:S(2)}, u32[]{:S(2)}) collective-permute-start(bf16[72,768]{1,0:T(8,128)(2,1)S(1)} %shard_map.73), channel_id=1, source_target_pairs={{4,0},{0,4},{12,8},{8,12},{20,16},{16,20},{28,24},{24,28},{5,1},{1... | collective-permute-start | bytes 331784 | tf_op jit(solution)/shard_map/ppermute | solution.py:291

commit v5 on v4

--- a/solution.py
+++ b/solution.py
@@ -149,15 +149,15 @@
     row_logw[...] = jnp.broadcast_to(as_column(rows_row[...] * LOG2E), row_logw.shape)
 
 
-def sibling_kernel(whole, x_first, x_second, y_first, y_second, out):
-    half = x_second.shape[0]
+def sibling_kernel(whole, a_first, a_second, b_first, b_second, out):
+    half = a_second.shape[0]
     block = 2 * half + SPARE
     out[0:block, :] = whole[...]
-    out[block : block + half, :] = x_first[0:half, :]
-    out[block + half : block + 2 * half, :] = x_second[...]
-    out[block + 2 * half : 2 * block, :] = x_first[half:, :]
-    out[2 * block : 2 * block + half, :] = y_first[...]
-    out[2 * block + half : 3 * block, :] = y_second[...]
+    out[block : block + half, :] = a_first[0:half, :]
+    out[block + half : block + 2 * half, :] = a_second[...]
+    out[block + 2 * half : 2 * block, :] = a_first[half:, :]
+    out[2 * block : 2 * block + half, :] = b_first[...]
+    out[2 * block + half : 3 * block, :] = b_second[...]
 
 
 def unpack(message, end=None):
@@ -169,14 +169,14 @@
     return (parts[0] + parts[1]) + parts[2]
 
 
-def near_kernel(factor, source, whole, x_first, x_second, y_first, y_second, sibling, scaled, targets):
-    half = x_second.shape[0]
+def near_kernel(factor, source, whole, a_first, a_second, b_first, b_second, sibling, scaled, targets):
+    half = a_second.shape[0]
     width = 2 * half
     block = width + SPARE
     targets[0:width, :] = whole[0:width, :]
-    for k, piece in enumerate((x_first, x_second)):
+    for k, piece in enumerate((a_first, a_second)):
         targets[2 * width + k * half : 2 * width + (k + 1) * half, :] = piece[0:half, :]
-    for k, piece in enumerate((y_first, y_second)):
+    for k, piece in enumerate((b_first, b_second)):
         targets[4 * width + k * half : 4 * width + (k + 1) * half, :] = piece[0:half, :]
     for k in range(3):
         start = (2 * k + 1) * width
@@ -195,20 +195,37 @@
     products(source, targets, factor, scaled)
 
 
+def neighbour_step(me, turn):
+    step = 2 + 2 * (me % 2)
+    return step if turn == 0 else 6 - step
+
+
+def positions(me):
+    sibling = me ^ 1
+    own = [me, me ^ neighbour_step(me, 0), me ^ neighbour_step(me, 1), me ^ 6]
+    other = [
+        sibling,
+        sibling ^ neighbour_step(sibling, 0),
+        sibling ^ neighbour_step(sibling, 1),
+        sibling ^ 6,
+    ]
+    return [block for pair in zip(own, other) for block in pair]
+
+
 def block_places(parts):
     return [(part, k * LANES) for part in parts for k in range(part.shape[1] // LANES)]
 
 
 def first_kernel(
-    near, far, small, x_first, y_second, far_a, sibling, sibling_a,
+    near, far, small, a_first, b_second, far_a, sibling, sibling_a,
     logw, message, target_logw, row_pot, ordered,
 ):
-    me = lax.axis_index("blk")
+    order = positions(lax.axis_index("blk"))
     places = block_places((near, far))
     block = sibling.shape[0] // 3
     smalls = [small[...], unpack(sibling, block)]
-    smalls += [unpack(x_first), unpack(sibling, 2 * block)]
-    smalls += [unpack(y_second), unpack(sibling, 3 * block)]
+    smalls += [unpack(a_first), unpack(sibling, 2 * block)]
+    smalls += [unpack(b_second), unpack(sibling, 3 * block)]
     smalls += [unpack(far_a), unpack(sibling_a)]
     columns = []
     for p in range(len(places)):
@@ -220,7 +237,7 @@
         return part[at, lane : lane + LANES]
 
     def partial_of(p, value):
-        ordered[pl.ds(jnp.bitwise_xor(me, p), 1), :] = value
+        ordered[pl.ds(order[p], 1), :] = value
 
     half_sweep(score_of, columns, near.shape[0], logw, row_pot, partial_of)
     message[...] = jnp.broadcast_to(ordered[...][None], message.shape)
@@ -229,14 +246,14 @@
 def second_kernel(
     copies, near, far, got, target_logw, logw, row, message, row_pot, ordered
 ):
-    me = lax.axis_index("blk")
+    order = positions(lax.axis_index("blk"))
     places = block_places((near, far))
     values = got[...]
     top = jnp.max(values, axis=0)
     ordered[...] = top + jnp.log2(jnp.sum(jnp.exp2(values - top[None]), axis=0))
     columns = []
     for p in range(len(places)):
-        total = ordered[pl.ds(jnp.bitwise_xor(me, p), 1), :]
+        total = ordered[pl.ds(order[p], 1), :]
         columns.append(target_logw[p : p + 1, :] * LOG2E - total)
 
     def score_of(at, p):
@@ -244,7 +261,7 @@
         return part[at, lane : lane + LANES]
 
     def partial_of(p, value):
-        at = pl.ds((len(places) - 1 - jnp.bitwise_xor(me, p)) * copies, copies)
+        at = pl.ds((len(places) - 1 - order[p]) * copies, copies)
         message[at, :] = jnp.broadcast_to(value, (copies, LANES))
 
     half_sweep(score_of, columns, near.shape[0], logw, row_pot, partial_of)
@@ -287,8 +304,13 @@
                 bytes_accessed=2 * (rows + targets) * depth,
             )
 
-        def over(array, step):
-            return lax.ppermute(array, "blk", [(i ^ step, i) for i in range(blk)])
+        def along(array, turn):
+            return lax.ppermute(
+                array, "blk", [(i ^ neighbour_step(i, turn), i) for i in range(blk)]
+            )
+
+        def to_sibling(array):
+            return fetch(array, "blk", 1, blk)
 
         def exchange(message):
             order = list(range(blk * grp))[::-1]
@@ -319,12 +341,12 @@
             ],
             compiler_params=params,
         )(*in_hbm(target_embed, target_init.reshape(1, width), target_logw.reshape(1, width)))
-        x_first = over(first, 1 * 2)
-        y_second = over(second, 2 * 2)
-        x_second = over(second_plain, 1 * 2)
-        y_first = over(first_plain, 2 * 2)
-        far_a = over(x_first, 2 * 2)
-        far_b = over(y_second, 1 * 2)
+        a_first = along(first, 0)
+        b_second = along(second, 1)
+        a_second = along(second_plain, 0)
+        b_first = along(first_plain, 1)
+        far_a = along(a_first, 1)
+        far_b = along(b_second, 0)
         source, logw, passed = pl.pallas_call(
             source_kernel,
             out_shape=(
@@ -337,7 +359,7 @@
             scratch_shapes=[pltpu.VMEM((1, rows), jnp.float32), pltpu.SemaphoreType.DMA((2,))],
             compiler_params=params,
         )(*in_hbm(source_embed, source_logw.reshape(1, rows)), whole)
-        near = (x_first, x_second, y_first, y_second)
+        near = (a_first, a_second, b_first, b_second)
         sibling = pl.pallas_call(
             sibling_kernel,
             out_shape=block_of(3 * (width + SPARE)),
@@ -346,7 +368,7 @@
             compiler_params=params,
             cost_estimate=cost(0, 0),
         )(passed, *near)
-        sibling = over(sibling, 1)
+        sibling = to_sibling(sibling)
 
         def passed_on(message, weight):
             return pl.pallas_call(
@@ -358,8 +380,8 @@
                 cost_estimate=cost(weight * width, 0),
             )(message)
 
-        sibling_a = over(passed_on(far_a, 0), 1)
-        sibling_b = over(passed_on(far_b, 50), 1)
+        sibling_a = to_sibling(passed_on(far_a, 0))
+        sibling_b = to_sibling(passed_on(far_b, 50))
 
         def products_of(kernel, blocks, weight, *pieces):
             return pl.pallas_call(
@@ -388,8 +410,8 @@
             scores_near,
             scores_far,
             small,
-            x_first,
-            y_second,
+            a_first,
+            b_second,
             far_a,
             sibling,
             sibling_a,

time: 41.6 us -> 41.5 us (level)
  starting transfers between devices: 9.61 us -> 9.13 us
    ppermute x9, starting transfers between devices: 9.61 us -> 9.13 us  [the longest x6 8.5 us: along(): lax.ppermute(array, 'blk', [(i ^ neighbour_step(i, turn), i) for i in ran...]
  transfers between devices with their start and end apart: 9 -> 9, of which waited for: 6 -> 5; matrix products, arithmetic and copies ran while one was open for 0% -> 0% of each run, Pallas kernels for 5% -> 5%
where the time goes in v5:
time: 41.5 us; the launch traced here: 41.3 us
  blocking collectives  21.8 us (53%)
  starting transfers between devices  9.13 us (22%)
  Pallas kernels  6.27 us (15%)
  waiting for transfers between devices  3.38 us (8%)
  between operations  0.74 us (2%)
    all_to_all x2, blocking collectives, exchange(): lax.all_to_all(message, ('blk', 'grp'), 0, 0, axis_index_groups=[order])  21.8 us
    ppermute x6, starting transfers between devices, along(): lax.ppermute(array, 'blk', [(i ^ neighbour_step(i, turn), i) for i in ran...  8.5 us
    ppermute x6, waiting for transfers between devices, along(): lax.ppermute(array, 'blk', [(i ^ neighbour_step(i, turn), i) for i in ran...  2.82 us
    pallas_call x1, Pallas kernels, shards_square(): pl.pallas_call(source_kernel, out_shape=(jax.ShapeDtypeStruct((rows, dept...  1.4 us
    pallas_call x2, Pallas kernels, products_of(): pl.pallas_call(functools.partial(kernel, factor), out_shape=values(rows,...  1.21 us
    pallas_call x1, Pallas kernels, shards_square(): pl.pallas_call(functools.partial(second_kernel, grp), out_shape=(values(1...  1.06 us
    pallas_call x1, Pallas kernels, shards_square(): pl.pallas_call(head_kernel, out_shape=(block_of(half + SPARE), block_of(h...  0.99 us
    pallas_call x1, Pallas kernels, shards_square(): pl.pallas_call(first_kernel, out_shape=(values(blk * grp, blk, width), va...  0.97 us
  transfers between devices with their start and end apart: 9, of which 5 were waited for; matrix products, arithmetic and copies ran while one was open for 0% of the time, Pallas kernels for 5%

profile of v5, /device:TPU:0, one launch (start us, length us, event | category | flops | bytes accessed | tf_op | source)
XLA Modules:
  0.0 41.3 jit_solution(16213786320730538093)
XLA Ops:
  0.6 1.0 %shard_map.68 = (bf16[72,768]{1,0:T(8,128)(2,1)S(1)}, bf16[72,768]{1,0:T(8,128)(2,1)S(1)}, bf16[136,768]{1,0:T(8,128)(2,1)S(1)}, f32[2,128]{1,0:T(2,128)S(1)}, b...) custom-call(bf16[128,768]{1,0:T(8,128)(2,1)} %own.1, f32[1,128]{1,0:T(1,128)} %bitcast.12, f32[1,128]{1,0:T(1,128)} %bitcast.13), custom_call_target="tpu_custom_call" | custom-call | tf_op jit(solution)/shard_map/pallas_call | solution.py:325
  1.6 3.0 %collective-permute-start = (bf16[72,768]{1,0:T(8,128)(2,1)S(1)}, bf16[72,768]{1,0:T(8,128)(2,1)S(1)}, u32[]{:S(2)}, u32[]{:S(2)}) collective-permute-start(bf16[72,768]{1,0:T(8,128)(2,1)S(1)} %get-tuple-element.19), channel_id=1, source_target_pairs={{8,0},{20,4},{0,8},{28,12},{24,16},{4,20},{16,24},{12,28},{9,1},{2... | collective-permute-start | bytes 331784 | tf_op jit(solution)/shard_map/ppermute | solution.py:308
  4.6 1.5 %collective-permute-start.3 = (bf16[72,768]{1,0:T(8,128)(2,1)S(1)}, bf16[72,768]{1,0:T(8,128)(2,1)S(1)}, u32[]{:S(2)}, u32[]{:S(2)}) collective-permute-start(bf16[72,768]{1,0:T(8,128)(2,1)S(1)} %get-tuple-element.22), channel_id=1, source_target_pairs={{16,0},{12,4},{24,8},{4,12},{0,16},{28,20},{8,24},{20,28},{17,1},{... | collective-permute-start | bytes 331784 | tf_op jit(solution)/shard_map/ppermute | solution.py:308
  6.2 0.5 %collective-permute-start.1 = (bf16[64,768]{1,0:T(8,128)(2,1)S(1)}, bf16[64,768]{1,0:T(8,128)(2,1)S(1)}, u32[]{:S(2)}, u32[]{:S(2)}) collective-permute-start(bf16[64,768]{1,0:T(8,128)(2,1)S(1)} %get-tuple-element.20), channel_id=1, source_target_pairs={{8,0},{20,4},{0,8},{28,12},{24,16},{4,20},{16,24},{12,28},{9,1},{2... | collective-permute-start | bytes 294920 | tf_op jit(solution)/shard_map/ppermute | solution.py:308
  6.7 0.1 collective-permute-start.2
  6.7 1.2 %collective-permute-done.a_first = bf16[72,768]{1,0:T(8,128)(2,1)S(1)} collective-permute-done((bf16[72,768]{1,0:T(8,128)(2,1)S(1)}, bf16[72,768]{1,0:T(8,128)(2,1)S(1)}, u32[]{:S(2)}, u32[]{:S(2)}) %collective-permute-start) | collective-permute-done | bytes 110624 | tf_op jit(solution)/shard_map/ppermute | solution.py:308
  8.0 1.6 %collective-permute-start.5 = (bf16[72,768]{1,0:T(8,128)(2,1)S(1)}, bf16[72,768]{1,0:T(8,128)(2,1)S(1)}, u32[]{:S(2)}, u32[]{:S(2)}) collective-permute-start(bf16[72,768]{1,0:T(8,128)(2,1)S(1)} %collective-permute-done.a_first), channel_id=1, source_target_pairs={{16,0},{12,4},{24,8},{4,12},{0,16},{28,20},{8,24},{20,28},{17,1},{... | collective-permute-start | bytes 331784 | tf_op jit(solution)/shard_map/ppermute | solution.py:308
  9.6 0.7 %collective-permute-done.3.b_second = bf16[72,768]{1,0:T(8,128)(2,1)S(1)} collective-permute-done((bf16[72,768]{1,0:T(8,128)(2,1)S(1)}, bf16[72,768]{1,0:T(8,128)(2,1)S(1)}, u32[]{:S(2)}, u32[]{:S(2)}) %collective-permute-start.3) | collective-permute-done | bytes 110624 | tf_op jit(solution)/shard_map/ppermute | solution.py:308
  10.3 1.8 %collective-permute-start.6 = (bf16[72,768]{1,0:T(8,128)(2,1)S(1)}, bf16[72,768]{1,0:T(8,128)(2,1)S(1)}, u32[]{:S(2)}, u32[]{:S(2)}) collective-permute-start(bf16[72,768]{1,0:T(8,128)(2,1)S(1)} %collective-permute-done.3.b_second), channel_id=1, source_target_pairs={{8,0},{20,4},{0,8},{28,12},{24,16},{4,20},{16,24},{12,28},{9,1},{2... | collective-permute-start | bytes 331784 | tf_op jit(solution)/shard_map/ppermute | solution.py:308
  12.1 1.4 %shard_map.69 = (bf16[512,768]{1,0:T(8,128)(2,1)S(1)}, f32[512,128]{1,0:T(8,128)S(1)}, bf16[136,768]{1,0:T(8,128)(2,1)S(1)}) custom-call(bf16[512,768]{1,0:T(8,128)(2,1)} %source.1, f32[1,512]{1,0:T(1,128)} %bitcast.11, bf16[136,768]{1,0:T(8,128)(2,1)S(1)} %get-tuple-element.17.whole), custom_call_target="tpu_custom_call" | custom-call | tf_op jit(solution)/shard_map/pallas_call | solution.py:350
  13.5 0.0 collective-permute-done.1.a_second
  13.5 0.0 collective-permute-done.2.b_first
  13.5 0.1 collective-permute-start.4
  13.6 0.1 collective-permute-done.5.message.far_a
  13.7 0.5 %collective-permute-start.7 = (bf16[72,768]{1,0:T(8,128)(2,1)S(1)}, bf16[72,768]{1,0:T(8,128)(2,1)S(1)}, u32[]{:S(2)}, u32[]{:S(2)}) collective-permute-start(bf16[72,768]{1,0:T(8,128)(2,1)S(1)} %shard_map.72), channel_id=1, source_target_pairs={{4,0},{0,4},{12,8},{8,12},{20,16},{16,20},{28,24},{24,28},{5,1},{1... | collective-permute-start | bytes 331784 | tf_op jit(solution)/shard_map/ppermute | solution.py:22
  14.2 0.8 %collective-permute-done.6.message.far_b = bf16[72,768]{1,0:T(8,128)(2,1)S(1)} collective-permute-done((bf16[72,768]{1,0:T(8,128)(2,1)S(1)}, bf16[72,768]{1,0:T(8,128)(2,1)S(1)}, u32[]{:S(2)}, u32[]{:S(2)}) %collective-permute-start.6) | collective-permute-done | bytes 110624 | tf_op jit(solution)/shard_map/ppermute | solution.py:308
  15.0 0.1 collective-permute-start.8
  15.1 0.6 %collective-permute-done.4.sibling = bf16[408,768]{1,0:T(8,128)(2,1)S(1)} collective-permute-done((bf16[408,768]{1,0:T(8,128)(2,1)S(1)}, bf16[408,768]{1,0:T(8,128)(2,1)S(1)}, u32[]{:S(2)}, u32[]{:S(2)}) %collective-permute-start.4) | collective-permute-done | bytes 626720 | tf_op jit(solution)/shard_map/ppermute | solution.py:22
  15.7 0.8 %shard_map.71.near = f32[512,768]{1,0:T(8,128)S(1)} custom-call(bf16[512,768]{1,0:T(8,128)(2,1)S(1)} %get-tuple-element.18.source, bf16[136,768]{1,0:T(8,128)(2,1)S(1)} %get-tuple-element.17.whole, bf16[72,768]{1,0:T(8,128)(2,1)S(1)} %collective-permute-done.a_first, bf16[64,768]{1,0:T(8,128)(2,1)S(1)} %collective-permute-done.1.a_second, ...), custom_call_target="tpu_custom_call" | custom-call | bytes 786432 | tf_op jit(solution)/shard_map/pallas_call | solution.py:387
  16.5 0.0 collective-permute-done.7.sibling_a
  16.5 0.0 collective-permute-done.8.sibling_b
  16.5 0.4 shard_map.74.far
  16.9 1.0 %shard_map.75 = (f32[32,8,128]{2,1,0:T(8,128)S(1)}, f32[8,128]{1,0:T(8,128)S(1)}) custom-call(f32[512,768]{1,0:T(8,128)S(1)} %shard_map.71.near, f32[512,256]{1,0:T(8,128)S(1)} %shard_map.74.far, f32[2,128]{1,0:T(2,128)S(1)} %get-tuple-element.24.small, bf16[72,768]{1,0:T(8,128)(2,1)S(1)} %collective-permute-done.a_first, ...), custom_call_target="tpu_custom_call" | custom-call | flops 8388608 | bytes 786432 | tf_op jit(solution)/shard_map/pallas_call | solution.py:401
  17.9 12.8 %all_to_all.16.got = f32[32,8,128]{2,1,0:T(8,128)S(1)} all-to-all(f32[32,8,128]{2,1,0:T(8,128)S(1)} %get-tuple-element.26), channel_id=1, replica_groups={{31,30,29,28,27,26,25,24,23,22,21,20,19,18,17,16,15,14,13,12,11,10,9,8,..., dimensions={0} | all-to-all | bytes 262144 | tf_op jit(solution)/shard_map/all_to_all | solution.py:317
  30.6 1.1 %shard_map.76 = (f32[1,512]{1,0:T(1,128)S(1)}, f32[32,128]{1,0:T(8,128)S(1)}) custom-call(f32[512,768]{1,0:T(8,128)S(1)} %shard_map.71.near, f32[512,256]{1,0:T(8,128)S(1)} %shard_map.74.far, f32[32,8,128]{2,1,0:T(8,128)S(1)} %all_to_all.16.got, f32[8,128]{1,0:T(8,128)S(1)} %get-tuple-element.27.target_logw, f32[512,128]{1,0:T(8,128)S(1)} %get-tuple-element.25.logw), custom_call_target="tpu_custom_call" | custom-call | flops 8388608 | bytes 786432 | tf_op jit(solution)/shard_map/pallas_call | solution.py:421
  31.7 9.0 %all_to_all.17 = f32[32,1,128]{2,1,0:T(1,128)S(1)} all-to-all(f32[32,1,128]{2,1,0:T(1,128)S(1)} %bitcast.10), channel_id=1, replica_groups={{31,30,29,28,27,26,25,24,23,22,21,20,19,18,17,16,15,14,13,12,11,10,9,8,..., dimensions={0} | all-to-all | bytes 32768 | tf_op jit(solution)/shard_map/all_to_all | solution.py:317
  40.7 0.6 %shard_map.77 = (f32[1,512]{1,0:T(1,128)}, f32[1,128]{1,0:T(1,128)}) custom-call(f32[32,128]{1,0:T(8,128)S(1)} %bitcast.9, f32[2,128]{1,0:T(2,128)S(1)} %get-tuple-element.24.small, f32[1,512]{1,0:T(1,128)S(1)} %get-tuple-element.29.row), custom_call_target="tpu_custom_call" | custom-call | tf_op jit(solution)/shard_map/pallas_call | solution.py:431
  (3 shorter events, 0.1 us)
Async XLA Ops:
  1.6 6.3 %collective-permute-start = (bf16[72,768]{1,0:T(8,128)(2,1)S(1)}, bf16[72,768]{1,0:T(8,128)(2,1)S(1)}, u32[]{:S(2)}, u32[]{:S(2)}) collective-permute-start(bf16[72,768]{1,0:T(8,128)(2,1)S(1)} %get-tuple-element.19), channel_id=1, source_target_pairs={{8,0},{20,4},{0,8},{28,12},{24,16},{4,20},{16,24},{12,28},{9,1},{2... | collective-permute-start | bytes 331784 | tf_op jit(solution)/shard_map/ppermute | solution.py:308
  4.6 5.6 %collective-permute-start.3 = (bf16[72,768]{1,0:T(8,128)(2,1)S(1)}, bf16[72,768]{1,0:T(8,128)(2,1)S(1)}, u32[]{:S(2)}, u32[]{:S(2)}) collective-permute-start(bf16[72,768]{1,0:T(8,128)(2,1)S(1)} %get-tuple-element.22), channel_id=1, source_target_pairs={{16,0},{12,4},{24,8},{4,12},{0,16},{28,20},{8,24},{20,28},{17,1},{... | collective-permute-start | bytes 331784 | tf_op jit(solution)/shard_map/ppermute | solution.py:308
  6.2 7.3 %collective-permute-start.1 = (bf16[64,768]{1,0:T(8,128)(2,1)S(1)}, bf16[64,768]{1,0:T(8,128)(2,1)S(1)}, u32[]{:S(2)}, u32[]{:S(2)}) collective-permute-start(bf16[64,768]{1,0:T(8,128)(2,1)S(1)} %get-tuple-element.20), channel_id=1, source_target_pairs={{8,0},{20,4},{0,8},{28,12},{24,16},{4,20},{16,24},{12,28},{9,1},{2... | collective-permute-start | bytes 294920 | tf_op jit(solution)/shard_map/ppermute | solution.py:308
  6.7 6.8 %collective-permute-start.2 = (bf16[64,768]{1,0:T(8,128)(2,1)S(1)}, bf16[64,768]{1,0:T(8,128)(2,1)S(1)}, u32[]{:S(2)}, u32[]{:S(2)}) collective-permute-start(bf16[64,768]{1,0:T(8,128)(2,1)S(1)} %get-tuple-element.21), channel_id=1, source_target_pairs={{16,0},{12,4},{24,8},{4,12},{0,16},{28,20},{8,24},{20,28},{17,1},{... | collective-permute-start | bytes 294920 | tf_op jit(solution)/shard_map/ppermute | solution.py:308
  8.0 5.7 %collective-permute-start.5 = (bf16[72,768]{1,0:T(8,128)(2,1)S(1)}, bf16[72,768]{1,0:T(8,128)(2,1)S(1)}, u32[]{:S(2)}, u32[]{:S(2)}) collective-permute-start(bf16[72,768]{1,0:T(8,128)(2,1)S(1)} %collective-permute-done.a_first), channel_id=1, source_target_pairs={{16,0},{12,4},{24,8},{4,12},{0,16},{28,20},{8,24},{20,28},{17,1},{... | collective-permute-start | bytes 331784 | tf_op jit(solution)/shard_map/ppermute | solution.py:308
  10.3 4.7 %collective-permute-start.6 = (bf16[72,768]{1,0:T(8,128)(2,1)S(1)}, bf16[72,768]{1,0:T(8,128)(2,1)S(1)}, u32[]{:S(2)}, u32[]{:S(2)}) collective-permute-start(bf16[72,768]{1,0:T(8,128)(2,1)S(1)} %collective-permute-done.3.b_second), channel_id=1, source_target_pairs={{8,0},{20,4},{0,8},{28,12},{24,16},{4,20},{16,24},{12,28},{9,1},{2... | collective-permute-start | bytes 331784 | tf_op jit(solution)/shard_map/ppermute | solution.py:308
  13.5 2.1 %collective-permute-start.4 = (bf16[408,768]{1,0:T(8,128)(2,1)S(1)}, bf16[408,768]{1,0:T(8,128)(2,1)S(1)}, u32[]{:S(2)}, u32[]{:S(2)}) collective-permute-start(bf16[408,768]{1,0:T(8,128)(2,1)S(1)} %shard_map.70), channel_id=1, source_target_pairs={{4,0},{0,4},{12,8},{8,12},{20,16},{16,20},{28,24},{24,28},{5,1},{1... | collective-permute-start | bytes 1880072 | tf_op jit(solution)/shard_map/ppermute | solution.py:22
  13.7 2.8 %collective-permute-start.7 = (bf16[72,768]{1,0:T(8,128)(2,1)S(1)}, bf16[72,768]{1,0:T(8,128)(2,1)S(1)}, u32[]{:S(2)}, u32[]{:S(2)}) collective-permute-start(bf16[72,768]{1,0:T(8,128)(2,1)S(1)} %shard_map.72), channel_id=1, source_target_pairs={{4,0},{0,4},{12,8},{8,12},{20,16},{16,20},{28,24},{24,28},{5,1},{1... | collective-permute-start | bytes 331784 | tf_op jit(solution)/shard_map/ppermute | solution.py:22
  15.0 1.5 %collective-permute-start.8 = (bf16[72,768]{1,0:T(8,128)(2,1)S(1)}, bf16[72,768]{1,0:T(8,128)(2,1)S(1)}, u32[]{:S(2)}, u32[]{:S(2)}) collective-permute-start(bf16[72,768]{1,0:T(8,128)(2,1)S(1)} %shard_map.73), channel_id=1, source_target_pairs={{4,0},{0,4},{12,8},{8,12},{20,16},{16,20},{28,24},{24,28},{5,1},{1... | collective-permute-start | bytes 331784 | tf_op jit(solution)/shard_map/ppermute | solution.py:22

commit v6 on v5

--- a/solution.py
+++ b/solution.py
@@ -59,50 +59,62 @@
     return jnp.concatenate(parts, axis=1)
 
 
-def half_sweep(score_of, columns, rows, logw, row_pot_of, partial_of):
-    blocks = len(columns)
-    chunk = 64
-    chunks = [pl.ds(start, chunk) for start in range(0, rows, chunk)]
+CHUNK = 64
+
+
+def chunks_of(rows):
+    return [pl.ds(start, CHUNK) for start in range(0, rows, CHUNK)]
+
+
+def row_sweep(score_of, blocks, rows, found_of, columns=None, others=None):
     tops = []
-    for at in chunks:
-        top = None
-        for p in range(blocks):
-            score = score_of(at, p) + columns[p]
+    for at in chunks_of(rows):
+        top = None if others is None else others[at, :]
+        for p in blocks:
+            score = score_of(at, p)
+            score = score if columns is None else score + columns[p]
             top = score if top is None else jnp.maximum(top, score)
         tops.append(jnp.max(top, axis=1, keepdims=True))
-    for at, top in zip(chunks, tops):
+    for at, top in zip(chunks_of(rows), tops):
         total = None
-        for p in range(blocks):
-            term = jnp.exp2(score_of(at, p) + (columns[p] - top))
+        for p in blocks:
+            shift = -top if columns is None else columns[p] - top
+            term = jnp.exp2(score_of(at, p) + shift)
             total = term if total is None else total + term
         total = jnp.sum(total, axis=1, keepdims=True)
-        row_pot_of[at, :] = logw[at, :] - (top + jnp.log2(total))
-    folds = (chunk // SUBLANES, SUBLANES, LANES)
-    found = [[] for _ in range(blocks)]
-    for at in chunks:
-        row_pot = row_pot_of[at, :]
-        for p in range(blocks):
-            score = score_of(at, p) + row_pot
-            top = jnp.max(score.reshape(folds), axis=0)
-            term = jnp.exp2(score.reshape(folds) - top[None])
-            found[p].append((top, jnp.sum(term, axis=0)))
-    for p in range(blocks):
+        if others is not None:
+            total = total + jnp.exp2(others[at, :] - top)
+        found_of(at, top + jnp.log2(total))
+
+
+def column_sweep(score_of, blocks, rows, row_pot, found_of):
+    folds = (CHUNK // SUBLANES, SUBLANES, LANES)
+    found = [[] for _ in blocks]
+    for at in chunks_of(rows):
+        addend = row_pot[at, :]
+        for p in blocks:
+            score = (score_of(at, p) + addend).reshape(folds)
+            top = jnp.max(score, axis=0)
+            found[p].append((top, jnp.sum(jnp.exp2(score - top[None]), axis=0)))
+    for p in blocks:
         top = functools.reduce(jnp.maximum, [each for each, _ in found[p]])
         top = jnp.max(top, axis=0, keepdims=True)
         total = sum(each * jnp.exp2(at_top - top) for at_top, each in found[p])
-        partial_of(p, top + jnp.log2(jnp.sum(total, axis=0, keepdims=True)))
-
-
-def products(source, targets, factor, out):
-    group = 2 * LANES
-    for start in range(0, targets.shape[0], group):
+        found_of(p, top + jnp.log2(jnp.sum(total, axis=0, keepdims=True)))
+
+
+def products(source, targets, factor, smalls, scaled, table):
+    for p, small in enumerate(smalls):
+        table[0, p : p + 1, :] = small[1:2] * LOG2E
+        table[1, p : p + 1, :] = small[0:1] * (inverse_eps * LOG2E)
+    for p in range(0, len(smalls), 2):
+        lanes = slice(p * LANES, (p + 2) * LANES)
         product = lax.dot_general(
-            source[...],
-            targets[start : start + group, :],
-            (((1,), (1,)), ((), ())),
+            source[...], targets[lanes, :], (((1,), (1,)), ((), ())),
             preferred_element_type=jnp.float32,
         )
-        out[:, start : start + group] = product * factor
+        shift = jnp.concatenate([table[1, p : p + 1, :], table[1, p + 1 : p + 2, :]], axis=1)
+        scaled[:, lanes] = product * factor + shift
 
 
 def head_kernel(
@@ -169,7 +181,10 @@
     return (parts[0] + parts[1]) + parts[2]
 
 
-def near_kernel(factor, source, whole, a_first, a_second, b_first, b_second, sibling, scaled, targets):
+def near_kernel(
+    factor, source, whole, a_first, a_second, b_first, b_second, sibling, scaled, table, found,
+    targets,
+):
     half = a_second.shape[0]
     width = 2 * half
     block = width + SPARE
@@ -181,18 +196,32 @@
     for k in range(3):
         start = (2 * k + 1) * width
         targets[start : start + width, :] = sibling[k * block : k * block + width, :]
-    products(source, targets, factor, scaled)
+    smalls = []
+    for k, message in enumerate((whole, a_first, b_second)):
+        smalls += [unpack(message), unpack(sibling, (k + 1) * block)]
+    products(source, targets, factor, smalls, scaled, table)
+
+    def score_of(at, p):
+        return scaled[at, p * LANES : (p + 1) * LANES]
+
+    def found_of(at, value):
+        found[at, :] = jnp.broadcast_to(value, (CHUNK, LANES))
+
+    row_sweep(score_of, range(len(smalls)), scaled.shape[0], found_of)
 
 
 def pass_kernel(message, out):
     out[...] = message[...]
 
 
-def far_kernel(factor, source, far_a, far_b, sibling_a, sibling_b, near, scaled, targets):
+def far_kernel(
+    factor, source, far_a, far_b, sibling_a, sibling_b, near, scaled, table, targets
+):
     half = targets.shape[0] // 4
     for k, piece in enumerate((far_a, far_b, sibling_a, sibling_b)):
         targets[k * half : (k + 1) * half, :] = piece[0:half, :]
-    products(source, targets, factor, scaled)
+    smalls = [unpack(far_a), unpack(sibling_a)]
+    products(source, targets, factor, smalls, scaled, table)
 
 
 def neighbour_step(me, turn):
@@ -212,59 +241,60 @@
     return [block for pair in zip(own, other) for block in pair]
 
 
-def block_places(parts):
-    return [(part, k * LANES) for part in parts for k in range(part.shape[1] // LANES)]
-
-
-def first_kernel(
-    near, far, small, a_first, b_second, far_a, sibling, sibling_a,
-    logw, message, target_logw, row_pot, ordered,
+class Held:
+
+    def __init__(self, near, near_table, far, far_table):
+        self.count = near.shape[1] // LANES
+        self.total = self.count + far.shape[1] // LANES
+        self.near, self.near_table, self.far, self.far_table = near, near_table, far, far_table
+
+    def score(self, at, p):
+        part, p = (self.near, p) if p < self.count else (self.far, p - self.count)
+        return part[at, p * LANES : (p + 1) * LANES]
+
+    def row(self, kind, p):
+        table, p = (self.near_table, p) if p < self.count else (self.far_table, p - self.count)
+        return table[kind, p : p + 1, :]
+
+
+def first_kernel(near, near_table, found, far, far_table, logw, message, row_pot, ordered):
+    order = positions(lax.axis_index("blk"))
+    held = Held(near, near_table, far, far_table)
+    rows = near.shape[0]
+
+    def row_found(at, value):
+        row_pot[at, :] = logw[at, :] - value
+
+    def column_found(p, value):
+        ordered[pl.ds(order[p], 1), :] = value - held.row(1, p)
+
+    row_sweep(held.score, range(held.count, held.total), rows, row_found, others=found)
+    column_sweep(held.score, range(held.total), rows, row_pot, column_found)
+    message[...] = jnp.broadcast_to(ordered[...][None], message.shape)
+
+
+def second_kernel(
+    copies, near, near_table, far, far_table, got, logw, row, message, row_pot, ordered
 ):
     order = positions(lax.axis_index("blk"))
-    places = block_places((near, far))
-    block = sibling.shape[0] // 3
-    smalls = [small[...], unpack(sibling, block)]
-    smalls += [unpack(a_first), unpack(sibling, 2 * block)]
-    smalls += [unpack(b_second), unpack(sibling, 3 * block)]
-    smalls += [unpack(far_a), unpack(sibling_a)]
-    columns = []
-    for p in range(len(places)):
-        columns.append(smalls[p][0:1] * (inverse_eps * LOG2E))
-        target_logw[p : p + 1, :] = smalls[p][1:2]
-
-    def score_of(at, p):
-        part, lane = places[p]
-        return part[at, lane : lane + LANES]
-
-    def partial_of(p, value):
-        ordered[pl.ds(order[p], 1), :] = value
-
-    half_sweep(score_of, columns, near.shape[0], logw, row_pot, partial_of)
-    message[...] = jnp.broadcast_to(ordered[...][None], message.shape)
-
-
-def second_kernel(
-    copies, near, far, got, target_logw, logw, row, message, row_pot, ordered
-):
-    order = positions(lax.axis_index("blk"))
-    places = block_places((near, far))
+    held = Held(near, near_table, far, far_table)
+    rows = near.shape[0]
     values = got[...]
     top = jnp.max(values, axis=0)
     ordered[...] = top + jnp.log2(jnp.sum(jnp.exp2(values - top[None]), axis=0))
     columns = []
-    for p in range(len(places)):
-        total = ordered[pl.ds(order[p], 1), :]
-        columns.append(target_logw[p : p + 1, :] * LOG2E - total)
-
-    def score_of(at, p):
-        part, lane = places[p]
-        return part[at, lane : lane + LANES]
-
-    def partial_of(p, value):
-        at = pl.ds((len(places) - 1 - order[p]) * copies, copies)
-        message[at, :] = jnp.broadcast_to(value, (copies, LANES))
-
-    half_sweep(score_of, columns, near.shape[0], logw, row_pot, partial_of)
+    for p in range(held.total):
+        columns.append(held.row(0, p) - ordered[pl.ds(order[p], 1), :] - held.row(1, p))
+
+    def row_found(at, value):
+        row_pot[at, :] = logw[at, :] - value
+
+    def column_found(p, value):
+        at = pl.ds((held.total - 1 - order[p]) * copies, copies)
+        message[at, :] = jnp.broadcast_to(value - held.row(1, p), (copies, LANES))
+
+    row_sweep(held.score, range(held.total), rows, row_found, columns=columns)
+    column_sweep(held.score, range(held.total), rows, row_pot, column_found)
     row[...] = as_row(row_pot[:, 0:1]) * (epsilon * LN2)
 
 
@@ -383,50 +413,49 @@
         sibling_a = to_sibling(passed_on(far_a, 0))
         sibling_b = to_sibling(passed_on(far_b, 50))
 
-        def products_of(kernel, blocks, weight, *pieces):
-            return pl.pallas_call(
-                functools.partial(kernel, factor),
-                out_shape=values(rows, blocks * width),
-                in_specs=[vmem] * (1 + len(pieces)),
-                out_specs=vmem,
-                scratch_shapes=[pltpu.VMEM((blocks * width, depth), target_embed.dtype)],
-                compiler_params=params,
-                cost_estimate=cost(weight * width, 0),
-            )(source, *pieces)
-
-        scores_near = products_of(near_kernel, 6, 0, whole, *near, sibling)
-        scores_far = products_of(far_kernel, 2, 0, far_a, far_b, sibling_a, sibling_b, scores_near)
+        def table():
+            return values(2, SUBLANES, width)
+
+        scores_near, table_near, found = pl.pallas_call(
+            functools.partial(near_kernel, factor),
+            out_shape=(values(rows, 6 * width), table(), values(rows, LANES)),
+            in_specs=[vmem] * 7,
+            out_specs=(vmem,) * 3,
+            scratch_shapes=[pltpu.VMEM((6 * width, depth), target_embed.dtype)],
+            compiler_params=params,
+            cost_estimate=cost(0, 0),
+        )(source, whole, *near, sibling)
+        scores_far, table_far = pl.pallas_call(
+            functools.partial(far_kernel, factor),
+            out_shape=(values(rows, 2 * width), table()),
+            in_specs=[vmem] * 6,
+            out_specs=(vmem, vmem),
+            scratch_shapes=[pltpu.VMEM((2 * width, depth), target_embed.dtype)],
+            compiler_params=params,
+            cost_estimate=cost(0, 0),
+        )(source, far_a, far_b, sibling_a, sibling_b, scores_near)
+        scores = (scores_far, table_far)
         row_scratch = pltpu.VMEM((rows, LANES), jnp.float32)
         block_scratch = pltpu.VMEM((blk, width), jnp.float32)
-        message, logw_all = pl.pallas_call(
+        message = pl.pallas_call(
             first_kernel,
-            out_shape=(values(blk * grp, blk, width), values(blk, width)),
-            in_specs=[vmem] * 9,
-            out_specs=(vmem, vmem),
+            out_shape=values(blk * grp, blk, width),
+            in_specs=[vmem] * 6,
+            out_specs=vmem,
             scratch_shapes=[row_scratch, block_scratch],
             compiler_params=params,
             cost_estimate=cost(0, 1),
-        )(
-            scores_near,
-            scores_far,
-            small,
-            a_first,
-            b_second,
-            far_a,
-            sibling,
-            sibling_a,
-            logw,
-        )
+        )(scores_near, table_near, found, *scores, logw)
         got = exchange(message)
         row, message = pl.pallas_call(
             functools.partial(second_kernel, grp),
             out_shape=(values(1, rows), values(blk * grp, width)),
-            in_specs=[vmem] * 5,
+            in_specs=[vmem] * 6,
             out_specs=(vmem, vmem),
             scratch_shapes=[row_scratch, block_scratch],
             compiler_params=params,
             cost_estimate=cost(0, 1),
-        )(scores_near, scores_far, got, logw_all, logw)
+        )(scores_near, table_near, *scores, got, logw)
         got = exchange(message)
         row_pot, column_pot = pl.pallas_call(
             last_kernel,

time: 41.5 us -> 41.2 us (level)
  transfers between devices with their start and end apart: 9 -> 9, of which waited for: 5 -> 5; matrix products, arithmetic and copies ran while one was open for 0% -> 0% of each run, Pallas kernels for 5% -> 6%
where the time goes in v6:
time: 41.2 us; the launch traced here: 41 us
  blocking collectives  21.5 us (52%)
  starting transfers between devices  9.13 us (22%)
  Pallas kernels  6.27 us (15%)
  waiting for transfers between devices  3.38 us (8%)
  between operations  0.74 us (2%)
    all_to_all x2, blocking collectives, exchange(): lax.all_to_all(message, ('blk', 'grp'), 0, 0, axis_index_groups=[order])  21.5 us
    ppermute x6, starting transfers between devices, along(): lax.ppermute(array, 'blk', [(i ^ neighbour_step(i, turn), i) for i in ran...  8.5 us
    ppermute x6, waiting for transfers between devices, along(): lax.ppermute(array, 'blk', [(i ^ neighbour_step(i, turn), i) for i in ran...  2.82 us
    pallas_call x1, Pallas kernels, shards_square(): pl.pallas_call(source_kernel, out_shape=(jax.ShapeDtypeStruct((rows, dept...  1.4 us
    pallas_call x1, Pallas kernels, shards_square(): pl.pallas_call(functools.partial(near_kernel, factor), out_shape=(values(...  1.1 us
    pallas_call x1, Pallas kernels, shards_square(): pl.pallas_call(functools.partial(second_kernel, grp), out_shape=(values(1...  1.03 us
    pallas_call x1, Pallas kernels, shards_square(): pl.pallas_call(head_kernel, out_shape=(block_of(half + SPARE), block_of(h...  0.99 us
  transfers between devices with their start and end apart: 9, of which 5 were waited for; matrix products, arithmetic and copies ran while one was open for 0% of the time, Pallas kernels for 6%

profile of v6, /device:TPU:0, one launch (start us, length us, event | category | flops | bytes accessed | tf_op | source)
XLA Modules:
  0.0 41.0 jit_solution(975329884211295732)
XLA Ops:
  0.6 1.0 %shard_map.68 = (bf16[72,768]{1,0:T(8,128)(2,1)S(1)}, bf16[72,768]{1,0:T(8,128)(2,1)S(1)}, bf16[136,768]{1,0:T(8,128)(2,1)S(1)}, f32[2,128]{1,0:T(2,128)S(1)}, b...) custom-call(bf16[128,768]{1,0:T(8,128)(2,1)} %own.1, f32[1,128]{1,0:T(1,128)} %bitcast.12, f32[1,128]{1,0:T(1,128)} %bitcast.13), custom_call_target="tpu_custom_call" | custom-call | tf_op jit(solution)/shard_map/pallas_call | solution.py:355
  1.6 3.0 %collective-permute-start = (bf16[72,768]{1,0:T(8,128)(2,1)S(1)}, bf16[72,768]{1,0:T(8,128)(2,1)S(1)}, u32[]{:S(2)}, u32[]{:S(2)}) collective-permute-start(bf16[72,768]{1,0:T(8,128)(2,1)S(1)} %get-tuple-element.22), channel_id=1, source_target_pairs={{8,0},{20,4},{0,8},{28,12},{24,16},{4,20},{16,24},{12,28},{9,1},{2... | collective-permute-start | bytes 331784 | tf_op jit(solution)/shard_map/ppermute | solution.py:338
  4.6 1.5 %collective-permute-start.3 = (bf16[72,768]{1,0:T(8,128)(2,1)S(1)}, bf16[72,768]{1,0:T(8,128)(2,1)S(1)}, u32[]{:S(2)}, u32[]{:S(2)}) collective-permute-start(bf16[72,768]{1,0:T(8,128)(2,1)S(1)} %get-tuple-element.25), channel_id=1, source_target_pairs={{16,0},{12,4},{24,8},{4,12},{0,16},{28,20},{8,24},{20,28},{17,1},{... | collective-permute-start | bytes 331784 | tf_op jit(solution)/shard_map/ppermute | solution.py:338
  6.2 0.5 %collective-permute-start.1 = (bf16[64,768]{1,0:T(8,128)(2,1)S(1)}, bf16[64,768]{1,0:T(8,128)(2,1)S(1)}, u32[]{:S(2)}, u32[]{:S(2)}) collective-permute-start(bf16[64,768]{1,0:T(8,128)(2,1)S(1)} %get-tuple-element.23), channel_id=1, source_target_pairs={{8,0},{20,4},{0,8},{28,12},{24,16},{4,20},{16,24},{12,28},{9,1},{2... | collective-permute-start | bytes 294920 | tf_op jit(solution)/shard_map/ppermute | solution.py:338
  6.7 0.1 collective-permute-start.2
  6.7 1.2 %collective-permute-done.a_first = bf16[72,768]{1,0:T(8,128)(2,1)S(1)} collective-permute-done((bf16[72,768]{1,0:T(8,128)(2,1)S(1)}, bf16[72,768]{1,0:T(8,128)(2,1)S(1)}, u32[]{:S(2)}, u32[]{:S(2)}) %collective-permute-start) | collective-permute-done | bytes 110624 | tf_op jit(solution)/shard_map/ppermute | solution.py:338
  8.0 1.6 %collective-permute-start.5 = (bf16[72,768]{1,0:T(8,128)(2,1)S(1)}, bf16[72,768]{1,0:T(8,128)(2,1)S(1)}, u32[]{:S(2)}, u32[]{:S(2)}) collective-permute-start(bf16[72,768]{1,0:T(8,128)(2,1)S(1)} %collective-permute-done.a_first), channel_id=1, source_target_pairs={{16,0},{12,4},{24,8},{4,12},{0,16},{28,20},{8,24},{20,28},{17,1},{... | collective-permute-start | bytes 331784 | tf_op jit(solution)/shard_map/ppermute | solution.py:338
  9.6 0.7 %collective-permute-done.3.b_second = bf16[72,768]{1,0:T(8,128)(2,1)S(1)} collective-permute-done((bf16[72,768]{1,0:T(8,128)(2,1)S(1)}, bf16[72,768]{1,0:T(8,128)(2,1)S(1)}, u32[]{:S(2)}, u32[]{:S(2)}) %collective-permute-start.3) | collective-permute-done | bytes 110624 | tf_op jit(solution)/shard_map/ppermute | solution.py:338
  10.3 1.8 %collective-permute-start.6 = (bf16[72,768]{1,0:T(8,128)(2,1)S(1)}, bf16[72,768]{1,0:T(8,128)(2,1)S(1)}, u32[]{:S(2)}, u32[]{:S(2)}) collective-permute-start(bf16[72,768]{1,0:T(8,128)(2,1)S(1)} %collective-permute-done.3.b_second), channel_id=1, source_target_pairs={{8,0},{20,4},{0,8},{28,12},{24,16},{4,20},{16,24},{12,28},{9,1},{2... | collective-permute-start | bytes 331784 | tf_op jit(solution)/shard_map/ppermute | solution.py:338
  12.1 1.4 %shard_map.69 = (bf16[512,768]{1,0:T(8,128)(2,1)S(1)}, f32[512,128]{1,0:T(8,128)S(1)}, bf16[136,768]{1,0:T(8,128)(2,1)S(1)}) custom-call(bf16[512,768]{1,0:T(8,128)(2,1)} %source.1, f32[1,512]{1,0:T(1,128)} %bitcast.11, bf16[136,768]{1,0:T(8,128)(2,1)S(1)} %get-tuple-element.20.whole), custom_call_target="tpu_custom_call" | custom-call | tf_op jit(solution)/shard_map/pallas_call | solution.py:380
  13.5 0.0 collective-permute-done.1.a_second
  13.5 0.0 collective-permute-done.2.b_first
  13.5 0.1 collective-permute-start.4
  13.6 0.1 collective-permute-done.5.message.far_a
  13.7 0.5 %collective-permute-start.7 = (bf16[72,768]{1,0:T(8,128)(2,1)S(1)}, bf16[72,768]{1,0:T(8,128)(2,1)S(1)}, u32[]{:S(2)}, u32[]{:S(2)}) collective-permute-start(bf16[72,768]{1,0:T(8,128)(2,1)S(1)} %shard_map.72), channel_id=1, source_target_pairs={{4,0},{0,4},{12,8},{8,12},{20,16},{16,20},{28,24},{24,28},{5,1},{1... | collective-permute-start | bytes 331784 | tf_op jit(solution)/shard_map/ppermute | solution.py:22
  14.2 0.8 %collective-permute-done.6.message.far_b = bf16[72,768]{1,0:T(8,128)(2,1)S(1)} collective-permute-done((bf16[72,768]{1,0:T(8,128)(2,1)S(1)}, bf16[72,768]{1,0:T(8,128)(2,1)S(1)}, u32[]{:S(2)}, u32[]{:S(2)}) %collective-permute-start.6) | collective-permute-done | bytes 110624 | tf_op jit(solution)/shard_map/ppermute | solution.py:338
  15.0 0.1 collective-permute-start.8
  15.1 0.6 %collective-permute-done.4.sibling = bf16[408,768]{1,0:T(8,128)(2,1)S(1)} collective-permute-done((bf16[408,768]{1,0:T(8,128)(2,1)S(1)}, bf16[408,768]{1,0:T(8,128)(2,1)S(1)}, u32[]{:S(2)}, u32[]{:S(2)}) %collective-permute-start.4) | collective-permute-done | bytes 626720 | tf_op jit(solution)/shard_map/ppermute | solution.py:22
  15.7 1.1 %shard_map.71 = (f32[512,768]{1,0:T(8,128)S(1)}, f32[2,8,128]{2,1,0:T(8,128)S(1)}, f32[512,128]{1,0:T(8,128)S(1)}) custom-call(bf16[512,768]{1,0:T(8,128)(2,1)S(1)} %get-tuple-element.21.source, bf16[136,768]{1,0:T(8,128)(2,1)S(1)} %get-tuple-element.20.whole, bf16[72,768]{1,0:T(8,128)(2,1)S(1)} %collective-permute-done.a_first, ...), custom_call_target="tpu_custom_call" | custom-call | bytes 786432 | tf_op jit(solution)/shard_map/pallas_call | solution.py:419
  16.8 0.0 collective-permute-done.7.sibling_a
  16.8 0.0 collective-permute-done.8.sibling_b
  16.8 0.4 shard_map.74
  17.2 0.7 %shard_map.75 = f32[32,8,128]{2,1,0:T(8,128)S(1)} custom-call(f32[512,768]{1,0:T(8,128)S(1)} %get-tuple-element.27.near, f32[2,8,128]{2,1,0:T(8,128)S(1)} %get-tuple-element.28.near_table, f32[512,128]{1,0:T(8,128)S(1)} %get-tuple-element.31.found, f32[512,256]{1,0:T(8,128)S(1)} %get-tuple-element.29.far, f32[2,8,128]{2,1,0:T(8,128)S(1)} %get-tuple-element.30.far_table, ...), custom_call_target="tpu_custom_call" | custom-call | flops 8388608 | bytes 786432 | tf_op jit(solution)/shard_map/pallas_call | solution.py:440
  17.9 12.5 %all_to_all.16.got = f32[32,8,128]{2,1,0:T(8,128)S(1)} all-to-all(f32[32,8,128]{2,1,0:T(8,128)S(1)} %shard_map.75), channel_id=1, replica_groups={{31,30,29,28,27,26,25,24,23,22,21,20,19,18,17,16,15,14,13,12,11,10,9,8,..., dimensions={0} | all-to-all | bytes 262144 | tf_op jit(solution)/shard_map/all_to_all | solution.py:347
  30.4 1.0 %shard_map.76 = (f32[1,512]{1,0:T(1,128)S(1)}, f32[32,128]{1,0:T(8,128)S(1)}) custom-call(f32[512,768]{1,0:T(8,128)S(1)} %get-tuple-element.27.near, f32[2,8,128]{2,1,0:T(8,128)S(1)} %get-tuple-element.28.near_table, f32[512,256]{1,0:T(8,128)S(1)} %get-tuple-element.29.far, f32[2,8,128]{2,1,0:T(8,128)S(1)} %get-tuple-element.30.far_table, ...), custom_call_target="tpu_custom_call" | custom-call | flops 8388608 | bytes 786432 | tf_op jit(solution)/shard_map/pallas_call | solution.py:450
  31.4 9.0 %all_to_all.17 = f32[32,1,128]{2,1,0:T(1,128)S(1)} all-to-all(f32[32,1,128]{2,1,0:T(1,128)S(1)} %bitcast.10), channel_id=1, replica_groups={{31,30,29,28,27,26,25,24,23,22,21,20,19,18,17,16,15,14,13,12,11,10,9,8,..., dimensions={0} | all-to-all | bytes 32768 | tf_op jit(solution)/shard_map/all_to_all | solution.py:347
  40.4 0.6 %shard_map.77 = (f32[1,512]{1,0:T(1,128)}, f32[1,128]{1,0:T(1,128)}) custom-call(f32[32,128]{1,0:T(8,128)S(1)} %bitcast.9, f32[2,128]{1,0:T(2,128)S(1)} %get-tuple-element.34.small, f32[1,512]{1,0:T(1,128)S(1)} %get-tuple-element.35.row), custom_call_target="tpu_custom_call" | custom-call | tf_op jit(solution)/shard_map/pallas_call | solution.py:460
  (3 shorter events, 0.1 us)
Async XLA Ops:
  1.6 6.3 %collective-permute-start = (bf16[72,768]{1,0:T(8,128)(2,1)S(1)}, bf16[72,768]{1,0:T(8,128)(2,1)S(1)}, u32[]{:S(2)}, u32[]{:S(2)}) collective-permute-start(bf16[72,768]{1,0:T(8,128)(2,1)S(1)} %get-tuple-element.22), channel_id=1, source_target_pairs={{8,0},{20,4},{0,8},{28,12},{24,16},{4,20},{16,24},{12,28},{9,1},{2... | collective-permute-start | bytes 331784 | tf_op jit(solution)/shard_map/ppermute | solution.py:338
  4.6 5.6 %collective-permute-start.3 = (bf16[72,768]{1,0:T(8,128)(2,1)S(1)}, bf16[72,768]{1,0:T(8,128)(2,1)S(1)}, u32[]{:S(2)}, u32[]{:S(2)}) collective-permute-start(bf16[72,768]{1,0:T(8,128)(2,1)S(1)} %get-tuple-element.25), channel_id=1, source_target_pairs={{16,0},{12,4},{24,8},{4,12},{0,16},{28,20},{8,24},{20,28},{17,1},{... | collective-permute-start | bytes 331784 | tf_op jit(solution)/shard_map/ppermute | solution.py:338
  6.2 7.3 %collective-permute-start.1 = (bf16[64,768]{1,0:T(8,128)(2,1)S(1)}, bf16[64,768]{1,0:T(8,128)(2,1)S(1)}, u32[]{:S(2)}, u32[]{:S(2)}) collective-permute-start(bf16[64,768]{1,0:T(8,128)(2,1)S(1)} %get-tuple-element.23), channel_id=1, source_target_pairs={{8,0},{20,4},{0,8},{28,12},{24,16},{4,20},{16,24},{12,28},{9,1},{2... | collective-permute-start | bytes 294920 | tf_op jit(solution)/shard_map/ppermute | solution.py:338
  6.7 6.8 %collective-permute-start.2 = (bf16[64,768]{1,0:T(8,128)(2,1)S(1)}, bf16[64,768]{1,0:T(8,128)(2,1)S(1)}, u32[]{:S(2)}, u32[]{:S(2)}) collective-permute-start(bf16[64,768]{1,0:T(8,128)(2,1)S(1)} %get-tuple-element.24), channel_id=1, source_target_pairs={{16,0},{12,4},{24,8},{4,12},{0,16},{28,20},{8,24},{20,28},{17,1},{... | collective-permute-start | bytes 294920 | tf_op jit(solution)/shard_map/ppermute | solution.py:338
  8.0 5.7 %collective-permute-start.5 = (bf16[72,768]{1,0:T(8,128)(2,1)S(1)}, bf16[72,768]{1,0:T(8,128)(2,1)S(1)}, u32[]{:S(2)}, u32[]{:S(2)}) collective-permute-start(bf16[72,768]{1,0:T(8,128)(2,1)S(1)} %collective-permute-done.a_first), channel_id=1, source_target_pairs={{16,0},{12,4},{24,8},{4,12},{0,16},{28,20},{8,24},{20,28},{17,1},{... | collective-permute-start | bytes 331784 | tf_op jit(solution)/shard_map/ppermute | solution.py:338
  10.3 4.7 %collective-permute-start.6 = (bf16[72,768]{1,0:T(8,128)(2,1)S(1)}, bf16[72,768]{1,0:T(8,128)(2,1)S(1)}, u32[]{:S(2)}, u32[]{:S(2)}) collective-permute-start(bf16[72,768]{1,0:T(8,128)(2,1)S(1)} %collective-permute-done.3.b_second), channel_id=1, source_target_pairs={{8,0},{20,4},{0,8},{28,12},{24,16},{4,20},{16,24},{12,28},{9,1},{2... | collective-permute-start | bytes 331784 | tf_op jit(solution)/shard_map/ppermute | solution.py:338
  13.5 2.1 %collective-permute-start.4 = (bf16[408,768]{1,0:T(8,128)(2,1)S(1)}, bf16[408,768]{1,0:T(8,128)(2,1)S(1)}, u32[]{:S(2)}, u32[]{:S(2)}) collective-permute-start(bf16[408,768]{1,0:T(8,128)(2,1)S(1)} %shard_map.70), channel_id=1, source_target_pairs={{4,0},{0,4},{12,8},{8,12},{20,16},{16,20},{28,24},{24,28},{5,1},{1... | collective-permute-start | bytes 1880072 | tf_op jit(solution)/shard_map/ppermute | solution.py:22
  13.7 3.1 %collective-permute-start.7 = (bf16[72,768]{1,0:T(8,128)(2,1)S(1)}, bf16[72,768]{1,0:T(8,128)(2,1)S(1)}, u32[]{:S(2)}, u32[]{:S(2)}) collective-permute-start(bf16[72,768]{1,0:T(8,128)(2,1)S(1)} %shard_map.72), channel_id=1, source_target_pairs={{4,0},{0,4},{12,8},{8,12},{20,16},{16,20},{28,24},{24,28},{5,1},{1... | collective-permute-start | bytes 331784 | tf_op jit(solution)/shard_map/ppermute | solution.py:22
  15.0 1.8 %collective-permute-start.8 = (bf16[72,768]{1,0:T(8,128)(2,1)S(1)}, bf16[72,768]{1,0:T(8,128)(2,1)S(1)}, u32[]{:S(2)}, u32[]{:S(2)}) collective-permute-start(bf16[72,768]{1,0:T(8,128)(2,1)S(1)} %shard_map.73), channel_id=1, source_target_pairs={{4,0},{0,4},{12,8},{8,12},{20,16},{16,20},{28,24},{24,28},{5,1},{1... | collective-permute-start | bytes 331784 | tf_op jit(solution)/shard_map/ppermute | solution.py:22

commit v7 on v6

--- a/solution.py
+++ b/solution.py
@@ -148,14 +148,17 @@
         rest = rest - part.astype(jnp.float32)
 
 
-def source_kernel(source, logw, whole, held, row_logw, passed, rows_row, sems):
+def source_kernel(
+    source, logw, first, second, held, row_logw, first_out, second_out, rows_row, sems
+):
     copies = [
         pltpu.make_async_copy(source, held, sems.at[0]),
         pltpu.make_async_copy(logw, rows_row, sems.at[1]),
     ]
     for copy in copies:
         copy.start()
-    passed[...] = whole[...]
+    first_out[...] = first[...]
+    second_out[...] = second[...]
     for copy in copies:
         copy.wait()
     row_logw[...] = jnp.broadcast_to(as_column(rows_row[...] * LOG2E), row_logw.shape)
@@ -371,24 +374,25 @@
             ],
             compiler_params=params,
         )(*in_hbm(target_embed, target_init.reshape(1, width), target_logw.reshape(1, width)))
+        source, logw, first_plain, second_plain = pl.pallas_call(
+            source_kernel,
+            out_shape=(
+                jax.ShapeDtypeStruct((rows, depth), source_embed.dtype),
+                values(rows, LANES),
+                block_of(half),
+                block_of(half),
+            ),
+            in_specs=[hbm] * 2 + [vmem] * 2,
+            out_specs=(vmem,) * 4,
+            scratch_shapes=[pltpu.VMEM((1, rows), jnp.float32), pltpu.SemaphoreType.DMA((2,))],
+            compiler_params=params,
+        )(*in_hbm(source_embed, source_logw.reshape(1, rows)), first_plain, second_plain)
         a_first = along(first, 0)
         b_second = along(second, 1)
         a_second = along(second_plain, 0)
         b_first = along(first_plain, 1)
         far_a = along(a_first, 1)
         far_b = along(b_second, 0)
-        source, logw, passed = pl.pallas_call(
-            source_kernel,
-            out_shape=(
-                jax.ShapeDtypeStruct((rows, depth), source_embed.dtype),
-                values(rows, LANES),
-                block_of(width + SPARE),
-            ),
-            in_specs=[hbm] * 2 + [vmem],
-            out_specs=(vmem,) * 3,
-            scratch_shapes=[pltpu.VMEM((1, rows), jnp.float32), pltpu.SemaphoreType.DMA((2,))],
-            compiler_params=params,
-        )(*in_hbm(source_embed, source_logw.reshape(1, rows)), whole)
         near = (a_first, a_second, b_first, b_second)
         sibling = pl.pallas_call(
             sibling_kernel,
@@ -397,7 +401,7 @@
             out_specs=vmem,
             compiler_params=params,
             cost_estimate=cost(0, 0),
-        )(passed, *near)
+        )(whole, *near)
         sibling = to_sibling(sibling)
 
         def passed_on(message, weight):

time: 41.2 us -> 41.6 us (level)
    all_to_all x2, blocking collectives: 21.5 us -> 21.9 us  [exchange(): lax.all_to_all(message, ('blk', 'grp'), 0, 0, axis_index_groups=[order])]
where the time goes in v7:
time: 41.6 us; the launch traced here: 41.4 us
  blocking collectives  21.9 us (53%)
  starting transfers between devices  9.17 us (22%)
  Pallas kernels  6.27 us (15%)
  waiting for transfers between devices  3.36 us (8%)
  between operations  0.72 us (2%)
    all_to_all x2, blocking collectives, exchange(): lax.all_to_all(message, ('blk', 'grp'), 0, 0, axis_index_groups=[order])  21.9 us
    ppermute x6, starting transfers between devices, along(): lax.ppermute(array, 'blk', [(i ^ neighbour_step(i, turn), i) for i in ran...  8.64 us
    ppermute x6, waiting for transfers between devices, along(): lax.ppermute(array, 'blk', [(i ^ neighbour_step(i, turn), i) for i in ran...  3.04 us
    pallas_call x1, Pallas kernels, shards_square(): pl.pallas_call(source_kernel, out_shape=(jax.ShapeDtypeStruct((rows, dept...  1.4 us
    pallas_call x1, Pallas kernels, shards_square(): pl.pallas_call(functools.partial(near_kernel, factor), out_shape=(values(...  1.1 us
    pallas_call x1, Pallas kernels, shards_square(): pl.pallas_call(functools.partial(second_kernel, grp), out_shape=(values(1...  1.03 us
    pallas_call x1, Pallas kernels, shards_square(): pl.pallas_call(head_kernel, out_shape=(block_of(half + SPARE), block_of(h...  0.99 us
  transfers between devices with their start and end apart: 9, of which 5 were waited for; matrix products, arithmetic and copies ran while one was open for 0% of the time, Pallas kernels for 6%

profile of v7, /device:TPU:0, one launch (start us, length us, event | category | flops | bytes accessed | tf_op | source)
XLA Modules:
  0.0 41.4 jit_solution(12461959088749194325)
XLA Ops:
  0.6 1.0 %shard_map.68 = (bf16[72,768]{1,0:T(8,128)(2,1)S(1)}, bf16[72,768]{1,0:T(8,128)(2,1)S(1)}, bf16[136,768]{1,0:T(8,128)(2,1)S(1)}, f32[2,128]{1,0:T(2,128)S(1)}, b...) custom-call(bf16[128,768]{1,0:T(8,128)(2,1)} %own.1, f32[1,128]{1,0:T(1,128)} %bitcast.12, f32[1,128]{1,0:T(1,128)} %bitcast.13), custom_call_target="tpu_custom_call" | custom-call | tf_op jit(solution)/shard_map/pallas_call | solution.py:358
  1.6 3.0 %collective-permute-start = (bf16[72,768]{1,0:T(8,128)(2,1)S(1)}, bf16[72,768]{1,0:T(8,128)(2,1)S(1)}, u32[]{:S(2)}, u32[]{:S(2)}) collective-permute-start(bf16[72,768]{1,0:T(8,128)(2,1)S(1)} %get-tuple-element.25), channel_id=1, source_target_pairs={{8,0},{20,4},{0,8},{28,12},{24,16},{4,20},{16,24},{12,28},{9,1},{2... | collective-permute-start | bytes 331784 | tf_op jit(solution)/shard_map/ppermute | solution.py:341
  4.6 1.5 %collective-permute-start.3 = (bf16[72,768]{1,0:T(8,128)(2,1)S(1)}, bf16[72,768]{1,0:T(8,128)(2,1)S(1)}, u32[]{:S(2)}, u32[]{:S(2)}) collective-permute-start(bf16[72,768]{1,0:T(8,128)(2,1)S(1)} %get-tuple-element.28), channel_id=1, source_target_pairs={{16,0},{12,4},{24,8},{4,12},{0,16},{28,20},{8,24},{20,28},{17,1},{... | collective-permute-start | bytes 331784 | tf_op jit(solution)/shard_map/ppermute | solution.py:341
  6.2 1.4 %shard_map.69 = (bf16[512,768]{1,0:T(8,128)(2,1)S(1)}, f32[512,128]{1,0:T(8,128)S(1)}, bf16[64,768]{1,0:T(8,128)(2,1)S(1)}, bf16[64,768]{1,0:T(8,128)(2,1)S(1)}) custom-call(bf16[512,768]{1,0:T(8,128)(2,1)} %source.1, f32[1,512]{1,0:T(1,128)} %bitcast.11, bf16[64,768]{1,0:T(8,128)(2,1)S(1)} %get-tuple-element.21.first, ...), custom_call_target="tpu_custom_call" | custom-call | tf_op jit(solution)/shard_map/pallas_call | solution.py:377
  7.6 0.6 %collective-permute-start.1 = (bf16[64,768]{1,0:T(8,128)(2,1)S(1)}, bf16[64,768]{1,0:T(8,128)(2,1)S(1)}, u32[]{:S(2)}, u32[]{:S(2)}) collective-permute-start(bf16[64,768]{1,0:T(8,128)(2,1)S(1)} %get-tuple-element.26), channel_id=1, source_target_pairs={{8,0},{20,4},{0,8},{28,12},{24,16},{4,20},{16,24},{12,28},{9,1},{2... | collective-permute-start | bytes 294920 | tf_op jit(solution)/shard_map/ppermute | solution.py:341
  8.2 0.1 collective-permute-start.2
  8.2 0.0 collective-permute-done.a_first
  8.2 2.0 %collective-permute-start.5 = (bf16[72,768]{1,0:T(8,128)(2,1)S(1)}, bf16[72,768]{1,0:T(8,128)(2,1)S(1)}, u32[]{:S(2)}, u32[]{:S(2)}) collective-permute-start(bf16[72,768]{1,0:T(8,128)(2,1)S(1)} %collective-permute-done.a_first), channel_id=1, source_target_pairs={{16,0},{12,4},{24,8},{4,12},{0,16},{28,20},{8,24},{20,28},{17,1},{... | collective-permute-start | bytes 331784 | tf_op jit(solution)/shard_map/ppermute | solution.py:341
  10.2 0.0 collective-permute-done.3.b_second
  10.2 1.5 %collective-permute-start.6 = (bf16[72,768]{1,0:T(8,128)(2,1)S(1)}, bf16[72,768]{1,0:T(8,128)(2,1)S(1)}, u32[]{:S(2)}, u32[]{:S(2)}) collective-permute-start(bf16[72,768]{1,0:T(8,128)(2,1)S(1)} %collective-permute-done.3.b_second), channel_id=1, source_target_pairs={{8,0},{20,4},{0,8},{28,12},{24,16},{4,20},{16,24},{12,28},{9,1},{2... | collective-permute-start | bytes 331784 | tf_op jit(solution)/shard_map/ppermute | solution.py:341
  11.7 1.3 %collective-permute-done.1.a_second = bf16[64,768]{1,0:T(8,128)(2,1)S(1)} collective-permute-done((bf16[64,768]{1,0:T(8,128)(2,1)S(1)}, bf16[64,768]{1,0:T(8,128)(2,1)S(1)}, u32[]{:S(2)}, u32[]{:S(2)}) %collective-permute-start.1) | collective-permute-done | bytes 98336 | tf_op jit(solution)/shard_map/ppermute | solution.py:341
  13.0 0.5 %collective-permute-done.2.b_first = bf16[64,768]{1,0:T(8,128)(2,1)S(1)} collective-permute-done((bf16[64,768]{1,0:T(8,128)(2,1)S(1)}, bf16[64,768]{1,0:T(8,128)(2,1)S(1)}, u32[]{:S(2)}, u32[]{:S(2)}) %collective-permute-start.2) | collective-permute-done | bytes 98336 | tf_op jit(solution)/shard_map/ppermute | solution.py:341
  13.5 0.1 collective-permute-start.4
  13.6 1.1 %collective-permute-done.5.message.far_a = bf16[72,768]{1,0:T(8,128)(2,1)S(1)} collective-permute-done((bf16[72,768]{1,0:T(8,128)(2,1)S(1)}, bf16[72,768]{1,0:T(8,128)(2,1)S(1)}, u32[]{:S(2)}, u32[]{:S(2)}) %collective-permute-start.5) | collective-permute-done | bytes 110624 | tf_op jit(solution)/shard_map/ppermute | solution.py:341
  14.7 0.1 collective-permute-start.7
  14.8 0.2 collective-permute-done.6.message.far_b
  15.0 0.4 collective-permute-start.8
  15.3 0.3 collective-permute-done.4.sibling
  15.7 1.1 %shard_map.71 = (f32[512,768]{1,0:T(8,128)S(1)}, f32[2,8,128]{2,1,0:T(8,128)S(1)}, f32[512,128]{1,0:T(8,128)S(1)}) custom-call(bf16[512,768]{1,0:T(8,128)(2,1)S(1)} %get-tuple-element.23.source, bf16[136,768]{1,0:T(8,128)(2,1)S(1)} %get-tuple-element.24.whole, bf16[72,768]{1,0:T(8,128)(2,1)S(1)} %collective-permute-done.a_first, ...), custom_call_target="tpu_custom_call" | custom-call | bytes 786432 | tf_op jit(solution)/shard_map/pallas_call | solution.py:423
  16.8 0.0 collective-permute-done.7.sibling_a
  16.8 0.0 collective-permute-done.8.sibling_b
  16.8 0.4 shard_map.74
  17.2 0.7 %shard_map.75 = f32[32,8,128]{2,1,0:T(8,128)S(1)} custom-call(f32[512,768]{1,0:T(8,128)S(1)} %get-tuple-element.29.near, f32[2,8,128]{2,1,0:T(8,128)S(1)} %get-tuple-element.30.near_table, f32[512,128]{1,0:T(8,128)S(1)} %get-tuple-element.33.found, f32[512,256]{1,0:T(8,128)S(1)} %get-tuple-element.31.far, f32[2,8,128]{2,1,0:T(8,128)S(1)} %get-tuple-element.32.far_table, ...), custom_call_target="tpu_custom_call" | custom-call | flops 8388608 | bytes 786432 | tf_op jit(solution)/shard_map/pallas_call | solution.py:444
  17.9 12.9 %all_to_all.16.got = f32[32,8,128]{2,1,0:T(8,128)S(1)} all-to-all(f32[32,8,128]{2,1,0:T(8,128)S(1)} %shard_map.75), channel_id=1, replica_groups={{31,30,29,28,27,26,25,24,23,22,21,20,19,18,17,16,15,14,13,12,11,10,9,8,..., dimensions={0} | all-to-all | bytes 262144 | tf_op jit(solution)/shard_map/all_to_all | solution.py:350
  30.8 1.0 %shard_map.76 = (f32[1,512]{1,0:T(1,128)S(1)}, f32[32,128]{1,0:T(8,128)S(1)}) custom-call(f32[512,768]{1,0:T(8,128)S(1)} %get-tuple-element.29.near, f32[2,8,128]{2,1,0:T(8,128)S(1)} %get-tuple-element.30.near_table, f32[512,256]{1,0:T(8,128)S(1)} %get-tuple-element.31.far, f32[2,8,128]{2,1,0:T(8,128)S(1)} %get-tuple-element.32.far_table, ...), custom_call_target="tpu_custom_call" | custom-call | flops 8388608 | bytes 786432 | tf_op jit(solution)/shard_map/pallas_call | solution.py:454
  31.8 9.0 %all_to_all.17 = f32[32,1,128]{2,1,0:T(1,128)S(1)} all-to-all(f32[32,1,128]{2,1,0:T(1,128)S(1)} %bitcast.10), channel_id=1, replica_groups={{31,30,29,28,27,26,25,24,23,22,21,20,19,18,17,16,15,14,13,12,11,10,9,8,..., dimensions={0} | all-to-all | bytes 32768 | tf_op jit(solution)/shard_map/all_to_all | solution.py:350
  40.9 0.6 %shard_map.77 = (f32[1,512]{1,0:T(1,128)}, f32[1,128]{1,0:T(1,128)}) custom-call(f32[32,128]{1,0:T(8,128)S(1)} %bitcast.9, f32[2,128]{1,0:T(2,128)S(1)} %get-tuple-element.36.small, f32[1,512]{1,0:T(1,128)S(1)} %get-tuple-element.37.row), custom_call_target="tpu_custom_call" | custom-call | tf_op jit(solution)/shard_map/pallas_call | solution.py:464
  (3 shorter events, 0.1 us)
Async XLA Ops:
  1.6 6.6 %collective-permute-start = (bf16[72,768]{1,0:T(8,128)(2,1)S(1)}, bf16[72,768]{1,0:T(8,128)(2,1)S(1)}, u32[]{:S(2)}, u32[]{:S(2)}) collective-permute-start(bf16[72,768]{1,0:T(8,128)(2,1)S(1)} %get-tuple-element.25), channel_id=1, source_target_pairs={{8,0},{20,4},{0,8},{28,12},{24,16},{4,20},{16,24},{12,28},{9,1},{2... | collective-permute-start | bytes 331784 | tf_op jit(solution)/shard_map/ppermute | solution.py:341
  4.6 5.6 %collective-permute-start.3 = (bf16[72,768]{1,0:T(8,128)(2,1)S(1)}, bf16[72,768]{1,0:T(8,128)(2,1)S(1)}, u32[]{:S(2)}, u32[]{:S(2)}) collective-permute-start(bf16[72,768]{1,0:T(8,128)(2,1)S(1)} %get-tuple-element.28), channel_id=1, source_target_pairs={{16,0},{12,4},{24,8},{4,12},{0,16},{28,20},{8,24},{20,28},{17,1},{... | collective-permute-start | bytes 331784 | tf_op jit(solution)/shard_map/ppermute | solution.py:341
  7.6 5.5 %collective-permute-start.1 = (bf16[64,768]{1,0:T(8,128)(2,1)S(1)}, bf16[64,768]{1,0:T(8,128)(2,1)S(1)}, u32[]{:S(2)}, u32[]{:S(2)}) collective-permute-start(bf16[64,768]{1,0:T(8,128)(2,1)S(1)} %get-tuple-element.26), channel_id=1, source_target_pairs={{8,0},{20,4},{0,8},{28,12},{24,16},{4,20},{16,24},{12,28},{9,1},{2... | collective-permute-start | bytes 294920 | tf_op jit(solution)/shard_map/ppermute | solution.py:341
  8.2 5.3 %collective-permute-start.2 = (bf16[64,768]{1,0:T(8,128)(2,1)S(1)}, bf16[64,768]{1,0:T(8,128)(2,1)S(1)}, u32[]{:S(2)}, u32[]{:S(2)}) collective-permute-start(bf16[64,768]{1,0:T(8,128)(2,1)S(1)} %get-tuple-element.27), channel_id=1, source_target_pairs={{16,0},{12,4},{24,8},{4,12},{0,16},{28,20},{8,24},{20,28},{17,1},{... | collective-permute-start | bytes 294920 | tf_op jit(solution)/shard_map/ppermute | solution.py:341
  8.2 6.5 %collective-permute-start.5 = (bf16[72,768]{1,0:T(8,128)(2,1)S(1)}, bf16[72,768]{1,0:T(8,128)(2,1)S(1)}, u32[]{:S(2)}, u32[]{:S(2)}) collective-permute-start(bf16[72,768]{1,0:T(8,128)(2,1)S(1)} %collective-permute-done.a_first), channel_id=1, source_target_pairs={{16,0},{12,4},{24,8},{4,12},{0,16},{28,20},{8,24},{20,28},{17,1},{... | collective-permute-start | bytes 331784 | tf_op jit(solution)/shard_map/ppermute | solution.py:341
  10.2 4.7 %collective-permute-start.6 = (bf16[72,768]{1,0:T(8,128)(2,1)S(1)}, bf16[72,768]{1,0:T(8,128)(2,1)S(1)}, u32[]{:S(2)}, u32[]{:S(2)}) collective-permute-start(bf16[72,768]{1,0:T(8,128)(2,1)S(1)} %collective-permute-done.3.b_second), channel_id=1, source_target_pairs={{8,0},{20,4},{0,8},{28,12},{24,16},{4,20},{16,24},{12,28},{9,1},{2... | collective-permute-start | bytes 331784 | tf_op jit(solution)/shard_map/ppermute | solution.py:341
  13.5 2.1 %collective-permute-start.4 = (bf16[408,768]{1,0:T(8,128)(2,1)S(1)}, bf16[408,768]{1,0:T(8,128)(2,1)S(1)}, u32[]{:S(2)}, u32[]{:S(2)}) collective-permute-start(bf16[408,768]{1,0:T(8,128)(2,1)S(1)} %shard_map.70), channel_id=1, source_target_pairs={{4,0},{0,4},{12,8},{8,12},{20,16},{16,20},{28,24},{24,28},{5,1},{1... | collective-permute-start | bytes 1880072 | tf_op jit(solution)/shard_map/ppermute | solution.py:22
  14.7 2.1 %collective-permute-start.7 = (bf16[72,768]{1,0:T(8,128)(2,1)S(1)}, bf16[72,768]{1,0:T(8,128)(2,1)S(1)}, u32[]{:S(2)}, u32[]{:S(2)}) collective-permute-start(bf16[72,768]{1,0:T(8,128)(2,1)S(1)} %shard_map.72), channel_id=1, source_target_pairs={{4,0},{0,4},{12,8},{8,12},{20,16},{16,20},{28,24},{24,28},{5,1},{1... | collective-permute-start | bytes 331784 | tf_op jit(solution)/shard_map/ppermute | solution.py:22
  15.0 1.8 %collective-permute-start.8 = (bf16[72,768]{1,0:T(8,128)(2,1)S(1)}, bf16[72,768]{1,0:T(8,128)(2,1)S(1)}, u32[]{:S(2)}, u32[]{:S(2)}) collective-permute-start(bf16[72,768]{1,0:T(8,128)(2,1)S(1)} %shard_map.73), channel_id=1, source_target_pairs={{4,0},{0,4},{12,8},{8,12},{20,16},{16,20},{28,24},{24,28},{5,1},{1... | collective-permute-start | bytes 331784 | tf_op jit(solution)/shard_map/ppermute | solution.py:22

commit v8 on v6

--- a/solution.py
+++ b/solution.py
@@ -274,7 +274,7 @@
 
 
 def second_kernel(
-    copies, near, near_table, far, far_table, got, logw, row, message, row_pot, ordered
+    near, near_table, far, far_table, got, logw, row, message, row_pot, ordered
 ):
     order = positions(lax.axis_index("blk"))
     held = Held(near, near_table, far, far_table)
@@ -290,8 +290,10 @@
         row_pot[at, :] = logw[at, :] - value
 
     def column_found(p, value):
-        at = pl.ds((held.total - 1 - order[p]) * copies, copies)
-        message[at, :] = jnp.broadcast_to(value - held.row(1, p), (copies, LANES))
+        value = (value - held.row(1, p))[None]
+        message[:, pl.ds(held.total - 1 - order[p], 1), :] = jnp.broadcast_to(
+            value, (message.shape[0], 1, LANES)
+        )
 
     row_sweep(held.score, range(held.total), rows, row_found, columns=columns)
     column_sweep(held.score, range(held.total), rows, row_pot, column_found)
@@ -343,7 +345,8 @@
             return fetch(array, "blk", 1, blk)
 
         def exchange(message):
-            order = list(range(blk * grp))[::-1]
+            order = [b * grp + g for g in reversed(range(grp)) for b in reversed(range(blk))]
+            message = message.reshape(blk * grp, -1, width)
             return lax.all_to_all(message, ("blk", "grp"), 0, 0, axis_index_groups=[order])
 
         def block_of(size):
@@ -376,7 +379,7 @@
         a_second = along(second_plain, 0)
         b_first = along(first_plain, 1)
         far_a = along(a_first, 1)
-        far_b = along(b_second, 0)
+        far_b = along(b_second[:half], 0)
         source, logw, passed = pl.pallas_call(
             source_kernel,
             out_shape=(
@@ -448,15 +451,15 @@
         )(scores_near, table_near, found, *scores, logw)
         got = exchange(message)
         row, message = pl.pallas_call(
-            functools.partial(second_kernel, grp),
-            out_shape=(values(1, rows), values(blk * grp, width)),
+            second_kernel,
+            out_shape=(values(1, rows), values(grp, blk, width)),
             in_specs=[vmem] * 6,
             out_specs=(vmem, vmem),
             scratch_shapes=[row_scratch, block_scratch],
             compiler_params=params,
             cost_estimate=cost(0, 1),
         )(scores_near, table_near, *scores, got, logw)
-        got = exchange(message)
+        got = exchange(message).reshape(blk * grp, width)
         row_pot, column_pot = pl.pallas_call(
             last_kernel,
             out_shape=(values(1, rows), values(1, width)),

time: 41.2 us -> 41.5 us (level)
  transfers between devices with their start and end apart: 9 -> 9, of which waited for: 5 -> 4; matrix products, arithmetic and copies ran while one was open for 0% -> 0% of each run, Pallas kernels for 6% -> 6%
where the time goes in v8:
time: 41.5 us; the launch traced here: 41.3 us
  blocking collectives  21.6 us (52%)
  starting transfers between devices  9.25 us (22%)
  Pallas kernels  6.31 us (15%)
  waiting for transfers between devices  3.31 us (8%)
  between operations  0.75 us (2%)
    all_to_all x2, blocking collectives, exchange(): lax.all_to_all(message, ('blk', 'grp'), 0, 0, axis_index_groups=[order])  21.6 us
    ppermute x6, starting transfers between devices, along(): lax.ppermute(array, 'blk', [(i ^ neighbour_step(i, turn), i) for i in ran...  8.56 us
    ppermute x6, waiting for transfers between devices, along(): lax.ppermute(array, 'blk', [(i ^ neighbour_step(i, turn), i) for i in ran...  2.62 us
    pallas_call x1, Pallas kernels, shards_square(): pl.pallas_call(source_kernel, out_shape=(jax.ShapeDtypeStruct((rows, dept...  1.4 us
    pallas_call x1, Pallas kernels, shards_square(): pl.pallas_call(functools.partial(near_kernel, factor), out_shape=(values(...  1.09 us
    pallas_call x1, Pallas kernels, shards_square(): pl.pallas_call(second_kernel, out_shape=(values(1, rows), values(grp, blk...  1.06 us
    pallas_call x1, Pallas kernels, shards_square(): pl.pallas_call(head_kernel, out_shape=(block_of(half + SPARE), block_of(h...  0.99 us
  transfers between devices with their start and end apart: 9, of which 4 were waited for; matrix products, arithmetic and copies ran while one was open for 0% of the time, Pallas kernels for 6%

profile of v8, /device:TPU:0, one launch (start us, length us, event | category | flops | bytes accessed | tf_op | source)
XLA Modules:
  0.0 41.3 jit_solution(16456759167591825862)
XLA Ops:
  0.6 1.0 %shard_map.68 = (bf16[72,768]{1,0:T(8,128)(2,1)S(1)}, bf16[72,768]{1,0:T(8,128)(2,1)S(1)}, bf16[136,768]{1,0:T(8,128)(2,1)S(1)}, f32[2,128]{1,0:T(2,128)S(1)}, b...) custom-call(bf16[128,768]{1,0:T(8,128)(2,1)} %own.1, f32[1,128]{1,0:T(1,128)} %bitcast.12, f32[1,128]{1,0:T(1,128)} %bitcast.13), custom_call_target="tpu_custom_call" | custom-call | tf_op jit(solution)/shard_map/pallas_call | solution.py:358
  1.6 3.0 %collective-permute-start = (bf16[72,768]{1,0:T(8,128)(2,1)S(1)}, bf16[72,768]{1,0:T(8,128)(2,1)S(1)}, u32[]{:S(2)}, u32[]{:S(2)}) collective-permute-start(bf16[72,768]{1,0:T(8,128)(2,1)S(1)} %get-tuple-element.22), channel_id=1, source_target_pairs={{8,0},{20,4},{0,8},{28,12},{24,16},{4,20},{16,24},{12,28},{9,1},{2... | collective-permute-start | bytes 331784 | tf_op jit(solution)/shard_map/ppermute | solution.py:340
  4.6 1.5 %collective-permute-start.3 = (bf16[72,768]{1,0:T(8,128)(2,1)S(1)}, bf16[72,768]{1,0:T(8,128)(2,1)S(1)}, u32[]{:S(2)}, u32[]{:S(2)}) collective-permute-start(bf16[72,768]{1,0:T(8,128)(2,1)S(1)} %get-tuple-element.25), channel_id=1, source_target_pairs={{16,0},{12,4},{24,8},{4,12},{0,16},{28,20},{8,24},{20,28},{17,1},{... | collective-permute-start | bytes 331784 | tf_op jit(solution)/shard_map/ppermute | solution.py:340
  6.2 0.5 %collective-permute-start.1 = (bf16[64,768]{1,0:T(8,128)(2,1)S(1)}, bf16[64,768]{1,0:T(8,128)(2,1)S(1)}, u32[]{:S(2)}, u32[]{:S(2)}) collective-permute-start(bf16[64,768]{1,0:T(8,128)(2,1)S(1)} %get-tuple-element.23), channel_id=1, source_target_pairs={{8,0},{20,4},{0,8},{28,12},{24,16},{4,20},{16,24},{12,28},{9,1},{2... | collective-permute-start | bytes 294920 | tf_op jit(solution)/shard_map/ppermute | solution.py:340
  6.7 0.1 collective-permute-start.2
  6.7 1.2 %collective-permute-done.a_first = bf16[72,768]{1,0:T(8,128)(2,1)S(1)} collective-permute-done((bf16[72,768]{1,0:T(8,128)(2,1)S(1)}, bf16[72,768]{1,0:T(8,128)(2,1)S(1)}, u32[]{:S(2)}, u32[]{:S(2)}) %collective-permute-start) | collective-permute-done | bytes 110624 | tf_op jit(solution)/shard_map/ppermute | solution.py:340
  8.0 1.6 %collective-permute-start.5 = (bf16[72,768]{1,0:T(8,128)(2,1)S(1)}, bf16[72,768]{1,0:T(8,128)(2,1)S(1)}, u32[]{:S(2)}, u32[]{:S(2)}) collective-permute-start(bf16[72,768]{1,0:T(8,128)(2,1)S(1)} %collective-permute-done.a_first), channel_id=1, source_target_pairs={{16,0},{12,4},{24,8},{4,12},{0,16},{28,20},{8,24},{20,28},{17,1},{... | collective-permute-start | bytes 331784 | tf_op jit(solution)/shard_map/ppermute | solution.py:340
  9.6 0.7 %collective-permute-done.3.b_second = bf16[72,768]{1,0:T(8,128)(2,1)S(1)} collective-permute-done((bf16[72,768]{1,0:T(8,128)(2,1)S(1)}, bf16[72,768]{1,0:T(8,128)(2,1)S(1)}, u32[]{:S(2)}, u32[]{:S(2)}) %collective-permute-start.3) | collective-permute-done | bytes 110624 | tf_op jit(solution)/shard_map/ppermute | solution.py:340
  10.3 1.9 %collective-permute-start.6 = (bf16[64,768]{1,0:T(8,128)(2,1)S(1)}, bf16[64,768]{1,0:T(8,128)(2,1)S(1)}, u32[]{:S(2)}, u32[]{:S(2)}) collective-permute-start(bf16[64,768]{1,0:T(8,128)(2,1)S(1)} %slice.4), channel_id=1, source_target_pairs={{8,0},{20,4},{0,8},{28,12},{24,16},{4,20},{16,24},{12,28},{9,1},{2... | collective-permute-start | bytes 294920 | tf_op jit(solution)/shard_map/ppermute | solution.py:340
  12.1 1.4 %shard_map.69 = (bf16[512,768]{1,0:T(8,128)(2,1)S(1)}, f32[512,128]{1,0:T(8,128)S(1)}, bf16[136,768]{1,0:T(8,128)(2,1)S(1)}) custom-call(bf16[512,768]{1,0:T(8,128)(2,1)} %source.1, f32[1,512]{1,0:T(1,128)} %bitcast.11, bf16[136,768]{1,0:T(8,128)(2,1)S(1)} %get-tuple-element.20.whole), custom_call_target="tpu_custom_call" | custom-call | tf_op jit(solution)/shard_map/pallas_call | solution.py:383
  13.5 0.0 collective-permute-done.1.a_second
  13.5 0.0 collective-permute-done.2.b_first
  13.6 0.1 collective-permute-start.4
  13.7 0.0 collective-permute-done.5.message.far_a
  13.7 0.6 %collective-permute-start.7 = (bf16[72,768]{1,0:T(8,128)(2,1)S(1)}, bf16[72,768]{1,0:T(8,128)(2,1)S(1)}, u32[]{:S(2)}, u32[]{:S(2)}) collective-permute-start(bf16[72,768]{1,0:T(8,128)(2,1)S(1)} %shard_map.72), channel_id=1, source_target_pairs={{4,0},{0,4},{12,8},{8,12},{20,16},{16,20},{28,24},{24,28},{5,1},{1... | collective-permute-start | bytes 331784 | tf_op jit(solution)/shard_map/ppermute | solution.py:22
  14.3 0.7 %collective-permute-done.6.message.far_b = bf16[64,768]{1,0:T(8,128)(2,1)S(1)} collective-permute-done((bf16[64,768]{1,0:T(8,128)(2,1)S(1)}, bf16[64,768]{1,0:T(8,128)(2,1)S(1)}, u32[]{:S(2)}, u32[]{:S(2)}) %collective-permute-start.6) | collective-permute-done | bytes 98336 | tf_op jit(solution)/shard_map/ppermute | solution.py:340
  15.0 0.1 collective-permute-start.8
  15.0 0.7 %collective-permute-done.4.sibling = bf16[408,768]{1,0:T(8,128)(2,1)S(1)} collective-permute-done((bf16[408,768]{1,0:T(8,128)(2,1)S(1)}, bf16[408,768]{1,0:T(8,128)(2,1)S(1)}, u32[]{:S(2)}, u32[]{:S(2)}) %collective-permute-start.4) | collective-permute-done | bytes 626720 | tf_op jit(solution)/shard_map/ppermute | solution.py:22
  15.7 1.1 %shard_map.71 = (f32[512,768]{1,0:T(8,128)S(1)}, f32[2,8,128]{2,1,0:T(8,128)S(1)}, f32[512,128]{1,0:T(8,128)S(1)}) custom-call(bf16[512,768]{1,0:T(8,128)(2,1)S(1)} %get-tuple-element.21.source, bf16[136,768]{1,0:T(8,128)(2,1)S(1)} %get-tuple-element.20.whole, bf16[72,768]{1,0:T(8,128)(2,1)S(1)} %collective-permute-done.a_first, ...), custom_call_target="tpu_custom_call" | custom-call | bytes 786432 | tf_op jit(solution)/shard_map/pallas_call | solution.py:422
  16.8 0.0 collective-permute-done.8.sibling_b
  16.8 0.0 collective-permute-done.7.sibling_a
  16.9 0.4 shard_map.74
  17.3 0.7 %shard_map.75 = f32[32,8,128]{2,1,0:T(8,128)S(1)} custom-call(f32[512,768]{1,0:T(8,128)S(1)} %get-tuple-element.27.near, f32[2,8,128]{2,1,0:T(8,128)S(1)} %get-tuple-element.28.near_table, f32[512,128]{1,0:T(8,128)S(1)} %get-tuple-element.31.found, f32[512,256]{1,0:T(8,128)S(1)} %get-tuple-element.29.far, f32[2,8,128]{2,1,0:T(8,128)S(1)} %get-tuple-element.30.far_table, ...), custom_call_target="tpu_custom_call" | custom-call | flops 8388608 | bytes 786432 | tf_op jit(solution)/shard_map/pallas_call | solution.py:443
  18.0 12.4 %all_to_all.10.got = f32[32,8,128]{2,1,0:T(8,128)S(1)} all-to-all(f32[32,8,128]{2,1,0:T(8,128)S(1)} %shard_map.75), channel_id=1, replica_groups={{31,27,23,19,15,11,7,3,30,26,22,18,14,10,6,2,29,25,21,17,13,9,5,1,28,24..., dimensions={0} | all-to-all | bytes 262144 | tf_op jit(solution)/shard_map/all_to_all | solution.py:350
  30.4 1.1 %shard_map.76 = (f32[1,512]{1,0:T(1,128)S(1)}, f32[4,8,128]{2,1,0:T(8,128)S(1)}) custom-call(f32[512,768]{1,0:T(8,128)S(1)} %get-tuple-element.27.near, f32[2,8,128]{2,1,0:T(8,128)S(1)} %get-tuple-element.28.near_table, f32[512,256]{1,0:T(8,128)S(1)} %get-tuple-element.29.far, f32[2,8,128]{2,1,0:T(8,128)S(1)} %get-tuple-element.30.far_table, ...), custom_call_target="tpu_custom_call" | custom-call | flops 8388608 | bytes 786432 | tf_op jit(solution)/shard_map/pallas_call | solution.py:453
  31.4 9.2 %all_to_all.11 = f32[32,1,128]{2,1,0:T(1,128)S(1)} all-to-all(f32[32,1,128]{2,1,0:T(1,128)S(1)} %bitcast.10), channel_id=1, replica_groups={{31,27,23,19,15,11,7,3,30,26,22,18,14,10,6,2,29,25,21,17,13,9,5,1,28,24..., dimensions={0} | all-to-all | bytes 32768 | tf_op jit(solution)/shard_map/all_to_all | solution.py:350
  40.7 0.6 %shard_map.77 = (f32[1,512]{1,0:T(1,128)}, f32[1,128]{1,0:T(1,128)}) custom-call(f32[32,128]{1,0:T(8,128)S(1)} %bitcast.9, f32[2,128]{1,0:T(2,128)S(1)} %get-tuple-element.34.small, f32[1,512]{1,0:T(1,128)S(1)} %get-tuple-element.35.row), custom_call_target="tpu_custom_call" | custom-call | tf_op jit(solution)/shard_map/pallas_call | solution.py:463
  (4 shorter events, 0.1 us)
Async XLA Ops:
  1.6 6.3 %collective-permute-start = (bf16[72,768]{1,0:T(8,128)(2,1)S(1)}, bf16[72,768]{1,0:T(8,128)(2,1)S(1)}, u32[]{:S(2)}, u32[]{:S(2)}) collective-permute-start(bf16[72,768]{1,0:T(8,128)(2,1)S(1)} %get-tuple-element.22), channel_id=1, source_target_pairs={{8,0},{20,4},{0,8},{28,12},{24,16},{4,20},{16,24},{12,28},{9,1},{2... | collective-permute-start | bytes 331784 | tf_op jit(solution)/shard_map/ppermute | solution.py:340
  4.6 5.6 %collective-permute-start.3 = (bf16[72,768]{1,0:T(8,128)(2,1)S(1)}, bf16[72,768]{1,0:T(8,128)(2,1)S(1)}, u32[]{:S(2)}, u32[]{:S(2)}) collective-permute-start(bf16[72,768]{1,0:T(8,128)(2,1)S(1)} %get-tuple-element.25), channel_id=1, source_target_pairs={{16,0},{12,4},{24,8},{4,12},{0,16},{28,20},{8,24},{20,28},{17,1},{... | collective-permute-start | bytes 331784 | tf_op jit(solution)/shard_map/ppermute | solution.py:340
  6.2 7.4 %collective-permute-start.1 = (bf16[64,768]{1,0:T(8,128)(2,1)S(1)}, bf16[64,768]{1,0:T(8,128)(2,1)S(1)}, u32[]{:S(2)}, u32[]{:S(2)}) collective-permute-start(bf16[64,768]{1,0:T(8,128)(2,1)S(1)} %get-tuple-element.23), channel_id=1, source_target_pairs={{8,0},{20,4},{0,8},{28,12},{24,16},{4,20},{16,24},{12,28},{9,1},{2... | collective-permute-start | bytes 294920 | tf_op jit(solution)/shard_map/ppermute | solution.py:340
  6.7 6.9 %collective-permute-start.2 = (bf16[64,768]{1,0:T(8,128)(2,1)S(1)}, bf16[64,768]{1,0:T(8,128)(2,1)S(1)}, u32[]{:S(2)}, u32[]{:S(2)}) collective-permute-start(bf16[64,768]{1,0:T(8,128)(2,1)S(1)} %get-tuple-element.24), channel_id=1, source_target_pairs={{16,0},{12,4},{24,8},{4,12},{0,16},{28,20},{8,24},{20,28},{17,1},{... | collective-permute-start | bytes 294920 | tf_op jit(solution)/shard_map/ppermute | solution.py:340
  8.0 5.7 %collective-permute-start.5 = (bf16[72,768]{1,0:T(8,128)(2,1)S(1)}, bf16[72,768]{1,0:T(8,128)(2,1)S(1)}, u32[]{:S(2)}, u32[]{:S(2)}) collective-permute-start(bf16[72,768]{1,0:T(8,128)(2,1)S(1)} %collective-permute-done.a_first), channel_id=1, source_target_pairs={{16,0},{12,4},{24,8},{4,12},{0,16},{28,20},{8,24},{20,28},{17,1},{... | collective-permute-start | bytes 331784 | tf_op jit(solution)/shard_map/ppermute | solution.py:340
  10.3 4.7 %collective-permute-start.6 = (bf16[64,768]{1,0:T(8,128)(2,1)S(1)}, bf16[64,768]{1,0:T(8,128)(2,1)S(1)}, u32[]{:S(2)}, u32[]{:S(2)}) collective-permute-start(bf16[64,768]{1,0:T(8,128)(2,1)S(1)} %slice.4), channel_id=1, source_target_pairs={{8,0},{20,4},{0,8},{28,12},{24,16},{4,20},{16,24},{12,28},{9,1},{2... | collective-permute-start | bytes 294920 | tf_op jit(solution)/shard_map/ppermute | solution.py:340
  13.6 2.1 %collective-permute-start.4 = (bf16[408,768]{1,0:T(8,128)(2,1)S(1)}, bf16[408,768]{1,0:T(8,128)(2,1)S(1)}, u32[]{:S(2)}, u32[]{:S(2)}) collective-permute-start(bf16[408,768]{1,0:T(8,128)(2,1)S(1)} %shard_map.70), channel_id=1, source_target_pairs={{4,0},{0,4},{12,8},{8,12},{20,16},{16,20},{28,24},{24,28},{5,1},{1... | collective-permute-start | bytes 1880072 | tf_op jit(solution)/shard_map/ppermute | solution.py:22
  13.7 3.1 %collective-permute-start.7 = (bf16[72,768]{1,0:T(8,128)(2,1)S(1)}, bf16[72,768]{1,0:T(8,128)(2,1)S(1)}, u32[]{:S(2)}, u32[]{:S(2)}) collective-permute-start(bf16[72,768]{1,0:T(8,128)(2,1)S(1)} %shard_map.72), channel_id=1, source_target_pairs={{4,0},{0,4},{12,8},{8,12},{20,16},{16,20},{28,24},{24,28},{5,1},{1... | collective-permute-start | bytes 331784 | tf_op jit(solution)/shard_map/ppermute | solution.py:22
  15.0 1.9 %collective-permute-start.8 = (bf16[64,768]{1,0:T(8,128)(2,1)S(1)}, bf16[64,768]{1,0:T(8,128)(2,1)S(1)}, u32[]{:S(2)}, u32[]{:S(2)}) collective-permute-start(bf16[64,768]{1,0:T(8,128)(2,1)S(1)} %shard_map.73), channel_id=1, source_target_pairs={{4,0},{0,4},{12,8},{8,12},{20,16},{16,20},{28,24},{24,28},{5,1},{1... | collective-permute-start | bytes 294920 | tf_op jit(solution)/shard_map/ppermute | solution.py:22

commit v9 on v6

--- a/solution.py
+++ b/solution.py
@@ -290,8 +290,10 @@
         row_pot[at, :] = logw[at, :] - value
 
     def column_found(p, value):
-        at = pl.ds((held.total - 1 - order[p]) * copies, copies)
-        message[at, :] = jnp.broadcast_to(value - held.row(1, p), (copies, LANES))
+        place = order[p] ^ (order[p] >> 1) ^ (order[p] >> 2)
+        message[pl.ds(place * copies, copies), :] = jnp.broadcast_to(
+            value - held.row(1, p), (copies, LANES)
+        )
 
     row_sweep(held.score, range(held.total), rows, row_found, columns=columns)
     column_sweep(held.score, range(held.total), rows, row_pot, column_found)
@@ -343,7 +345,11 @@
             return fetch(array, "blk", 1, blk)
 
         def exchange(message):
-            order = list(range(blk * grp))[::-1]
+            order = []
+            for k in range(blk):
+                column = [(k ^ (k >> 1)) * grp + g for g in range(grp)]
+                order += column if k % 2 == 0 else column[::-1]
+            message = message.reshape(blk * grp, -1, width)
             return lax.all_to_all(message, ("blk", "grp"), 0, 0, axis_index_groups=[order])
 
         def block_of(size):
@@ -376,7 +382,7 @@
         a_second = along(second_plain, 0)
         b_first = along(first_plain, 1)
         far_a = along(a_first, 1)
-        far_b = along(b_second, 0)
+        far_b = along(b_second[:half], 0)
         source, logw, passed = pl.pallas_call(
             source_kernel,
             out_shape=(
@@ -456,7 +462,7 @@
             compiler_params=params,
             cost_estimate=cost(0, 1),
         )(scores_near, table_near, *scores, got, logw)
-        got = exchange(message)
+        got = exchange(message).reshape(blk * grp, width)
         row_pot, column_pot = pl.pallas_call(
             last_kernel,
             out_shape=(values(1, rows), values(1, width)),

time: 41.2 us -> 41.7 us (1.012)
  transfers between devices with their start and end apart: 9 -> 9, of which waited for: 5 -> 4; matrix products, arithmetic and copies ran while one was open for 0% -> 0% of each run, Pallas kernels for 6% -> 6%
where the time goes in v9:
time: 41.7 us; the launch traced here: 41.5 us
  blocking collectives  21.9 us (53%)
  starting transfers between devices  9.25 us (22%)
  Pallas kernels  6.32 us (15%)
  waiting for transfers between devices  3.31 us (8%)
  between operations  0.75 us (2%)
    all_to_all x2, blocking collectives, exchange(): lax.all_to_all(message, ('blk', 'grp'), 0, 0, axis_index_groups=[order])  21.9 us
    ppermute x6, starting transfers between devices, along(): lax.ppermute(array, 'blk', [(i ^ neighbour_step(i, turn), i) for i in ran...  8.56 us
    ppermute x6, waiting for transfers between devices, along(): lax.ppermute(array, 'blk', [(i ^ neighbour_step(i, turn), i) for i in ran...  2.62 us
    pallas_call x1, Pallas kernels, shards_square(): pl.pallas_call(source_kernel, out_shape=(jax.ShapeDtypeStruct((rows, dept...  1.4 us
    pallas_call x1, Pallas kernels, shards_square(): pl.pallas_call(functools.partial(near_kernel, factor), out_shape=(values(...  1.09 us
    pallas_call x1, Pallas kernels, shards_square(): pl.pallas_call(functools.partial(second_kernel, grp), out_shape=(values(1...  1.06 us
    pallas_call x1, Pallas kernels, shards_square(): pl.pallas_call(head_kernel, out_shape=(block_of(half + SPARE), block_of(h...  0.99 us
  transfers between devices with their start and end apart: 9, of which 4 were waited for; matrix products, arithmetic and copies ran while one was open for 0% of the time, Pallas kernels for 6%

profile of v9, /device:TPU:0, one launch (start us, length us, event | category | flops | bytes accessed | tf_op | source)
XLA Modules:
  0.0 41.5 jit_solution(3175330362954552988)
XLA Ops:
  0.6 1.0 %shard_map.68 = (bf16[72,768]{1,0:T(8,128)(2,1)S(1)}, bf16[72,768]{1,0:T(8,128)(2,1)S(1)}, bf16[136,768]{1,0:T(8,128)(2,1)S(1)}, f32[2,128]{1,0:T(2,128)S(1)}, b...) custom-call(bf16[128,768]{1,0:T(8,128)(2,1)} %own.1, f32[1,128]{1,0:T(1,128)} %bitcast.12, f32[1,128]{1,0:T(1,128)} %bitcast.13), custom_call_target="tpu_custom_call" | custom-call | tf_op jit(solution)/shard_map/pallas_call | solution.py:361
  1.6 3.0 %collective-permute-start = (bf16[72,768]{1,0:T(8,128)(2,1)S(1)}, bf16[72,768]{1,0:T(8,128)(2,1)S(1)}, u32[]{:S(2)}, u32[]{:S(2)}) collective-permute-start(bf16[72,768]{1,0:T(8,128)(2,1)S(1)} %get-tuple-element.22), channel_id=1, source_target_pairs={{8,0},{20,4},{0,8},{28,12},{24,16},{4,20},{16,24},{12,28},{9,1},{2... | collective-permute-start | bytes 331784 | tf_op jit(solution)/shard_map/ppermute | solution.py:340
  4.6 1.5 %collective-permute-start.3 = (bf16[72,768]{1,0:T(8,128)(2,1)S(1)}, bf16[72,768]{1,0:T(8,128)(2,1)S(1)}, u32[]{:S(2)}, u32[]{:S(2)}) collective-permute-start(bf16[72,768]{1,0:T(8,128)(2,1)S(1)} %get-tuple-element.25), channel_id=1, source_target_pairs={{16,0},{12,4},{24,8},{4,12},{0,16},{28,20},{8,24},{20,28},{17,1},{... | collective-permute-start | bytes 331784 | tf_op jit(solution)/shard_map/ppermute | solution.py:340
  6.2 0.5 %collective-permute-start.1 = (bf16[64,768]{1,0:T(8,128)(2,1)S(1)}, bf16[64,768]{1,0:T(8,128)(2,1)S(1)}, u32[]{:S(2)}, u32[]{:S(2)}) collective-permute-start(bf16[64,768]{1,0:T(8,128)(2,1)S(1)} %get-tuple-element.23), channel_id=1, source_target_pairs={{8,0},{20,4},{0,8},{28,12},{24,16},{4,20},{16,24},{12,28},{9,1},{2... | collective-permute-start | bytes 294920 | tf_op jit(solution)/shard_map/ppermute | solution.py:340
  6.7 0.1 collective-permute-start.2
  6.7 1.2 %collective-permute-done.a_first = bf16[72,768]{1,0:T(8,128)(2,1)S(1)} collective-permute-done((bf16[72,768]{1,0:T(8,128)(2,1)S(1)}, bf16[72,768]{1,0:T(8,128)(2,1)S(1)}, u32[]{:S(2)}, u32[]{:S(2)}) %collective-permute-start) | collective-permute-done | bytes 110624 | tf_op jit(solution)/shard_map/ppermute | solution.py:340
  8.0 1.6 %collective-permute-start.5 = (bf16[72,768]{1,0:T(8,128)(2,1)S(1)}, bf16[72,768]{1,0:T(8,128)(2,1)S(1)}, u32[]{:S(2)}, u32[]{:S(2)}) collective-permute-start(bf16[72,768]{1,0:T(8,128)(2,1)S(1)} %collective-permute-done.a_first), channel_id=1, source_target_pairs={{16,0},{12,4},{24,8},{4,12},{0,16},{28,20},{8,24},{20,28},{17,1},{... | collective-permute-start | bytes 331784 | tf_op jit(solution)/shard_map/ppermute | solution.py:340
  9.6 0.7 %collective-permute-done.3.b_second = bf16[72,768]{1,0:T(8,128)(2,1)S(1)} collective-permute-done((bf16[72,768]{1,0:T(8,128)(2,1)S(1)}, bf16[72,768]{1,0:T(8,128)(2,1)S(1)}, u32[]{:S(2)}, u32[]{:S(2)}) %collective-permute-start.3) | collective-permute-done | bytes 110624 | tf_op jit(solution)/shard_map/ppermute | solution.py:340
  10.3 1.9 %collective-permute-start.6 = (bf16[64,768]{1,0:T(8,128)(2,1)S(1)}, bf16[64,768]{1,0:T(8,128)(2,1)S(1)}, u32[]{:S(2)}, u32[]{:S(2)}) collective-permute-start(bf16[64,768]{1,0:T(8,128)(2,1)S(1)} %slice.4), channel_id=1, source_target_pairs={{8,0},{20,4},{0,8},{28,12},{24,16},{4,20},{16,24},{12,28},{9,1},{2... | collective-permute-start | bytes 294920 | tf_op jit(solution)/shard_map/ppermute | solution.py:340
  12.1 1.4 %shard_map.69 = (bf16[512,768]{1,0:T(8,128)(2,1)S(1)}, f32[512,128]{1,0:T(8,128)S(1)}, bf16[136,768]{1,0:T(8,128)(2,1)S(1)}) custom-call(bf16[512,768]{1,0:T(8,128)(2,1)} %source.1, f32[1,512]{1,0:T(1,128)} %bitcast.11, bf16[136,768]{1,0:T(8,128)(2,1)S(1)} %get-tuple-element.20.whole), custom_call_target="tpu_custom_call" | custom-call | tf_op jit(solution)/shard_map/pallas_call | solution.py:386
  13.5 0.0 collective-permute-done.1.a_second
  13.5 0.0 collective-permute-done.2.b_first
  13.6 0.1 collective-permute-start.4
  13.7 0.0 collective-permute-done.5.message.far_a
  13.7 0.6 %collective-permute-start.7 = (bf16[72,768]{1,0:T(8,128)(2,1)S(1)}, bf16[72,768]{1,0:T(8,128)(2,1)S(1)}, u32[]{:S(2)}, u32[]{:S(2)}) collective-permute-start(bf16[72,768]{1,0:T(8,128)(2,1)S(1)} %shard_map.72), channel_id=1, source_target_pairs={{4,0},{0,4},{12,8},{8,12},{20,16},{16,20},{28,24},{24,28},{5,1},{1... | collective-permute-start | bytes 331784 | tf_op jit(solution)/shard_map/ppermute | solution.py:22
  14.3 0.7 %collective-permute-done.6.message.far_b = bf16[64,768]{1,0:T(8,128)(2,1)S(1)} collective-permute-done((bf16[64,768]{1,0:T(8,128)(2,1)S(1)}, bf16[64,768]{1,0:T(8,128)(2,1)S(1)}, u32[]{:S(2)}, u32[]{:S(2)}) %collective-permute-start.6) | collective-permute-done | bytes 98336 | tf_op jit(solution)/shard_map/ppermute | solution.py:340
  15.0 0.1 collective-permute-start.8
  15.0 0.7 %collective-permute-done.4.sibling = bf16[408,768]{1,0:T(8,128)(2,1)S(1)} collective-permute-done((bf16[408,768]{1,0:T(8,128)(2,1)S(1)}, bf16[408,768]{1,0:T(8,128)(2,1)S(1)}, u32[]{:S(2)}, u32[]{:S(2)}) %collective-permute-start.4) | collective-permute-done | bytes 626720 | tf_op jit(solution)/shard_map/ppermute | solution.py:22
  15.7 1.1 %shard_map.71 = (f32[512,768]{1,0:T(8,128)S(1)}, f32[2,8,128]{2,1,0:T(8,128)S(1)}, f32[512,128]{1,0:T(8,128)S(1)}) custom-call(bf16[512,768]{1,0:T(8,128)(2,1)S(1)} %get-tuple-element.21.source, bf16[136,768]{1,0:T(8,128)(2,1)S(1)} %get-tuple-element.20.whole, bf16[72,768]{1,0:T(8,128)(2,1)S(1)} %collective-permute-done.a_first, ...), custom_call_target="tpu_custom_call" | custom-call | bytes 786432 | tf_op jit(solution)/shard_map/pallas_call | solution.py:425
  16.8 0.0 collective-permute-done.8.sibling_b
  16.8 0.0 collective-permute-done.7.sibling_a
  16.9 0.4 shard_map.74
  17.3 0.7 %shard_map.75 = f32[32,8,128]{2,1,0:T(8,128)S(1)} custom-call(f32[512,768]{1,0:T(8,128)S(1)} %get-tuple-element.27.near, f32[2,8,128]{2,1,0:T(8,128)S(1)} %get-tuple-element.28.near_table, f32[512,128]{1,0:T(8,128)S(1)} %get-tuple-element.31.found, f32[512,256]{1,0:T(8,128)S(1)} %get-tuple-element.29.far, f32[2,8,128]{2,1,0:T(8,128)S(1)} %get-tuple-element.30.far_table, ...), custom_call_target="tpu_custom_call" | custom-call | flops 8388608 | bytes 786432 | tf_op jit(solution)/shard_map/pallas_call | solution.py:446
  18.0 13.0 %all_to_all.10.got = f32[32,8,128]{2,1,0:T(8,128)S(1)} all-to-all(f32[32,8,128]{2,1,0:T(8,128)S(1)} %shard_map.75), channel_id=1, replica_groups={{0,1,2,3,7,6,5,4,12,13,14,15,11,10,9,8,24,25,26,27,31,30,29,28,20,21,22..., dimensions={0} | all-to-all | bytes 262144 | tf_op jit(solution)/shard_map/all_to_all | solution.py:353
  31.0 1.1 %shard_map.76 = (f32[1,512]{1,0:T(1,128)S(1)}, f32[32,128]{1,0:T(8,128)S(1)}) custom-call(f32[512,768]{1,0:T(8,128)S(1)} %get-tuple-element.27.near, f32[2,8,128]{2,1,0:T(8,128)S(1)} %get-tuple-element.28.near_table, f32[512,256]{1,0:T(8,128)S(1)} %get-tuple-element.29.far, f32[2,8,128]{2,1,0:T(8,128)S(1)} %get-tuple-element.30.far_table, ...), custom_call_target="tpu_custom_call" | custom-call | flops 8388608 | bytes 786432 | tf_op jit(solution)/shard_map/pallas_call | solution.py:456
  32.1 8.9 %all_to_all.11 = f32[32,1,128]{2,1,0:T(1,128)S(1)} all-to-all(f32[32,1,128]{2,1,0:T(1,128)S(1)} %bitcast.10), channel_id=1, replica_groups={{0,1,2,3,7,6,5,4,12,13,14,15,11,10,9,8,24,25,26,27,31,30,29,28,20,21,22..., dimensions={0} | all-to-all | bytes 32768 | tf_op jit(solution)/shard_map/all_to_all | solution.py:353
  41.0 0.6 %shard_map.77 = (f32[1,512]{1,0:T(1,128)}, f32[1,128]{1,0:T(1,128)}) custom-call(f32[32,128]{1,0:T(8,128)S(1)} %bitcast.9, f32[2,128]{1,0:T(2,128)S(1)} %get-tuple-element.34.small, f32[1,512]{1,0:T(1,128)S(1)} %get-tuple-element.35.row), custom_call_target="tpu_custom_call" | custom-call | tf_op jit(solution)/shard_map/pallas_call | solution.py:466
  (4 shorter events, 0.1 us)
Async XLA Ops:
  1.6 6.3 %collective-permute-start = (bf16[72,768]{1,0:T(8,128)(2,1)S(1)}, bf16[72,768]{1,0:T(8,128)(2,1)S(1)}, u32[]{:S(2)}, u32[]{:S(2)}) collective-permute-start(bf16[72,768]{1,0:T(8,128)(2,1)S(1)} %get-tuple-element.22), channel_id=1, source_target_pairs={{8,0},{20,4},{0,8},{28,12},{24,16},{4,20},{16,24},{12,28},{9,1},{2... | collective-permute-start | bytes 331784 | tf_op jit(solution)/shard_map/ppermute | solution.py:340
  4.6 5.6 %collective-permute-start.3 = (bf16[72,768]{1,0:T(8,128)(2,1)S(1)}, bf16[72,768]{1,0:T(8,128)(2,1)S(1)}, u32[]{:S(2)}, u32[]{:S(2)}) collective-permute-start(bf16[72,768]{1,0:T(8,128)(2,1)S(1)} %get-tuple-element.25), channel_id=1, source_target_pairs={{16,0},{12,4},{24,8},{4,12},{0,16},{28,20},{8,24},{20,28},{17,1},{... | collective-permute-start | bytes 331784 | tf_op jit(solution)/shard_map/ppermute | solution.py:340
  6.2 7.4 %collective-permute-start.1 = (bf16[64,768]{1,0:T(8,128)(2,1)S(1)}, bf16[64,768]{1,0:T(8,128)(2,1)S(1)}, u32[]{:S(2)}, u32[]{:S(2)}) collective-permute-start(bf16[64,768]{1,0:T(8,128)(2,1)S(1)} %get-tuple-element.23), channel_id=1, source_target_pairs={{8,0},{20,4},{0,8},{28,12},{24,16},{4,20},{16,24},{12,28},{9,1},{2... | collective-permute-start | bytes 294920 | tf_op jit(solution)/shard_map/ppermute | solution.py:340
  6.7 6.9 %collective-permute-start.2 = (bf16[64,768]{1,0:T(8,128)(2,1)S(1)}, bf16[64,768]{1,0:T(8,128)(2,1)S(1)}, u32[]{:S(2)}, u32[]{:S(2)}) collective-permute-start(bf16[64,768]{1,0:T(8,128)(2,1)S(1)} %get-tuple-element.24), channel_id=1, source_target_pairs={{16,0},{12,4},{24,8},{4,12},{0,16},{28,20},{8,24},{20,28},{17,1},{... | collective-permute-start | bytes 294920 | tf_op jit(solution)/shard_map/ppermute | solution.py:340
  8.0 5.7 %collective-permute-start.5 = (bf16[72,768]{1,0:T(8,128)(2,1)S(1)}, bf16[72,768]{1,0:T(8,128)(2,1)S(1)}, u32[]{:S(2)}, u32[]{:S(2)}) collective-permute-start(bf16[72,768]{1,0:T(8,128)(2,1)S(1)} %collective-permute-done.a_first), channel_id=1, source_target_pairs={{16,0},{12,4},{24,8},{4,12},{0,16},{28,20},{8,24},{20,28},{17,1},{... | collective-permute-start | bytes 331784 | tf_op jit(solution)/shard_map/ppermute | solution.py:340
  10.3 4.7 %collective-permute-start.6 = (bf16[64,768]{1,0:T(8,128)(2,1)S(1)}, bf16[64,768]{1,0:T(8,128)(2,1)S(1)}, u32[]{:S(2)}, u32[]{:S(2)}) collective-permute-start(bf16[64,768]{1,0:T(8,128)(2,1)S(1)} %slice.4), channel_id=1, source_target_pairs={{8,0},{20,4},{0,8},{28,12},{24,16},{4,20},{16,24},{12,28},{9,1},{2... | collective-permute-start | bytes 294920 | tf_op jit(solution)/shard_map/ppermute | solution.py:340
  13.6 2.1 %collective-permute-start.4 = (bf16[408,768]{1,0:T(8,128)(2,1)S(1)}, bf16[408,768]{1,0:T(8,128)(2,1)S(1)}, u32[]{:S(2)}, u32[]{:S(2)}) collective-permute-start(bf16[408,768]{1,0:T(8,128)(2,1)S(1)} %shard_map.70), channel_id=1, source_target_pairs={{4,0},{0,4},{12,8},{8,12},{20,16},{16,20},{28,24},{24,28},{5,1},{1... | collective-permute-start | bytes 1880072 | tf_op jit(solution)/shard_map/ppermute | solution.py:22
  13.7 3.1 %collective-permute-start.7 = (bf16[72,768]{1,0:T(8,128)(2,1)S(1)}, bf16[72,768]{1,0:T(8,128)(2,1)S(1)}, u32[]{:S(2)}, u32[]{:S(2)}) collective-permute-start(bf16[72,768]{1,0:T(8,128)(2,1)S(1)} %shard_map.72), channel_id=1, source_target_pairs={{4,0},{0,4},{12,8},{8,12},{20,16},{16,20},{28,24},{24,28},{5,1},{1... | collective-permute-start | bytes 331784 | tf_op jit(solution)/shard_map/ppermute | solution.py:22
  15.0 1.9 %collective-permute-start.8 = (bf16[64,768]{1,0:T(8,128)(2,1)S(1)}, bf16[64,768]{1,0:T(8,128)(2,1)S(1)}, u32[]{:S(2)}, u32[]{:S(2)}) collective-permute-start(bf16[64,768]{1,0:T(8,128)(2,1)S(1)} %shard_map.73), channel_id=1, source_target_pairs={{4,0},{0,4},{12,8},{8,12},{20,16},{16,20},{28,24},{24,28},{5,1},{1... | collective-permute-start | bytes 294920 | tf_op jit(solution)/shard_map/ppermute | solution.py:22

commit v10 on v6

--- a/solution.py
+++ b/solution.py
@@ -108,12 +108,13 @@
         table[0, p : p + 1, :] = small[1:2] * LOG2E
         table[1, p : p + 1, :] = small[0:1] * (inverse_eps * LOG2E)
     for p in range(0, len(smalls), 2):
-        lanes = slice(p * LANES, (p + 2) * LANES)
+        end = min(p + 2, len(smalls))
+        lanes = slice(p * LANES, end * LANES)
         product = lax.dot_general(
             source[...], targets[lanes, :], (((1,), (1,)), ((), ())),
             preferred_element_type=jnp.float32,
         )
-        shift = jnp.concatenate([table[1, p : p + 1, :], table[1, p + 1 : p + 2, :]], axis=1)
+        shift = jnp.concatenate([table[1, q : q + 1, :] for q in range(p, end)], axis=1)
         scaled[:, lanes] = product * factor + shift
 
 
@@ -181,36 +182,38 @@
     return (parts[0] + parts[1]) + parts[2]
 
 
-def near_kernel(
-    factor, source, whole, a_first, a_second, b_first, b_second, sibling, scaled, table, found,
-    targets,
+def own_kernel(
+    factor, source, whole, a_first, a_second, b_first, b_second, scaled, table, targets
 ):
     half = a_second.shape[0]
-    width = 2 * half
+    pieces = (whole, whole, a_first, a_second, b_first, b_second)
+    targets[0 : 2 * half, :] = whole[0 : 2 * half, :]
+    for k in range(2, 6):
+        targets[k * half : (k + 1) * half, :] = pieces[k][0:half, :]
+    smalls = [unpack(whole), unpack(a_first), unpack(b_second)]
+    products(source, targets, factor, smalls, scaled, table)
+
+
+def sibling_scores_kernel(factor, source, sibling, own, scaled, table, found, targets):
+    width = targets.shape[0] // 3
     block = width + SPARE
-    targets[0:width, :] = whole[0:width, :]
-    for k, piece in enumerate((a_first, a_second)):
-        targets[2 * width + k * half : 2 * width + (k + 1) * half, :] = piece[0:half, :]
-    for k, piece in enumerate((b_first, b_second)):
-        targets[4 * width + k * half : 4 * width + (k + 1) * half, :] = piece[0:half, :]
+    smalls = []
     for k in range(3):
-        start = (2 * k + 1) * width
-        targets[start : start + width, :] = sibling[k * block : k * block + width, :]
-    smalls = []
-    for k, message in enumerate((whole, a_first, b_second)):
-        smalls += [unpack(message), unpack(sibling, (k + 1) * block)]
+        targets[k * width : (k + 1) * width, :] = sibling[k * block : k * block + width, :]
+        smalls.append(unpack(sibling, (k + 1) * block))
     products(source, targets, factor, smalls, scaled, table)
 
     def score_of(at, p):
-        return scaled[at, p * LANES : (p + 1) * LANES]
+        part = (own, scaled)[p % 2]
+        return part[at, p // 2 * LANES : (p // 2 + 1) * LANES]
 
     def found_of(at, value):
         found[at, :] = jnp.broadcast_to(value, (CHUNK, LANES))
 
-    row_sweep(score_of, range(len(smalls)), scaled.shape[0], found_of)
-
-
-def pass_kernel(message, out):
+    row_sweep(score_of, range(6), scaled.shape[0], found_of)
+
+
+def pass_kernel(message, tie, out):
     out[...] = message[...]
 
 
@@ -243,24 +246,29 @@
 
 class Held:
 
-    def __init__(self, near, near_table, far, far_table):
-        self.count = near.shape[1] // LANES
-        self.total = self.count + far.shape[1] // LANES
-        self.near, self.near_table, self.far, self.far_table = near, near_table, far, far_table
+    def __init__(self, own, own_table, sibling, sibling_table, far, far_table):
+        self.near = own.shape[1] // LANES * 2
+        self.total = self.near + far.shape[1] // LANES
+        self.scores, self.tables = (own, sibling, far), (own_table, sibling_table, far_table)
+
+    def place(self, p):
+        return (p % 2, p // 2) if p < self.near else (2, p - self.near)
 
     def score(self, at, p):
-        part, p = (self.near, p) if p < self.count else (self.far, p - self.count)
-        return part[at, p * LANES : (p + 1) * LANES]
+        part, k = self.place(p)
+        return self.scores[part][at, k * LANES : (k + 1) * LANES]
 
     def row(self, kind, p):
-        table, p = (self.near_table, p) if p < self.count else (self.far_table, p - self.count)
-        return table[kind, p : p + 1, :]
-
-
-def first_kernel(near, near_table, found, far, far_table, logw, message, row_pot, ordered):
+        part, k = self.place(p)
+        return self.tables[part][kind, k : k + 1, :]
+
+
+def first_kernel(
+    own, own_table, sibling, sibling_table, far, far_table, found, logw, message, row_pot, ordered
+):
     order = positions(lax.axis_index("blk"))
-    held = Held(near, near_table, far, far_table)
-    rows = near.shape[0]
+    held = Held(own, own_table, sibling, sibling_table, far, far_table)
+    rows = own.shape[0]
 
     def row_found(at, value):
         row_pot[at, :] = logw[at, :] - value
@@ -268,17 +276,18 @@
     def column_found(p, value):
         ordered[pl.ds(order[p], 1), :] = value - held.row(1, p)
 
-    row_sweep(held.score, range(held.count, held.total), rows, row_found, others=found)
+    row_sweep(held.score, range(held.near, held.total), rows, row_found, others=found)
     column_sweep(held.score, range(held.total), rows, row_pot, column_found)
     message[...] = jnp.broadcast_to(ordered[...][None], message.shape)
 
 
 def second_kernel(
-    copies, near, near_table, far, far_table, got, logw, row, message, row_pot, ordered
+    copies, own, own_table, sibling, sibling_table, far, far_table, got, logw, row, message,
+    row_pot, ordered,
 ):
     order = positions(lax.axis_index("blk"))
-    held = Held(near, near_table, far, far_table)
-    rows = near.shape[0]
+    held = Held(own, own_table, sibling, sibling_table, far, far_table)
+    rows = own.shape[0]
     values = got[...]
     top = jnp.max(values, axis=0)
     ordered[...] = top + jnp.log2(jnp.sum(jnp.exp2(values - top[None]), axis=0))
@@ -376,7 +385,7 @@
         a_second = along(second_plain, 0)
         b_first = along(first_plain, 1)
         far_a = along(a_first, 1)
-        far_b = along(b_second, 0)
+        far_b = along(b_second[:half], 0)
         source, logw, passed = pl.pallas_call(
             source_kernel,
             out_shape=(
@@ -400,62 +409,60 @@
         )(passed, *near)
         sibling = to_sibling(sibling)
 
-        def passed_on(message, weight):
+        def table():
+            return values(2, SUBLANES, width)
+
+        def scores_of(kernel, blocks, pieces, extra=()):
+            return pl.pallas_call(
+                functools.partial(kernel, factor),
+                out_shape=(values(rows, blocks * width), table(), *extra),
+                in_specs=[vmem] * (1 + len(pieces)),
+                out_specs=(vmem,) * (2 + len(extra)),
+                scratch_shapes=[pltpu.VMEM((blocks * width, depth), target_embed.dtype)],
+                compiler_params=params,
+                cost_estimate=cost(0, 0),
+            )(source, *pieces)
+
+        own = scores_of(own_kernel, 3, (whole, *near))
+
+        def passed_on(message, tie, weight):
             return pl.pallas_call(
                 pass_kernel,
                 out_shape=jax.ShapeDtypeStruct(message.shape, message.dtype),
-                in_specs=[vmem],
+                in_specs=[vmem] * 2,
                 out_specs=vmem,
                 compiler_params=params,
                 cost_estimate=cost(weight * width, 0),
-            )(message)
-
-        sibling_a = to_sibling(passed_on(far_a, 0))
-        sibling_b = to_sibling(passed_on(far_b, 50))
-
-        def table():
-            return values(2, SUBLANES, width)
-
-        scores_near, table_near, found = pl.pallas_call(
-            functools.partial(near_kernel, factor),
-            out_shape=(values(rows, 6 * width), table(), values(rows, LANES)),
-            in_specs=[vmem] * 7,
-            out_specs=(vmem,) * 3,
-            scratch_shapes=[pltpu.VMEM((6 * width, depth), target_embed.dtype)],
-            compiler_params=params,
-            cost_estimate=cost(0, 0),
-        )(source, whole, *near, sibling)
-        scores_far, table_far = pl.pallas_call(
-            functools.partial(far_kernel, factor),
-            out_shape=(values(rows, 2 * width), table()),
-            in_specs=[vmem] * 6,
-            out_specs=(vmem, vmem),
-            scratch_shapes=[pltpu.VMEM((2 * width, depth), target_embed.dtype)],
-            compiler_params=params,
-            cost_estimate=cost(0, 0),
-        )(source, far_a, far_b, sibling_a, sibling_b, scores_near)
-        scores = (scores_far, table_far)
+            )(message, tie)
+
+        sibling_a = to_sibling(passed_on(far_a, own[1], 0))
+        sibling_b = to_sibling(passed_on(far_b, own[1], 50))
+        *other, found = scores_of(
+            sibling_scores_kernel, 3, (sibling, own[0]), (values(rows, LANES),)
+        )
+        far = scores_of(far_kernel, 2, (far_a, far_b, sibling_a, sibling_b, other[0]))
+        scores = (*own, *other, *far)
         row_scratch = pltpu.VMEM((rows, LANES), jnp.float32)
         block_scratch = pltpu.VMEM((blk, width), jnp.float32)
         message = pl.pallas_call(
             first_kernel,
             out_shape=values(blk * grp, blk, width),
-            in_specs=[vmem] * 6,
+            in_specs=[vmem] * 8,
             out_specs=vmem,
             scratch_shapes=[row_scratch, block_scratch],
             compiler_params=params,
             cost_estimate=cost(0, 1),
-        )(scores_near, table_near, found, *scores, logw)
+        )(*scores, found, logw)
         got = exchange(message)
         row, message = pl.pallas_call(
             functools.partial(second_kernel, grp),
             out_shape=(values(1, rows), values(blk * grp, width)),
-            in_specs=[vmem] * 6,
+            in_specs=[vmem] * 8,
             out_specs=(vmem, vmem),
             scratch_shapes=[row_scratch, block_scratch],
             compiler_params=params,
             cost_estimate=cost(0, 1),
-        )(scores_near, table_near, *scores, got, logw)
+        )(*scores, got, logw)
         got = exchange(message)
         row_pot, column_pot = pl.pallas_call(
             last_kernel,

time: 41.2 us -> 41.2 us (level)
  waiting for transfers between devices: 3.38 us -> 2.7 us
  Pallas kernels: 6.27 us -> 6.7 us
    ppermute x6, waiting for transfers between devices: 2.82 us -> 2 us  [along(): lax.ppermute(array, 'blk', [(i ^ neighbour_step(i, turn), i) for i in ran...]
    pallas_call x2 -> x3, Pallas kernels: 1.5 us -> 1.87 us  [scores_of(): pl.pallas_call(functools.partial(kernel, factor), out_shape=(values(rows,...]
  transfers between devices with their start and end apart: 9 -> 9, of which waited for: 5 -> 4; matrix products, arithmetic and copies ran while one was open for 0% -> 0% of each run, Pallas kernels for 6% -> 7%
where the time goes in v10:
time: 41.2 us; the launch traced here: 41 us
  blocking collectives  21.6 us (52%)
  starting transfers between devices  9.26 us (22%)
  Pallas kernels  6.7 us (16%)
  waiting for transfers between devices  2.7 us (7%)
  between operations  0.76 us (2%)
    all_to_all x2, blocking collectives, exchange(): lax.all_to_all(message, ('blk', 'grp'), 0, 0, axis_index_groups=[order])  21.6 us
    ppermute x6, starting transfers between devices, along(): lax.ppermute(array, 'blk', [(i ^ neighbour_step(i, turn), i) for i in ran...  8.56 us
    ppermute x6, waiting for transfers between devices, along(): lax.ppermute(array, 'blk', [(i ^ neighbour_step(i, turn), i) for i in ran...  2 us
    pallas_call x3, Pallas kernels, scores_of(): pl.pallas_call(functools.partial(kernel, factor), out_shape=(values(rows,...  1.87 us
    pallas_call x1, Pallas kernels, shards_square(): pl.pallas_call(source_kernel, out_shape=(jax.ShapeDtypeStruct((rows, dept...  1.4 us
    pallas_call x1, Pallas kernels, shards_square(): pl.pallas_call(functools.partial(second_kernel, grp), out_shape=(values(1...  1.07 us
    pallas_call x1, Pallas kernels, shards_square(): pl.pallas_call(head_kernel, out_shape=(block_of(half + SPARE), block_of(h...  0.99 us
  transfers between devices with their start and end apart: 9, of which 4 were waited for; matrix products, arithmetic and copies ran while one was open for 0% of the time, Pallas kernels for 7%

profile of v10, /device:TPU:0, one launch (start us, length us, event | category | flops | bytes accessed | tf_op | source)
XLA Modules:
  0.0 41.0 jit_solution(2610193660305304916)
XLA Ops:
  0.6 1.0 %shard_map.68 = (bf16[72,768]{1,0:T(8,128)(2,1)S(1)}, bf16[72,768]{1,0:T(8,128)(2,1)S(1)}, bf16[136,768]{1,0:T(8,128)(2,1)S(1)}, f32[2,128]{1,0:T(2,128)S(1)}, b...) custom-call(bf16[128,768]{1,0:T(8,128)(2,1)} %own.1, f32[1,128]{1,0:T(1,128)} %bitcast.12, f32[1,128]{1,0:T(1,128)} %bitcast.13), custom_call_target="tpu_custom_call" | custom-call | tf_op jit(solution)/shard_map/pallas_call | solution.py:364
  1.6 3.0 %collective-permute-start = (bf16[72,768]{1,0:T(8,128)(2,1)S(1)}, bf16[72,768]{1,0:T(8,128)(2,1)S(1)}, u32[]{:S(2)}, u32[]{:S(2)}) collective-permute-start(bf16[72,768]{1,0:T(8,128)(2,1)S(1)} %get-tuple-element.24), channel_id=1, source_target_pairs={{8,0},{20,4},{0,8},{28,12},{24,16},{4,20},{16,24},{12,28},{9,1},{2... | collective-permute-start | bytes 331784 | tf_op jit(solution)/shard_map/ppermute | solution.py:347
  4.6 1.5 %collective-permute-start.3 = (bf16[72,768]{1,0:T(8,128)(2,1)S(1)}, bf16[72,768]{1,0:T(8,128)(2,1)S(1)}, u32[]{:S(2)}, u32[]{:S(2)}) collective-permute-start(bf16[72,768]{1,0:T(8,128)(2,1)S(1)} %get-tuple-element.27), channel_id=1, source_target_pairs={{16,0},{12,4},{24,8},{4,12},{0,16},{28,20},{8,24},{20,28},{17,1},{... | collective-permute-start | bytes 331784 | tf_op jit(solution)/shard_map/ppermute | solution.py:347
  6.2 0.5 %collective-permute-start.1 = (bf16[64,768]{1,0:T(8,128)(2,1)S(1)}, bf16[64,768]{1,0:T(8,128)(2,1)S(1)}, u32[]{:S(2)}, u32[]{:S(2)}) collective-permute-start(bf16[64,768]{1,0:T(8,128)(2,1)S(1)} %get-tuple-element.25), channel_id=1, source_target_pairs={{8,0},{20,4},{0,8},{28,12},{24,16},{4,20},{16,24},{12,28},{9,1},{2... | collective-permute-start | bytes 294920 | tf_op jit(solution)/shard_map/ppermute | solution.py:347
  6.7 0.1 collective-permute-start.2
  6.7 1.2 %collective-permute-done.a_first = bf16[72,768]{1,0:T(8,128)(2,1)S(1)} collective-permute-done((bf16[72,768]{1,0:T(8,128)(2,1)S(1)}, bf16[72,768]{1,0:T(8,128)(2,1)S(1)}, u32[]{:S(2)}, u32[]{:S(2)}) %collective-permute-start) | collective-permute-done | bytes 110624 | tf_op jit(solution)/shard_map/ppermute | solution.py:347
  8.0 1.6 %collective-permute-start.5 = (bf16[72,768]{1,0:T(8,128)(2,1)S(1)}, bf16[72,768]{1,0:T(8,128)(2,1)S(1)}, u32[]{:S(2)}, u32[]{:S(2)}) collective-permute-start(bf16[72,768]{1,0:T(8,128)(2,1)S(1)} %collective-permute-done.a_first), channel_id=1, source_target_pairs={{16,0},{12,4},{24,8},{4,12},{0,16},{28,20},{8,24},{20,28},{17,1},{... | collective-permute-start | bytes 331784 | tf_op jit(solution)/shard_map/ppermute | solution.py:347
  9.6 0.7 %collective-permute-done.3.b_second = bf16[72,768]{1,0:T(8,128)(2,1)S(1)} collective-permute-done((bf16[72,768]{1,0:T(8,128)(2,1)S(1)}, bf16[72,768]{1,0:T(8,128)(2,1)S(1)}, u32[]{:S(2)}, u32[]{:S(2)}) %collective-permute-start.3) | collective-permute-done | bytes 110624 | tf_op jit(solution)/shard_map/ppermute | solution.py:347
  10.3 1.9 %collective-permute-start.6 = (bf16[64,768]{1,0:T(8,128)(2,1)S(1)}, bf16[64,768]{1,0:T(8,128)(2,1)S(1)}, u32[]{:S(2)}, u32[]{:S(2)}) collective-permute-start(bf16[64,768]{1,0:T(8,128)(2,1)S(1)} %slice.4), channel_id=1, source_target_pairs={{8,0},{20,4},{0,8},{28,12},{24,16},{4,20},{16,24},{12,28},{9,1},{2... | collective-permute-start | bytes 294920 | tf_op jit(solution)/shard_map/ppermute | solution.py:347
  12.1 1.4 %shard_map.69 = (bf16[512,768]{1,0:T(8,128)(2,1)S(1)}, f32[512,128]{1,0:T(8,128)S(1)}, bf16[136,768]{1,0:T(8,128)(2,1)S(1)}) custom-call(bf16[512,768]{1,0:T(8,128)(2,1)} %source.1, f32[1,512]{1,0:T(1,128)} %bitcast.11, bf16[136,768]{1,0:T(8,128)(2,1)S(1)} %get-tuple-element.22.whole), custom_call_target="tpu_custom_call" | custom-call | tf_op jit(solution)/shard_map/pallas_call | solution.py:389
  13.5 0.0 collective-permute-done.1.a_second
  13.5 0.0 collective-permute-done.2.b_first
  13.6 0.1 collective-permute-start.4
  13.7 0.6 %shard_map.70 = (f32[512,384]{1,0:T(8,128)S(1)}, f32[2,8,128]{2,1,0:T(8,128)S(1)}) custom-call(bf16[512,768]{1,0:T(8,128)(2,1)S(1)} %get-tuple-element.23.source, bf16[136,768]{1,0:T(8,128)(2,1)S(1)} %get-tuple-element.22.whole, bf16[72,768]{1,0:T(8,128)(2,1)S(1)} %collective-permute-done.a_first, bf16[64,768]{1,0:T(8,128)(2,1)S(1)} %collective-permute-done.1.a_second, ...), custom_call_target="tpu_custom_call" | custom-call | bytes 786432 | tf_op jit(solution)/shard_map/pallas_call | solution.py:416
  14.3 0.0 collective-permute-done.5.message.far_a
  14.3 0.6 %collective-permute-start.7 = (bf16[72,768]{1,0:T(8,128)(2,1)S(1)}, bf16[72,768]{1,0:T(8,128)(2,1)S(1)}, u32[]{:S(2)}, u32[]{:S(2)}) collective-permute-start(bf16[72,768]{1,0:T(8,128)(2,1)S(1)} %shard_map.73), channel_id=1, source_target_pairs={{4,0},{0,4},{12,8},{8,12},{20,16},{16,20},{28,24},{24,28},{5,1},{1... | collective-permute-start | bytes 331784 | tf_op jit(solution)/shard_map/ppermute | solution.py:22
  14.9 0.1 collective-permute-done.6.message.far_b
  15.0 0.1 collective-permute-start.8
  15.0 0.7 %collective-permute-done.4.sibling = bf16[408,768]{1,0:T(8,128)(2,1)S(1)} collective-permute-done((bf16[408,768]{1,0:T(8,128)(2,1)S(1)}, bf16[408,768]{1,0:T(8,128)(2,1)S(1)}, u32[]{:S(2)}, u32[]{:S(2)}) %collective-permute-start.4) | collective-permute-done | bytes 626720 | tf_op jit(solution)/shard_map/ppermute | solution.py:22
  15.7 0.9 %shard_map.72 = (f32[512,384]{1,0:T(8,128)S(1)}, f32[2,8,128]{2,1,0:T(8,128)S(1)}, f32[512,128]{1,0:T(8,128)S(1)}) custom-call(bf16[512,768]{1,0:T(8,128)(2,1)S(1)} %get-tuple-element.23.source, bf16[408,768]{1,0:T(8,128)(2,1)S(1)} %collective-permute-done.4.sibling, f32[512,384]{1,0:T(8,128)S(1)} %get-tuple-element.28.own), custom_call_target="tpu_custom_call" | custom-call | bytes 786432 | tf_op jit(solution)/shard_map/pallas_call | solution.py:416
  16.6 0.0 collective-permute-done.8.sibling_b
  16.6 0.0 collective-permute-done.7.sibling_a
  16.6 0.4 shard_map.75
  17.0 0.7 %shard_map.76 = f32[32,8,128]{2,1,0:T(8,128)S(1)} custom-call(f32[512,384]{1,0:T(8,128)S(1)} %get-tuple-element.28.own, f32[2,8,128]{2,1,0:T(8,128)S(1)} %get-tuple-element.29.tie.own_table, f32[512,384]{1,0:T(8,128)S(1)} %get-tuple-element.31.near.sibling, f32[2,8,128]{2,1,0:T(8,128)S(1)} %get-tuple-element.32.sibling_table, ...), custom_call_target="tpu_custom_call" | custom-call | flops 8388608 | bytes 786432 | tf_op jit(solution)/shard_map/pallas_call | solution.py:447
  17.8 12.6 %all_to_all.16.got = f32[32,8,128]{2,1,0:T(8,128)S(1)} all-to-all(f32[32,8,128]{2,1,0:T(8,128)S(1)} %shard_map.76), channel_id=1, replica_groups={{31,30,29,28,27,26,25,24,23,22,21,20,19,18,17,16,15,14,13,12,11,10,9,8,..., dimensions={0} | all-to-all | bytes 262144 | tf_op jit(solution)/shard_map/all_to_all | solution.py:356
  30.3 1.1 %shard_map.77 = (f32[1,512]{1,0:T(1,128)S(1)}, f32[32,128]{1,0:T(8,128)S(1)}) custom-call(f32[512,384]{1,0:T(8,128)S(1)} %get-tuple-element.28.own, f32[2,8,128]{2,1,0:T(8,128)S(1)} %get-tuple-element.29.tie.own_table, f32[512,384]{1,0:T(8,128)S(1)} %get-tuple-element.31.near.sibling, f32[2,8,128]{2,1,0:T(8,128)S(1)} %get-tuple-element.32.sibling_table, ...), custom_call_target="tpu_custom_call" | custom-call | flops 8388608 | bytes 786432 | tf_op jit(solution)/shard_map/pallas_call | solution.py:457
  31.4 9.0 %all_to_all.17 = f32[32,1,128]{2,1,0:T(1,128)S(1)} all-to-all(f32[32,1,128]{2,1,0:T(1,128)S(1)} %bitcast.10), channel_id=1, replica_groups={{31,30,29,28,27,26,25,24,23,22,21,20,19,18,17,16,15,14,13,12,11,10,9,8,..., dimensions={0} | all-to-all | bytes 32768 | tf_op jit(solution)/shard_map/all_to_all | solution.py:356
  40.4 0.6 %shard_map.78 = (f32[1,512]{1,0:T(1,128)}, f32[1,128]{1,0:T(1,128)}) custom-call(f32[32,128]{1,0:T(8,128)S(1)} %bitcast.9, f32[2,128]{1,0:T(2,128)S(1)} %get-tuple-element.38.small, f32[1,512]{1,0:T(1,128)S(1)} %get-tuple-element.39.row), custom_call_target="tpu_custom_call" | custom-call | tf_op jit(solution)/shard_map/pallas_call | solution.py:467
  (4 shorter events, 0.1 us)
Async XLA Ops:
  1.6 6.3 %collective-permute-start = (bf16[72,768]{1,0:T(8,128)(2,1)S(1)}, bf16[72,768]{1,0:T(8,128)(2,1)S(1)}, u32[]{:S(2)}, u32[]{:S(2)}) collective-permute-start(bf16[72,768]{1,0:T(8,128)(2,1)S(1)} %get-tuple-element.24), channel_id=1, source_target_pairs={{8,0},{20,4},{0,8},{28,12},{24,16},{4,20},{16,24},{12,28},{9,1},{2... | collective-permute-start | bytes 331784 | tf_op jit(solution)/shard_map/ppermute | solution.py:347
  4.6 5.6 %collective-permute-start.3 = (bf16[72,768]{1,0:T(8,128)(2,1)S(1)}, bf16[72,768]{1,0:T(8,128)(2,1)S(1)}, u32[]{:S(2)}, u32[]{:S(2)}) collective-permute-start(bf16[72,768]{1,0:T(8,128)(2,1)S(1)} %get-tuple-element.27), channel_id=1, source_target_pairs={{16,0},{12,4},{24,8},{4,12},{0,16},{28,20},{8,24},{20,28},{17,1},{... | collective-permute-start | bytes 331784 | tf_op jit(solution)/shard_map/ppermute | solution.py:347
  6.2 7.4 %collective-permute-start.1 = (bf16[64,768]{1,0:T(8,128)(2,1)S(1)}, bf16[64,768]{1,0:T(8,128)(2,1)S(1)}, u32[]{:S(2)}, u32[]{:S(2)}) collective-permute-start(bf16[64,768]{1,0:T(8,128)(2,1)S(1)} %get-tuple-element.25), channel_id=1, source_target_pairs={{8,0},{20,4},{0,8},{28,12},{24,16},{4,20},{16,24},{12,28},{9,1},{2... | collective-permute-start | bytes 294920 | tf_op jit(solution)/shard_map/ppermute | solution.py:347
  6.7 6.9 %collective-permute-start.2 = (bf16[64,768]{1,0:T(8,128)(2,1)S(1)}, bf16[64,768]{1,0:T(8,128)(2,1)S(1)}, u32[]{:S(2)}, u32[]{:S(2)}) collective-permute-start(bf16[64,768]{1,0:T(8,128)(2,1)S(1)} %get-tuple-element.26), channel_id=1, source_target_pairs={{16,0},{12,4},{24,8},{4,12},{0,16},{28,20},{8,24},{20,28},{17,1},{... | collective-permute-start | bytes 294920 | tf_op jit(solution)/shard_map/ppermute | solution.py:347
  8.0 6.3 %collective-permute-start.5 = (bf16[72,768]{1,0:T(8,128)(2,1)S(1)}, bf16[72,768]{1,0:T(8,128)(2,1)S(1)}, u32[]{:S(2)}, u32[]{:S(2)}) collective-permute-start(bf16[72,768]{1,0:T(8,128)(2,1)S(1)} %collective-permute-done.a_first), channel_id=1, source_target_pairs={{16,0},{12,4},{24,8},{4,12},{0,16},{28,20},{8,24},{20,28},{17,1},{... | collective-permute-start | bytes 331784 | tf_op jit(solution)/shard_map/ppermute | solution.py:347
  10.3 4.7 %collective-permute-start.6 = (bf16[64,768]{1,0:T(8,128)(2,1)S(1)}, bf16[64,768]{1,0:T(8,128)(2,1)S(1)}, u32[]{:S(2)}, u32[]{:S(2)}) collective-permute-start(bf16[64,768]{1,0:T(8,128)(2,1)S(1)} %slice.4), channel_id=1, source_target_pairs={{8,0},{20,4},{0,8},{28,12},{24,16},{4,20},{16,24},{12,28},{9,1},{2... | collective-permute-start | bytes 294920 | tf_op jit(solution)/shard_map/ppermute | solution.py:347
  13.6 2.1 %collective-permute-start.4 = (bf16[408,768]{1,0:T(8,128)(2,1)S(1)}, bf16[408,768]{1,0:T(8,128)(2,1)S(1)}, u32[]{:S(2)}, u32[]{:S(2)}) collective-permute-start(bf16[408,768]{1,0:T(8,128)(2,1)S(1)} %shard_map.71), channel_id=1, source_target_pairs={{4,0},{0,4},{12,8},{8,12},{20,16},{16,20},{28,24},{24,28},{5,1},{1... | collective-permute-start | bytes 1880072 | tf_op jit(solution)/shard_map/ppermute | solution.py:22
  14.3 2.3 %collective-permute-start.7 = (bf16[72,768]{1,0:T(8,128)(2,1)S(1)}, bf16[72,768]{1,0:T(8,128)(2,1)S(1)}, u32[]{:S(2)}, u32[]{:S(2)}) collective-permute-start(bf16[72,768]{1,0:T(8,128)(2,1)S(1)} %shard_map.73), channel_id=1, source_target_pairs={{4,0},{0,4},{12,8},{8,12},{20,16},{16,20},{28,24},{24,28},{5,1},{1... | collective-permute-start | bytes 331784 | tf_op jit(solution)/shard_map/ppermute | solution.py:22
  15.0 1.6 %collective-permute-start.8 = (bf16[64,768]{1,0:T(8,128)(2,1)S(1)}, bf16[64,768]{1,0:T(8,128)(2,1)S(1)}, u32[]{:S(2)}, u32[]{:S(2)}) collective-permute-start(bf16[64,768]{1,0:T(8,128)(2,1)S(1)} %shard_map.74), channel_id=1, source_target_pairs={{4,0},{0,4},{12,8},{8,12},{20,16},{16,20},{28,24},{24,28},{5,1},{1... | collective-permute-start | bytes 294920 | tf_op jit(solution)/shard_map/ppermute | solution.py:22

commit v11 on v10

--- a/solution.py
+++ b/solution.py
@@ -66,20 +66,25 @@
     return [pl.ds(start, CHUNK) for start in range(0, rows, CHUNK)]
 
 
-def row_sweep(score_of, blocks, rows, found_of, columns=None, others=None):
+def row_sweep(score_of, blocks, rows, found_of, columns=None, others=None, kept=None):
     tops = []
     for at in chunks_of(rows):
         top = None if others is None else others[at, :]
         for p in blocks:
             score = score_of(at, p)
-            score = score if columns is None else score + columns[p]
+            if columns is not None:
+                score = score + columns[p]
+                kept[at, p * LANES : (p + 1) * LANES] = score
             top = score if top is None else jnp.maximum(top, score)
         tops.append(jnp.max(top, axis=1, keepdims=True))
     for at, top in zip(chunks_of(rows), tops):
         total = None
         for p in blocks:
-            shift = -top if columns is None else columns[p] - top
-            term = jnp.exp2(score_of(at, p) + shift)
+            if columns is None:
+                score = score_of(at, p)
+            else:
+                score = kept[at, p * LANES : (p + 1) * LANES]
+            term = jnp.exp2(score - top)
             total = term if total is None else total + term
         total = jnp.sum(total, axis=1, keepdims=True)
         if others is not None:
@@ -283,7 +288,7 @@
 
 def second_kernel(
     copies, own, own_table, sibling, sibling_table, far, far_table, got, logw, row, message,
-    row_pot, ordered,
+    row_pot, ordered, kept,
 ):
     order = positions(lax.axis_index("blk"))
     held = Held(own, own_table, sibling, sibling_table, far, far_table)
@@ -302,7 +307,7 @@
         at = pl.ds((held.total - 1 - order[p]) * copies, copies)
         message[at, :] = jnp.broadcast_to(value - held.row(1, p), (copies, LANES))
 
-    row_sweep(held.score, range(held.total), rows, row_found, columns=columns)
+    row_sweep(held.score, range(held.total), rows, row_found, columns=columns, kept=kept)
     column_sweep(held.score, range(held.total), rows, row_pot, column_found)
     row[...] = as_row(row_pot[:, 0:1]) * (epsilon * LN2)
 
@@ -459,7 +464,11 @@
             out_shape=(values(1, rows), values(blk * grp, width)),
             in_specs=[vmem] * 8,
             out_specs=(vmem, vmem),
-            scratch_shapes=[row_scratch, block_scratch],
+            scratch_shapes=[
+                row_scratch,
+                block_scratch,
+                pltpu.VMEM((rows, blk * width), jnp.float32),
+            ],
             compiler_params=params,
             cost_estimate=cost(0, 1),
         )(*scores, got, logw)

time: 41.2 us -> 41.2 us (level)
  no operation moved by 1% of the time
where the time goes in v11:
time: 41.2 us; the launch traced here: 41 us
  blocking collectives  21.6 us (52%)
  starting transfers between devices  9.26 us (22%)
  Pallas kernels  6.73 us (16%)
  waiting for transfers between devices  2.7 us (7%)
  between operations  0.76 us (2%)
    all_to_all x2, blocking collectives, exchange(): lax.all_to_all(message, ('blk', 'grp'), 0, 0, axis_index_groups=[order])  21.6 us
    ppermute x6, starting transfers between devices, along(): lax.ppermute(array, 'blk', [(i ^ neighbour_step(i, turn), i) for i in ran...  8.56 us
    ppermute x6, waiting for transfers between devices, along(): lax.ppermute(array, 'blk', [(i ^ neighbour_step(i, turn), i) for i in ran...  2 us
    pallas_call x3, Pallas kernels, scores_of(): pl.pallas_call(functools.partial(kernel, factor), out_shape=(values(rows,...  1.87 us
    pallas_call x1, Pallas kernels, shards_square(): pl.pallas_call(source_kernel, out_shape=(jax.ShapeDtypeStruct((rows, dept...  1.4 us
    pallas_call x1, Pallas kernels, shards_square(): pl.pallas_call(functools.partial(second_kernel, grp), out_shape=(values(1...  1.09 us
    pallas_call x1, Pallas kernels, shards_square(): pl.pallas_call(head_kernel, out_shape=(block_of(half + SPARE), block_of(h...  0.99 us
  transfers between devices with their start and end apart: 9, of which 4 were waited for; matrix products, arithmetic and copies ran while one was open for 0% of the time, Pallas kernels for 7%

profile of v11, /device:TPU:0, one launch (start us, length us, event | category | flops | bytes accessed | tf_op | source)
XLA Modules:
  0.0 41.0 jit_solution(16883441538546851113)
XLA Ops:
  0.6 1.0 %shard_map.68 = (bf16[72,768]{1,0:T(8,128)(2,1)S(1)}, bf16[72,768]{1,0:T(8,128)(2,1)S(1)}, bf16[136,768]{1,0:T(8,128)(2,1)S(1)}, f32[2,128]{1,0:T(2,128)S(1)}, b...) custom-call(bf16[128,768]{1,0:T(8,128)(2,1)} %own.1, f32[1,128]{1,0:T(1,128)} %bitcast.12, f32[1,128]{1,0:T(1,128)} %bitcast.13), custom_call_target="tpu_custom_call" | custom-call | tf_op jit(solution)/shard_map/pallas_call | solution.py:369
  1.6 3.0 %collective-permute-start = (bf16[72,768]{1,0:T(8,128)(2,1)S(1)}, bf16[72,768]{1,0:T(8,128)(2,1)S(1)}, u32[]{:S(2)}, u32[]{:S(2)}) collective-permute-start(bf16[72,768]{1,0:T(8,128)(2,1)S(1)} %get-tuple-element.24), channel_id=1, source_target_pairs={{8,0},{20,4},{0,8},{28,12},{24,16},{4,20},{16,24},{12,28},{9,1},{2... | collective-permute-start | bytes 331784 | tf_op jit(solution)/shard_map/ppermute | solution.py:352
  4.6 1.5 %collective-permute-start.3 = (bf16[72,768]{1,0:T(8,128)(2,1)S(1)}, bf16[72,768]{1,0:T(8,128)(2,1)S(1)}, u32[]{:S(2)}, u32[]{:S(2)}) collective-permute-start(bf16[72,768]{1,0:T(8,128)(2,1)S(1)} %get-tuple-element.27), channel_id=1, source_target_pairs={{16,0},{12,4},{24,8},{4,12},{0,16},{28,20},{8,24},{20,28},{17,1},{... | collective-permute-start | bytes 331784 | tf_op jit(solution)/shard_map/ppermute | solution.py:352
  6.2 0.5 %collective-permute-start.1 = (bf16[64,768]{1,0:T(8,128)(2,1)S(1)}, bf16[64,768]{1,0:T(8,128)(2,1)S(1)}, u32[]{:S(2)}, u32[]{:S(2)}) collective-permute-start(bf16[64,768]{1,0:T(8,128)(2,1)S(1)} %get-tuple-element.25), channel_id=1, source_target_pairs={{8,0},{20,4},{0,8},{28,12},{24,16},{4,20},{16,24},{12,28},{9,1},{2... | collective-permute-start | bytes 294920 | tf_op jit(solution)/shard_map/ppermute | solution.py:352
  6.7 0.1 collective-permute-start.2
  6.7 1.2 %collective-permute-done.a_first = bf16[72,768]{1,0:T(8,128)(2,1)S(1)} collective-permute-done((bf16[72,768]{1,0:T(8,128)(2,1)S(1)}, bf16[72,768]{1,0:T(8,128)(2,1)S(1)}, u32[]{:S(2)}, u32[]{:S(2)}) %collective-permute-start) | collective-permute-done | bytes 110624 | tf_op jit(solution)/shard_map/ppermute | solution.py:352
  8.0 1.6 %collective-permute-start.5 = (bf16[72,768]{1,0:T(8,128)(2,1)S(1)}, bf16[72,768]{1,0:T(8,128)(2,1)S(1)}, u32[]{:S(2)}, u32[]{:S(2)}) collective-permute-start(bf16[72,768]{1,0:T(8,128)(2,1)S(1)} %collective-permute-done.a_first), channel_id=1, source_target_pairs={{16,0},{12,4},{24,8},{4,12},{0,16},{28,20},{8,24},{20,28},{17,1},{... | collective-permute-start | bytes 331784 | tf_op jit(solution)/shard_map/ppermute | solution.py:352
  9.6 0.7 %collective-permute-done.3.b_second = bf16[72,768]{1,0:T(8,128)(2,1)S(1)} collective-permute-done((bf16[72,768]{1,0:T(8,128)(2,1)S(1)}, bf16[72,768]{1,0:T(8,128)(2,1)S(1)}, u32[]{:S(2)}, u32[]{:S(2)}) %collective-permute-start.3) | collective-permute-done | bytes 110624 | tf_op jit(solution)/shard_map/ppermute | solution.py:352
  10.3 1.9 %collective-permute-start.6 = (bf16[64,768]{1,0:T(8,128)(2,1)S(1)}, bf16[64,768]{1,0:T(8,128)(2,1)S(1)}, u32[]{:S(2)}, u32[]{:S(2)}) collective-permute-start(bf16[64,768]{1,0:T(8,128)(2,1)S(1)} %slice.4), channel_id=1, source_target_pairs={{8,0},{20,4},{0,8},{28,12},{24,16},{4,20},{16,24},{12,28},{9,1},{2... | collective-permute-start | bytes 294920 | tf_op jit(solution)/shard_map/ppermute | solution.py:352
  12.1 1.4 %shard_map.69 = (bf16[512,768]{1,0:T(8,128)(2,1)S(1)}, f32[512,128]{1,0:T(8,128)S(1)}, bf16[136,768]{1,0:T(8,128)(2,1)S(1)}) custom-call(bf16[512,768]{1,0:T(8,128)(2,1)} %source.1, f32[1,512]{1,0:T(1,128)} %bitcast.11, bf16[136,768]{1,0:T(8,128)(2,1)S(1)} %get-tuple-element.22.whole), custom_call_target="tpu_custom_call" | custom-call | tf_op jit(solution)/shard_map/pallas_call | solution.py:394
  13.5 0.0 collective-permute-done.1.a_second
  13.5 0.0 collective-permute-done.2.b_first
  13.6 0.1 collective-permute-start.4
  13.7 0.6 %shard_map.70 = (f32[512,384]{1,0:T(8,128)S(1)}, f32[2,8,128]{2,1,0:T(8,128)S(1)}) custom-call(bf16[512,768]{1,0:T(8,128)(2,1)S(1)} %get-tuple-element.23.source, bf16[136,768]{1,0:T(8,128)(2,1)S(1)} %get-tuple-element.22.whole, bf16[72,768]{1,0:T(8,128)(2,1)S(1)} %collective-permute-done.a_first, bf16[64,768]{1,0:T(8,128)(2,1)S(1)} %collective-permute-done.1.a_second, ...), custom_call_target="tpu_custom_call" | custom-call | bytes 786432 | tf_op jit(solution)/shard_map/pallas_call | solution.py:421
  14.3 0.0 collective-permute-done.5.message.far_a
  14.3 0.6 %collective-permute-start.7 = (bf16[72,768]{1,0:T(8,128)(2,1)S(1)}, bf16[72,768]{1,0:T(8,128)(2,1)S(1)}, u32[]{:S(2)}, u32[]{:S(2)}) collective-permute-start(bf16[72,768]{1,0:T(8,128)(2,1)S(1)} %shard_map.73), channel_id=1, source_target_pairs={{4,0},{0,4},{12,8},{8,12},{20,16},{16,20},{28,24},{24,28},{5,1},{1... | collective-permute-start | bytes 331784 | tf_op jit(solution)/shard_map/ppermute | solution.py:22
  14.9 0.1 collective-permute-done.6.message.far_b
  15.0 0.1 collective-permute-start.8
  15.0 0.7 %collective-permute-done.4.sibling = bf16[408,768]{1,0:T(8,128)(2,1)S(1)} collective-permute-done((bf16[408,768]{1,0:T(8,128)(2,1)S(1)}, bf16[408,768]{1,0:T(8,128)(2,1)S(1)}, u32[]{:S(2)}, u32[]{:S(2)}) %collective-permute-start.4) | collective-permute-done | bytes 626720 | tf_op jit(solution)/shard_map/ppermute | solution.py:22
  15.7 0.9 %shard_map.72 = (f32[512,384]{1,0:T(8,128)S(1)}, f32[2,8,128]{2,1,0:T(8,128)S(1)}, f32[512,128]{1,0:T(8,128)S(1)}) custom-call(bf16[512,768]{1,0:T(8,128)(2,1)S(1)} %get-tuple-element.23.source, bf16[408,768]{1,0:T(8,128)(2,1)S(1)} %collective-permute-done.4.sibling, f32[512,384]{1,0:T(8,128)S(1)} %get-tuple-element.28.own), custom_call_target="tpu_custom_call" | custom-call | bytes 786432 | tf_op jit(solution)/shard_map/pallas_call | solution.py:421
  16.6 0.0 collective-permute-done.8.sibling_b
  16.6 0.0 collective-permute-done.7.sibling_a
  16.6 0.4 shard_map.75
  17.0 0.7 %shard_map.76 = f32[32,8,128]{2,1,0:T(8,128)S(1)} custom-call(f32[512,384]{1,0:T(8,128)S(1)} %get-tuple-element.28.own, f32[2,8,128]{2,1,0:T(8,128)S(1)} %get-tuple-element.29.tie.own_table, f32[512,384]{1,0:T(8,128)S(1)} %get-tuple-element.31.near.sibling, f32[2,8,128]{2,1,0:T(8,128)S(1)} %get-tuple-element.32.sibling_table, ...), custom_call_target="tpu_custom_call" | custom-call | flops 8388608 | bytes 786432 | tf_op jit(solution)/shard_map/pallas_call | solution.py:452
  17.8 12.6 %all_to_all.16.got = f32[32,8,128]{2,1,0:T(8,128)S(1)} all-to-all(f32[32,8,128]{2,1,0:T(8,128)S(1)} %shard_map.76), channel_id=1, replica_groups={{31,30,29,28,27,26,25,24,23,22,21,20,19,18,17,16,15,14,13,12,11,10,9,8,..., dimensions={0} | all-to-all | bytes 262144 | tf_op jit(solution)/shard_map/all_to_all | solution.py:361
  30.3 1.1 %shard_map.77 = (f32[1,512]{1,0:T(1,128)S(1)}, f32[32,128]{1,0:T(8,128)S(1)}) custom-call(f32[512,384]{1,0:T(8,128)S(1)} %get-tuple-element.28.own, f32[2,8,128]{2,1,0:T(8,128)S(1)} %get-tuple-element.29.tie.own_table, f32[512,384]{1,0:T(8,128)S(1)} %get-tuple-element.31.near.sibling, f32[2,8,128]{2,1,0:T(8,128)S(1)} %get-tuple-element.32.sibling_table, ...), custom_call_target="tpu_custom_call" | custom-call | flops 8388608 | bytes 786432 | tf_op jit(solution)/shard_map/pallas_call | solution.py:462
  31.4 9.0 %all_to_all.17 = f32[32,1,128]{2,1,0:T(1,128)S(1)} all-to-all(f32[32,1,128]{2,1,0:T(1,128)S(1)} %bitcast.10), channel_id=1, replica_groups={{31,30,29,28,27,26,25,24,23,22,21,20,19,18,17,16,15,14,13,12,11,10,9,8,..., dimensions={0} | all-to-all | bytes 32768 | tf_op jit(solution)/shard_map/all_to_all | solution.py:361
  40.5 0.6 %shard_map.78 = (f32[1,512]{1,0:T(1,128)}, f32[1,128]{1,0:T(1,128)}) custom-call(f32[32,128]{1,0:T(8,128)S(1)} %bitcast.9, f32[2,128]{1,0:T(2,128)S(1)} %get-tuple-element.38.small, f32[1,512]{1,0:T(1,128)S(1)} %get-tuple-element.39.row), custom_call_target="tpu_custom_call" | custom-call | tf_op jit(solution)/shard_map/pallas_call | solution.py:476
  (4 shorter events, 0.1 us)
Async XLA Ops:
  1.6 6.3 %collective-permute-start = (bf16[72,768]{1,0:T(8,128)(2,1)S(1)}, bf16[72,768]{1,0:T(8,128)(2,1)S(1)}, u32[]{:S(2)}, u32[]{:S(2)}) collective-permute-start(bf16[72,768]{1,0:T(8,128)(2,1)S(1)} %get-tuple-element.24), channel_id=1, source_target_pairs={{8,0},{20,4},{0,8},{28,12},{24,16},{4,20},{16,24},{12,28},{9,1},{2... | collective-permute-start | bytes 331784 | tf_op jit(solution)/shard_map/ppermute | solution.py:352
  4.6 5.6 %collective-permute-start.3 = (bf16[72,768]{1,0:T(8,128)(2,1)S(1)}, bf16[72,768]{1,0:T(8,128)(2,1)S(1)}, u32[]{:S(2)}, u32[]{:S(2)}) collective-permute-start(bf16[72,768]{1,0:T(8,128)(2,1)S(1)} %get-tuple-element.27), channel_id=1, source_target_pairs={{16,0},{12,4},{24,8},{4,12},{0,16},{28,20},{8,24},{20,28},{17,1},{... | collective-permute-start | bytes 331784 | tf_op jit(solution)/shard_map/ppermute | solution.py:352
  6.2 7.4 %collective-permute-start.1 = (bf16[64,768]{1,0:T(8,128)(2,1)S(1)}, bf16[64,768]{1,0:T(8,128)(2,1)S(1)}, u32[]{:S(2)}, u32[]{:S(2)}) collective-permute-start(bf16[64,768]{1,0:T(8,128)(2,1)S(1)} %get-tuple-element.25), channel_id=1, source_target_pairs={{8,0},{20,4},{0,8},{28,12},{24,16},{4,20},{16,24},{12,28},{9,1},{2... | collective-permute-start | bytes 294920 | tf_op jit(solution)/shard_map/ppermute | solution.py:352
  6.7 6.9 %collective-permute-start.2 = (bf16[64,768]{1,0:T(8,128)(2,1)S(1)}, bf16[64,768]{1,0:T(8,128)(2,1)S(1)}, u32[]{:S(2)}, u32[]{:S(2)}) collective-permute-start(bf16[64,768]{1,0:T(8,128)(2,1)S(1)} %get-tuple-element.26), channel_id=1, source_target_pairs={{16,0},{12,4},{24,8},{4,12},{0,16},{28,20},{8,24},{20,28},{17,1},{... | collective-permute-start | bytes 294920 | tf_op jit(solution)/shard_map/ppermute | solution.py:352
  8.0 6.3 %collective-permute-start.5 = (bf16[72,768]{1,0:T(8,128)(2,1)S(1)}, bf16[72,768]{1,0:T(8,128)(2,1)S(1)}, u32[]{:S(2)}, u32[]{:S(2)}) collective-permute-start(bf16[72,768]{1,0:T(8,128)(2,1)S(1)} %collective-permute-done.a_first), channel_id=1, source_target_pairs={{16,0},{12,4},{24,8},{4,12},{0,16},{28,20},{8,24},{20,28},{17,1},{... | collective-permute-start | bytes 331784 | tf_op jit(solution)/shard_map/ppermute | solution.py:352
  10.3 4.7 %collective-permute-start.6 = (bf16[64,768]{1,0:T(8,128)(2,1)S(1)}, bf16[64,768]{1,0:T(8,128)(2,1)S(1)}, u32[]{:S(2)}, u32[]{:S(2)}) collective-permute-start(bf16[64,768]{1,0:T(8,128)(2,1)S(1)} %slice.4), channel_id=1, source_target_pairs={{8,0},{20,4},{0,8},{28,12},{24,16},{4,20},{16,24},{12,28},{9,1},{2... | collective-permute-start | bytes 294920 | tf_op jit(solution)/shard_map/ppermute | solution.py:352
  13.6 2.1 %collective-permute-start.4 = (bf16[408,768]{1,0:T(8,128)(2,1)S(1)}, bf16[408,768]{1,0:T(8,128)(2,1)S(1)}, u32[]{:S(2)}, u32[]{:S(2)}) collective-permute-start(bf16[408,768]{1,0:T(8,128)(2,1)S(1)} %shard_map.71), channel_id=1, source_target_pairs={{4,0},{0,4},{12,8},{8,12},{20,16},{16,20},{28,24},{24,28},{5,1},{1... | collective-permute-start | bytes 1880072 | tf_op jit(solution)/shard_map/ppermute | solution.py:22
  14.3 2.3 %collective-permute-start.7 = (bf16[72,768]{1,0:T(8,128)(2,1)S(1)}, bf16[72,768]{1,0:T(8,128)(2,1)S(1)}, u32[]{:S(2)}, u32[]{:S(2)}) collective-permute-start(bf16[72,768]{1,0:T(8,128)(2,1)S(1)} %shard_map.73), channel_id=1, source_target_pairs={{4,0},{0,4},{12,8},{8,12},{20,16},{16,20},{28,24},{24,28},{5,1},{1... | collective-permute-start | bytes 331784 | tf_op jit(solution)/shard_map/ppermute | solution.py:22
  15.0 1.6 %collective-permute-start.8 = (bf16[64,768]{1,0:T(8,128)(2,1)S(1)}, bf16[64,768]{1,0:T(8,128)(2,1)S(1)}, u32[]{:S(2)}, u32[]{:S(2)}) collective-permute-start(bf16[64,768]{1,0:T(8,128)(2,1)S(1)} %shard_map.74), channel_id=1, source_target_pairs={{4,0},{0,4},{12,8},{8,12},{20,16},{16,20},{28,24},{24,28},{5,1},{1... | collective-permute-start | bytes 294920 | tf_op jit(solution)/shard_map/ppermute | solution.py:22

commit v12 on v10

--- a/solution.py
+++ b/solution.py
@@ -89,18 +89,20 @@
 
 def column_sweep(score_of, blocks, rows, row_pot, found_of):
     folds = (CHUNK // SUBLANES, SUBLANES, LANES)
-    found = [[] for _ in blocks]
-    for at in chunks_of(rows):
-        addend = row_pot[at, :]
-        for p in blocks:
-            score = (score_of(at, p) + addend).reshape(folds)
-            top = jnp.max(score, axis=0)
-            found[p].append((top, jnp.sum(jnp.exp2(score - top[None]), axis=0)))
-    for p in blocks:
-        top = functools.reduce(jnp.maximum, [each for each, _ in found[p]])
-        top = jnp.max(top, axis=0, keepdims=True)
-        total = sum(each * jnp.exp2(at_top - top) for at_top, each in found[p])
-        found_of(p, top + jnp.log2(jnp.sum(total, axis=0, keepdims=True)))
+    for start in range(0, len(blocks), 2):
+        pair = blocks[start : start + 2]
+        found = {p: [] for p in pair}
+        for at in chunks_of(rows):
+            addend = row_pot[at, :]
+            for p in pair:
+                score = (score_of(at, p) + addend).reshape(folds)
+                top = jnp.max(score, axis=0)
+                found[p].append((top, jnp.sum(jnp.exp2(score - top[None]), axis=0)))
+        for p in pair:
+            top = functools.reduce(jnp.maximum, [each for each, _ in found[p]])
+            top = jnp.max(top, axis=0, keepdims=True)
+            total = sum(each * jnp.exp2(at_top - top) for at_top, each in found[p])
+            found_of(p, top + jnp.log2(jnp.sum(total, axis=0, keepdims=True)))
 
 
 def products(source, targets, factor, smalls, scaled, table):
@@ -122,7 +124,7 @@
     own, init, target_logw, first, second, whole, small, first_plain, second_plain, init_row,
     logw_row, sems,
 ):
-    rows, half = own.shape[0], first_plain.shape[0]
+    rows, cut, rest_rows = own.shape[0], first_plain.shape[0], second_plain.shape[0]
     copies = [
         pltpu.make_async_copy(own, whole.at[0:rows], sems.at[0]),
         pltpu.make_async_copy(init, init_row, sems.at[1]),
@@ -133,9 +135,9 @@
     for copy in copies:
         copy.wait()
     for out in (first, first_plain):
-        out[0:half, :] = whole[0:half, :]
+        out[0:cut, :] = whole[0:cut, :]
     for out in (second, second_plain):
-        out[0:half, :] = whole[half:rows, :]
+        out[0:rest_rows, :] = whole[cut:rows, :]
     small[0:1, :] = init_row[...]
     small[1:2, :] = logw_row[...]
     filler = jnp.zeros((SPARE - 2, LANES), jnp.float32)
@@ -143,8 +145,8 @@
     for k in range(whole.shape[1] // LANES):
         lanes = slice(k * LANES, (k + 1) * LANES)
         part = (rest if k < 3 else jnp.zeros_like(rest)).astype(whole.dtype)
-        first[half:, lanes] = part
-        second[half:, lanes] = part
+        first[cut:, lanes] = part
+        second[rest_rows:, lanes] = part
         whole[rows:, lanes] = part
         rest = rest - part.astype(jnp.float32)
 
@@ -162,15 +164,20 @@
     row_logw[...] = jnp.broadcast_to(as_column(rows_row[...] * LOG2E), row_logw.shape)
 
 
+def fill(out, start, *halves):
+    cut, rest_rows = halves[0][1], halves[1][1]
+    out[start : start + cut, :] = halves[0][0][0:cut, :]
+    out[start + cut : start + cut + rest_rows, :] = halves[1][0][0:rest_rows, :]
+
+
 def sibling_kernel(whole, a_first, a_second, b_first, b_second, out):
-    half = a_second.shape[0]
-    block = 2 * half + SPARE
+    cut, rest_rows = b_first.shape[0], a_second.shape[0]
+    block = cut + rest_rows + SPARE
     out[0:block, :] = whole[...]
-    out[block : block + half, :] = a_first[0:half, :]
-    out[block + half : block + 2 * half, :] = a_second[...]
-    out[block + 2 * half : 2 * block, :] = a_first[half:, :]
-    out[2 * block : 2 * block + half, :] = b_first[...]
-    out[2 * block + half : 3 * block, :] = b_second[...]
+    fill(out, block, (a_first, cut), (a_second, rest_rows))
+    out[2 * block - SPARE : 2 * block, :] = a_first[cut:, :]
+    fill(out, 2 * block, (b_first, cut), (b_second, rest_rows))
+    out[3 * block - SPARE : 3 * block, :] = b_second[rest_rows:, :]
 
 
 def unpack(message, end=None):
@@ -185,11 +192,11 @@
 def own_kernel(
     factor, source, whole, a_first, a_second, b_first, b_second, scaled, table, targets
 ):
-    half = a_second.shape[0]
-    pieces = (whole, whole, a_first, a_second, b_first, b_second)
-    targets[0 : 2 * half, :] = whole[0 : 2 * half, :]
-    for k in range(2, 6):
-        targets[k * half : (k + 1) * half, :] = pieces[k][0:half, :]
+    cut, rest_rows = b_first.shape[0], a_second.shape[0]
+    width = cut + rest_rows
+    targets[0:width, :] = whole[0:width, :]
+    fill(targets, width, (a_first, cut), (a_second, rest_rows))
+    fill(targets, 2 * width, (b_first, cut), (b_second, rest_rows))
     smalls = [unpack(whole), unpack(a_first), unpack(b_second)]
     products(source, targets, factor, smalls, scaled, table)
 
@@ -220,9 +227,11 @@
 def far_kernel(
     factor, source, far_a, far_b, sibling_a, sibling_b, near, scaled, table, targets
 ):
-    half = targets.shape[0] // 4
-    for k, piece in enumerate((far_a, far_b, sibling_a, sibling_b)):
-        targets[k * half : (k + 1) * half, :] = piece[0:half, :]
+    width = targets.shape[0] // 2
+    rest_rows = far_b.shape[0]
+    cut = width - rest_rows
+    fill(targets, 0, (far_a, cut), (far_b, rest_rows))
+    fill(targets, width, (sibling_a, cut), (sibling_b, rest_rows))
     smalls = [unpack(far_a), unpack(sibling_a)]
     products(source, targets, factor, smalls, scaled, table)
 
@@ -328,7 +337,7 @@
     def shards_square(source_embed, target_embed, target_init, source_logw, target_logw):
         rows, depth = source_embed.shape
         width = target_embed.shape[0]
-        half = width // 2
+        cut = width // 2
         factor = inverse_eps * LOG2E / math.sqrt(depth)
         vmem, hbm = pl.BlockSpec(memory_space=pltpu.VMEM), pl.BlockSpec(memory_space=pltpu.HBM)
         params = pltpu.CompilerParams(vmem_limit_bytes=16 * 1024 * 1024)
@@ -364,12 +373,12 @@
         first, second, whole, small, first_plain, second_plain = pl.pallas_call(
             head_kernel,
             out_shape=(
-                block_of(half + SPARE),
-                block_of(half + SPARE),
+                block_of(cut + SPARE),
+                block_of(width - cut + SPARE),
                 block_of(width + SPARE),
                 values(2, width),
-                block_of(half),
-                block_of(half),
+                block_of(cut),
+                block_of(width - cut),
             ),
             in_specs=[hbm] * 3,
             out_specs=(vmem,) * 6,
@@ -385,7 +394,7 @@
         a_second = along(second_plain, 0)
         b_first = along(first_plain, 1)
         far_a = along(a_first, 1)
-        far_b = along(b_second[:half], 0)
+        far_b = along(b_second[: width - cut], 0)
         source, logw, passed = pl.pallas_call(
             source_kernel,
             out_shape=(

time: 41.2 us -> 41.2 us (level)
  no operation moved by 1% of the time
where the time goes in v12:
time: 41.2 us; the launch traced here: 41 us
  blocking collectives  21.6 us (52%)
  starting transfers between devices  9.26 us (22%)
  Pallas kernels  6.72 us (16%)
  waiting for transfers between devices  2.7 us (7%)
  between operations  0.76 us (2%)
    all_to_all x2, blocking collectives, exchange(): lax.all_to_all(message, ('blk', 'grp'), 0, 0, axis_index_groups=[order])  21.6 us
    ppermute x6, starting transfers between devices, along(): lax.ppermute(array, 'blk', [(i ^ neighbour_step(i, turn), i) for i in ran...  8.56 us
    ppermute x6, waiting for transfers between devices, along(): lax.ppermute(array, 'blk', [(i ^ neighbour_step(i, turn), i) for i in ran...  2 us
    pallas_call x3, Pallas kernels, scores_of(): pl.pallas_call(functools.partial(kernel, factor), out_shape=(values(rows,...  1.87 us
    pallas_call x1, Pallas kernels, shards_square(): pl.pallas_call(source_kernel, out_shape=(jax.ShapeDtypeStruct((rows, dept...  1.4 us
    pallas_call x1, Pallas kernels, shards_square(): pl.pallas_call(functools.partial(second_kernel, grp), out_shape=(values(1...  1.07 us
    pallas_call x1, Pallas kernels, shards_square(): pl.pallas_call(head_kernel, out_shape=(block_of(cut + SPARE), block_of(wi...  0.99 us
  transfers between devices with their start and end apart: 9, of which 4 were waited for; matrix products, arithmetic and copies ran while one was open for 0% of the time, Pallas kernels for 7%

profile of v12, /device:TPU:0, one launch (start us, length us, event | category | flops | bytes accessed | tf_op | source)
XLA Modules:
  0.0 41.0 jit_solution(2321792199978164832)
XLA Ops:
  0.6 1.0 %shard_map.68 = (bf16[72,768]{1,0:T(8,128)(2,1)S(1)}, bf16[72,768]{1,0:T(8,128)(2,1)S(1)}, bf16[136,768]{1,0:T(8,128)(2,1)S(1)}, f32[2,128]{1,0:T(2,128)S(1)}, b...) custom-call(bf16[128,768]{1,0:T(8,128)(2,1)} %own.1, f32[1,128]{1,0:T(1,128)} %bitcast.12, f32[1,128]{1,0:T(1,128)} %bitcast.13), custom_call_target="tpu_custom_call" | custom-call | tf_op jit(solution)/shard_map/pallas_call | solution.py:373
  1.6 3.0 %collective-permute-start = (bf16[72,768]{1,0:T(8,128)(2,1)S(1)}, bf16[72,768]{1,0:T(8,128)(2,1)S(1)}, u32[]{:S(2)}, u32[]{:S(2)}) collective-permute-start(bf16[72,768]{1,0:T(8,128)(2,1)S(1)} %get-tuple-element.24), channel_id=1, source_target_pairs={{8,0},{20,4},{0,8},{28,12},{24,16},{4,20},{16,24},{12,28},{9,1},{2... | collective-permute-start | bytes 331784 | tf_op jit(solution)/shard_map/ppermute | solution.py:356
  4.6 1.5 %collective-permute-start.3 = (bf16[72,768]{1,0:T(8,128)(2,1)S(1)}, bf16[72,768]{1,0:T(8,128)(2,1)S(1)}, u32[]{:S(2)}, u32[]{:S(2)}) collective-permute-start(bf16[72,768]{1,0:T(8,128)(2,1)S(1)} %get-tuple-element.27), channel_id=1, source_target_pairs={{16,0},{12,4},{24,8},{4,12},{0,16},{28,20},{8,24},{20,28},{17,1},{... | collective-permute-start | bytes 331784 | tf_op jit(solution)/shard_map/ppermute | solution.py:356
  6.2 0.5 %collective-permute-start.1 = (bf16[64,768]{1,0:T(8,128)(2,1)S(1)}, bf16[64,768]{1,0:T(8,128)(2,1)S(1)}, u32[]{:S(2)}, u32[]{:S(2)}) collective-permute-start(bf16[64,768]{1,0:T(8,128)(2,1)S(1)} %get-tuple-element.25), channel_id=1, source_target_pairs={{8,0},{20,4},{0,8},{28,12},{24,16},{4,20},{16,24},{12,28},{9,1},{2... | collective-permute-start | bytes 294920 | tf_op jit(solution)/shard_map/ppermute | solution.py:356
  6.7 0.1 collective-permute-start.2
  6.7 1.2 %collective-permute-done.a_first = bf16[72,768]{1,0:T(8,128)(2,1)S(1)} collective-permute-done((bf16[72,768]{1,0:T(8,128)(2,1)S(1)}, bf16[72,768]{1,0:T(8,128)(2,1)S(1)}, u32[]{:S(2)}, u32[]{:S(2)}) %collective-permute-start) | collective-permute-done | bytes 110624 | tf_op jit(solution)/shard_map/ppermute | solution.py:356
  8.0 1.6 %collective-permute-start.5 = (bf16[72,768]{1,0:T(8,128)(2,1)S(1)}, bf16[72,768]{1,0:T(8,128)(2,1)S(1)}, u32[]{:S(2)}, u32[]{:S(2)}) collective-permute-start(bf16[72,768]{1,0:T(8,128)(2,1)S(1)} %collective-permute-done.a_first), channel_id=1, source_target_pairs={{16,0},{12,4},{24,8},{4,12},{0,16},{28,20},{8,24},{20,28},{17,1},{... | collective-permute-start | bytes 331784 | tf_op jit(solution)/shard_map/ppermute | solution.py:356
  9.6 0.7 %collective-permute-done.3.b_second = bf16[72,768]{1,0:T(8,128)(2,1)S(1)} collective-permute-done((bf16[72,768]{1,0:T(8,128)(2,1)S(1)}, bf16[72,768]{1,0:T(8,128)(2,1)S(1)}, u32[]{:S(2)}, u32[]{:S(2)}) %collective-permute-start.3) | collective-permute-done | bytes 110624 | tf_op jit(solution)/shard_map/ppermute | solution.py:356
  10.3 1.9 %collective-permute-start.6 = (bf16[64,768]{1,0:T(8,128)(2,1)S(1)}, bf16[64,768]{1,0:T(8,128)(2,1)S(1)}, u32[]{:S(2)}, u32[]{:S(2)}) collective-permute-start(bf16[64,768]{1,0:T(8,128)(2,1)S(1)} %slice.4), channel_id=1, source_target_pairs={{8,0},{20,4},{0,8},{28,12},{24,16},{4,20},{16,24},{12,28},{9,1},{2... | collective-permute-start | bytes 294920 | tf_op jit(solution)/shard_map/ppermute | solution.py:356
  12.1 1.4 %shard_map.69 = (bf16[512,768]{1,0:T(8,128)(2,1)S(1)}, f32[512,128]{1,0:T(8,128)S(1)}, bf16[136,768]{1,0:T(8,128)(2,1)S(1)}) custom-call(bf16[512,768]{1,0:T(8,128)(2,1)} %source.1, f32[1,512]{1,0:T(1,128)} %bitcast.11, bf16[136,768]{1,0:T(8,128)(2,1)S(1)} %get-tuple-element.22.whole), custom_call_target="tpu_custom_call" | custom-call | tf_op jit(solution)/shard_map/pallas_call | solution.py:398
  13.5 0.0 collective-permute-done.1.a_second
  13.5 0.0 collective-permute-done.2.b_first
  13.6 0.1 collective-permute-start.4
  13.7 0.6 %shard_map.70 = (f32[512,384]{1,0:T(8,128)S(1)}, f32[2,8,128]{2,1,0:T(8,128)S(1)}) custom-call(bf16[512,768]{1,0:T(8,128)(2,1)S(1)} %get-tuple-element.23.source, bf16[136,768]{1,0:T(8,128)(2,1)S(1)} %get-tuple-element.22.whole, bf16[72,768]{1,0:T(8,128)(2,1)S(1)} %collective-permute-done.a_first, bf16[64,768]{1,0:T(8,128)(2,1)S(1)} %collective-permute-done.1.a_second, ...), custom_call_target="tpu_custom_call" | custom-call | bytes 786432 | tf_op jit(solution)/shard_map/pallas_call | solution.py:425
  14.3 0.0 collective-permute-done.5.message.far_a
  14.3 0.6 %collective-permute-start.7 = (bf16[72,768]{1,0:T(8,128)(2,1)S(1)}, bf16[72,768]{1,0:T(8,128)(2,1)S(1)}, u32[]{:S(2)}, u32[]{:S(2)}) collective-permute-start(bf16[72,768]{1,0:T(8,128)(2,1)S(1)} %shard_map.73), channel_id=1, source_target_pairs={{4,0},{0,4},{12,8},{8,12},{20,16},{16,20},{28,24},{24,28},{5,1},{1... | collective-permute-start | bytes 331784 | tf_op jit(solution)/shard_map/ppermute | solution.py:22
  14.9 0.1 collective-permute-done.6.message.far_b
  15.0 0.1 collective-permute-start.8
  15.0 0.7 %collective-permute-done.4.sibling = bf16[408,768]{1,0:T(8,128)(2,1)S(1)} collective-permute-done((bf16[408,768]{1,0:T(8,128)(2,1)S(1)}, bf16[408,768]{1,0:T(8,128)(2,1)S(1)}, u32[]{:S(2)}, u32[]{:S(2)}) %collective-permute-start.4) | collective-permute-done | bytes 626720 | tf_op jit(solution)/shard_map/ppermute | solution.py:22
  15.7 0.9 %shard_map.72 = (f32[512,384]{1,0:T(8,128)S(1)}, f32[2,8,128]{2,1,0:T(8,128)S(1)}, f32[512,128]{1,0:T(8,128)S(1)}) custom-call(bf16[512,768]{1,0:T(8,128)(2,1)S(1)} %get-tuple-element.23.source, bf16[408,768]{1,0:T(8,128)(2,1)S(1)} %collective-permute-done.4.sibling, f32[512,384]{1,0:T(8,128)S(1)} %get-tuple-element.28.own), custom_call_target="tpu_custom_call" | custom-call | bytes 786432 | tf_op jit(solution)/shard_map/pallas_call | solution.py:425
  16.6 0.0 collective-permute-done.8.sibling_b
  16.6 0.0 collective-permute-done.7.sibling_a
  16.6 0.4 shard_map.75
  17.0 0.8 %shard_map.76 = f32[32,8,128]{2,1,0:T(8,128)S(1)} custom-call(f32[512,384]{1,0:T(8,128)S(1)} %get-tuple-element.28.own, f32[2,8,128]{2,1,0:T(8,128)S(1)} %get-tuple-element.29.tie.own_table, f32[512,384]{1,0:T(8,128)S(1)} %get-tuple-element.31.near.sibling, f32[2,8,128]{2,1,0:T(8,128)S(1)} %get-tuple-element.32.sibling_table, ...), custom_call_target="tpu_custom_call" | custom-call | flops 8388608 | bytes 786432 | tf_op jit(solution)/shard_map/pallas_call | solution.py:456
  17.8 12.6 %all_to_all.16.got = f32[32,8,128]{2,1,0:T(8,128)S(1)} all-to-all(f32[32,8,128]{2,1,0:T(8,128)S(1)} %shard_map.76), channel_id=1, replica_groups={{31,30,29,28,27,26,25,24,23,22,21,20,19,18,17,16,15,14,13,12,11,10,9,8,..., dimensions={0} | all-to-all | bytes 262144 | tf_op jit(solution)/shard_map/all_to_all | solution.py:365
  30.3 1.1 %shard_map.77 = (f32[1,512]{1,0:T(1,128)S(1)}, f32[32,128]{1,0:T(8,128)S(1)}) custom-call(f32[512,384]{1,0:T(8,128)S(1)} %get-tuple-element.28.own, f32[2,8,128]{2,1,0:T(8,128)S(1)} %get-tuple-element.29.tie.own_table, f32[512,384]{1,0:T(8,128)S(1)} %get-tuple-element.31.near.sibling, f32[2,8,128]{2,1,0:T(8,128)S(1)} %get-tuple-element.32.sibling_table, ...), custom_call_target="tpu_custom_call" | custom-call | flops 8388608 | bytes 786432 | tf_op jit(solution)/shard_map/pallas_call | solution.py:466
  31.4 9.0 %all_to_all.17 = f32[32,1,128]{2,1,0:T(1,128)S(1)} all-to-all(f32[32,1,128]{2,1,0:T(1,128)S(1)} %bitcast.10), channel_id=1, replica_groups={{31,30,29,28,27,26,25,24,23,22,21,20,19,18,17,16,15,14,13,12,11,10,9,8,..., dimensions={0} | all-to-all | bytes 32768 | tf_op jit(solution)/shard_map/all_to_all | solution.py:365
  40.5 0.6 %shard_map.78 = (f32[1,512]{1,0:T(1,128)}, f32[1,128]{1,0:T(1,128)}) custom-call(f32[32,128]{1,0:T(8,128)S(1)} %bitcast.9, f32[2,128]{1,0:T(2,128)S(1)} %get-tuple-element.38.small, f32[1,512]{1,0:T(1,128)S(1)} %get-tuple-element.39.row), custom_call_target="tpu_custom_call" | custom-call | tf_op jit(solution)/shard_map/pallas_call | solution.py:476
  (4 shorter events, 0.1 us)
Async XLA Ops:
  1.6 6.3 %collective-permute-start = (bf16[72,768]{1,0:T(8,128)(2,1)S(1)}, bf16[72,768]{1,0:T(8,128)(2,1)S(1)}, u32[]{:S(2)}, u32[]{:S(2)}) collective-permute-start(bf16[72,768]{1,0:T(8,128)(2,1)S(1)} %get-tuple-element.24), channel_id=1, source_target_pairs={{8,0},{20,4},{0,8},{28,12},{24,16},{4,20},{16,24},{12,28},{9,1},{2... | collective-permute-start | bytes 331784 | tf_op jit(solution)/shard_map/ppermute | solution.py:356
  4.6 5.6 %collective-permute-start.3 = (bf16[72,768]{1,0:T(8,128)(2,1)S(1)}, bf16[72,768]{1,0:T(8,128)(2,1)S(1)}, u32[]{:S(2)}, u32[]{:S(2)}) collective-permute-start(bf16[72,768]{1,0:T(8,128)(2,1)S(1)} %get-tuple-element.27), channel_id=1, source_target_pairs={{16,0},{12,4},{24,8},{4,12},{0,16},{28,20},{8,24},{20,28},{17,1},{... | collective-permute-start | bytes 331784 | tf_op jit(solution)/shard_map/ppermute | solution.py:356
  6.2 7.4 %collective-permute-start.1 = (bf16[64,768]{1,0:T(8,128)(2,1)S(1)}, bf16[64,768]{1,0:T(8,128)(2,1)S(1)}, u32[]{:S(2)}, u32[]{:S(2)}) collective-permute-start(bf16[64,768]{1,0:T(8,128)(2,1)S(1)} %get-tuple-element.25), channel_id=1, source_target_pairs={{8,0},{20,4},{0,8},{28,12},{24,16},{4,20},{16,24},{12,28},{9,1},{2... | collective-permute-start | bytes 294920 | tf_op jit(solution)/shard_map/ppermute | solution.py:356
  6.7 6.9 %collective-permute-start.2 = (bf16[64,768]{1,0:T(8,128)(2,1)S(1)}, bf16[64,768]{1,0:T(8,128)(2,1)S(1)}, u32[]{:S(2)}, u32[]{:S(2)}) collective-permute-start(bf16[64,768]{1,0:T(8,128)(2,1)S(1)} %get-tuple-element.26), channel_id=1, source_target_pairs={{16,0},{12,4},{24,8},{4,12},{0,16},{28,20},{8,24},{20,28},{17,1},{... | collective-permute-start | bytes 294920 | tf_op jit(solution)/shard_map/ppermute | solution.py:356
  8.0 6.3 %collective-permute-start.5 = (bf16[72,768]{1,0:T(8,128)(2,1)S(1)}, bf16[72,768]{1,0:T(8,128)(2,1)S(1)}, u32[]{:S(2)}, u32[]{:S(2)}) collective-permute-start(bf16[72,768]{1,0:T(8,128)(2,1)S(1)} %collective-permute-done.a_first), channel_id=1, source_target_pairs={{16,0},{12,4},{24,8},{4,12},{0,16},{28,20},{8,24},{20,28},{17,1},{... | collective-permute-start | bytes 331784 | tf_op jit(solution)/shard_map/ppermute | solution.py:356
  10.3 4.7 %collective-permute-start.6 = (bf16[64,768]{1,0:T(8,128)(2,1)S(1)}, bf16[64,768]{1,0:T(8,128)(2,1)S(1)}, u32[]{:S(2)}, u32[]{:S(2)}) collective-permute-start(bf16[64,768]{1,0:T(8,128)(2,1)S(1)} %slice.4), channel_id=1, source_target_pairs={{8,0},{20,4},{0,8},{28,12},{24,16},{4,20},{16,24},{12,28},{9,1},{2... | collective-permute-start | bytes 294920 | tf_op jit(solution)/shard_map/ppermute | solution.py:356
  13.6 2.1 %collective-permute-start.4 = (bf16[408,768]{1,0:T(8,128)(2,1)S(1)}, bf16[408,768]{1,0:T(8,128)(2,1)S(1)}, u32[]{:S(2)}, u32[]{:S(2)}) collective-permute-start(bf16[408,768]{1,0:T(8,128)(2,1)S(1)} %shard_map.71), channel_id=1, source_target_pairs={{4,0},{0,4},{12,8},{8,12},{20,16},{16,20},{28,24},{24,28},{5,1},{1... | collective-permute-start | bytes 1880072 | tf_op jit(solution)/shard_map/ppermute | solution.py:22
  14.3 2.3 %collective-permute-start.7 = (bf16[72,768]{1,0:T(8,128)(2,1)S(1)}, bf16[72,768]{1,0:T(8,128)(2,1)S(1)}, u32[]{:S(2)}, u32[]{:S(2)}) collective-permute-start(bf16[72,768]{1,0:T(8,128)(2,1)S(1)} %shard_map.73), channel_id=1, source_target_pairs={{4,0},{0,4},{12,8},{8,12},{20,16},{16,20},{28,24},{24,28},{5,1},{1... | collective-permute-start | bytes 331784 | tf_op jit(solution)/shard_map/ppermute | solution.py:22
  15.0 1.6 %collective-permute-start.8 = (bf16[64,768]{1,0:T(8,128)(2,1)S(1)}, bf16[64,768]{1,0:T(8,128)(2,1)S(1)}, u32[]{:S(2)}, u32[]{:S(2)}) collective-permute-start(bf16[64,768]{1,0:T(8,128)(2,1)S(1)} %shard_map.74), channel_id=1, source_target_pairs={{4,0},{0,4},{12,8},{8,12},{20,16},{16,20},{28,24},{24,28},{5,1},{1... | collective-permute-start | bytes 294920 | tf_op jit(solution)/shard_map/ppermute | solution.py:22

commit v13 on v10

--- a/solution.py
+++ b/solution.py
@@ -353,7 +353,9 @@
 
         def exchange(message):
             order = list(range(blk * grp))[::-1]
-            return lax.all_to_all(message, ("blk", "grp"), 0, 0, axis_index_groups=[order])
+            flat = message.reshape(blk * grp, 1, -1)
+            got = lax.all_to_all(flat, ("blk", "grp"), 0, 0, axis_index_groups=[order])
+            return got.reshape(message.shape)
 
         def block_of(size):
             return jax.ShapeDtypeStruct((size, depth), target_embed.dtype)

time: 41.2 us -> 41.2 us (level)
  no operation moved by 1% of the time
where the time goes in v13:
time: 41.2 us; the launch traced here: 41 us
  blocking collectives  21.6 us (52%)
  starting transfers between devices  9.26 us (22%)
  Pallas kernels  6.7 us (16%)
  waiting for transfers between devices  2.7 us (7%)
  between operations  0.76 us (2%)
    all_to_all x2, blocking collectives, exchange(): got = lax.all_to_all(flat, ('blk', 'grp'), 0, 0, axis_index_groups=[order])  21.6 us
    ppermute x6, starting transfers between devices, along(): lax.ppermute(array, 'blk', [(i ^ neighbour_step(i, turn), i) for i in ran...  8.56 us
    ppermute x6, waiting for transfers between devices, along(): lax.ppermute(array, 'blk', [(i ^ neighbour_step(i, turn), i) for i in ran...  2 us
    pallas_call x3, Pallas kernels, scores_of(): pl.pallas_call(functools.partial(kernel, factor), out_shape=(values(rows,...  1.87 us
    pallas_call x1, Pallas kernels, shards_square(): pl.pallas_call(source_kernel, out_shape=(jax.ShapeDtypeStruct((rows, dept...  1.4 us
    pallas_call x1, Pallas kernels, shards_square(): pl.pallas_call(functools.partial(second_kernel, grp), out_shape=(values(1...  1.07 us
    pallas_call x1, Pallas kernels, shards_square(): pl.pallas_call(head_kernel, out_shape=(block_of(half + SPARE), block_of(h...  0.99 us
  transfers between devices with their start and end apart: 9, of which 4 were waited for; matrix products, arithmetic and copies ran while one was open for 0% of the time, Pallas kernels for 7%

profile of v13, /device:TPU:0, one launch (start us, length us, event | category | flops | bytes accessed | tf_op | source)
XLA Modules:
  0.0 41.0 jit_solution(2610193660305304916)
XLA Ops:
  0.6 1.0 %shard_map.68 = (bf16[72,768]{1,0:T(8,128)(2,1)S(1)}, bf16[72,768]{1,0:T(8,128)(2,1)S(1)}, bf16[136,768]{1,0:T(8,128)(2,1)S(1)}, f32[2,128]{1,0:T(2,128)S(1)}, b...) custom-call(bf16[128,768]{1,0:T(8,128)(2,1)} %own.1, f32[1,128]{1,0:T(1,128)} %bitcast.16, f32[1,128]{1,0:T(1,128)} %bitcast.17), custom_call_target="tpu_custom_call" | custom-call | tf_op jit(solution)/shard_map/pallas_call | solution.py:366
  1.6 3.0 %collective-permute-start = (bf16[72,768]{1,0:T(8,128)(2,1)S(1)}, bf16[72,768]{1,0:T(8,128)(2,1)S(1)}, u32[]{:S(2)}, u32[]{:S(2)}) collective-permute-start(bf16[72,768]{1,0:T(8,128)(2,1)S(1)} %get-tuple-element.24), channel_id=1, source_target_pairs={{8,0},{20,4},{0,8},{28,12},{24,16},{4,20},{16,24},{12,28},{9,1},{2... | collective-permute-start | bytes 331784 | tf_op jit(solution)/shard_map/ppermute | solution.py:347
  4.6 1.5 %collective-permute-start.3 = (bf16[72,768]{1,0:T(8,128)(2,1)S(1)}, bf16[72,768]{1,0:T(8,128)(2,1)S(1)}, u32[]{:S(2)}, u32[]{:S(2)}) collective-permute-start(bf16[72,768]{1,0:T(8,128)(2,1)S(1)} %get-tuple-element.27), channel_id=1, source_target_pairs={{16,0},{12,4},{24,8},{4,12},{0,16},{28,20},{8,24},{20,28},{17,1},{... | collective-permute-start | bytes 331784 | tf_op jit(solution)/shard_map/ppermute | solution.py:347
  6.2 0.5 %collective-permute-start.1 = (bf16[64,768]{1,0:T(8,128)(2,1)S(1)}, bf16[64,768]{1,0:T(8,128)(2,1)S(1)}, u32[]{:S(2)}, u32[]{:S(2)}) collective-permute-start(bf16[64,768]{1,0:T(8,128)(2,1)S(1)} %get-tuple-element.25), channel_id=1, source_target_pairs={{8,0},{20,4},{0,8},{28,12},{24,16},{4,20},{16,24},{12,28},{9,1},{2... | collective-permute-start | bytes 294920 | tf_op jit(solution)/shard_map/ppermute | solution.py:347
  6.7 0.1 collective-permute-start.2
  6.7 1.2 %collective-permute-done.a_first = bf16[72,768]{1,0:T(8,128)(2,1)S(1)} collective-permute-done((bf16[72,768]{1,0:T(8,128)(2,1)S(1)}, bf16[72,768]{1,0:T(8,128)(2,1)S(1)}, u32[]{:S(2)}, u32[]{:S(2)}) %collective-permute-start) | collective-permute-done | bytes 110624 | tf_op jit(solution)/shard_map/ppermute | solution.py:347
  8.0 1.6 %collective-permute-start.5 = (bf16[72,768]{1,0:T(8,128)(2,1)S(1)}, bf16[72,768]{1,0:T(8,128)(2,1)S(1)}, u32[]{:S(2)}, u32[]{:S(2)}) collective-permute-start(bf16[72,768]{1,0:T(8,128)(2,1)S(1)} %collective-permute-done.a_first), channel_id=1, source_target_pairs={{16,0},{12,4},{24,8},{4,12},{0,16},{28,20},{8,24},{20,28},{17,1},{... | collective-permute-start | bytes 331784 | tf_op jit(solution)/shard_map/ppermute | solution.py:347
  9.6 0.7 %collective-permute-done.3.b_second = bf16[72,768]{1,0:T(8,128)(2,1)S(1)} collective-permute-done((bf16[72,768]{1,0:T(8,128)(2,1)S(1)}, bf16[72,768]{1,0:T(8,128)(2,1)S(1)}, u32[]{:S(2)}, u32[]{:S(2)}) %collective-permute-start.3) | collective-permute-done | bytes 110624 | tf_op jit(solution)/shard_map/ppermute | solution.py:347
  10.3 1.9 %collective-permute-start.6 = (bf16[64,768]{1,0:T(8,128)(2,1)S(1)}, bf16[64,768]{1,0:T(8,128)(2,1)S(1)}, u32[]{:S(2)}, u32[]{:S(2)}) collective-permute-start(bf16[64,768]{1,0:T(8,128)(2,1)S(1)} %slice.4), channel_id=1, source_target_pairs={{8,0},{20,4},{0,8},{28,12},{24,16},{4,20},{16,24},{12,28},{9,1},{2... | collective-permute-start | bytes 294920 | tf_op jit(solution)/shard_map/ppermute | solution.py:347
  12.1 1.4 %shard_map.69 = (bf16[512,768]{1,0:T(8,128)(2,1)S(1)}, f32[512,128]{1,0:T(8,128)S(1)}, bf16[136,768]{1,0:T(8,128)(2,1)S(1)}) custom-call(bf16[512,768]{1,0:T(8,128)(2,1)} %source.1, f32[1,512]{1,0:T(1,128)} %bitcast.15, bf16[136,768]{1,0:T(8,128)(2,1)S(1)} %get-tuple-element.22.whole), custom_call_target="tpu_custom_call" | custom-call | tf_op jit(solution)/shard_map/pallas_call | solution.py:391
  13.5 0.0 collective-permute-done.1.a_second
  13.5 0.0 collective-permute-done.2.b_first
  13.6 0.1 collective-permute-start.4
  13.7 0.6 %shard_map.70 = (f32[512,384]{1,0:T(8,128)S(1)}, f32[2,8,128]{2,1,0:T(8,128)S(1)}) custom-call(bf16[512,768]{1,0:T(8,128)(2,1)S(1)} %get-tuple-element.23.source, bf16[136,768]{1,0:T(8,128)(2,1)S(1)} %get-tuple-element.22.whole, bf16[72,768]{1,0:T(8,128)(2,1)S(1)} %collective-permute-done.a_first, bf16[64,768]{1,0:T(8,128)(2,1)S(1)} %collective-permute-done.1.a_second, ...), custom_call_target="tpu_custom_call" | custom-call | bytes 786432 | tf_op jit(solution)/shard_map/pallas_call | solution.py:418
  14.3 0.0 collective-permute-done.5.message.far_a
  14.3 0.6 %collective-permute-start.7 = (bf16[72,768]{1,0:T(8,128)(2,1)S(1)}, bf16[72,768]{1,0:T(8,128)(2,1)S(1)}, u32[]{:S(2)}, u32[]{:S(2)}) collective-permute-start(bf16[72,768]{1,0:T(8,128)(2,1)S(1)} %shard_map.73), channel_id=1, source_target_pairs={{4,0},{0,4},{12,8},{8,12},{20,16},{16,20},{28,24},{24,28},{5,1},{1... | collective-permute-start | bytes 331784 | tf_op jit(solution)/shard_map/ppermute | solution.py:22
  14.9 0.1 collective-permute-done.6.message.far_b
  15.0 0.1 collective-permute-start.8
  15.0 0.7 %collective-permute-done.4.sibling = bf16[408,768]{1,0:T(8,128)(2,1)S(1)} collective-permute-done((bf16[408,768]{1,0:T(8,128)(2,1)S(1)}, bf16[408,768]{1,0:T(8,128)(2,1)S(1)}, u32[]{:S(2)}, u32[]{:S(2)}) %collective-permute-start.4) | collective-permute-done | bytes 626720 | tf_op jit(solution)/shard_map/ppermute | solution.py:22
  15.7 0.9 %shard_map.72 = (f32[512,384]{1,0:T(8,128)S(1)}, f32[2,8,128]{2,1,0:T(8,128)S(1)}, f32[512,128]{1,0:T(8,128)S(1)}) custom-call(bf16[512,768]{1,0:T(8,128)(2,1)S(1)} %get-tuple-element.23.source, bf16[408,768]{1,0:T(8,128)(2,1)S(1)} %collective-permute-done.4.sibling, f32[512,384]{1,0:T(8,128)S(1)} %get-tuple-element.28.own), custom_call_target="tpu_custom_call" | custom-call | bytes 786432 | tf_op jit(solution)/shard_map/pallas_call | solution.py:418
  16.6 0.0 collective-permute-done.8.sibling_b
  16.6 0.0 collective-permute-done.7.sibling_a
  16.6 0.4 shard_map.75
  17.0 0.7 %shard_map.76 = f32[32,8,128]{2,1,0:T(8,128)S(1)} custom-call(f32[512,384]{1,0:T(8,128)S(1)} %get-tuple-element.28.own, f32[2,8,128]{2,1,0:T(8,128)S(1)} %get-tuple-element.29.tie.own_table, f32[512,384]{1,0:T(8,128)S(1)} %get-tuple-element.31.near.sibling, f32[2,8,128]{2,1,0:T(8,128)S(1)} %get-tuple-element.32.sibling_table, ...), custom_call_target="tpu_custom_call" | custom-call | flops 8388608 | bytes 786432 | tf_op jit(solution)/shard_map/pallas_call | solution.py:449
  17.8 12.6 %all_to_all.10 = f32[32,1,1024]{2,1,0:T(1,128)S(1)} all-to-all(f32[32,1,1024]{2,1,0:T(1,128)S(1)} %bitcast.12), channel_id=1, replica_groups={{31,30,29,28,27,26,25,24,23,22,21,20,19,18,17,16,15,14,13,12,11,10,9,8,..., dimensions={0} | all-to-all | bytes 262144 | tf_op jit(solution)/shard_map/all_to_all | solution.py:357
  30.3 1.1 %shard_map.77 = (f32[1,512]{1,0:T(1,128)S(1)}, f32[32,128]{1,0:T(8,128)S(1)}) custom-call(f32[512,384]{1,0:T(8,128)S(1)} %get-tuple-element.28.own, f32[2,8,128]{2,1,0:T(8,128)S(1)} %get-tuple-element.29.tie.own_table, f32[512,384]{1,0:T(8,128)S(1)} %get-tuple-element.31.near.sibling, f32[2,8,128]{2,1,0:T(8,128)S(1)} %get-tuple-element.32.sibling_table, ...), custom_call_target="tpu_custom_call" | custom-call | flops 8388608 | bytes 786432 | tf_op jit(solution)/shard_map/pallas_call | solution.py:459
  31.4 9.0 %all_to_all.11 = f32[32,1,128]{2,1,0:T(1,128)S(1)} all-to-all(f32[32,1,128]{2,1,0:T(1,128)S(1)} %bitcast.14), channel_id=1, replica_groups={{31,30,29,28,27,26,25,24,23,22,21,20,19,18,17,16,15,14,13,12,11,10,9,8,..., dimensions={0} | all-to-all | bytes 32768 | tf_op jit(solution)/shard_map/all_to_all | solution.py:357
  40.4 0.6 %shard_map.78 = (f32[1,512]{1,0:T(1,128)}, f32[1,128]{1,0:T(1,128)}) custom-call(f32[32,128]{1,0:T(8,128)S(1)} %bitcast.13, f32[2,128]{1,0:T(2,128)S(1)} %get-tuple-element.38.small, f32[1,512]{1,0:T(1,128)S(1)} %get-tuple-element.39.row), custom_call_target="tpu_custom_call" | custom-call | tf_op jit(solution)/shard_map/pallas_call | solution.py:469
  (4 shorter events, 0.1 us)
Async XLA Ops:
  1.6 6.3 %collective-permute-start = (bf16[72,768]{1,0:T(8,128)(2,1)S(1)}, bf16[72,768]{1,0:T(8,128)(2,1)S(1)}, u32[]{:S(2)}, u32[]{:S(2)}) collective-permute-start(bf16[72,768]{1,0:T(8,128)(2,1)S(1)} %get-tuple-element.24), channel_id=1, source_target_pairs={{8,0},{20,4},{0,8},{28,12},{24,16},{4,20},{16,24},{12,28},{9,1},{2... | collective-permute-start | bytes 331784 | tf_op jit(solution)/shard_map/ppermute | solution.py:347
  4.6 5.6 %collective-permute-start.3 = (bf16[72,768]{1,0:T(8,128)(2,1)S(1)}, bf16[72,768]{1,0:T(8,128)(2,1)S(1)}, u32[]{:S(2)}, u32[]{:S(2)}) collective-permute-start(bf16[72,768]{1,0:T(8,128)(2,1)S(1)} %get-tuple-element.27), channel_id=1, source_target_pairs={{16,0},{12,4},{24,8},{4,12},{0,16},{28,20},{8,24},{20,28},{17,1},{... | collective-permute-start | bytes 331784 | tf_op jit(solution)/shard_map/ppermute | solution.py:347
  6.2 7.4 %collective-permute-start.1 = (bf16[64,768]{1,0:T(8,128)(2,1)S(1)}, bf16[64,768]{1,0:T(8,128)(2,1)S(1)}, u32[]{:S(2)}, u32[]{:S(2)}) collective-permute-start(bf16[64,768]{1,0:T(8,128)(2,1)S(1)} %get-tuple-element.25), channel_id=1, source_target_pairs={{8,0},{20,4},{0,8},{28,12},{24,16},{4,20},{16,24},{12,28},{9,1},{2... | collective-permute-start | bytes 294920 | tf_op jit(solution)/shard_map/ppermute | solution.py:347
  6.7 6.9 %collective-permute-start.2 = (bf16[64,768]{1,0:T(8,128)(2,1)S(1)}, bf16[64,768]{1,0:T(8,128)(2,1)S(1)}, u32[]{:S(2)}, u32[]{:S(2)}) collective-permute-start(bf16[64,768]{1,0:T(8,128)(2,1)S(1)} %get-tuple-element.26), channel_id=1, source_target_pairs={{16,0},{12,4},{24,8},{4,12},{0,16},{28,20},{8,24},{20,28},{17,1},{... | collective-permute-start | bytes 294920 | tf_op jit(solution)/shard_map/ppermute | solution.py:347
  8.0 6.3 %collective-permute-start.5 = (bf16[72,768]{1,0:T(8,128)(2,1)S(1)}, bf16[72,768]{1,0:T(8,128)(2,1)S(1)}, u32[]{:S(2)}, u32[]{:S(2)}) collective-permute-start(bf16[72,768]{1,0:T(8,128)(2,1)S(1)} %collective-permute-done.a_first), channel_id=1, source_target_pairs={{16,0},{12,4},{24,8},{4,12},{0,16},{28,20},{8,24},{20,28},{17,1},{... | collective-permute-start | bytes 331784 | tf_op jit(solution)/shard_map/ppermute | solution.py:347
  10.3 4.7 %collective-permute-start.6 = (bf16[64,768]{1,0:T(8,128)(2,1)S(1)}, bf16[64,768]{1,0:T(8,128)(2,1)S(1)}, u32[]{:S(2)}, u32[]{:S(2)}) collective-permute-start(bf16[64,768]{1,0:T(8,128)(2,1)S(1)} %slice.4), channel_id=1, source_target_pairs={{8,0},{20,4},{0,8},{28,12},{24,16},{4,20},{16,24},{12,28},{9,1},{2... | collective-permute-start | bytes 294920 | tf_op jit(solution)/shard_map/ppermute | solution.py:347
  13.6 2.1 %collective-permute-start.4 = (bf16[408,768]{1,0:T(8,128)(2,1)S(1)}, bf16[408,768]{1,0:T(8,128)(2,1)S(1)}, u32[]{:S(2)}, u32[]{:S(2)}) collective-permute-start(bf16[408,768]{1,0:T(8,128)(2,1)S(1)} %shard_map.71), channel_id=1, source_target_pairs={{4,0},{0,4},{12,8},{8,12},{20,16},{16,20},{28,24},{24,28},{5,1},{1... | collective-permute-start | bytes 1880072 | tf_op jit(solution)/shard_map/ppermute | solution.py:22
  14.3 2.3 %collective-permute-start.7 = (bf16[72,768]{1,0:T(8,128)(2,1)S(1)}, bf16[72,768]{1,0:T(8,128)(2,1)S(1)}, u32[]{:S(2)}, u32[]{:S(2)}) collective-permute-start(bf16[72,768]{1,0:T(8,128)(2,1)S(1)} %shard_map.73), channel_id=1, source_target_pairs={{4,0},{0,4},{12,8},{8,12},{20,16},{16,20},{28,24},{24,28},{5,1},{1... | collective-permute-start | bytes 331784 | tf_op jit(solution)/shard_map/ppermute | solution.py:22
  15.0 1.6 %collective-permute-start.8 = (bf16[64,768]{1,0:T(8,128)(2,1)S(1)}, bf16[64,768]{1,0:T(8,128)(2,1)S(1)}, u32[]{:S(2)}, u32[]{:S(2)}) collective-permute-start(bf16[64,768]{1,0:T(8,128)(2,1)S(1)} %shard_map.74), channel_id=1, source_target_pairs={{4,0},{0,4},{12,8},{8,12},{20,16},{16,20},{28,24},{24,28},{5,1},{1... | collective-permute-start | bytes 294920 | tf_op jit(solution)/shard_map/ppermute | solution.py:22

commit v14 on v10

--- a/solution.py
+++ b/solution.py
@@ -123,19 +123,22 @@
     logw_row, sems,
 ):
     rows, half = own.shape[0], first_plain.shape[0]
-    copies = [
-        pltpu.make_async_copy(own, whole.at[0:rows], sems.at[0]),
-        pltpu.make_async_copy(init, init_row, sems.at[1]),
-        pltpu.make_async_copy(target_logw, logw_row, sems.at[2]),
+    vectors = [
+        pltpu.make_async_copy(init, init_row, sems.at[0]),
+        pltpu.make_async_copy(target_logw, logw_row, sems.at[1]),
     ]
-    for copy in copies:
+    upper, lower = own.at[0:half], own.at[half:rows]
+    blocks = [
+        pltpu.make_async_copy(upper, first.at[0:half], sems.at[2]),
+        pltpu.make_async_copy(lower, second.at[0:half], sems.at[3]),
+        pltpu.make_async_copy(upper, first_plain, sems.at[4]),
+        pltpu.make_async_copy(lower, second_plain, sems.at[5]),
+        pltpu.make_async_copy(own, whole.at[0:rows], sems.at[6]),
+    ]
+    for copy in vectors + blocks:
         copy.start()
-    for copy in copies:
+    for copy in vectors:
         copy.wait()
-    for out in (first, first_plain):
-        out[0:half, :] = whole[0:half, :]
-    for out in (second, second_plain):
-        out[0:half, :] = whole[half:rows, :]
     small[0:1, :] = init_row[...]
     small[1:2, :] = logw_row[...]
     filler = jnp.zeros((SPARE - 2, LANES), jnp.float32)
@@ -147,6 +150,8 @@
         second[half:, lanes] = part
         whole[rows:, lanes] = part
         rest = rest - part.astype(jnp.float32)
+    for copy in blocks:
+        copy.wait()
 
 
 def source_kernel(source, logw, whole, held, row_logw, passed, rows_row, sems):
@@ -376,7 +381,7 @@
             scratch_shapes=[
                 pltpu.VMEM((1, width), jnp.float32),
                 pltpu.VMEM((1, width), jnp.float32),
-                pltpu.SemaphoreType.DMA((3,)),
+                pltpu.SemaphoreType.DMA((7,)),
             ],
             compiler_params=params,
         )(*in_hbm(target_embed, target_init.reshape(1, width), target_logw.reshape(1, width)))

time: 41.2 us -> 41.4 us (level)
  no operation moved by 1% of the time
where the time goes in v14:
time: 41.4 us; the launch traced here: 41.2 us
  blocking collectives  21.6 us (52%)
  starting transfers between devices  9.26 us (22%)
  Pallas kernels  6.93 us (17%)
  waiting for transfers between devices  2.69 us (6%)
  between operations  0.76 us (2%)
    all_to_all x2, blocking collectives, exchange(): lax.all_to_all(message, ('blk', 'grp'), 0, 0, axis_index_groups=[order])  21.6 us
    ppermute x6, starting transfers between devices, along(): lax.ppermute(array, 'blk', [(i ^ neighbour_step(i, turn), i) for i in ran...  8.56 us
    ppermute x6, waiting for transfers between devices, along(): lax.ppermute(array, 'blk', [(i ^ neighbour_step(i, turn), i) for i in ran...  2 us
    pallas_call x3, Pallas kernels, scores_of(): pl.pallas_call(functools.partial(kernel, factor), out_shape=(values(rows,...  1.87 us
    pallas_call x1, Pallas kernels, shards_square(): pl.pallas_call(source_kernel, out_shape=(jax.ShapeDtypeStruct((rows, dept...  1.4 us
    pallas_call x1, Pallas kernels, shards_square(): pl.pallas_call(head_kernel, out_shape=(block_of(half + SPARE), block_of(h...  1.21 us
    pallas_call x1, Pallas kernels, shards_square(): pl.pallas_call(functools.partial(second_kernel, grp), out_shape=(values(1...  1.07 us
  transfers between devices with their start and end apart: 9, of which 4 were waited for; matrix products, arithmetic and copies ran while one was open for 0% of the time, Pallas kernels for 7%

profile of v14, /device:TPU:0, one launch (start us, length us, event | category | flops | bytes accessed | tf_op | source)
XLA Modules:
  0.0 41.2 jit_solution(16022114524107856647)
XLA Ops:
  0.6 1.2 %shard_map.68 = (bf16[72,768]{1,0:T(8,128)(2,1)S(1)}, bf16[72,768]{1,0:T(8,128)(2,1)S(1)}, bf16[136,768]{1,0:T(8,128)(2,1)S(1)}, f32[2,128]{1,0:T(2,128)S(1)}, b...) custom-call(bf16[128,768]{1,0:T(8,128)(2,1)} %own.1, f32[1,128]{1,0:T(1,128)} %bitcast.12, f32[1,128]{1,0:T(1,128)} %bitcast.13), custom_call_target="tpu_custom_call" | custom-call | tf_op jit(solution)/shard_map/pallas_call | solution.py:369
  1.8 3.0 %collective-permute-start = (bf16[72,768]{1,0:T(8,128)(2,1)S(1)}, bf16[72,768]{1,0:T(8,128)(2,1)S(1)}, u32[]{:S(2)}, u32[]{:S(2)}) collective-permute-start(bf16[72,768]{1,0:T(8,128)(2,1)S(1)} %get-tuple-element.24), channel_id=1, source_target_pairs={{8,0},{20,4},{0,8},{28,12},{24,16},{4,20},{16,24},{12,28},{9,1},{2... | collective-permute-start | bytes 331784 | tf_op jit(solution)/shard_map/ppermute | solution.py:352
  4.9 1.5 %collective-permute-start.3 = (bf16[72,768]{1,0:T(8,128)(2,1)S(1)}, bf16[72,768]{1,0:T(8,128)(2,1)S(1)}, u32[]{:S(2)}, u32[]{:S(2)}) collective-permute-start(bf16[72,768]{1,0:T(8,128)(2,1)S(1)} %get-tuple-element.27), channel_id=1, source_target_pairs={{16,0},{12,4},{24,8},{4,12},{0,16},{28,20},{8,24},{20,28},{17,1},{... | collective-permute-start | bytes 331784 | tf_op jit(solution)/shard_map/ppermute | solution.py:352
  6.4 0.5 %collective-permute-start.1 = (bf16[64,768]{1,0:T(8,128)(2,1)S(1)}, bf16[64,768]{1,0:T(8,128)(2,1)S(1)}, u32[]{:S(2)}, u32[]{:S(2)}) collective-permute-start(bf16[64,768]{1,0:T(8,128)(2,1)S(1)} %get-tuple-element.25), channel_id=1, source_target_pairs={{8,0},{20,4},{0,8},{28,12},{24,16},{4,20},{16,24},{12,28},{9,1},{2... | collective-permute-start | bytes 294920 | tf_op jit(solution)/shard_map/ppermute | solution.py:352
  6.9 0.1 collective-permute-start.2
  7.0 1.2 %collective-permute-done.a_first = bf16[72,768]{1,0:T(8,128)(2,1)S(1)} collective-permute-done((bf16[72,768]{1,0:T(8,128)(2,1)S(1)}, bf16[72,768]{1,0:T(8,128)(2,1)S(1)}, u32[]{:S(2)}, u32[]{:S(2)}) %collective-permute-start) | collective-permute-done | bytes 110624 | tf_op jit(solution)/shard_map/ppermute | solution.py:352
  8.2 1.6 %collective-permute-start.5 = (bf16[72,768]{1,0:T(8,128)(2,1)S(1)}, bf16[72,768]{1,0:T(8,128)(2,1)S(1)}, u32[]{:S(2)}, u32[]{:S(2)}) collective-permute-start(bf16[72,768]{1,0:T(8,128)(2,1)S(1)} %collective-permute-done.a_first), channel_id=1, source_target_pairs={{16,0},{12,4},{24,8},{4,12},{0,16},{28,20},{8,24},{20,28},{17,1},{... | collective-permute-start | bytes 331784 | tf_op jit(solution)/shard_map/ppermute | solution.py:352
  9.8 0.7 %collective-permute-done.3.b_second = bf16[72,768]{1,0:T(8,128)(2,1)S(1)} collective-permute-done((bf16[72,768]{1,0:T(8,128)(2,1)S(1)}, bf16[72,768]{1,0:T(8,128)(2,1)S(1)}, u32[]{:S(2)}, u32[]{:S(2)}) %collective-permute-start.3) | collective-permute-done | bytes 110624 | tf_op jit(solution)/shard_map/ppermute | solution.py:352
  10.5 1.9 %collective-permute-start.6 = (bf16[64,768]{1,0:T(8,128)(2,1)S(1)}, bf16[64,768]{1,0:T(8,128)(2,1)S(1)}, u32[]{:S(2)}, u32[]{:S(2)}) collective-permute-start(bf16[64,768]{1,0:T(8,128)(2,1)S(1)} %slice.4), channel_id=1, source_target_pairs={{8,0},{20,4},{0,8},{28,12},{24,16},{4,20},{16,24},{12,28},{9,1},{2... | collective-permute-start | bytes 294920 | tf_op jit(solution)/shard_map/ppermute | solution.py:352
  12.3 1.4 %shard_map.69 = (bf16[512,768]{1,0:T(8,128)(2,1)S(1)}, f32[512,128]{1,0:T(8,128)S(1)}, bf16[136,768]{1,0:T(8,128)(2,1)S(1)}) custom-call(bf16[512,768]{1,0:T(8,128)(2,1)} %source.1, f32[1,512]{1,0:T(1,128)} %bitcast.11, bf16[136,768]{1,0:T(8,128)(2,1)S(1)} %get-tuple-element.22.whole), custom_call_target="tpu_custom_call" | custom-call | tf_op jit(solution)/shard_map/pallas_call | solution.py:394
  13.8 0.0 collective-permute-done.1.a_second
  13.8 0.0 collective-permute-done.2.b_first
  13.8 0.1 collective-permute-start.4
  13.9 0.6 %shard_map.70 = (f32[512,384]{1,0:T(8,128)S(1)}, f32[2,8,128]{2,1,0:T(8,128)S(1)}) custom-call(bf16[512,768]{1,0:T(8,128)(2,1)S(1)} %get-tuple-element.23.source, bf16[136,768]{1,0:T(8,128)(2,1)S(1)} %get-tuple-element.22.whole, bf16[72,768]{1,0:T(8,128)(2,1)S(1)} %collective-permute-done.a_first, bf16[64,768]{1,0:T(8,128)(2,1)S(1)} %collective-permute-done.1.a_second, ...), custom_call_target="tpu_custom_call" | custom-call | bytes 786432 | tf_op jit(solution)/shard_map/pallas_call | solution.py:421
  14.5 0.0 collective-permute-done.5.message.far_a
  14.5 0.6 %collective-permute-start.7 = (bf16[72,768]{1,0:T(8,128)(2,1)S(1)}, bf16[72,768]{1,0:T(8,128)(2,1)S(1)}, u32[]{:S(2)}, u32[]{:S(2)}) collective-permute-start(bf16[72,768]{1,0:T(8,128)(2,1)S(1)} %shard_map.73), channel_id=1, source_target_pairs={{4,0},{0,4},{12,8},{8,12},{20,16},{16,20},{28,24},{24,28},{5,1},{1... | collective-permute-start | bytes 331784 | tf_op jit(solution)/shard_map/ppermute | solution.py:22
  15.1 0.1 collective-permute-done.6.message.far_b
  15.2 0.1 collective-permute-start.8
  15.3 0.7 %collective-permute-done.4.sibling = bf16[408,768]{1,0:T(8,128)(2,1)S(1)} collective-permute-done((bf16[408,768]{1,0:T(8,128)(2,1)S(1)}, bf16[408,768]{1,0:T(8,128)(2,1)S(1)}, u32[]{:S(2)}, u32[]{:S(2)}) %collective-permute-start.4) | collective-permute-done | bytes 626720 | tf_op jit(solution)/shard_map/ppermute | solution.py:22
  16.0 0.9 %shard_map.72 = (f32[512,384]{1,0:T(8,128)S(1)}, f32[2,8,128]{2,1,0:T(8,128)S(1)}, f32[512,128]{1,0:T(8,128)S(1)}) custom-call(bf16[512,768]{1,0:T(8,128)(2,1)S(1)} %get-tuple-element.23.source, bf16[408,768]{1,0:T(8,128)(2,1)S(1)} %collective-permute-done.4.sibling, f32[512,384]{1,0:T(8,128)S(1)} %get-tuple-element.28.own), custom_call_target="tpu_custom_call" | custom-call | bytes 786432 | tf_op jit(solution)/shard_map/pallas_call | solution.py:421
  16.8 0.0 collective-permute-done.8.sibling_b
  16.8 0.0 collective-permute-done.7.sibling_a
  16.8 0.4 shard_map.75
  17.3 0.7 %shard_map.76 = f32[32,8,128]{2,1,0:T(8,128)S(1)} custom-call(f32[512,384]{1,0:T(8,128)S(1)} %get-tuple-element.28.own, f32[2,8,128]{2,1,0:T(8,128)S(1)} %get-tuple-element.29.tie.own_table, f32[512,384]{1,0:T(8,128)S(1)} %get-tuple-element.31.near.sibling, f32[2,8,128]{2,1,0:T(8,128)S(1)} %get-tuple-element.32.sibling_table, ...), custom_call_target="tpu_custom_call" | custom-call | flops 8388608 | bytes 786432 | tf_op jit(solution)/shard_map/pallas_call | solution.py:452
  18.0 12.6 %all_to_all.16.got = f32[32,8,128]{2,1,0:T(8,128)S(1)} all-to-all(f32[32,8,128]{2,1,0:T(8,128)S(1)} %shard_map.76), channel_id=1, replica_groups={{31,30,29,28,27,26,25,24,23,22,21,20,19,18,17,16,15,14,13,12,11,10,9,8,..., dimensions={0} | all-to-all | bytes 262144 | tf_op jit(solution)/shard_map/all_to_all | solution.py:361
  30.5 1.1 %shard_map.77 = (f32[1,512]{1,0:T(1,128)S(1)}, f32[32,128]{1,0:T(8,128)S(1)}) custom-call(f32[512,384]{1,0:T(8,128)S(1)} %get-tuple-element.28.own, f32[2,8,128]{2,1,0:T(8,128)S(1)} %get-tuple-element.29.tie.own_table, f32[512,384]{1,0:T(8,128)S(1)} %get-tuple-element.31.near.sibling, f32[2,8,128]{2,1,0:T(8,128)S(1)} %get-tuple-element.32.sibling_table, ...), custom_call_target="tpu_custom_call" | custom-call | flops 8388608 | bytes 786432 | tf_op jit(solution)/shard_map/pallas_call | solution.py:462
  31.6 9.0 %all_to_all.17 = f32[32,1,128]{2,1,0:T(1,128)S(1)} all-to-all(f32[32,1,128]{2,1,0:T(1,128)S(1)} %bitcast.10), channel_id=1, replica_groups={{31,30,29,28,27,26,25,24,23,22,21,20,19,18,17,16,15,14,13,12,11,10,9,8,..., dimensions={0} | all-to-all | bytes 32768 | tf_op jit(solution)/shard_map/all_to_all | solution.py:361
  40.7 0.6 %shard_map.78 = (f32[1,512]{1,0:T(1,128)}, f32[1,128]{1,0:T(1,128)}) custom-call(f32[32,128]{1,0:T(8,128)S(1)} %bitcast.9, f32[2,128]{1,0:T(2,128)S(1)} %get-tuple-element.38.small, f32[1,512]{1,0:T(1,128)S(1)} %get-tuple-element.39.row), custom_call_target="tpu_custom_call" | custom-call | tf_op jit(solution)/shard_map/pallas_call | solution.py:472
  (4 shorter events, 0.1 us)
Async XLA Ops:
  1.8 6.3 %collective-permute-start = (bf16[72,768]{1,0:T(8,128)(2,1)S(1)}, bf16[72,768]{1,0:T(8,128)(2,1)S(1)}, u32[]{:S(2)}, u32[]{:S(2)}) collective-permute-start(bf16[72,768]{1,0:T(8,128)(2,1)S(1)} %get-tuple-element.24), channel_id=1, source_target_pairs={{8,0},{20,4},{0,8},{28,12},{24,16},{4,20},{16,24},{12,28},{9,1},{2... | collective-permute-start | bytes 331784 | tf_op jit(solution)/shard_map/ppermute | solution.py:352
  4.9 5.6 %collective-permute-start.3 = (bf16[72,768]{1,0:T(8,128)(2,1)S(1)}, bf16[72,768]{1,0:T(8,128)(2,1)S(1)}, u32[]{:S(2)}, u32[]{:S(2)}) collective-permute-start(bf16[72,768]{1,0:T(8,128)(2,1)S(1)} %get-tuple-element.27), channel_id=1, source_target_pairs={{16,0},{12,4},{24,8},{4,12},{0,16},{28,20},{8,24},{20,28},{17,1},{... | collective-permute-start | bytes 331784 | tf_op jit(solution)/shard_map/ppermute | solution.py:352
  6.4 7.4 %collective-permute-start.1 = (bf16[64,768]{1,0:T(8,128)(2,1)S(1)}, bf16[64,768]{1,0:T(8,128)(2,1)S(1)}, u32[]{:S(2)}, u32[]{:S(2)}) collective-permute-start(bf16[64,768]{1,0:T(8,128)(2,1)S(1)} %get-tuple-element.25), channel_id=1, source_target_pairs={{8,0},{20,4},{0,8},{28,12},{24,16},{4,20},{16,24},{12,28},{9,1},{2... | collective-permute-start | bytes 294920 | tf_op jit(solution)/shard_map/ppermute | solution.py:352
  6.9 6.9 %collective-permute-start.2 = (bf16[64,768]{1,0:T(8,128)(2,1)S(1)}, bf16[64,768]{1,0:T(8,128)(2,1)S(1)}, u32[]{:S(2)}, u32[]{:S(2)}) collective-permute-start(bf16[64,768]{1,0:T(8,128)(2,1)S(1)} %get-tuple-element.26), channel_id=1, source_target_pairs={{16,0},{12,4},{24,8},{4,12},{0,16},{28,20},{8,24},{20,28},{17,1},{... | collective-permute-start | bytes 294920 | tf_op jit(solution)/shard_map/ppermute | solution.py:352
  8.2 6.3 %collective-permute-start.5 = (bf16[72,768]{1,0:T(8,128)(2,1)S(1)}, bf16[72,768]{1,0:T(8,128)(2,1)S(1)}, u32[]{:S(2)}, u32[]{:S(2)}) collective-permute-start(bf16[72,768]{1,0:T(8,128)(2,1)S(1)} %collective-permute-done.a_first), channel_id=1, source_target_pairs={{16,0},{12,4},{24,8},{4,12},{0,16},{28,20},{8,24},{20,28},{17,1},{... | collective-permute-start | bytes 331784 | tf_op jit(solution)/shard_map/ppermute | solution.py:352
  10.5 4.7 %collective-permute-start.6 = (bf16[64,768]{1,0:T(8,128)(2,1)S(1)}, bf16[64,768]{1,0:T(8,128)(2,1)S(1)}, u32[]{:S(2)}, u32[]{:S(2)}) collective-permute-start(bf16[64,768]{1,0:T(8,128)(2,1)S(1)} %slice.4), channel_id=1, source_target_pairs={{8,0},{20,4},{0,8},{28,12},{24,16},{4,20},{16,24},{12,28},{9,1},{2... | collective-permute-start | bytes 294920 | tf_op jit(solution)/shard_map/ppermute | solution.py:352
  13.8 2.1 %collective-permute-start.4 = (bf16[408,768]{1,0:T(8,128)(2,1)S(1)}, bf16[408,768]{1,0:T(8,128)(2,1)S(1)}, u32[]{:S(2)}, u32[]{:S(2)}) collective-permute-start(bf16[408,768]{1,0:T(8,128)(2,1)S(1)} %shard_map.71), channel_id=1, source_target_pairs={{4,0},{0,4},{12,8},{8,12},{20,16},{16,20},{28,24},{24,28},{5,1},{1... | collective-permute-start | bytes 1880072 | tf_op jit(solution)/shard_map/ppermute | solution.py:22
  14.5 2.3 %collective-permute-start.7 = (bf16[72,768]{1,0:T(8,128)(2,1)S(1)}, bf16[72,768]{1,0:T(8,128)(2,1)S(1)}, u32[]{:S(2)}, u32[]{:S(2)}) collective-permute-start(bf16[72,768]{1,0:T(8,128)(2,1)S(1)} %shard_map.73), channel_id=1, source_target_pairs={{4,0},{0,4},{12,8},{8,12},{20,16},{16,20},{28,24},{24,28},{5,1},{1... | collective-permute-start | bytes 331784 | tf_op jit(solution)/shard_map/ppermute | solution.py:22
  15.2 1.6 %collective-permute-start.8 = (bf16[64,768]{1,0:T(8,128)(2,1)S(1)}, bf16[64,768]{1,0:T(8,128)(2,1)S(1)}, u32[]{:S(2)}, u32[]{:S(2)}) collective-permute-start(bf16[64,768]{1,0:T(8,128)(2,1)S(1)} %shard_map.74), channel_id=1, source_target_pairs={{4,0},{0,4},{12,8},{8,12},{20,16},{16,20},{28,24},{24,28},{5,1},{1... | collective-permute-start | bytes 294920 | tf_op jit(solution)/shard_map/ppermute | solution.py:22

commit v15 on v10

--- a/solution.py
+++ b/solution.py
@@ -60,10 +60,11 @@
 
 
 CHUNK = 64
-
-
-def chunks_of(rows):
-    return [pl.ds(start, CHUNK) for start in range(0, rows, CHUNK)]
+TALL = 128
+
+
+def chunks_of(rows, size=CHUNK):
+    return [pl.ds(start, size) for start in range(0, rows, size)]
 
 
 def row_sweep(score_of, blocks, rows, found_of, columns=None, others=None):
@@ -88,9 +89,9 @@
 
 
 def column_sweep(score_of, blocks, rows, row_pot, found_of):
-    folds = (CHUNK // SUBLANES, SUBLANES, LANES)
+    folds = (TALL // SUBLANES, SUBLANES, LANES)
     found = [[] for _ in blocks]
-    for at in chunks_of(rows):
+    for at in chunks_of(rows, TALL):
         addend = row_pot[at, :]
         for p in blocks:
             score = (score_of(at, p) + addend).reshape(folds)

time: 41.2 us -> 41.2 us (level)
  no operation moved by 1% of the time
where the time goes in v15:
time: 41.2 us; the launch traced here: 41 us
  blocking collectives  21.6 us (52%)
  starting transfers between devices  9.26 us (22%)
  Pallas kernels  6.69 us (16%)
  waiting for transfers between devices  2.7 us (7%)
  between operations  0.76 us (2%)
    all_to_all x2, blocking collectives, exchange(): lax.all_to_all(message, ('blk', 'grp'), 0, 0, axis_index_groups=[order])  21.6 us
    ppermute x6, starting transfers between devices, along(): lax.ppermute(array, 'blk', [(i ^ neighbour_step(i, turn), i) for i in ran...  8.56 us
    ppermute x6, waiting for transfers between devices, along(): lax.ppermute(array, 'blk', [(i ^ neighbour_step(i, turn), i) for i in ran...  2 us
    pallas_call x3, Pallas kernels, scores_of(): pl.pallas_call(functools.partial(kernel, factor), out_shape=(values(rows,...  1.87 us
    pallas_call x1, Pallas kernels, shards_square(): pl.pallas_call(source_kernel, out_shape=(jax.ShapeDtypeStruct((rows, dept...  1.4 us
    pallas_call x1, Pallas kernels, shards_square(): pl.pallas_call(functools.partial(second_kernel, grp), out_shape=(values(1...  1.06 us
    pallas_call x1, Pallas kernels, shards_square(): pl.pallas_call(head_kernel, out_shape=(block_of(half + SPARE), block_of(h...  0.99 us
  transfers between devices with their start and end apart: 9, of which 4 were waited for; matrix products, arithmetic and copies ran while one was open for 0% of the time, Pallas kernels for 7%

profile of v15, /device:TPU:0, one launch (start us, length us, event | category | flops | bytes accessed | tf_op | source)
XLA Modules:
  0.0 41.0 jit_solution(2388852501736271901)
XLA Ops:
  0.6 1.0 %shard_map.68 = (bf16[72,768]{1,0:T(8,128)(2,1)S(1)}, bf16[72,768]{1,0:T(8,128)(2,1)S(1)}, bf16[136,768]{1,0:T(8,128)(2,1)S(1)}, f32[2,128]{1,0:T(2,128)S(1)}, b...) custom-call(bf16[128,768]{1,0:T(8,128)(2,1)} %own.1, f32[1,128]{1,0:T(1,128)} %bitcast.12, f32[1,128]{1,0:T(1,128)} %bitcast.13), custom_call_target="tpu_custom_call" | custom-call | tf_op jit(solution)/shard_map/pallas_call | solution.py:365
  1.6 3.0 %collective-permute-start = (bf16[72,768]{1,0:T(8,128)(2,1)S(1)}, bf16[72,768]{1,0:T(8,128)(2,1)S(1)}, u32[]{:S(2)}, u32[]{:S(2)}) collective-permute-start(bf16[72,768]{1,0:T(8,128)(2,1)S(1)} %get-tuple-element.24), channel_id=1, source_target_pairs={{8,0},{20,4},{0,8},{28,12},{24,16},{4,20},{16,24},{12,28},{9,1},{2... | collective-permute-start | bytes 331784 | tf_op jit(solution)/shard_map/ppermute | solution.py:348
  4.6 1.5 %collective-permute-start.3 = (bf16[72,768]{1,0:T(8,128)(2,1)S(1)}, bf16[72,768]{1,0:T(8,128)(2,1)S(1)}, u32[]{:S(2)}, u32[]{:S(2)}) collective-permute-start(bf16[72,768]{1,0:T(8,128)(2,1)S(1)} %get-tuple-element.27), channel_id=1, source_target_pairs={{16,0},{12,4},{24,8},{4,12},{0,16},{28,20},{8,24},{20,28},{17,1},{... | collective-permute-start | bytes 331784 | tf_op jit(solution)/shard_map/ppermute | solution.py:348
  6.2 0.5 %collective-permute-start.1 = (bf16[64,768]{1,0:T(8,128)(2,1)S(1)}, bf16[64,768]{1,0:T(8,128)(2,1)S(1)}, u32[]{:S(2)}, u32[]{:S(2)}) collective-permute-start(bf16[64,768]{1,0:T(8,128)(2,1)S(1)} %get-tuple-element.25), channel_id=1, source_target_pairs={{8,0},{20,4},{0,8},{28,12},{24,16},{4,20},{16,24},{12,28},{9,1},{2... | collective-permute-start | bytes 294920 | tf_op jit(solution)/shard_map/ppermute | solution.py:348
  6.7 0.1 collective-permute-start.2
  6.7 1.2 %collective-permute-done.a_first = bf16[72,768]{1,0:T(8,128)(2,1)S(1)} collective-permute-done((bf16[72,768]{1,0:T(8,128)(2,1)S(1)}, bf16[72,768]{1,0:T(8,128)(2,1)S(1)}, u32[]{:S(2)}, u32[]{:S(2)}) %collective-permute-start) | collective-permute-done | bytes 110624 | tf_op jit(solution)/shard_map/ppermute | solution.py:348
  8.0 1.6 %collective-permute-start.5 = (bf16[72,768]{1,0:T(8,128)(2,1)S(1)}, bf16[72,768]{1,0:T(8,128)(2,1)S(1)}, u32[]{:S(2)}, u32[]{:S(2)}) collective-permute-start(bf16[72,768]{1,0:T(8,128)(2,1)S(1)} %collective-permute-done.a_first), channel_id=1, source_target_pairs={{16,0},{12,4},{24,8},{4,12},{0,16},{28,20},{8,24},{20,28},{17,1},{... | collective-permute-start | bytes 331784 | tf_op jit(solution)/shard_map/ppermute | solution.py:348
  9.6 0.7 %collective-permute-done.3.b_second = bf16[72,768]{1,0:T(8,128)(2,1)S(1)} collective-permute-done((bf16[72,768]{1,0:T(8,128)(2,1)S(1)}, bf16[72,768]{1,0:T(8,128)(2,1)S(1)}, u32[]{:S(2)}, u32[]{:S(2)}) %collective-permute-start.3) | collective-permute-done | bytes 110624 | tf_op jit(solution)/shard_map/ppermute | solution.py:348
  10.3 1.9 %collective-permute-start.6 = (bf16[64,768]{1,0:T(8,128)(2,1)S(1)}, bf16[64,768]{1,0:T(8,128)(2,1)S(1)}, u32[]{:S(2)}, u32[]{:S(2)}) collective-permute-start(bf16[64,768]{1,0:T(8,128)(2,1)S(1)} %slice.4), channel_id=1, source_target_pairs={{8,0},{20,4},{0,8},{28,12},{24,16},{4,20},{16,24},{12,28},{9,1},{2... | collective-permute-start | bytes 294920 | tf_op jit(solution)/shard_map/ppermute | solution.py:348
  12.1 1.4 %shard_map.69 = (bf16[512,768]{1,0:T(8,128)(2,1)S(1)}, f32[512,128]{1,0:T(8,128)S(1)}, bf16[136,768]{1,0:T(8,128)(2,1)S(1)}) custom-call(bf16[512,768]{1,0:T(8,128)(2,1)} %source.1, f32[1,512]{1,0:T(1,128)} %bitcast.11, bf16[136,768]{1,0:T(8,128)(2,1)S(1)} %get-tuple-element.22.whole), custom_call_target="tpu_custom_call" | custom-call | tf_op jit(solution)/shard_map/pallas_call | solution.py:390
  13.5 0.0 collective-permute-done.1.a_second
  13.5 0.0 collective-permute-done.2.b_first
  13.6 0.1 collective-permute-start.4
  13.7 0.6 %shard_map.70 = (f32[512,384]{1,0:T(8,128)S(1)}, f32[2,8,128]{2,1,0:T(8,128)S(1)}) custom-call(bf16[512,768]{1,0:T(8,128)(2,1)S(1)} %get-tuple-element.23.source, bf16[136,768]{1,0:T(8,128)(2,1)S(1)} %get-tuple-element.22.whole, bf16[72,768]{1,0:T(8,128)(2,1)S(1)} %collective-permute-done.a_first, bf16[64,768]{1,0:T(8,128)(2,1)S(1)} %collective-permute-done.1.a_second, ...), custom_call_target="tpu_custom_call" | custom-call | bytes 786432 | tf_op jit(solution)/shard_map/pallas_call | solution.py:417
  14.3 0.0 collective-permute-done.5.message.far_a
  14.3 0.6 %collective-permute-start.7 = (bf16[72,768]{1,0:T(8,128)(2,1)S(1)}, bf16[72,768]{1,0:T(8,128)(2,1)S(1)}, u32[]{:S(2)}, u32[]{:S(2)}) collective-permute-start(bf16[72,768]{1,0:T(8,128)(2,1)S(1)} %shard_map.73), channel_id=1, source_target_pairs={{4,0},{0,4},{12,8},{8,12},{20,16},{16,20},{28,24},{24,28},{5,1},{1... | collective-permute-start | bytes 331784 | tf_op jit(solution)/shard_map/ppermute | solution.py:22
  14.9 0.1 collective-permute-done.6.message.far_b
  15.0 0.1 collective-permute-start.8
  15.0 0.7 %collective-permute-done.4.sibling = bf16[408,768]{1,0:T(8,128)(2,1)S(1)} collective-permute-done((bf16[408,768]{1,0:T(8,128)(2,1)S(1)}, bf16[408,768]{1,0:T(8,128)(2,1)S(1)}, u32[]{:S(2)}, u32[]{:S(2)}) %collective-permute-start.4) | collective-permute-done | bytes 626720 | tf_op jit(solution)/shard_map/ppermute | solution.py:22
  15.7 0.9 %shard_map.72 = (f32[512,384]{1,0:T(8,128)S(1)}, f32[2,8,128]{2,1,0:T(8,128)S(1)}, f32[512,128]{1,0:T(8,128)S(1)}) custom-call(bf16[512,768]{1,0:T(8,128)(2,1)S(1)} %get-tuple-element.23.source, bf16[408,768]{1,0:T(8,128)(2,1)S(1)} %collective-permute-done.4.sibling, f32[512,384]{1,0:T(8,128)S(1)} %get-tuple-element.28.own), custom_call_target="tpu_custom_call" | custom-call | bytes 786432 | tf_op jit(solution)/shard_map/pallas_call | solution.py:417
  16.6 0.0 collective-permute-done.8.sibling_b
  16.6 0.0 collective-permute-done.7.sibling_a
  16.6 0.4 shard_map.75
  17.0 0.7 %shard_map.76 = f32[32,8,128]{2,1,0:T(8,128)S(1)} custom-call(f32[512,384]{1,0:T(8,128)S(1)} %get-tuple-element.28.own, f32[2,8,128]{2,1,0:T(8,128)S(1)} %get-tuple-element.29.tie.own_table, f32[512,384]{1,0:T(8,128)S(1)} %get-tuple-element.31.near.sibling, f32[2,8,128]{2,1,0:T(8,128)S(1)} %get-tuple-element.32.sibling_table, ...), custom_call_target="tpu_custom_call" | custom-call | flops 8388608 | bytes 786432 | tf_op jit(solution)/shard_map/pallas_call | solution.py:448
  17.8 12.6 %all_to_all.16.got = f32[32,8,128]{2,1,0:T(8,128)S(1)} all-to-all(f32[32,8,128]{2,1,0:T(8,128)S(1)} %shard_map.76), channel_id=1, replica_groups={{31,30,29,28,27,26,25,24,23,22,21,20,19,18,17,16,15,14,13,12,11,10,9,8,..., dimensions={0} | all-to-all | bytes 262144 | tf_op jit(solution)/shard_map/all_to_all | solution.py:357
  30.3 1.1 %shard_map.77 = (f32[1,512]{1,0:T(1,128)S(1)}, f32[32,128]{1,0:T(8,128)S(1)}) custom-call(f32[512,384]{1,0:T(8,128)S(1)} %get-tuple-element.28.own, f32[2,8,128]{2,1,0:T(8,128)S(1)} %get-tuple-element.29.tie.own_table, f32[512,384]{1,0:T(8,128)S(1)} %get-tuple-element.31.near.sibling, f32[2,8,128]{2,1,0:T(8,128)S(1)} %get-tuple-element.32.sibling_table, ...), custom_call_target="tpu_custom_call" | custom-call | flops 8388608 | bytes 786432 | tf_op jit(solution)/shard_map/pallas_call | solution.py:458
  31.4 9.0 %all_to_all.17 = f32[32,1,128]{2,1,0:T(1,128)S(1)} all-to-all(f32[32,1,128]{2,1,0:T(1,128)S(1)} %bitcast.10), channel_id=1, replica_groups={{31,30,29,28,27,26,25,24,23,22,21,20,19,18,17,16,15,14,13,12,11,10,9,8,..., dimensions={0} | all-to-all | bytes 32768 | tf_op jit(solution)/shard_map/all_to_all | solution.py:357
  40.4 0.6 %shard_map.78 = (f32[1,512]{1,0:T(1,128)}, f32[1,128]{1,0:T(1,128)}) custom-call(f32[32,128]{1,0:T(8,128)S(1)} %bitcast.9, f32[2,128]{1,0:T(2,128)S(1)} %get-tuple-element.38.small, f32[1,512]{1,0:T(1,128)S(1)} %get-tuple-element.39.row), custom_call_target="tpu_custom_call" | custom-call | tf_op jit(solution)/shard_map/pallas_call | solution.py:468
  (4 shorter events, 0.1 us)
Async XLA Ops:
  1.6 6.3 %collective-permute-start = (bf16[72,768]{1,0:T(8,128)(2,1)S(1)}, bf16[72,768]{1,0:T(8,128)(2,1)S(1)}, u32[]{:S(2)}, u32[]{:S(2)}) collective-permute-start(bf16[72,768]{1,0:T(8,128)(2,1)S(1)} %get-tuple-element.24), channel_id=1, source_target_pairs={{8,0},{20,4},{0,8},{28,12},{24,16},{4,20},{16,24},{12,28},{9,1},{2... | collective-permute-start | bytes 331784 | tf_op jit(solution)/shard_map/ppermute | solution.py:348
  4.6 5.6 %collective-permute-start.3 = (bf16[72,768]{1,0:T(8,128)(2,1)S(1)}, bf16[72,768]{1,0:T(8,128)(2,1)S(1)}, u32[]{:S(2)}, u32[]{:S(2)}) collective-permute-start(bf16[72,768]{1,0:T(8,128)(2,1)S(1)} %get-tuple-element.27), channel_id=1, source_target_pairs={{16,0},{12,4},{24,8},{4,12},{0,16},{28,20},{8,24},{20,28},{17,1},{... | collective-permute-start | bytes 331784 | tf_op jit(solution)/shard_map/ppermute | solution.py:348
  6.2 7.4 %collective-permute-start.1 = (bf16[64,768]{1,0:T(8,128)(2,1)S(1)}, bf16[64,768]{1,0:T(8,128)(2,1)S(1)}, u32[]{:S(2)}, u32[]{:S(2)}) collective-permute-start(bf16[64,768]{1,0:T(8,128)(2,1)S(1)} %get-tuple-element.25), channel_id=1, source_target_pairs={{8,0},{20,4},{0,8},{28,12},{24,16},{4,20},{16,24},{12,28},{9,1},{2... | collective-permute-start | bytes 294920 | tf_op jit(solution)/shard_map/ppermute | solution.py:348
  6.7 6.9 %collective-permute-start.2 = (bf16[64,768]{1,0:T(8,128)(2,1)S(1)}, bf16[64,768]{1,0:T(8,128)(2,1)S(1)}, u32[]{:S(2)}, u32[]{:S(2)}) collective-permute-start(bf16[64,768]{1,0:T(8,128)(2,1)S(1)} %get-tuple-element.26), channel_id=1, source_target_pairs={{16,0},{12,4},{24,8},{4,12},{0,16},{28,20},{8,24},{20,28},{17,1},{... | collective-permute-start | bytes 294920 | tf_op jit(solution)/shard_map/ppermute | solution.py:348
  8.0 6.3 %collective-permute-start.5 = (bf16[72,768]{1,0:T(8,128)(2,1)S(1)}, bf16[72,768]{1,0:T(8,128)(2,1)S(1)}, u32[]{:S(2)}, u32[]{:S(2)}) collective-permute-start(bf16[72,768]{1,0:T(8,128)(2,1)S(1)} %collective-permute-done.a_first), channel_id=1, source_target_pairs={{16,0},{12,4},{24,8},{4,12},{0,16},{28,20},{8,24},{20,28},{17,1},{... | collective-permute-start | bytes 331784 | tf_op jit(solution)/shard_map/ppermute | solution.py:348
  10.3 4.7 %collective-permute-start.6 = (bf16[64,768]{1,0:T(8,128)(2,1)S(1)}, bf16[64,768]{1,0:T(8,128)(2,1)S(1)}, u32[]{:S(2)}, u32[]{:S(2)}) collective-permute-start(bf16[64,768]{1,0:T(8,128)(2,1)S(1)} %slice.4), channel_id=1, source_target_pairs={{8,0},{20,4},{0,8},{28,12},{24,16},{4,20},{16,24},{12,28},{9,1},{2... | collective-permute-start | bytes 294920 | tf_op jit(solution)/shard_map/ppermute | solution.py:348
  13.6 2.1 %collective-permute-start.4 = (bf16[408,768]{1,0:T(8,128)(2,1)S(1)}, bf16[408,768]{1,0:T(8,128)(2,1)S(1)}, u32[]{:S(2)}, u32[]{:S(2)}) collective-permute-start(bf16[408,768]{1,0:T(8,128)(2,1)S(1)} %shard_map.71), channel_id=1, source_target_pairs={{4,0},{0,4},{12,8},{8,12},{20,16},{16,20},{28,24},{24,28},{5,1},{1... | collective-permute-start | bytes 1880072 | tf_op jit(solution)/shard_map/ppermute | solution.py:22
  14.3 2.3 %collective-permute-start.7 = (bf16[72,768]{1,0:T(8,128)(2,1)S(1)}, bf16[72,768]{1,0:T(8,128)(2,1)S(1)}, u32[]{:S(2)}, u32[]{:S(2)}) collective-permute-start(bf16[72,768]{1,0:T(8,128)(2,1)S(1)} %shard_map.73), channel_id=1, source_target_pairs={{4,0},{0,4},{12,8},{8,12},{20,16},{16,20},{28,24},{24,28},{5,1},{1... | collective-permute-start | bytes 331784 | tf_op jit(solution)/shard_map/ppermute | solution.py:22
  15.0 1.6 %collective-permute-start.8 = (bf16[64,768]{1,0:T(8,128)(2,1)S(1)}, bf16[64,768]{1,0:T(8,128)(2,1)S(1)}, u32[]{:S(2)}, u32[]{:S(2)}) collective-permute-start(bf16[64,768]{1,0:T(8,128)(2,1)S(1)} %shard_map.74), channel_id=1, source_target_pairs={{4,0},{0,4},{12,8},{8,12},{20,16},{16,20},{28,24},{24,28},{5,1},{1... | collective-permute-start | bytes 294920 | tf_op jit(solution)/shard_map/ppermute | solution.py:22

commit v16 on v10

--- a/solution.py
+++ b/solution.py
@@ -119,10 +119,9 @@
 
 
 def head_kernel(
-    own, init, target_logw, first, second, whole, small, first_plain, second_plain, init_row,
-    logw_row, sems,
+    own, init, target_logw, first, second, whole, small, init_row, logw_row, sems
 ):
-    rows, half = own.shape[0], first_plain.shape[0]
+    rows, half = own.shape[0], second.shape[0]
     copies = [
         pltpu.make_async_copy(own, whole.at[0:rows], sems.at[0]),
         pltpu.make_async_copy(init, init_row, sems.at[1]),
@@ -132,10 +131,8 @@
         copy.start()
     for copy in copies:
         copy.wait()
-    for out in (first, first_plain):
-        out[0:half, :] = whole[0:half, :]
-    for out in (second, second_plain):
-        out[0:half, :] = whole[half:rows, :]
+    first[0:half, :] = whole[0:half, :]
+    second[...] = whole[half:rows, :]
     small[0:1, :] = init_row[...]
     small[1:2, :] = logw_row[...]
     filler = jnp.zeros((SPARE - 2, LANES), jnp.float32)
@@ -144,7 +141,6 @@
         lanes = slice(k * LANES, (k + 1) * LANES)
         part = (rest if k < 3 else jnp.zeros_like(rest)).astype(whole.dtype)
         first[half:, lanes] = part
-        second[half:, lanes] = part
         whole[rows:, lanes] = part
         rest = rest - part.astype(jnp.float32)
 
@@ -169,8 +165,9 @@
     out[block : block + half, :] = a_first[0:half, :]
     out[block + half : block + 2 * half, :] = a_second[...]
     out[block + 2 * half : 2 * block, :] = a_first[half:, :]
-    out[2 * block : 2 * block + half, :] = b_first[...]
-    out[2 * block + half : 3 * block, :] = b_second[...]
+    out[2 * block : 2 * block + half, :] = b_first[0:half, :]
+    out[2 * block + half : 2 * block + 2 * half, :] = b_second[...]
+    out[2 * block + 2 * half : 3 * block, :] = b_first[half:, :]
 
 
 def unpack(message, end=None):
@@ -190,7 +187,7 @@
     targets[0 : 2 * half, :] = whole[0 : 2 * half, :]
     for k in range(2, 6):
         targets[k * half : (k + 1) * half, :] = pieces[k][0:half, :]
-    smalls = [unpack(whole), unpack(a_first), unpack(b_second)]
+    smalls = [unpack(whole), unpack(a_first), unpack(b_first)]
     products(source, targets, factor, smalls, scaled, table)
 
 
@@ -361,18 +358,16 @@
         def in_hbm(*arrays):
             return [pltpu.with_memory_space_constraint(each, pltpu.HBM) for each in arrays]
 
-        first, second, whole, small, first_plain, second_plain = pl.pallas_call(
+        first, second, whole, small = pl.pallas_call(
             head_kernel,
             out_shape=(
                 block_of(half + SPARE),
-                block_of(half + SPARE),
+                block_of(half),
                 block_of(width + SPARE),
                 values(2, width),
-                block_of(half),
-                block_of(half),
             ),
             in_specs=[hbm] * 3,
-            out_specs=(vmem,) * 6,
+            out_specs=(vmem,) * 4,
             scratch_shapes=[
                 pltpu.VMEM((1, width), jnp.float32),
                 pltpu.VMEM((1, width), jnp.float32),
@@ -382,10 +377,10 @@
         )(*in_hbm(target_embed, target_init.reshape(1, width), target_logw.reshape(1, width)))
         a_first = along(first, 0)
         b_second = along(second, 1)
-        a_second = along(second_plain, 0)
-        b_first = along(first_plain, 1)
+        a_second = along(second, 0)
+        b_first = along(first, 1)
         far_a = along(a_first, 1)
-        far_b = along(b_second[:half], 0)
+        far_b = along(b_second, 0)
         source, logw, passed = pl.pallas_call(
             source_kernel,
             out_shape=(

time: 41.2 us -> 41.1 us (level)
  waiting for transfers between devices: 2.7 us -> 2.01 us
  starting transfers between devices: 9.26 us -> 9.9 us
    ppermute x6, waiting for transfers between devices: 2 us -> 1.33 us  [along(): lax.ppermute(array, 'blk', [(i ^ neighbour_step(i, turn), i) for i in ran...]
    ppermute x6, starting transfers between devices: 8.56 us -> 9.2 us  [along(): lax.ppermute(array, 'blk', [(i ^ neighbour_step(i, turn), i) for i in ran...]
  transfers between devices with their start and end apart: 9 -> 9, of which waited for: 4 -> 3; matrix products, arithmetic and copies ran while one was open for 0% -> 0% of each run, Pallas kernels for 7% -> 7%
where the time goes in v16:
time: 41.1 us; the launch traced here: 41 us
  blocking collectives  21.6 us (53%)
  starting transfers between devices  9.9 us (24%)
  Pallas kernels  6.7 us (16%)
  waiting for transfers between devices  2.01 us (5%)
  between operations  0.76 us (2%)
    all_to_all x2, blocking collectives, exchange(): lax.all_to_all(message, ('blk', 'grp'), 0, 0, axis_index_groups=[order])  21.6 us
    ppermute x6, starting transfers between devices, along(): lax.ppermute(array, 'blk', [(i ^ neighbour_step(i, turn), i) for i in ran...  9.2 us
    pallas_call x3, Pallas kernels, scores_of(): pl.pallas_call(functools.partial(kernel, factor), out_shape=(values(rows,...  1.87 us
    pallas_call x1, Pallas kernels, shards_square(): pl.pallas_call(source_kernel, out_shape=(jax.ShapeDtypeStruct((rows, dept...  1.4 us
    ppermute x6, waiting for transfers between devices, along(): lax.ppermute(array, 'blk', [(i ^ neighbour_step(i, turn), i) for i in ran...  1.33 us
    pallas_call x1, Pallas kernels, shards_square(): pl.pallas_call(functools.partial(second_kernel, grp), out_shape=(values(1...  1.07 us
    pallas_call x1, Pallas kernels, shards_square(): pl.pallas_call(head_kernel, out_shape=(block_of(half + SPARE), block_of(h...  0.98 us
  transfers between devices with their start and end apart: 9, of which 3 were waited for; matrix products, arithmetic and copies ran while one was open for 0% of the time, Pallas kernels for 7%

profile of v16, /device:TPU:0, one launch (start us, length us, event | category | flops | bytes accessed | tf_op | source)
XLA Modules:
  0.0 41.0 jit_solution(329757987705892093)
XLA Ops:
  0.6 1.0 %shard_map.68 = (bf16[72,768]{1,0:T(8,128)(2,1)S(1)}, bf16[64,768]{1,0:T(8,128)(2,1)S(1)}, bf16[136,768]{1,0:T(8,128)(2,1)S(1)}, f32[2,128]{1,0:T(2,128)S(1)}) custom-call(bf16[128,768]{1,0:T(8,128)(2,1)} %own.1, f32[1,128]{1,0:T(1,128)} %bitcast.12, f32[1,128]{1,0:T(1,128)} %bitcast.13), custom_call_target="tpu_custom_call" | custom-call | tf_op jit(solution)/shard_map/pallas_call | solution.py:361
  1.6 3.0 %collective-permute-start = (bf16[72,768]{1,0:T(8,128)(2,1)S(1)}, bf16[72,768]{1,0:T(8,128)(2,1)S(1)}, u32[]{:S(2)}, u32[]{:S(2)}) collective-permute-start(bf16[72,768]{1,0:T(8,128)(2,1)S(1)} %get-tuple-element.22), channel_id=1, source_target_pairs={{8,0},{20,4},{0,8},{28,12},{24,16},{4,20},{16,24},{12,28},{9,1},{2... | collective-permute-start | bytes 331784 | tf_op jit(solution)/shard_map/ppermute | solution.py:344
  4.6 1.5 %collective-permute-start.3 = (bf16[64,768]{1,0:T(8,128)(2,1)S(1)}, bf16[64,768]{1,0:T(8,128)(2,1)S(1)}, u32[]{:S(2)}, u32[]{:S(2)}) collective-permute-start(bf16[64,768]{1,0:T(8,128)(2,1)S(1)} %get-tuple-element.23), channel_id=1, source_target_pairs={{16,0},{12,4},{24,8},{4,12},{0,16},{28,20},{8,24},{20,28},{17,1},{... | collective-permute-start | bytes 294920 | tf_op jit(solution)/shard_map/ppermute | solution.py:344
  6.1 0.5 %collective-permute-start.2 = (bf16[72,768]{1,0:T(8,128)(2,1)S(1)}, bf16[72,768]{1,0:T(8,128)(2,1)S(1)}, u32[]{:S(2)}, u32[]{:S(2)}) collective-permute-start(bf16[72,768]{1,0:T(8,128)(2,1)S(1)} %get-tuple-element.22), channel_id=1, source_target_pairs={{16,0},{12,4},{24,8},{4,12},{0,16},{28,20},{8,24},{20,28},{17,1},{... | collective-permute-start | bytes 331784 | tf_op jit(solution)/shard_map/ppermute | solution.py:344
  6.6 0.1 collective-permute-start.1
  6.7 1.2 %collective-permute-done.a_first = bf16[72,768]{1,0:T(8,128)(2,1)S(1)} collective-permute-done((bf16[72,768]{1,0:T(8,128)(2,1)S(1)}, bf16[72,768]{1,0:T(8,128)(2,1)S(1)}, u32[]{:S(2)}, u32[]{:S(2)}) %collective-permute-start) | collective-permute-done | bytes 110624 | tf_op jit(solution)/shard_map/ppermute | solution.py:344
  8.0 2.3 %collective-permute-start.5 = (bf16[72,768]{1,0:T(8,128)(2,1)S(1)}, bf16[72,768]{1,0:T(8,128)(2,1)S(1)}, u32[]{:S(2)}, u32[]{:S(2)}) collective-permute-start(bf16[72,768]{1,0:T(8,128)(2,1)S(1)} %collective-permute-done.a_first), channel_id=1, source_target_pairs={{16,0},{12,4},{24,8},{4,12},{0,16},{28,20},{8,24},{20,28},{17,1},{... | collective-permute-start | bytes 331784 | tf_op jit(solution)/shard_map/ppermute | solution.py:344
  10.3 0.0 collective-permute-done.3.b_second
  10.3 1.8 %collective-permute-start.6 = (bf16[64,768]{1,0:T(8,128)(2,1)S(1)}, bf16[64,768]{1,0:T(8,128)(2,1)S(1)}, u32[]{:S(2)}, u32[]{:S(2)}) collective-permute-start(bf16[64,768]{1,0:T(8,128)(2,1)S(1)} %collective-permute-done.3.b_second), channel_id=1, source_target_pairs={{8,0},{20,4},{0,8},{28,12},{24,16},{4,20},{16,24},{12,28},{9,1},{2... | collective-permute-start | bytes 294920 | tf_op jit(solution)/shard_map/ppermute | solution.py:344
  12.1 1.4 %shard_map.69 = (bf16[512,768]{1,0:T(8,128)(2,1)S(1)}, f32[512,128]{1,0:T(8,128)S(1)}, bf16[136,768]{1,0:T(8,128)(2,1)S(1)}) custom-call(bf16[512,768]{1,0:T(8,128)(2,1)} %source.1, f32[1,512]{1,0:T(1,128)} %bitcast.11, bf16[136,768]{1,0:T(8,128)(2,1)S(1)} %get-tuple-element.20.whole), custom_call_target="tpu_custom_call" | custom-call | tf_op jit(solution)/shard_map/pallas_call | solution.py:384
  13.5 0.0 collective-permute-done.1.a_second
  13.5 0.0 collective-permute-done.2.b_first
  13.5 0.1 collective-permute-start.4
  13.6 0.6 %shard_map.70 = (f32[512,384]{1,0:T(8,128)S(1)}, f32[2,8,128]{2,1,0:T(8,128)S(1)}) custom-call(bf16[512,768]{1,0:T(8,128)(2,1)S(1)} %get-tuple-element.21.source, bf16[136,768]{1,0:T(8,128)(2,1)S(1)} %get-tuple-element.20.whole, bf16[72,768]{1,0:T(8,128)(2,1)S(1)} %collective-permute-done.a_first, bf16[64,768]{1,0:T(8,128)(2,1)S(1)} %collective-permute-done.1.a_second, ...), custom_call_target="tpu_custom_call" | custom-call | bytes 786432 | tf_op jit(solution)/shard_map/pallas_call | solution.py:411
  14.2 0.0 collective-permute-done.5.message.far_a
  14.3 0.6 %collective-permute-start.7 = (bf16[72,768]{1,0:T(8,128)(2,1)S(1)}, bf16[72,768]{1,0:T(8,128)(2,1)S(1)}, u32[]{:S(2)}, u32[]{:S(2)}) collective-permute-start(bf16[72,768]{1,0:T(8,128)(2,1)S(1)} %shard_map.73), channel_id=1, source_target_pairs={{4,0},{0,4},{12,8},{8,12},{20,16},{16,20},{28,24},{24,28},{5,1},{1... | collective-permute-start | bytes 331784 | tf_op jit(solution)/shard_map/ppermute | solution.py:22
  14.8 0.1 collective-permute-done.6.message.far_b
  14.9 0.1 collective-permute-start.8
  15.0 0.7 %collective-permute-done.4.sibling = bf16[408,768]{1,0:T(8,128)(2,1)S(1)} collective-permute-done((bf16[408,768]{1,0:T(8,128)(2,1)S(1)}, bf16[408,768]{1,0:T(8,128)(2,1)S(1)}, u32[]{:S(2)}, u32[]{:S(2)}) %collective-permute-start.4) | collective-permute-done | bytes 626720 | tf_op jit(solution)/shard_map/ppermute | solution.py:22
  15.7 0.9 %shard_map.72 = (f32[512,384]{1,0:T(8,128)S(1)}, f32[2,8,128]{2,1,0:T(8,128)S(1)}, f32[512,128]{1,0:T(8,128)S(1)}) custom-call(bf16[512,768]{1,0:T(8,128)(2,1)S(1)} %get-tuple-element.21.source, bf16[408,768]{1,0:T(8,128)(2,1)S(1)} %collective-permute-done.4.sibling, f32[512,384]{1,0:T(8,128)S(1)} %get-tuple-element.24.own), custom_call_target="tpu_custom_call" | custom-call | bytes 786432 | tf_op jit(solution)/shard_map/pallas_call | solution.py:411
  16.5 0.0 collective-permute-done.8.sibling_b
  16.5 0.0 collective-permute-done.7.sibling_a
  16.6 0.4 %shard_map.75 = (f32[512,256]{1,0:T(8,128)S(1)}, f32[2,8,128]{2,1,0:T(8,128)S(1)}) custom-call(bf16[512,768]{1,0:T(8,128)(2,1)S(1)} %get-tuple-element.21.source, bf16[72,768]{1,0:T(8,128)(2,1)S(1)} %collective-permute-done.5.message.far_a, bf16[64,768]{1,0:T(8,128)(2,1)S(1)} %collective-permute-done.6.message.far_b, ...), custom_call_target="tpu_custom_call" | custom-call | bytes 786432 | tf_op jit(solution)/shard_map/pallas_call | solution.py:411
  17.0 0.7 %shard_map.76 = f32[32,8,128]{2,1,0:T(8,128)S(1)} custom-call(f32[512,384]{1,0:T(8,128)S(1)} %get-tuple-element.24.own, f32[2,8,128]{2,1,0:T(8,128)S(1)} %get-tuple-element.25.tie.own_table, f32[512,384]{1,0:T(8,128)S(1)} %get-tuple-element.27.near.sibling, f32[2,8,128]{2,1,0:T(8,128)S(1)} %get-tuple-element.28.sibling_table, ...), custom_call_target="tpu_custom_call" | custom-call | flops 8388608 | bytes 786432 | tf_op jit(solution)/shard_map/pallas_call | solution.py:442
  17.7 12.6 %all_to_all.16.got = f32[32,8,128]{2,1,0:T(8,128)S(1)} all-to-all(f32[32,8,128]{2,1,0:T(8,128)S(1)} %shard_map.76), channel_id=1, replica_groups={{31,30,29,28,27,26,25,24,23,22,21,20,19,18,17,16,15,14,13,12,11,10,9,8,..., dimensions={0} | all-to-all | bytes 262144 | tf_op jit(solution)/shard_map/all_to_all | solution.py:353
  30.3 1.1 %shard_map.77 = (f32[1,512]{1,0:T(1,128)S(1)}, f32[32,128]{1,0:T(8,128)S(1)}) custom-call(f32[512,384]{1,0:T(8,128)S(1)} %get-tuple-element.24.own, f32[2,8,128]{2,1,0:T(8,128)S(1)} %get-tuple-element.25.tie.own_table, f32[512,384]{1,0:T(8,128)S(1)} %get-tuple-element.27.near.sibling, f32[2,8,128]{2,1,0:T(8,128)S(1)} %get-tuple-element.28.sibling_table, ...), custom_call_target="tpu_custom_call" | custom-call | flops 8388608 | bytes 786432 | tf_op jit(solution)/shard_map/pallas_call | solution.py:452
  31.3 9.0 %all_to_all.17 = f32[32,1,128]{2,1,0:T(1,128)S(1)} all-to-all(f32[32,1,128]{2,1,0:T(1,128)S(1)} %bitcast.10), channel_id=1, replica_groups={{31,30,29,28,27,26,25,24,23,22,21,20,19,18,17,16,15,14,13,12,11,10,9,8,..., dimensions={0} | all-to-all | bytes 32768 | tf_op jit(solution)/shard_map/all_to_all | solution.py:353
  40.4 0.6 %shard_map.78 = (f32[1,512]{1,0:T(1,128)}, f32[1,128]{1,0:T(1,128)}) custom-call(f32[32,128]{1,0:T(8,128)S(1)} %bitcast.9, f32[2,128]{1,0:T(2,128)S(1)} %get-tuple-element.34.small, f32[1,512]{1,0:T(1,128)S(1)} %get-tuple-element.35.row), custom_call_target="tpu_custom_call" | custom-call | tf_op jit(solution)/shard_map/pallas_call | solution.py:462
  (3 shorter events, 0.1 us)
Async XLA Ops:
  1.6 6.3 %collective-permute-start = (bf16[72,768]{1,0:T(8,128)(2,1)S(1)}, bf16[72,768]{1,0:T(8,128)(2,1)S(1)}, u32[]{:S(2)}, u32[]{:S(2)}) collective-permute-start(bf16[72,768]{1,0:T(8,128)(2,1)S(1)} %get-tuple-element.22), channel_id=1, source_target_pairs={{8,0},{20,4},{0,8},{28,12},{24,16},{4,20},{16,24},{12,28},{9,1},{2... | collective-permute-start | bytes 331784 | tf_op jit(solution)/shard_map/ppermute | solution.py:344
  4.6 5.7 %collective-permute-start.3 = (bf16[64,768]{1,0:T(8,128)(2,1)S(1)}, bf16[64,768]{1,0:T(8,128)(2,1)S(1)}, u32[]{:S(2)}, u32[]{:S(2)}) collective-permute-start(bf16[64,768]{1,0:T(8,128)(2,1)S(1)} %get-tuple-element.23), channel_id=1, source_target_pairs={{16,0},{12,4},{24,8},{4,12},{0,16},{28,20},{8,24},{20,28},{17,1},{... | collective-permute-start | bytes 294920 | tf_op jit(solution)/shard_map/ppermute | solution.py:344
  6.1 7.3 %collective-permute-start.2 = (bf16[72,768]{1,0:T(8,128)(2,1)S(1)}, bf16[72,768]{1,0:T(8,128)(2,1)S(1)}, u32[]{:S(2)}, u32[]{:S(2)}) collective-permute-start(bf16[72,768]{1,0:T(8,128)(2,1)S(1)} %get-tuple-element.22), channel_id=1, source_target_pairs={{16,0},{12,4},{24,8},{4,12},{0,16},{28,20},{8,24},{20,28},{17,1},{... | collective-permute-start | bytes 331784 | tf_op jit(solution)/shard_map/ppermute | solution.py:344
  6.6 6.8 %collective-permute-start.1 = (bf16[64,768]{1,0:T(8,128)(2,1)S(1)}, bf16[64,768]{1,0:T(8,128)(2,1)S(1)}, u32[]{:S(2)}, u32[]{:S(2)}) collective-permute-start(bf16[64,768]{1,0:T(8,128)(2,1)S(1)} %get-tuple-element.23), channel_id=1, source_target_pairs={{8,0},{20,4},{0,8},{28,12},{24,16},{4,20},{16,24},{12,28},{9,1},{2... | collective-permute-start | bytes 294920 | tf_op jit(solution)/shard_map/ppermute | solution.py:344
  8.0 6.3 %collective-permute-start.5 = (bf16[72,768]{1,0:T(8,128)(2,1)S(1)}, bf16[72,768]{1,0:T(8,128)(2,1)S(1)}, u32[]{:S(2)}, u32[]{:S(2)}) collective-permute-start(bf16[72,768]{1,0:T(8,128)(2,1)S(1)} %collective-permute-done.a_first), channel_id=1, source_target_pairs={{16,0},{12,4},{24,8},{4,12},{0,16},{28,20},{8,24},{20,28},{17,1},{... | collective-permute-start | bytes 331784 | tf_op jit(solution)/shard_map/ppermute | solution.py:344
  10.3 4.6 %collective-permute-start.6 = (bf16[64,768]{1,0:T(8,128)(2,1)S(1)}, bf16[64,768]{1,0:T(8,128)(2,1)S(1)}, u32[]{:S(2)}, u32[]{:S(2)}) collective-permute-start(bf16[64,768]{1,0:T(8,128)(2,1)S(1)} %collective-permute-done.3.b_second), channel_id=1, source_target_pairs={{8,0},{20,4},{0,8},{28,12},{24,16},{4,20},{16,24},{12,28},{9,1},{2... | collective-permute-start | bytes 294920 | tf_op jit(solution)/shard_map/ppermute | solution.py:344
  13.5 2.1 %collective-permute-start.4 = (bf16[408,768]{1,0:T(8,128)(2,1)S(1)}, bf16[408,768]{1,0:T(8,128)(2,1)S(1)}, u32[]{:S(2)}, u32[]{:S(2)}) collective-permute-start(bf16[408,768]{1,0:T(8,128)(2,1)S(1)} %shard_map.71), channel_id=1, source_target_pairs={{4,0},{0,4},{12,8},{8,12},{20,16},{16,20},{28,24},{24,28},{5,1},{1... | collective-permute-start | bytes 1880072 | tf_op jit(solution)/shard_map/ppermute | solution.py:22
  14.3 2.3 %collective-permute-start.7 = (bf16[72,768]{1,0:T(8,128)(2,1)S(1)}, bf16[72,768]{1,0:T(8,128)(2,1)S(1)}, u32[]{:S(2)}, u32[]{:S(2)}) collective-permute-start(bf16[72,768]{1,0:T(8,128)(2,1)S(1)} %shard_map.73), channel_id=1, source_target_pairs={{4,0},{0,4},{12,8},{8,12},{20,16},{16,20},{28,24},{24,28},{5,1},{1... | collective-permute-start | bytes 331784 | tf_op jit(solution)/shard_map/ppermute | solution.py:22
  14.9 1.6 %collective-permute-start.8 = (bf16[64,768]{1,0:T(8,128)(2,1)S(1)}, bf16[64,768]{1,0:T(8,128)(2,1)S(1)}, u32[]{:S(2)}, u32[]{:S(2)}) collective-permute-start(bf16[64,768]{1,0:T(8,128)(2,1)S(1)} %shard_map.74), channel_id=1, source_target_pairs={{4,0},{0,4},{12,8},{8,12},{20,16},{16,20},{28,24},{24,28},{5,1},{1... | collective-permute-start | bytes 294920 | tf_op jit(solution)/shard_map/ppermute | solution.py:22

commit v17 on v16

--- a/solution.py
+++ b/solution.py
@@ -225,7 +225,7 @@
 
 
 def neighbour_step(me, turn):
-    step = 2 + 2 * (me % 2)
+    step = 4 - 2 * (me % 2)
     return step if turn == 0 else 6 - step
 
 

time: 41.1 us -> 41.1 us (level)
  no operation moved by 1% of the time
where the time goes in v17:
time: 41.1 us; the launch traced here: 41 us
  blocking collectives  21.6 us (53%)
  starting transfers between devices  9.85 us (24%)
  Pallas kernels  6.7 us (16%)
  waiting for transfers between devices  2.06 us (5%)
  between operations  0.76 us (2%)
    all_to_all x2, blocking collectives, exchange(): lax.all_to_all(message, ('blk', 'grp'), 0, 0, axis_index_groups=[order])  21.6 us
    ppermute x6, starting transfers between devices, along(): lax.ppermute(array, 'blk', [(i ^ neighbour_step(i, turn), i) for i in ran...  9.15 us
    pallas_call x3, Pallas kernels, scores_of(): pl.pallas_call(functools.partial(kernel, factor), out_shape=(values(rows,...  1.87 us
    pallas_call x1, Pallas kernels, shards_square(): pl.pallas_call(source_kernel, out_shape=(jax.ShapeDtypeStruct((rows, dept...  1.4 us
    ppermute x6, waiting for transfers between devices, along(): lax.ppermute(array, 'blk', [(i ^ neighbour_step(i, turn), i) for i in ran...  1.39 us
    pallas_call x1, Pallas kernels, shards_square(): pl.pallas_call(functools.partial(second_kernel, grp), out_shape=(values(1...  1.07 us
    pallas_call x1, Pallas kernels, shards_square(): pl.pallas_call(head_kernel, out_shape=(block_of(half + SPARE), block_of(h...  0.98 us
  transfers between devices with their start and end apart: 9, of which 3 were waited for; matrix products, arithmetic and copies ran while one was open for 0% of the time, Pallas kernels for 7%

profile of v17, /device:TPU:0, one launch (start us, length us, event | category | flops | bytes accessed | tf_op | source)
XLA Modules:
  0.0 41.0 jit_solution(10543483935204393119)
XLA Ops:
  0.6 1.0 %shard_map.68 = (bf16[72,768]{1,0:T(8,128)(2,1)S(1)}, bf16[64,768]{1,0:T(8,128)(2,1)S(1)}, bf16[136,768]{1,0:T(8,128)(2,1)S(1)}, f32[2,128]{1,0:T(2,128)S(1)}) custom-call(bf16[128,768]{1,0:T(8,128)(2,1)} %own.1, f32[1,128]{1,0:T(1,128)} %bitcast.12, f32[1,128]{1,0:T(1,128)} %bitcast.13), custom_call_target="tpu_custom_call" | custom-call | tf_op jit(solution)/shard_map/pallas_call | solution.py:361
  1.6 3.0 %collective-permute-start = (bf16[72,768]{1,0:T(8,128)(2,1)S(1)}, bf16[72,768]{1,0:T(8,128)(2,1)S(1)}, u32[]{:S(2)}, u32[]{:S(2)}) collective-permute-start(bf16[72,768]{1,0:T(8,128)(2,1)S(1)} %get-tuple-element.22), channel_id=1, source_target_pairs={{16,0},{12,4},{24,8},{4,12},{0,16},{28,20},{8,24},{20,28},{17,1},{... | collective-permute-start | bytes 331784 | tf_op jit(solution)/shard_map/ppermute | solution.py:344
  4.7 1.5 %collective-permute-start.3 = (bf16[64,768]{1,0:T(8,128)(2,1)S(1)}, bf16[64,768]{1,0:T(8,128)(2,1)S(1)}, u32[]{:S(2)}, u32[]{:S(2)}) collective-permute-start(bf16[64,768]{1,0:T(8,128)(2,1)S(1)} %get-tuple-element.23), channel_id=1, source_target_pairs={{8,0},{20,4},{0,8},{28,12},{24,16},{4,20},{16,24},{12,28},{9,1},{2... | collective-permute-start | bytes 294920 | tf_op jit(solution)/shard_map/ppermute | solution.py:344
  6.1 0.5 %collective-permute-start.2 = (bf16[72,768]{1,0:T(8,128)(2,1)S(1)}, bf16[72,768]{1,0:T(8,128)(2,1)S(1)}, u32[]{:S(2)}, u32[]{:S(2)}) collective-permute-start(bf16[72,768]{1,0:T(8,128)(2,1)S(1)} %get-tuple-element.22), channel_id=1, source_target_pairs={{8,0},{20,4},{0,8},{28,12},{24,16},{4,20},{16,24},{12,28},{9,1},{2... | collective-permute-start | bytes 331784 | tf_op jit(solution)/shard_map/ppermute | solution.py:344
  6.7 0.1 collective-permute-start.1
  6.8 1.3 %collective-permute-done.a_first = bf16[72,768]{1,0:T(8,128)(2,1)S(1)} collective-permute-done((bf16[72,768]{1,0:T(8,128)(2,1)S(1)}, bf16[72,768]{1,0:T(8,128)(2,1)S(1)}, u32[]{:S(2)}, u32[]{:S(2)}) %collective-permute-start) | collective-permute-done | bytes 110624 | tf_op jit(solution)/shard_map/ppermute | solution.py:344
  8.0 2.2 %collective-permute-start.5 = (bf16[72,768]{1,0:T(8,128)(2,1)S(1)}, bf16[72,768]{1,0:T(8,128)(2,1)S(1)}, u32[]{:S(2)}, u32[]{:S(2)}) collective-permute-start(bf16[72,768]{1,0:T(8,128)(2,1)S(1)} %collective-permute-done.a_first), channel_id=1, source_target_pairs={{8,0},{20,4},{0,8},{28,12},{24,16},{4,20},{16,24},{12,28},{9,1},{2... | collective-permute-start | bytes 331784 | tf_op jit(solution)/shard_map/ppermute | solution.py:344
  10.3 0.0 collective-permute-done.3.b_second
  10.3 1.8 %collective-permute-start.6 = (bf16[64,768]{1,0:T(8,128)(2,1)S(1)}, bf16[64,768]{1,0:T(8,128)(2,1)S(1)}, u32[]{:S(2)}, u32[]{:S(2)}) collective-permute-start(bf16[64,768]{1,0:T(8,128)(2,1)S(1)} %collective-permute-done.3.b_second), channel_id=1, source_target_pairs={{16,0},{12,4},{24,8},{4,12},{0,16},{28,20},{8,24},{20,28},{17,1},{... | collective-permute-start | bytes 294920 | tf_op jit(solution)/shard_map/ppermute | solution.py:344
  12.1 1.4 %shard_map.69 = (bf16[512,768]{1,0:T(8,128)(2,1)S(1)}, f32[512,128]{1,0:T(8,128)S(1)}, bf16[136,768]{1,0:T(8,128)(2,1)S(1)}) custom-call(bf16[512,768]{1,0:T(8,128)(2,1)} %source.1, f32[1,512]{1,0:T(1,128)} %bitcast.11, bf16[136,768]{1,0:T(8,128)(2,1)S(1)} %get-tuple-element.20.whole), custom_call_target="tpu_custom_call" | custom-call | tf_op jit(solution)/shard_map/pallas_call | solution.py:384
  13.5 0.0 collective-permute-done.1.a_second
  13.5 0.0 collective-permute-done.2.b_first
  13.5 0.1 collective-permute-start.4
  13.6 0.6 %shard_map.70 = (f32[512,384]{1,0:T(8,128)S(1)}, f32[2,8,128]{2,1,0:T(8,128)S(1)}) custom-call(bf16[512,768]{1,0:T(8,128)(2,1)S(1)} %get-tuple-element.21.source, bf16[136,768]{1,0:T(8,128)(2,1)S(1)} %get-tuple-element.20.whole, bf16[72,768]{1,0:T(8,128)(2,1)S(1)} %collective-permute-done.a_first, bf16[64,768]{1,0:T(8,128)(2,1)S(1)} %collective-permute-done.1.a_second, ...), custom_call_target="tpu_custom_call" | custom-call | bytes 786432 | tf_op jit(solution)/shard_map/pallas_call | solution.py:411
  14.2 0.0 collective-permute-done.5.message.far_a
  14.3 0.6 %collective-permute-start.7 = (bf16[72,768]{1,0:T(8,128)(2,1)S(1)}, bf16[72,768]{1,0:T(8,128)(2,1)S(1)}, u32[]{:S(2)}, u32[]{:S(2)}) collective-permute-start(bf16[72,768]{1,0:T(8,128)(2,1)S(1)} %shard_map.73), channel_id=1, source_target_pairs={{4,0},{0,4},{12,8},{8,12},{20,16},{16,20},{28,24},{24,28},{5,1},{1... | collective-permute-start | bytes 331784 | tf_op jit(solution)/shard_map/ppermute | solution.py:22
  14.8 0.1 collective-permute-done.6.message.far_b
  14.9 0.1 collective-permute-start.8
  15.0 0.7 %collective-permute-done.4.sibling = bf16[408,768]{1,0:T(8,128)(2,1)S(1)} collective-permute-done((bf16[408,768]{1,0:T(8,128)(2,1)S(1)}, bf16[408,768]{1,0:T(8,128)(2,1)S(1)}, u32[]{:S(2)}, u32[]{:S(2)}) %collective-permute-start.4) | collective-permute-done | bytes 626720 | tf_op jit(solution)/shard_map/ppermute | solution.py:22
  15.7 0.9 %shard_map.72 = (f32[512,384]{1,0:T(8,128)S(1)}, f32[2,8,128]{2,1,0:T(8,128)S(1)}, f32[512,128]{1,0:T(8,128)S(1)}) custom-call(bf16[512,768]{1,0:T(8,128)(2,1)S(1)} %get-tuple-element.21.source, bf16[408,768]{1,0:T(8,128)(2,1)S(1)} %collective-permute-done.4.sibling, f32[512,384]{1,0:T(8,128)S(1)} %get-tuple-element.24.own), custom_call_target="tpu_custom_call" | custom-call | bytes 786432 | tf_op jit(solution)/shard_map/pallas_call | solution.py:411
  16.5 0.0 collective-permute-done.8.sibling_b
  16.5 0.0 collective-permute-done.7.sibling_a
  16.6 0.4 %shard_map.75 = (f32[512,256]{1,0:T(8,128)S(1)}, f32[2,8,128]{2,1,0:T(8,128)S(1)}) custom-call(bf16[512,768]{1,0:T(8,128)(2,1)S(1)} %get-tuple-element.21.source, bf16[72,768]{1,0:T(8,128)(2,1)S(1)} %collective-permute-done.5.message.far_a, bf16[64,768]{1,0:T(8,128)(2,1)S(1)} %collective-permute-done.6.message.far_b, ...), custom_call_target="tpu_custom_call" | custom-call | bytes 786432 | tf_op jit(solution)/shard_map/pallas_call | solution.py:411
  17.0 0.7 %shard_map.76 = f32[32,8,128]{2,1,0:T(8,128)S(1)} custom-call(f32[512,384]{1,0:T(8,128)S(1)} %get-tuple-element.24.own, f32[2,8,128]{2,1,0:T(8,128)S(1)} %get-tuple-element.25.tie.own_table, f32[512,384]{1,0:T(8,128)S(1)} %get-tuple-element.27.near.sibling, f32[2,8,128]{2,1,0:T(8,128)S(1)} %get-tuple-element.28.sibling_table, ...), custom_call_target="tpu_custom_call" | custom-call | flops 8388608 | bytes 786432 | tf_op jit(solution)/shard_map/pallas_call | solution.py:442
  17.7 12.6 %all_to_all.16.got = f32[32,8,128]{2,1,0:T(8,128)S(1)} all-to-all(f32[32,8,128]{2,1,0:T(8,128)S(1)} %shard_map.76), channel_id=1, replica_groups={{31,30,29,28,27,26,25,24,23,22,21,20,19,18,17,16,15,14,13,12,11,10,9,8,..., dimensions={0} | all-to-all | bytes 262144 | tf_op jit(solution)/shard_map/all_to_all | solution.py:353
  30.3 1.1 %shard_map.77 = (f32[1,512]{1,0:T(1,128)S(1)}, f32[32,128]{1,0:T(8,128)S(1)}) custom-call(f32[512,384]{1,0:T(8,128)S(1)} %get-tuple-element.24.own, f32[2,8,128]{2,1,0:T(8,128)S(1)} %get-tuple-element.25.tie.own_table, f32[512,384]{1,0:T(8,128)S(1)} %get-tuple-element.27.near.sibling, f32[2,8,128]{2,1,0:T(8,128)S(1)} %get-tuple-element.28.sibling_table, ...), custom_call_target="tpu_custom_call" | custom-call | flops 8388608 | bytes 786432 | tf_op jit(solution)/shard_map/pallas_call | solution.py:452
  31.3 9.0 %all_to_all.17 = f32[32,1,128]{2,1,0:T(1,128)S(1)} all-to-all(f32[32,1,128]{2,1,0:T(1,128)S(1)} %bitcast.10), channel_id=1, replica_groups={{31,30,29,28,27,26,25,24,23,22,21,20,19,18,17,16,15,14,13,12,11,10,9,8,..., dimensions={0} | all-to-all | bytes 32768 | tf_op jit(solution)/shard_map/all_to_all | solution.py:353
  40.4 0.6 %shard_map.78 = (f32[1,512]{1,0:T(1,128)}, f32[1,128]{1,0:T(1,128)}) custom-call(f32[32,128]{1,0:T(8,128)S(1)} %bitcast.9, f32[2,128]{1,0:T(2,128)S(1)} %get-tuple-element.34.small, f32[1,512]{1,0:T(1,128)S(1)} %get-tuple-element.35.row), custom_call_target="tpu_custom_call" | custom-call | tf_op jit(solution)/shard_map/pallas_call | solution.py:462
  (3 shorter events, 0.1 us)
Async XLA Ops:
  1.6 6.4 %collective-permute-start = (bf16[72,768]{1,0:T(8,128)(2,1)S(1)}, bf16[72,768]{1,0:T(8,128)(2,1)S(1)}, u32[]{:S(2)}, u32[]{:S(2)}) collective-permute-start(bf16[72,768]{1,0:T(8,128)(2,1)S(1)} %get-tuple-element.22), channel_id=1, source_target_pairs={{16,0},{12,4},{24,8},{4,12},{0,16},{28,20},{8,24},{20,28},{17,1},{... | collective-permute-start | bytes 331784 | tf_op jit(solution)/shard_map/ppermute | solution.py:344
  4.7 5.6 %collective-permute-start.3 = (bf16[64,768]{1,0:T(8,128)(2,1)S(1)}, bf16[64,768]{1,0:T(8,128)(2,1)S(1)}, u32[]{:S(2)}, u32[]{:S(2)}) collective-permute-start(bf16[64,768]{1,0:T(8,128)(2,1)S(1)} %get-tuple-element.23), channel_id=1, source_target_pairs={{8,0},{20,4},{0,8},{28,12},{24,16},{4,20},{16,24},{12,28},{9,1},{2... | collective-permute-start | bytes 294920 | tf_op jit(solution)/shard_map/ppermute | solution.py:344
  6.1 7.3 %collective-permute-start.2 = (bf16[72,768]{1,0:T(8,128)(2,1)S(1)}, bf16[72,768]{1,0:T(8,128)(2,1)S(1)}, u32[]{:S(2)}, u32[]{:S(2)}) collective-permute-start(bf16[72,768]{1,0:T(8,128)(2,1)S(1)} %get-tuple-element.22), channel_id=1, source_target_pairs={{8,0},{20,4},{0,8},{28,12},{24,16},{4,20},{16,24},{12,28},{9,1},{2... | collective-permute-start | bytes 331784 | tf_op jit(solution)/shard_map/ppermute | solution.py:344
  6.7 6.8 %collective-permute-start.1 = (bf16[64,768]{1,0:T(8,128)(2,1)S(1)}, bf16[64,768]{1,0:T(8,128)(2,1)S(1)}, u32[]{:S(2)}, u32[]{:S(2)}) collective-permute-start(bf16[64,768]{1,0:T(8,128)(2,1)S(1)} %get-tuple-element.23), channel_id=1, source_target_pairs={{16,0},{12,4},{24,8},{4,12},{0,16},{28,20},{8,24},{20,28},{17,1},{... | collective-permute-start | bytes 294920 | tf_op jit(solution)/shard_map/ppermute | solution.py:344
  8.0 6.2 %collective-permute-start.5 = (bf16[72,768]{1,0:T(8,128)(2,1)S(1)}, bf16[72,768]{1,0:T(8,128)(2,1)S(1)}, u32[]{:S(2)}, u32[]{:S(2)}) collective-permute-start(bf16[72,768]{1,0:T(8,128)(2,1)S(1)} %collective-permute-done.a_first), channel_id=1, source_target_pairs={{8,0},{20,4},{0,8},{28,12},{24,16},{4,20},{16,24},{12,28},{9,1},{2... | collective-permute-start | bytes 331784 | tf_op jit(solution)/shard_map/ppermute | solution.py:344
  10.3 4.6 %collective-permute-start.6 = (bf16[64,768]{1,0:T(8,128)(2,1)S(1)}, bf16[64,768]{1,0:T(8,128)(2,1)S(1)}, u32[]{:S(2)}, u32[]{:S(2)}) collective-permute-start(bf16[64,768]{1,0:T(8,128)(2,1)S(1)} %collective-permute-done.3.b_second), channel_id=1, source_target_pairs={{16,0},{12,4},{24,8},{4,12},{0,16},{28,20},{8,24},{20,28},{17,1},{... | collective-permute-start | bytes 294920 | tf_op jit(solution)/shard_map/ppermute | solution.py:344
  13.5 2.1 %collective-permute-start.4 = (bf16[408,768]{1,0:T(8,128)(2,1)S(1)}, bf16[408,768]{1,0:T(8,128)(2,1)S(1)}, u32[]{:S(2)}, u32[]{:S(2)}) collective-permute-start(bf16[408,768]{1,0:T(8,128)(2,1)S(1)} %shard_map.71), channel_id=1, source_target_pairs={{4,0},{0,4},{12,8},{8,12},{20,16},{16,20},{28,24},{24,28},{5,1},{1... | collective-permute-start | bytes 1880072 | tf_op jit(solution)/shard_map/ppermute | solution.py:22
  14.3 2.3 %collective-permute-start.7 = (bf16[72,768]{1,0:T(8,128)(2,1)S(1)}, bf16[72,768]{1,0:T(8,128)(2,1)S(1)}, u32[]{:S(2)}, u32[]{:S(2)}) collective-permute-start(bf16[72,768]{1,0:T(8,128)(2,1)S(1)} %shard_map.73), channel_id=1, source_target_pairs={{4,0},{0,4},{12,8},{8,12},{20,16},{16,20},{28,24},{24,28},{5,1},{1... | collective-permute-start | bytes 331784 | tf_op jit(solution)/shard_map/ppermute | solution.py:22
  14.9 1.6 %collective-permute-start.8 = (bf16[64,768]{1,0:T(8,128)(2,1)S(1)}, bf16[64,768]{1,0:T(8,128)(2,1)S(1)}, u32[]{:S(2)}, u32[]{:S(2)}) collective-permute-start(bf16[64,768]{1,0:T(8,128)(2,1)S(1)} %shard_map.74), channel_id=1, source_target_pairs={{4,0},{0,4},{12,8},{8,12},{20,16},{16,20},{28,24},{24,28},{5,1},{1... | collective-permute-start | bytes 294920 | tf_op jit(solution)/shard_map/ppermute | solution.py:22
